TPU v7x, 32 devices: a whole 2x2x4 slice. The times are simulated.
32 devices in a mesh: dp: 16 (over z, y, core), tensor: 2 (over x).
Axes of the slice: x: 2, y: 2, z: 4, core: 2. Of those that a mesh axis runs over, the one named last changes fastest.
Arguments:
- tokens: bfloat16 [16384, 1024], P('dp'), may hold values from -6 to 6
- segments: int32 [16, 1024], P('dp'), may hold values from 0 to 3, never falling along the last dimension, each value on 1 to 800 neighbouring positions
- cotangent: bfloat16 [16384, 1024], P('dp'), may hold values from -6 to 6
- input_gain: bfloat16 [1024], replicated, may hold values from 0.5 to 1.5
- query_weight: bfloat16 [1024, 512], P(None, 'tensor'), may hold values from -0.1875 to 0.1875
- key_value_weight: bfloat16 [1024, 256], replicated, may hold values from -0.1875 to 0.1875
- attnout_weight: bfloat16 [512, 1024], P('tensor'), may hold values from -0.75 to 0.75
- gating_weight: bfloat16 [1024, 1536], P(None, 'tensor'), may hold values from -0.1875 to 0.1875
- inner_weight: bfloat16 [1024, 1536], P(None, 'tensor'), may hold values from -0.1875 to 0.1875
- state_weight: bfloat16 [1024, 256], replicated, may hold values from -0.1875 to 0.1875
- step_weight: bfloat16 [1024, 24], P(None, 'tensor'), may hold values from -0.1875 to 0.1875
- conv_inner: bfloat16 [4, 1536], P(None, 'tensor'), may hold values from -3 to 3
- conv_state: bfloat16 [4, 256], replicated, may hold values from -3 to 3
- inner_bias: bfloat16 [1536], P('tensor'), may hold values from -0.5 to 0.5
- state_bias: bfloat16 [256], replicated, may hold values from -0.5 to 0.5
- step_bias: bfloat16 [24], P('tensor'), may hold values from -5 to -1
- decay_log: bfloat16 [24], P('tensor'), may hold values from 0 to 2.765625
- skip_scale: bfloat16 [24], P('tensor'), may hold values from 0.5 to 1.5
- mixer_gain: bfloat16 [1536], P('tensor'), may hold values from 0.5 to 1.5
- mixer_out: bfloat16 [1536, 1024], P('tensor'), may hold values from -0.15625 to 0.15625
- post_gain: bfloat16 [1024], replicated, may hold values from 0.5 to 1.5
- gate_weight: bfloat16 [1024, 2048], P(None, 'tensor'), may hold values from -0.1875 to 0.1875
- up_weight: bfloat16 [1024, 2048], P(None, 'tensor'), may hold values from -0.1875 to 0.1875
- down_weight: bfloat16 [2048, 1024], P('tensor'), may hold values from -0.125 to 0.125
Outputs:
- tokens_grad: float32 [16384, 1024], P('dp')
- input_gain_grad: float32 [1024], replicated
- query_grad: float32 [1024, 512], P(None, 'tensor')
- keyval_grad: float32 [1024, 256], replicated
- attnout_grad: float32 [512, 1024], P('tensor')
- gating_grad: float32 [1024, 1536], P(None, 'tensor')
- inner_grad: float32 [1024, 1536], P(None, 'tensor')
- state_grad: float32 [1024, 256], replicated
- step_grad: float32 [1024, 24], P(None, 'tensor')
- conv_inner_grad: float32 [4, 1536], P(None, 'tensor')
- conv_state_grad: float32 [4, 256], replicated
- inner_bias_grad: float32 [1536], P('tensor')
- state_bias_grad: float32 [256], replicated
- step_bias_grad: float32 [24], P('tensor')
- decay_grad: float32 [24], P('tensor')
- skip_grad: float32 [24], P('tensor')
- mixer_gain_grad: float32 [1536], P('tensor')
- mixer_out_grad: float32 [1536, 1024], P('tensor')
- post_gain_grad: float32 [1024], replicated
- gate_grad: float32 [1024, 2048], P(None, 'tensor')
- up_grad: float32 [1024, 2048], P(None, 'tensor')
- down_grad: float32 [2048, 1024], P('tensor')
Inputs may be any that keep to these rules, and one draw needn't show every extreme that they name: `segments`: within a sequence the numbers never fall; a document holds 1 to 1024 * 25 // 32 tokens and one holds exactly that many.
All inputs are finite; a program needn't handle non-finite values.
Results may differ from a plain program's by a relative error of at most 0.028.
Values may be sent and summed in bfloat16 or wider, within the bound.
No kernel may reach another device: no remote copies, remote signals or barrier semaphores. Data moves between devices by JAX's collectives and lax.ppermute only.
A program may use at most 192 MiB of HBM per device.

v0:
```python
import jax
import jax.numpy as jnp
from jax import lax
from jax.sharding import PartitionSpec as P

QUERY_HEADS = 8
KEYVALUE_HEADS = 2
HEAD_SIZE = 64
P_SIZE = 64
NS = 128
DSSM = 1536


EPS = 1e-05
ROPE_BASE = 100000000000.0
NEG_FILL = -1e30


def matmul(left, right):
    return jnp.dot(left, right, preferred_element_type=jnp.float32)


def rotary_tables(document_length):
    half = HEAD_SIZE // 2
    freqs = jnp.exp(-jnp.log(ROPE_BASE) * (2.0 * jnp.arange(half, dtype=jnp.float32) / HEAD_SIZE))
    angles = jnp.arange(document_length, dtype=jnp.float32)[:, None] * freqs[None, :]
    return (jnp.cos(angles), jnp.sin(angles))


def rotate(value, cosine, sine):
    half = value.shape[-1] // 2
    first = value[..., :half]
    second = value[..., half:]
    return jnp.concatenate([first * cosine - second * sine, first * sine + second * cosine], -1)


def rotate_back(grad, cosine, sine):
    half = grad.shape[-1] // 2
    first = grad[..., :half]
    second = grad[..., half:]
    return jnp.concatenate([first * cosine + second * sine, second * cosine - first * sine], -1)


def silu_slope(value):
    sigma = jax.nn.sigmoid(value)
    return sigma * (1.0 + value * (1.0 - sigma))


def seg_keep(segments, offset):
    document_length = segments.shape[1]
    moved = jnp.pad(segments, ((0, 0), (offset, 0)), constant_values=-1)[:, :document_length]
    return (moved == segments).astype(jnp.float32)[:, :, None]


def move_down(value, offset):
    document_length = value.shape[1]
    return jnp.pad(value, ((0, 0), (offset, 0), (0, 0)))[:, :document_length]


def move_up(value, offset):
    return jnp.pad(value, ((0, 0), (0, offset), (0, 0)))[:, offset:]


def conv_forward(value, kernel, bias, segments):
    taps = kernel.shape[0]
    total = jnp.zeros_like(value) + bias.astype(jnp.float32)
    for tap in range(taps):
        offset = taps - 1 - tap
        total = total + kernel[tap].astype(jnp.float32) * move_down(value, offset) * seg_keep(
            segments, offset
        )
    return total


def conv_backward(grad, value, kernel, segments):
    taps = kernel.shape[0]
    grad_in = jnp.zeros_like(value)
    kernel_rows = []
    for tap in range(taps):
        offset = taps - 1 - tap
        masked = grad * seg_keep(segments, offset)
        kernel_rows.append(jnp.sum(masked * move_down(value, offset), axis=(0, 1)))
        grad_in = grad_in + kernel[tap].astype(jnp.float32) * move_up(masked, offset)
    return (grad_in, jnp.stack(kernel_rows))


def ssd_parts(step_block, rate, coef_b, coef_c, heads_block, allowed):
    coupling = jnp.einsum("tn,sn->ts", coef_c, coef_b, preferred_element_type=jnp.float32)
    cumulative = jnp.cumsum(step_block * rate, axis=0).T
    difference = cumulative[:, :, None] - cumulative[:, None, :]
    decay = jnp.where(allowed[None], jnp.exp(jnp.where(allowed[None], difference, 0.0)), 0.0)
    mixing = (coupling[None] * decay).astype(jnp.bfloat16)
    driven = (heads_block * step_block.T[:, :, None]).astype(jnp.bfloat16)
    return (coupling, decay, mixing, driven)


def local(
    tokens,
    segments,
    cotangent,
    input_gain,
    query_weight,
    key_value_weight,
    attnout_weight,
    gating_weight,
    inner_weight,
    state_weight,
    step_weight,
    conv_inner,
    conv_state,
    inner_bias,
    state_bias,
    step_bias,
    decay_log,
    skip_scale,
    mixer_gain,
    mixer_out,
    post_gain,
    gate_weight,
    up_weight,
    down_weight,
):
    seq_count, document_length = segments.shape
    rows = seq_count * document_length
    heads = query_weight.shape[1] // HEAD_SIZE
    ssm_heads = step_weight.shape[1]
    query_group = QUERY_HEADS // KEYVALUE_HEADS
    shared_key_head = lax.axis_index("tensor") * heads // query_group
    scale = HEAD_SIZE ** (-0.5)
    cosine, sine = rotary_tables(document_length)
    positions = jnp.arange(document_length)

    def allowed_of(seg_ids):
        return (positions[:, None] >= positions[None, :]) & (seg_ids[:, None] == seg_ids[None, :])

    inputs = tokens.astype(jnp.float32)
    inv_first = lax.rsqrt(jnp.mean(inputs * inputs, -1, keepdims=True) + EPS)
    unit_first = inputs * inv_first
    in_gain = input_gain.astype(jnp.float32)
    normed = (unit_first * in_gain).astype(jnp.bfloat16)
    key_cols = lax.dynamic_slice_in_dim(key_value_weight, shared_key_head * HEAD_SIZE, HEAD_SIZE, 1)
    value_columns = lax.dynamic_slice_in_dim(
        key_value_weight, (KEYVALUE_HEADS + shared_key_head) * HEAD_SIZE, HEAD_SIZE, 1
    )
    query_pre = matmul(normed, query_weight)
    key_pre = matmul(normed, key_cols)
    value_pre = matmul(normed, value_columns)
    queries = rotate(
        query_pre.reshape(seq_count, document_length, heads, HEAD_SIZE).transpose(0, 2, 1, 3),
        cosine,
        sine,
    ).astype(jnp.bfloat16)
    key_rows = rotate(key_pre.reshape(seq_count, document_length, HEAD_SIZE), cosine, sine).astype(
        jnp.bfloat16
    )
    value_rows = value_pre.reshape(seq_count, document_length, HEAD_SIZE).astype(jnp.bfloat16)

    def attend(seq_item):
        query_block, key_block, value_block, seg_ids = seq_item
        allowed = allowed_of(seg_ids)[None]
        scores = (
            jnp.einsum("htd,sd->hts", query_block, key_block, preferred_element_type=jnp.float32)
            * scale
        )
        scores = jnp.where(allowed, scores, NEG_FILL)
        top = jnp.max(scores, -1, keepdims=True)
        weights = jnp.exp(scores - top)
        total = jnp.sum(weights, -1, keepdims=True)
        probs = (weights / total).astype(jnp.bfloat16)
        attended = jnp.einsum("hts,sd->htd", probs, value_block, preferred_element_type=jnp.float32)
        return (attended.astype(jnp.bfloat16), (top + jnp.log(total))[..., 0])

    attended, logsum = lax.map(attend, (queries, key_rows, value_rows, segments))
    attn_flat = attended.transpose(0, 2, 1, 3).reshape(rows, heads * HEAD_SIZE)
    attn_part = matmul(attn_flat, attnout_weight)
    gating = matmul(normed, gating_weight)
    inner = matmul(normed, inner_weight).reshape(seq_count, document_length, -1)
    state_in = matmul(normed, state_weight).reshape(seq_count, document_length, -1)
    step_raw = matmul(normed, step_weight)
    inner_pre = conv_forward(inner, conv_inner, inner_bias, segments)
    inner_act = jax.nn.silu(inner_pre)
    state_pre = conv_forward(state_in, conv_state, state_bias, segments)
    state_act = jax.nn.silu(state_pre)
    coef_b = state_act[..., :NS].astype(jnp.bfloat16)
    coef_c = state_act[..., NS:].astype(jnp.bfloat16)
    step_arg = step_raw.reshape(seq_count, document_length, ssm_heads) + step_bias.astype(
        jnp.float32
    )
    step = jax.nn.softplus(step_arg)
    rate = -jnp.exp(decay_log.astype(jnp.float32))
    heads_in = inner_act.reshape(seq_count, document_length, ssm_heads, P_SIZE).transpose(
        0, 2, 1, 3
    )

    def scan_forward(seq_item):
        step_block, coef_b_block, coef_c_block, heads_block, seg_ids = seq_item
        parts = ssd_parts(
            step_block, rate, coef_b_block, coef_c_block, heads_block, allowed_of(seg_ids)
        )
        return jnp.einsum("hts,hsp->htp", parts[2], parts[3], preferred_element_type=jnp.float32)

    core = lax.map(scan_forward, (step, coef_b, coef_c, heads_in, segments))
    skip = skip_scale.astype(jnp.float32)[None, :, None, None]
    ssm_out = (core + skip * heads_in).transpose(0, 2, 1, 3).reshape(rows, ssm_heads * P_SIZE)
    sigma_gate = jax.nn.sigmoid(gating)
    gate_act = gating * sigma_gate
    gated = ssm_out * gate_act
    square_sum = lax.psum(jnp.sum(gated * gated, -1, keepdims=True), "tensor")
    inv_gate = lax.rsqrt(square_sum / DSSM + EPS)
    mixer_scale = mixer_gain.astype(jnp.float32)
    mixed = (gated * inv_gate * mixer_scale).astype(jnp.bfloat16)
    branch_part = attn_part + matmul(mixed, mixer_out)
    out_gain = post_gain.astype(jnp.float32)
    branch = lax.psum(branch_part.astype(jnp.bfloat16), "tensor").astype(jnp.float32)
    middle = inputs + branch
    inv_second = lax.rsqrt(jnp.mean(middle * middle, -1, keepdims=True) + EPS)
    unit_second = middle * inv_second
    post = (unit_second * out_gain).astype(jnp.bfloat16)
    gate = matmul(post, gate_weight)
    upward = matmul(post, up_weight)
    sigma = jax.nn.sigmoid(gate)
    hidden = (gate * sigma * upward).astype(jnp.bfloat16)
    down_wgrad = jnp.einsum("tf,td->fd", hidden, cotangent, preferred_element_type=jnp.float32)
    hidden_grad = jnp.einsum(
        "td,fd->tf", cotangent, down_weight, preferred_element_type=jnp.float32
    )
    up_act_grad = (hidden_grad * gate * sigma).astype(jnp.bfloat16)
    gate_act_grad = (hidden_grad * upward * sigma * (1.0 + gate * (1.0 - sigma))).astype(
        jnp.bfloat16
    )
    gate_wgrad = jnp.einsum("tc,tf->cf", post, gate_act_grad, preferred_element_type=jnp.float32)
    up_wgrad = jnp.einsum("tc,tf->cf", post, up_act_grad, preferred_element_type=jnp.float32)
    post_part = jnp.einsum(
        "tf,cf->tc", gate_act_grad, gate_weight, preferred_element_type=jnp.float32
    ) + jnp.einsum("tf,cf->tc", up_act_grad, up_weight, preferred_element_type=jnp.float32)
    post_gain_part = jnp.sum(post_part * unit_second, 0)
    post_full = lax.psum(post_part.astype(jnp.bfloat16), "tensor").astype(jnp.float32)
    scaled_post = post_full * out_gain
    middle_grad = cotangent.astype(jnp.float32) + inv_second * (
        scaled_post - unit_second * jnp.mean(scaled_post * unit_second, -1, keepdims=True)
    )
    branch_grad = middle_grad.astype(jnp.bfloat16)
    attnout_wgrad = jnp.einsum(
        "tk,td->kd", attn_flat, branch_grad, preferred_element_type=jnp.float32
    )
    attended_grad = jnp.einsum(
        "td,kd->tk", branch_grad, attnout_weight, preferred_element_type=jnp.float32
    )
    attended_grad = (
        attended_grad.astype(jnp.bfloat16)
        .reshape(seq_count, document_length, heads, HEAD_SIZE)
        .transpose(0, 2, 1, 3)
    )

    def attend_back(seq_item):
        query_block, key_block, value_block, seg_ids, logsum_block, grad_block = seq_item
        allowed = allowed_of(seg_ids)[None]
        scores = (
            jnp.einsum("htd,sd->hts", query_block, key_block, preferred_element_type=jnp.float32)
            * scale
        )
        probs = jnp.where(allowed, jnp.exp(scores - logsum_block[..., None]), 0.0)
        value_grad = jnp.einsum(
            "hts,htd->hsd",
            probs.astype(jnp.bfloat16),
            grad_block,
            preferred_element_type=jnp.float32,
        )
        prob_grad = jnp.einsum(
            "htd,sd->hts", grad_block, value_block, preferred_element_type=jnp.float32
        )
        delta = jnp.sum(probs * prob_grad, -1, keepdims=True)
        score_grad = (probs * (prob_grad - delta)).astype(jnp.bfloat16)
        query_grad = (
            jnp.einsum("hts,sd->htd", score_grad, key_block, preferred_element_type=jnp.float32)
            * scale
        )
        key_grad = (
            jnp.einsum("hts,htd->hsd", score_grad, query_block, preferred_element_type=jnp.float32)
            * scale
        )
        return (query_grad, key_grad, value_grad)

    query_rot_grad, key_rot_grad, value_head_grad = lax.map(
        attend_back, (queries, key_rows, value_rows, segments, logsum, attended_grad)
    )
    query_pre_grad = (
        rotate_back(query_rot_grad, cosine, sine)
        .astype(jnp.bfloat16)
        .transpose(0, 2, 1, 3)
        .reshape(rows, heads * HEAD_SIZE)
    )
    key_pre_grad = rotate_back(key_rot_grad, cosine, sine).astype(jnp.bfloat16)
    value_pre_grad = value_head_grad.astype(jnp.bfloat16)
    normed_seq = normed.reshape(seq_count, document_length, -1)
    query_wgrad = jnp.einsum(
        "tc,tk->ck", normed, query_pre_grad, preferred_element_type=jnp.float32
    )
    key_wgrad = jnp.einsum(
        "slc,shld->cd", normed_seq, key_pre_grad, preferred_element_type=jnp.float32
    )
    value_weight_grad = jnp.einsum(
        "slc,shld->cd", normed_seq, value_pre_grad, preferred_element_type=jnp.float32
    )
    key_value_weight_grad = jnp.zeros(key_value_weight.shape, jnp.float32)
    key_value_weight_grad = lax.dynamic_update_slice_in_dim(
        key_value_weight_grad, key_wgrad, shared_key_head * HEAD_SIZE, 1
    )
    key_value_weight_grad = lax.dynamic_update_slice_in_dim(
        key_value_weight_grad, value_weight_grad, (KEYVALUE_HEADS + shared_key_head) * HEAD_SIZE, 1
    )
    normed_part = (
        jnp.einsum("tk,ck->tc", query_pre_grad, query_weight, preferred_element_type=jnp.float32)
        + jnp.einsum(
            "shld,cd->slc", key_pre_grad, key_cols, preferred_element_type=jnp.float32
        ).reshape(rows, -1)
        + jnp.einsum(
            "shld,cd->slc", value_pre_grad, value_columns, preferred_element_type=jnp.float32
        ).reshape(rows, -1)
    )
    mixout_wgrad = jnp.einsum("tk,td->kd", mixed, branch_grad, preferred_element_type=jnp.float32)
    mixed_grad = jnp.einsum("td,kd->tk", branch_grad, mixer_out, preferred_element_type=jnp.float32)
    mixer_gain_wgrad = jnp.sum(mixed_grad * gated * inv_gate, 0)
    weighted = mixed_grad * mixer_scale
    cross = lax.psum(jnp.sum(weighted * gated, -1, keepdims=True), "tensor")
    gated_grad = inv_gate * weighted - gated * (inv_gate * inv_gate * inv_gate) * cross / DSSM
    ssm_grad = gated_grad * gate_act
    gating_act_grad = (
        gated_grad * ssm_out * sigma_gate * (1.0 + gating * (1.0 - sigma_gate))
    ).astype(jnp.bfloat16)
    ssm_heads_grad = ssm_grad.reshape(seq_count, document_length, ssm_heads, P_SIZE).transpose(
        0, 2, 1, 3
    )
    core_grad = ssm_heads_grad.astype(jnp.bfloat16)
    skip_wgrad = jnp.sum(ssm_heads_grad * heads_in, axis=(0, 2, 3))

    def scan_back(seq_item):
        step_block, coef_b_block, coef_c_block, heads_block, seg_ids, core_block = seq_item
        coupling, decay, mixing, driven = ssd_parts(
            step_block, rate, coef_b_block, coef_c_block, heads_block, allowed_of(seg_ids)
        )
        mix_grad = jnp.einsum(
            "htp,hsp->hts", core_block, driven, preferred_element_type=jnp.float32
        )
        driven_grad = jnp.einsum(
            "hts,htp->hsp", mixing, core_block, preferred_element_type=jnp.float32
        )
        rounded = (mix_grad * decay).astype(jnp.bfloat16)
        coef_c_grad = jnp.einsum(
            "hts,sn->tn", rounded, coef_b_block, preferred_element_type=jnp.float32
        )
        coef_b_grad = jnp.einsum(
            "hts,tn->sn", rounded, coef_c_block, preferred_element_type=jnp.float32
        )
        spread = mix_grad * coupling[None] * decay
        cumulative_grad = jnp.sum(spread, 2) - jnp.sum(spread, 1)
        log_grad = jnp.flip(jnp.cumsum(jnp.flip(cumulative_grad, 1), 1), 1)
        heads_grad = driven_grad * step_block.T[:, :, None]
        step_grad = (jnp.sum(driven_grad * heads_block, -1) + log_grad * rate[:, None]).T
        rate_grad = jnp.sum(log_grad * step_block.T, 1)
        return (heads_grad, step_grad, rate_grad, coef_b_grad, coef_c_grad)

    heads_grad, step_grad, rate_grad, coef_b_grad, coef_c_grad = lax.map(
        scan_back, (step, coef_b, coef_c, heads_in, segments, core_grad)
    )
    heads_total = heads_grad + ssm_heads_grad * skip
    inner_act_grad = heads_total.transpose(0, 2, 1, 3).reshape(seq_count, document_length, -1)
    step_total = step_grad * jax.nn.sigmoid(step_arg)
    step_bias_wgrad = jnp.sum(step_total, axis=(0, 1))
    decay_wgrad = jnp.sum(rate_grad, 0) * rate
    step_raw_grad = step_total.reshape(rows, ssm_heads).astype(jnp.bfloat16)
    inner_pre_grad = inner_act_grad * silu_slope(inner_pre)
    inner_bias_wgrad = jnp.sum(inner_pre_grad, axis=(0, 1))
    inner_grad, conv_inner_wgrad = conv_backward(inner_pre_grad, inner, conv_inner, segments)
    inner_grad = inner_grad.reshape(rows, -1).astype(jnp.bfloat16)
    state_act_grad = jnp.concatenate([coef_b_grad, coef_c_grad], -1)
    state_pre_grad = state_act_grad * silu_slope(state_pre)
    state_bias_wgrad = jnp.sum(state_pre_grad, axis=(0, 1))
    state_grad, conv_state_wgrad = conv_backward(state_pre_grad, state_in, conv_state, segments)
    state_grad = state_grad.reshape(rows, -1).astype(jnp.bfloat16)
    gating_wgrad = jnp.einsum(
        "tc,tk->ck", normed, gating_act_grad, preferred_element_type=jnp.float32
    )
    inner_wgrad = jnp.einsum("tc,tk->ck", normed, inner_grad, preferred_element_type=jnp.float32)
    step_wgrad = jnp.einsum("tc,tk->ck", normed, step_raw_grad, preferred_element_type=jnp.float32)
    state_wgrad = jnp.einsum("tc,tk->ck", normed, state_grad, preferred_element_type=jnp.float32)
    normed_part = (
        normed_part
        + jnp.einsum(
            "tk,ck->tc", gating_act_grad, gating_weight, preferred_element_type=jnp.float32
        )
        + jnp.einsum("tk,ck->tc", inner_grad, inner_weight, preferred_element_type=jnp.float32)
        + jnp.einsum("tk,ck->tc", step_raw_grad, step_weight, preferred_element_type=jnp.float32)
        + jnp.einsum("tk,ck->tc", state_grad, state_weight, preferred_element_type=jnp.float32)
    )
    input_gain_part = jnp.sum(normed_part * unit_first, 0)
    normed_full = lax.psum(normed_part.astype(jnp.bfloat16), "tensor").astype(jnp.float32)
    scaled_in = normed_full * in_gain
    tokens_grad = middle_grad + inv_first * (
        scaled_in - unit_first * jnp.mean(scaled_in * unit_first, -1, keepdims=True)
    )
    (
        query_wgrad,
        attnout_wgrad,
        gating_wgrad,
        inner_wgrad,
        step_wgrad,
        conv_inner_wgrad,
        inner_bias_wgrad,
        step_bias_wgrad,
        decay_wgrad,
        skip_wgrad,
        mixer_gain_wgrad,
        mixout_wgrad,
        gate_wgrad,
        up_wgrad,
        down_wgrad,
    ) = (
        lax.psum(query_wgrad.astype(jnp.bfloat16), "dp").astype(jnp.float32),
        lax.psum(attnout_wgrad.astype(jnp.bfloat16), "dp").astype(jnp.float32),
        lax.psum(gating_wgrad.astype(jnp.bfloat16), "dp").astype(jnp.float32),
        lax.psum(inner_wgrad.astype(jnp.bfloat16), "dp").astype(jnp.float32),
        lax.psum(step_wgrad.astype(jnp.bfloat16), "dp").astype(jnp.float32),
        lax.psum(conv_inner_wgrad.astype(jnp.bfloat16), "dp").astype(jnp.float32),
        lax.psum(inner_bias_wgrad.astype(jnp.bfloat16), "dp").astype(jnp.float32),
        lax.psum(step_bias_wgrad.astype(jnp.bfloat16), "dp").astype(jnp.float32),
        lax.psum(decay_wgrad.astype(jnp.bfloat16), "dp").astype(jnp.float32),
        lax.psum(skip_wgrad.astype(jnp.bfloat16), "dp").astype(jnp.float32),
        lax.psum(mixer_gain_wgrad.astype(jnp.bfloat16), "dp").astype(jnp.float32),
        lax.psum(mixout_wgrad.astype(jnp.bfloat16), "dp").astype(jnp.float32),
        lax.psum(gate_wgrad.astype(jnp.bfloat16), "dp").astype(jnp.float32),
        lax.psum(up_wgrad.astype(jnp.bfloat16), "dp").astype(jnp.float32),
        lax.psum(down_wgrad.astype(jnp.bfloat16), "dp").astype(jnp.float32),
    )
    (
        key_value_weight_grad,
        state_wgrad,
        conv_state_wgrad,
        state_bias_wgrad,
        input_gain_part,
        post_gain_part,
    ) = lax.psum(
        (
            key_value_weight_grad,
            state_wgrad,
            conv_state_wgrad,
            state_bias_wgrad,
            input_gain_part,
            post_gain_part,
        ),
        ("dp", "tensor"),
    )
    return (
        tokens_grad,
        input_gain_part,
        query_wgrad,
        key_value_weight_grad,
        attnout_wgrad,
        gating_wgrad,
        inner_wgrad,
        state_wgrad,
        step_wgrad,
        conv_inner_wgrad,
        conv_state_wgrad,
        inner_bias_wgrad,
        state_bias_wgrad,
        step_bias_wgrad,
        decay_wgrad,
        skip_wgrad,
        mixer_gain_wgrad,
        mixout_wgrad,
        post_gain_part,
        gate_wgrad,
        up_wgrad,
        down_wgrad,
    )


def solution(mesh):
    placed = (
        P("dp", None),
        P("dp", None),
        P("dp", None),
        P(),
        P(None, "tensor"),
        P(),
        P("tensor", None),
        P(None, "tensor"),
        P(None, "tensor"),
        P(),
        P(None, "tensor"),
        P(None, "tensor"),
        P(),
        P("tensor"),
        P(),
        P("tensor"),
        P("tensor"),
        P("tensor"),
        P("tensor"),
        P("tensor", None),
        P(),
        P(None, "tensor"),
        P(None, "tensor"),
        P("tensor", None),
    )
    return jax.shard_map(
        local,
        mesh=mesh,
        in_specs=placed,
        out_specs=(
            P("dp", None),
            P(),
            P(None, "tensor"),
            P(),
            P("tensor", None),
            P(None, "tensor"),
            P(None, "tensor"),
            P(),
            P(None, "tensor"),
            P(None, "tensor"),
            P(),
            P("tensor"),
            P(),
            P("tensor"),
            P("tensor"),
            P("tensor"),
            P("tensor"),
            P("tensor", None),
            P(),
            P(None, "tensor"),
            P(None, "tensor"),
            P("tensor", None),
        ),
        check_vma=False,
    )
```

profile of v0, /device:TPU:0, one launch (start us, length us, event | category | flops | bytes accessed | tf_op | source)
XLA Modules:
  0.0 881.8 jit_solution(154024279300663042)
XLA Ops:
  21.6 2.6 copy.77
  29.0 3.4 reduce-window.14
  47.6 2.7 fusion.73
  50.4 4.3 fusion.34
  54.7 3.6 copy.80
  58.2 19.1 %bitcast_add_fusion.1 = f32[1,12,1024,64]{2,3,1,0:T(8,128)} fusion(f32[1,12,1024,64]{2,3,1,0:T(8,128)} %bitcast.229, f32[12,1024]{1,0:T(8,128)S(1)} %bitcast.263, f32[1024,1024]{1,0:T(8,128)} %fusion.73, pred[1024,1024]{1,0:T(8,128)(4,1)} %copy.77, f32[12]{0:T(128)S(1)} %copy-done.141, f32[12,1024,64]{1,2,0:T(8,128)} %bitcast.230, ...), kind=kOutput, calls=%fused_computation.69 | convolution fusion | flops 1676673024 | bytes 14778416 | tf_op jit(solution)/shard_map/while/body/eval_jaxpr/hts,hsp->htp/dot_general | solution.py:200
  77.4 7.5 multiply_reduce_fusion.12
  84.9 6.0 psum.182
  92.4 4.2 select_reduce_fusion
  96.6 3.7 fusion.4
  102.4 5.1 fusion.52
  112.2 64.4 %all-reduce.25.cloned.1.call-done = bf16[1024,1024]{1,0:T(8,128)(2,1)} async-done(((bf16[1024,1024]{1,0:T(8,128)(2,1)}), bf16[1024,1024]{1,0:T(8,128)(2,1)}) %all-reduce.25.cloned.1.call-update) | async-done | bytes 2097168 | tf_op jit(solution)/shard_map/psum | solution.py:214
  176.6 3.1 multiply_reduce_fusion.3
  187.8 3.9 multiply_convert_fusion.6
  194.1 5.2 fusion.111
  199.6 6.1 convolution_convert_fusion
  205.8 3.9 fusion.36
  209.7 52.7 %all-reduce.27.cloned.1.call-done = bf16[1024,1024]{1,0:T(8,128)(2,1)} async-done(((bf16[1024,1024]{1,0:T(8,128)(2,1)}), bf16[1024,1024]{1,0:T(8,128)(2,1)}) %all-reduce.27.cloned.1.call-update) | async-done | bytes 2097168 | tf_op jit(solution)/shard_map/psum | solution.py:237
  262.4 5.6 multiply_reduce_fusion.1
  273.2 4.3 multiply_reduce_fusion.4
  277.5 4.9 psum.185
  282.5 6.8 fusion.32
  290.9 27.4 %fusion = (f32[12,1024]{1,0:T(8,128)S(1)}, f32[12,1024]{1,0:T(8,128)S(1)}, bf16[1024,1024]{1,0:T(8,128)(2,1)S(1)}) fusion(f32[12,1024]{1,0:T(8,128)S(1)} %bitcast.264, f32[1024,1024]{1,0:T(8,128)S(1)} %copy-done.31, pred[1024,1024]{1,0:T(8,128)(4,1)S(1)} %copy-done.67, f32[12,1024,64]{1,2,0:T(8,128)S(1)} %bitcast.232, ...), kind=kOutput, calls=%fused_computation.5 | convolution fusion | flops 1750310912 | bytes 13828096 | tf_op jit(solution)/shard_map/while/body/eval_jaxpr/htp,hsp->hts/dot_general | solution.py:342
  318.4 21.5 %multiply_reduce_fusion.5 = (bf16[12]{0:T(256)(128)(2,1)}, f32[1,12,1024,64]{2,3,1,0:T(8,128)}, f32[12,1024,64]{1,2,0:T(8,128)}) fusion(f32[1,12,1024,64]{2,3,1,0:T(8,128)} %bitcast.236, f32[1,12,1024,64]{2,3,1,0:T(8,128)} %bitcast.231, f32[12]{0:T(128)S(1)} %copy-done.142, f32[12,1024]{1,0:T(8,128)S(1)} %get-tuple-element.228, ...), kind=kOutput, calls=%fused_computation.72 | convolution fusion | flops 1678245888 | bytes 17924168 | tf_op jit(solution)/shard_map/while/body/eval_jaxpr/hts,htp->hsp/dot_general | solution.py:345
  342.2 7.8 fusion.53
  350.0 12.3 %multiply_reduce_fusion = (f32[4,1024]{1,0:T(4,128)S(1)}, f32[4,1024,1024]{1,2,0:T(8,128)}) fusion(f32[4,1024,1024]{1,2,0:T(8,128)} %copy-done.6, f32[4,1024]{1,0:T(4,128)S(1)} %log_add_fusion, pred[1024,1024]{0,1:T(8,128)(4,1)S(1)} %copy-done.16, bf16[4,1024,64]{1,2,0:T(8,128)(2,1)S(1)} %bitcast.241, bf16[1024,64,1]{0,1,2:T(8,128)(2,1)S(1)} %copy-done.73), kind=kOutput, calls=%fused_computation.10 | convolution fusion | flops 557838336 | bytes 35291136 | tf_op jit(solution)/shard_map/while/body/eval_jaxpr/htd,sd->hts/dot_general | solution.py:269
  362.3 12.2 %multiply_convert_fusion.4 = bf16[4,1024,1024]{1,2,0:T(8,128)(2,1)S(1)} fusion(f32[4,1024,1024]{1,2,0:T(8,128)} %get-tuple-element.248, f32[4,1024,1024]{1,2,0:T(8,128)} %copy-done.6, f32[4,1024]{1,0:T(4,128)S(1)} %get-tuple-element.247, f32[4,1024]{1,0:T(4,128)S(1)} %log_add_fusion, pred[1024,1024]{0,1:T(8,128)(4,1)S(1)} %copy-done.16), kind=kLoop, calls=%fused_computation.9 | loop fusion | flops 25165824 | bytes 43024384 | tf_op jit(solution)/shard_map/while/body/eval_jaxpr/convert_element_type | solution.py:273
  374.6 2.7 fusion.45
  382.0 3.5 copy.84
  386.2 3.4 reduce-window.16
  390.6 5.9 fusion.120
  403.7 4.6 multiply_reduce_fusion.9
  408.4 4.0 fusion.108
  412.4 3.8 fusion.38
  420.4 6.4 fusion.112
  427.1 5.5 convolution_convert_fusion.1
  435.9 3.0 convolution_convert_fusion.4
  438.9 3.1 convolution_convert_fusion.3
  442.0 3.0 convolution_convert_fusion.2
  446.1 60.6 %all-reduce.17 = (bf16[1024,12]{0,1:T(8,128)(2,1)S(1)}, bf16[4,768]{1,0:T(4,128)(2,1)S(1)}, bf16[768]{0:T(1024)(128)(2,1)S(1)}, bf16[12]{0:T(256)(128)(2,1)S(1)}...) all-reduce(bf16[1024,12]{0,1:T(8,128)(2,1)S(1)} %convolution_conver, ...), channel_id=1, replica_groups=mesh['dp'=16,'tensor'=2] {'dp'}, use_global_device_ids=true, to_apply=%region_32.33 | all-reduce | flops 16932 | bytes 67728 | tf_op jit(solution)/shard_map/psum | solution.py:423
  512.2 4.8 dynamic_update_slice.35
  518.6 3.8 dynamic_update_slice.36
  522.5 3.1 fusion.66
  527.2 4.2 fusion.19
  531.4 38.8 %all-reduce.15 = (f32[1024]{0:T(1024)}, f32[4,256]{1,0:T(4,128)}, f32[256]{0:T(256)}, f32[1024]{0:T(1024)}) all-reduce(f32[1024]{0:T(1024)S(1)} %get-tuple-element.146, f32[4,256]{1,0:T(4,128)S(1)} %pad_maximum_fusion.5, f32[256]{0:T(256)S(1)} %get-tuple-element.148, ...), channel_id=1, replica_groups=mesh['dp'=16,'tensor'=2] {'dp','tensor'}, use_global_device_ids=true, to_apply=%region_25.26 | all-reduce | flops 3328 | bytes 26624 | tf_op jit(solution)/shard_map/psum | solution.py:442
  570.2 6.6 fusion.18
  576.9 153.0 %all-reduce.33.cloned.1.call-done = (bf16[1024,256]{1,0:T(8,128)(2,1)}, bf16[256,1024]{1,0:T(8,128)(2,1)}, bf16[1024,768]{1,0:T(8,128)(2,1)}, bf16[1024,768]{1,0...) async-done(((bf16[1024,256]{1,0:T(8,128)(2,1)}, bf16[256,1024]{1,0:T(8,128)(2,1)}, ...) | async-done | bytes 12058640 | tf_op jit(solution)/shard_map/psum | solution.py:419
  747.7 122.6 %all-reduce.31.cloned.1.call-done = (f32[1024,256]{1,0:T(8,128)}, f32[1024,256]{1,0:T(8,128)}) async-done(((f32[1024,256]{1,0:T(8,128)}, f32[1024,256]{1,0:T(8,128)}), (f32[1024,256]{1,0:T(8,128)}, f32[1024,256]{1,0:T(8,128)})) %all-reduce.31.cloned.1.call-update) | async-done | bytes 2097168 | tf_op jit(solution)/shard_map/psum | solution.py:442
  (416 shorter events, 114.8 us)
Async XLA Ops:
  7.2 176.8 %copy-start = (bf16[1024,1024]{1,0:T(8,128)(2,1)S(1)}, bf16[1024,1024]{1,0:T(8,128)(2,1)}, u32[]{:S(2)}) copy-start(bf16[1024,1024]{1,0:T(8,128)(2,1)} %param.46) | copy-start | bytes 6291460
  7.2 169.4 %all-reduce.25.cloned.1.call-start = ((), (), s32[]{:S(2)}) async-start(), calls=%async_computation | async-start | bytes 4194304 | tf_op jit(solution)/shard_map/psum | solution.py:214
  7.3 12.9 %copy-start.125 = (f32[32]{0:T(128)}, f32[32]{0:T(128)S(1)}, u32[]{:S(2)}) copy-start(f32[32]{0:T(128)S(1)} %multiply_exponential_fusion) | copy-start | bytes 388
  12.8 269.6 %copy-start.112 = (f32[768]{0:T(1024)}, f32[768]{0:T(1024)S(1)}, u32[]{:S(2)}) copy-start(f32[768]{0:T(1024)S(1)} %convert_element_type.439) | copy-start | bytes 9220
  13.5 10.7 %copy-start.95 = (f32[1024]{0:T(1024)}, f32[1024]{0:T(1024)S(1)}, u32[]{:S(2)}) copy-start(f32[1024]{0:T(1024)S(1)} %convert_element_type.411) | copy-start | bytes 12292
  16.3 7.9 copy-start.97
  17.7 27.1 %copy-start.114 = (f32[1,256]{1,0:T(1,128)}, f32[1,256]{1,0:T(1,128)S(1)}, u32[]{:S(2)}) copy-start(f32[1,256]{1,0:T(1,128)S(1)} %get-tuple-element.233) | copy-start | bytes 3076
  17.7 27.1 %copy-start.116 = (f32[1,256]{1,0:T(1,128)}, f32[1,256]{1,0:T(1,128)S(1)}, u32[]{:S(2)}) copy-start(f32[1,256]{1,0:T(1,128)S(1)} %get-tuple-element.234) | copy-start | bytes 3076
  17.7 27.1 %copy-start.118 = (f32[1,256]{1,0:T(1,128)}, f32[1,256]{1,0:T(1,128)S(1)}, u32[]{:S(2)}) copy-start(f32[1,256]{1,0:T(1,128)S(1)} %get-tuple-element.235) | copy-start | bytes 3076
  18.7 31.7 %copy-start.84 = (f32[1,1024]{1,0:T(1,128)}, f32[1,1024]{1,0:T(1,128)S(1)}, u32[]{:S(2)}) copy-start(f32[1,1024]{1,0:T(1,128)S(1)} %get-tuple-element.230) | copy-start | bytes 12292
  18.7 31.6 %copy-start.86 = (f32[1,1024]{1,0:T(1,128)}, f32[1,1024]{1,0:T(1,128)S(1)}, u32[]{:S(2)}) copy-start(f32[1,1024]{1,0:T(1,128)S(1)} %get-tuple-element.231) | copy-start | bytes 12292
  18.7 31.6 %copy-start.88 = (f32[1,1024]{1,0:T(1,128)}, f32[1,1024]{1,0:T(1,128)S(1)}, u32[]{:S(2)}) copy-start(f32[1,1024]{1,0:T(1,128)S(1)} %get-tuple-element.232) | copy-start | bytes 12292
  19.6 30.7 %copy-start.99 = (f32[768]{0:T(1024)}, f32[768]{0:T(1024)S(1)}, u32[]{:S(2)}) copy-start(f32[768]{0:T(1024)S(1)} %get-tuple-element.153) | copy-start | bytes 9220
  19.6 30.7 %copy-start.101 = (f32[768]{0:T(1024)}, f32[768]{0:T(1024)S(1)}, u32[]{:S(2)}) copy-start(f32[768]{0:T(1024)S(1)} %get-tuple-element.168) | copy-start | bytes 9220
  19.6 30.7 %copy-start.103 = (f32[768]{0:T(1024)}, f32[768]{0:T(1024)S(1)}, u32[]{:S(2)}) copy-start(f32[768]{0:T(1024)S(1)} %get-tuple-element.169) | copy-start | bytes 9220
  19.6 30.7 %copy-start.105 = (f32[768]{0:T(1024)}, f32[768]{0:T(1024)S(1)}, u32[]{:S(2)}) copy-start(f32[768]{0:T(1024)S(1)} %get-tuple-element.170) | copy-start | bytes 9220
  20.2 70.8 %copy-start.59 = (f32[1024,32]{0,1:T(8,128)}, f32[1024,32]{0,1:T(8,128)S(1)}, u32[]{:S(2)}) copy-start(f32[1024,32]{0,1:T(8,128)S(1)} %get-tuple-element.237) | copy-start | bytes 393220
  20.2 70.8 %copy-start.61 = (f32[1024,32]{0,1:T(8,128)}, f32[1024,32]{0,1:T(8,128)S(1)}, u32[]{:S(2)}) copy-start(f32[1024,32]{0,1:T(8,128)S(1)} %get-tuple-element.238) | copy-start | bytes 393220
  29.0 7.1 copy-start.50
  29.0 9.6 %copy-start.126 = (f32[32]{0:T(128)S(1)}, f32[32]{0:T(128)}, u32[]{:S(2)}) copy-start(f32[32]{0:T(128)} %copy-done.125) | copy-start | bytes 388
  36.1 64.2 %copy-start.72 = (bf16[1024,64,1]{0,1,2:T(8,128)(2,1)}, bf16[1024,64,1]{0,1,2:T(8,128)(2,1)S(1)}, u32[]{:S(2)}) copy-start(bf16[1024,64,1]{0,1,2:T(8,128)(2,1)S(1)} %fusion.56) | copy-start | bytes 393220
  39.2 53.2 %copy-start.78 = (bf16[1024,32]{0,1:T(8,128)(2,1)}, bf16[1024,32]{0,1:T(8,128)(2,1)S(1)}, u32[]{:S(2)}) copy-start(bf16[1024,32]{0,1:T(8,128)(2,1)S(1)} %get-tuple-element.224) | copy-start | bytes 196612
  39.2 53.2 %copy-start.80 = (bf16[1024,32]{0,1:T(8,128)(2,1)}, bf16[1024,32]{0,1:T(8,128)(2,1)S(1)}, u32[]{:S(2)}) copy-start(bf16[1024,32]{0,1:T(8,128)(2,1)S(1)} %get-tuple-element.225) | copy-start | bytes 196612
  58.2 19.1 %copy-start.4 = (bf16[1024,1024]{1,0:T(8,128)(2,1)S(1)}, bf16[1024,1024]{1,0:T(8,128)(2,1)}, u32[]{:S(2)}) copy-start(bf16[1024,1024]{1,0:T(8,128)(2,1)} %copy-done.2) | copy-start | bytes 6291460
  90.9 191.5 %copy-start.110 = (f32[1024,1]{0,1:T(1,128)}, f32[1024,1]{0,1:T(1,128)S(1)}, u32[]{:S(2)}) copy-start(f32[1024,1]{0,1:T(1,128)S(1)} %get-tuple-element.203) | copy-start | bytes 12292
  111.7 150.8 %all-reduce.27.cloned.1.call-start = ((), (), s32[]{:S(2)}) async-start(), calls=%async_computation.1 | async-start | bytes 4194304 | tf_op jit(solution)/shard_map/psum | solution.py:237
  112.2 155.9 %copy-start.90 = (f32[1024]{0:T(1024)}, f32[1024]{0:T(1024)S(1)}, u32[]{:S(2)}) copy-start(f32[1024]{0:T(1024)S(1)} %convert_element_type.443) | copy-start | bytes 12292
  180.1 88.0 %copy-start.92 = (f32[1024]{0:T(1024)}, f32[1024]{0:T(1024)S(1)}, u32[]{:S(2)}) copy-start(f32[1024]{0:T(1024)S(1)} %add_rsqrt_fusion) | copy-start | bytes 12292
  199.3 326.3 %all-reduce.29.cloned.1.call-start = ((), (), s32[]{:S(2)}) async-start(), calls=%async_computation.2 | async-start | bytes 4194304 | tf_op jit(solution)/shard_map/psum | solution.py:397
  205.8 56.7 %copy-start.8 = (bf16[1024,1024]{1,0:T(8,128)(2,1)S(1)}, bf16[1024,1024]{1,0:T(8,128)(2,1)}, u32[]{:S(2)}) copy-start(bf16[1024,1024]{1,0:T(8,128)(2,1)} %param.24) | copy-start | bytes 6291460
  270.1 7.5 copy-start.48
  282.5 8.5 copy-start.22
  282.5 8.5 copy-start.31
  282.5 8.5 copy-start.67
  290.9 27.5 %copy-start.142 = (f32[12]{0:T(128)S(1)}, f32[12]{0:T(128)}, u32[]{:S(2)}) copy-start(f32[12]{0:T(128)} %convert_element_type.438) | copy-start | bytes 148
  318.4 21.5 %copy-start.28 = (bf16[1,1024,256]{2,1,0:T(8,128)(2,1)S(1)}, bf16[1,1024,256]{2,1,0:T(8,128)(2,1)}, u32[]{:S(2)}) copy-start(bf16[1,1024,256]{2,1,0:T(8,128)(2,1)} %copy-done.27) | copy-start | bytes 1572868
  342.2 7.8 copy-start.73
  350.0 50.4 %copy-start.75 = (bf16[1024,64]{0,1:T(8,128)(2,1)}, bf16[1024,64]{0,1:T(8,128)(2,1)S(1)}, u32[]{:S(2)}) copy-start(bf16[1024,64]{0,1:T(8,128)(2,1)S(1)} %fusion.53) | copy-start | bytes 393220
  362.3 12.3 %copy-start.64 = (bf16[4,1024,32]{1,2,0:T(8,128)(2,1)S(1)}, bf16[4,1024,32]{1,2,0:T(8,128)(2,1)}, u32[]{:S(2)}) copy-start(bf16[4,1024,32]{1,2,0:T(8,128)(2,1)} %copy-done.63) | copy-start | bytes 786436
  362.3 12.3 %copy-start.66 = (bf16[4,1024,32]{1,2,0:T(8,128)(2,1)S(1)}, bf16[4,1024,32]{1,2,0:T(8,128)(2,1)}, u32[]{:S(2)}) copy-start(bf16[4,1024,32]{1,2,0:T(8,128)(2,1)} %copy-done.65) | copy-start | bytes 786436
  420.4 6.7 copy-start.46
  426.8 303.1 %all-reduce.33.cloned.1.call-start = ((), (), s32[]{:S(2)}) async-start(), calls=%async_computation.4 | async-start | bytes 24117248 | tf_op jit(solution)/shard_map/psum | solution.py:419
  445.0 425.3 %all-reduce.31.cloned.1.call-start = ((), (), s32[]{:S(2)}) async-start(), calls=%async_computation.3 | async-start | bytes 4194304 | tf_op jit(solution)/shard_map/psum | solution.py:442
  510.6 6.4 copy-start.76
  527.2 43.0 %copy-start.91 = (f32[1024]{0:T(1024)S(1)}, f32[1024]{0:T(1024)}, u32[]{:S(2)}) copy-start(f32[1024]{0:T(1024)} %copy-done.90) | copy-start | bytes 12292
  527.2 43.0 %copy-start.93 = (f32[1024]{0:T(1024)S(1)}, f32[1024]{0:T(1024)}, u32[]{:S(2)}) copy-start(f32[1024]{0:T(1024)} %copy-done.92) | copy-start | bytes 12292
  527.2 43.0 %copy-start.108 = (f32[1024]{0:T(1024)S(1)}, f32[1024]{0:T(1024)}, u32[]{:S(2)}) copy-start(f32[1024]{0:T(1024)} %copy-done.107) | copy-start | bytes 12292
  745.2 129.6 %copy-start.1 = (bf16[1024,1024]{1,0:T(8,128)(2,1)S(1)}, bf16[1024,1024]{1,0:T(8,128)(2,1)}, u32[]{:S(2)}) copy-start(bf16[1024,1024]{1,0:T(8,128)(2,1)} %param.46) | copy-start | bytes 6291460
  (106 other events, 348.6 us)
Sparse Core Ops, SparseCore 0:
  111.8 64.7 all-reduce.24
  199.5 62.9 all-reduce.26
  426.9 62.9 all-reduce.28
  497.5 232.3 all-reduce.32
  736.7 133.5 all-reduce.30
where the time goes:
time: 891 us; the launch traced here: 882 us
  waiting for transfers between devices  393 us (44%)
  matrix products  206 us (23%)
  other arithmetic  112 us (13%)
  blocking collectives  110 us (12%)
  local copies, waits for them, and re-layouts  44 us (5%)
  between operations  16 us (2%)
    psum x1, waiting for transfers between devices, local(): lax.psum(query_wgrad.astype(jnp.bfloat16), 'dp').astype(jnp.float32)  153 us
    psum x1, waiting for transfers between devices, local(): lax.psum((key_value_weight_grad, state_wgrad, conv_state_wgrad, state_bia...  123 us
    psum x1, waiting for transfers between devices, local(): lax.psum(branch_part.astype(jnp.bfloat16), 'tensor').astype(jnp.float32)  64.4 us
    psum x1, blocking collectives, local(): lax.psum(step_wgrad.astype(jnp.bfloat16), 'dp').astype(jnp.float32)  60.6 us
    psum x1, waiting for transfers between devices, local(): lax.psum(post_part.astype(jnp.bfloat16), 'tensor').astype(jnp.float32)  52.7 us
    psum x1, blocking collectives, local(): lax.psum((key_value_weight_grad, state_wgrad, conv_state_wgrad, state_bia...  38.8 us
    dot_general x11, matrix products, matmul(): return jnp.dot(left, right, preferred_element_type=jnp.float32)  28 us
    dot_general x1, matrix products, scan_back(): jnp.einsum('htp,hsp->hts', core_block, driven, preferred_element_type=jnp...  27.4 us
  transfers between devices with their start and end apart: 5, of which 4 were waited for; matrix products, arithmetic and copies ran while one was open for 9% of the time, Pallas kernels for 0%

commit v1 on v0

--- a/solution.py
+++ b/solution.py
@@ -92,6 +92,49 @@
     mixing = (coupling[None] * decay).astype(jnp.bfloat16)
     driven = (heads_block * step_block.T[:, :, None]).astype(jnp.bfloat16)
     return (coupling, decay, mixing, driven)
+
+
+def pair_sum(value):
+    if lax.axis_size("tensor") == 2:
+        other = lax.ppermute(value, "tensor", [(0, 1), (1, 0)])
+        return value.astype(jnp.float32) + other.astype(jnp.float32)
+    return lax.psum(value, "tensor").astype(jnp.float32)
+
+
+def swap_bit(value, bit):
+    size = lax.axis_size("dp")
+    return lax.ppermute(value, "dp", [(i, i ^ bit) for i in range(size)])
+
+
+def shared_sum(rows, first_shared):
+    tail = pair_sum(rows[:, first_shared:]).astype(rows.dtype)
+    return jnp.concatenate([rows[:, :first_shared], tail], 1) if first_shared else tail
+
+
+def tree_sum(value, first_shared=None):
+    size = lax.axis_size("dp")
+    rows = value.shape[0]
+    if size & (size - 1) or rows % (16 * size):
+        total = lax.psum(value, "dp")
+        return total if first_shared is None else shared_sum(total, first_shared)
+    bits = [1 << i for i in range(size.bit_length() - 1)]
+    me = lax.axis_index("dp")
+    for bit in bits:
+        half = value.shape[0] // 2
+        low, high = value[:half], value[half:]
+        upper = (me & bit) != 0
+        got = swap_bit(jnp.where(upper, low, high), bit)
+        kept = jnp.where(upper, high, low)
+        value = (kept.astype(jnp.float32) + got.astype(jnp.float32)).astype(value.dtype)
+    if first_shared is not None:
+        value = shared_sum(value, first_shared)
+    for bit in reversed(bits):
+        upper = (me & bit) != 0
+        got = swap_bit(value, bit)
+        value = jnp.where(
+            upper, jnp.concatenate([got, value], 0), jnp.concatenate([value, got], 0)
+        )
+    return value
 
 
 def local(
@@ -205,13 +248,13 @@
     sigma_gate = jax.nn.sigmoid(gating)
     gate_act = gating * sigma_gate
     gated = ssm_out * gate_act
-    square_sum = lax.psum(jnp.sum(gated * gated, -1, keepdims=True), "tensor")
+    square_sum = pair_sum(jnp.sum(gated * gated, -1))[:, None]
     inv_gate = lax.rsqrt(square_sum / DSSM + EPS)
     mixer_scale = mixer_gain.astype(jnp.float32)
     mixed = (gated * inv_gate * mixer_scale).astype(jnp.bfloat16)
     branch_part = attn_part + matmul(mixed, mixer_out)
     out_gain = post_gain.astype(jnp.float32)
-    branch = lax.psum(branch_part.astype(jnp.bfloat16), "tensor").astype(jnp.float32)
+    branch = pair_sum(branch_part.astype(jnp.bfloat16))
     middle = inputs + branch
     inv_second = lax.rsqrt(jnp.mean(middle * middle, -1, keepdims=True) + EPS)
     unit_second = middle * inv_second
@@ -234,7 +277,16 @@
         "tf,cf->tc", gate_act_grad, gate_weight, preferred_element_type=jnp.float32
     ) + jnp.einsum("tf,cf->tc", up_act_grad, up_weight, preferred_element_type=jnp.float32)
     post_gain_part = jnp.sum(post_part * unit_second, 0)
-    post_full = lax.psum(post_part.astype(jnp.bfloat16), "tensor").astype(jnp.float32)
+    post_full = pair_sum(post_part.astype(jnp.bfloat16))
+    down_wgrad, gate_wgrad, up_wgrad, post_full = lax.optimization_barrier(
+        (
+            down_wgrad.astype(jnp.bfloat16),
+            gate_wgrad.astype(jnp.bfloat16),
+            up_wgrad.astype(jnp.bfloat16),
+            post_full,
+        )
+    )
+    down_wgrad, gate_wgrad, up_wgrad = lax.psum((down_wgrad, gate_wgrad, up_wgrad), "dp")
     scaled_post = post_full * out_gain
     middle_grad = cotangent.astype(jnp.float32) + inv_second * (
         scaled_post - unit_second * jnp.mean(scaled_post * unit_second, -1, keepdims=True)
@@ -301,13 +353,6 @@
     )
     value_weight_grad = jnp.einsum(
         "slc,shld->cd", normed_seq, value_pre_grad, preferred_element_type=jnp.float32
-    )
-    key_value_weight_grad = jnp.zeros(key_value_weight.shape, jnp.float32)
-    key_value_weight_grad = lax.dynamic_update_slice_in_dim(
-        key_value_weight_grad, key_wgrad, shared_key_head * HEAD_SIZE, 1
-    )
-    key_value_weight_grad = lax.dynamic_update_slice_in_dim(
-        key_value_weight_grad, value_weight_grad, (KEYVALUE_HEADS + shared_key_head) * HEAD_SIZE, 1
     )
     normed_part = (
         jnp.einsum("tk,ck->tc", query_pre_grad, query_weight, preferred_element_type=jnp.float32)
@@ -322,7 +367,7 @@
     mixed_grad = jnp.einsum("td,kd->tk", branch_grad, mixer_out, preferred_element_type=jnp.float32)
     mixer_gain_wgrad = jnp.sum(mixed_grad * gated * inv_gate, 0)
     weighted = mixed_grad * mixer_scale
-    cross = lax.psum(jnp.sum(weighted * gated, -1, keepdims=True), "tensor")
+    cross = pair_sum(jnp.sum(weighted * gated, -1))[:, None]
     gated_grad = inv_gate * weighted - gated * (inv_gate * inv_gate * inv_gate) * cross / DSSM
     ssm_grad = gated_grad * gate_act
     gating_act_grad = (
@@ -394,62 +439,119 @@
         + jnp.einsum("tk,ck->tc", state_grad, state_weight, preferred_element_type=jnp.float32)
     )
     input_gain_part = jnp.sum(normed_part * unit_first, 0)
-    normed_full = lax.psum(normed_part.astype(jnp.bfloat16), "tensor").astype(jnp.float32)
+    normed_full = pair_sum(normed_part.astype(jnp.bfloat16))
     scaled_in = normed_full * in_gain
     tokens_grad = middle_grad + inv_first * (
         scaled_in - unit_first * jnp.mean(scaled_in * unit_first, -1, keepdims=True)
     )
-    (
-        query_wgrad,
-        attnout_wgrad,
-        gating_wgrad,
-        inner_wgrad,
-        step_wgrad,
-        conv_inner_wgrad,
-        inner_bias_wgrad,
+    low = jnp.bfloat16
+    if lax.axis_size("tensor") == 2 and KEYVALUE_HEADS == 2:
+        keyval_part = jnp.concatenate([key_wgrad, value_weight_grad], 1)
+    else:
+        keyval_part = jnp.zeros(key_value_weight.shape, jnp.float32)
+        keyval_part = lax.dynamic_update_slice_in_dim(
+            keyval_part, key_wgrad, shared_key_head * HEAD_SIZE, 1
+        )
+        keyval_part = lax.dynamic_update_slice_in_dim(
+            keyval_part, value_weight_grad, (KEYVALUE_HEADS + shared_key_head) * HEAD_SIZE, 1
+        )
+        keyval_part = lax.psum(keyval_part, "tensor")
+    first_total = tree_sum(
+        jnp.concatenate(
+            [query_wgrad.astype(low), keyval_part.astype(low), gating_wgrad.astype(low)], 1
+        )
+    ).astype(jnp.float32)
+    second_total = tree_sum(
+        jnp.concatenate([attnout_wgrad.astype(low), mixout_wgrad.astype(low)], 0)
+    ).astype(jnp.float32)
+    width = query_wgrad.shape[1]
+    kv_width = keyval_part.shape[1]
+    query_wgrad = first_total[:, :width]
+    keyval_part = first_total[:, width : width + kv_width]
+    gating_wgrad = first_total[:, width + kv_width :]
+    attnout_wgrad = second_total[: heads * HEAD_SIZE]
+    mixout_wgrad = second_total[heads * HEAD_SIZE :]
+    if lax.axis_size("tensor") == 2 and KEYVALUE_HEADS == 2:
+        other = lax.ppermute(keyval_part.astype(low), "tensor", [(0, 1), (1, 0)])
+        mine = keyval_part.astype(low)
+        is_first = lax.axis_index("tensor") == 0
+        head_0 = jnp.where(is_first, mine, other)
+        head_1 = jnp.where(is_first, other, mine)
+        key_value_weight_grad = jnp.concatenate(
+            [
+                head_0[:, :HEAD_SIZE],
+                head_1[:, :HEAD_SIZE],
+                head_0[:, HEAD_SIZE:],
+                head_1[:, HEAD_SIZE:],
+            ],
+            1,
+        ).astype(jnp.float32)
+    else:
+        key_value_weight_grad = keyval_part
+    own = [
         step_bias_wgrad,
         decay_wgrad,
         skip_wgrad,
         mixer_gain_wgrad,
-        mixout_wgrad,
-        gate_wgrad,
-        up_wgrad,
-        down_wgrad,
-    ) = (
-        lax.psum(query_wgrad.astype(jnp.bfloat16), "dp").astype(jnp.float32),
-        lax.psum(attnout_wgrad.astype(jnp.bfloat16), "dp").astype(jnp.float32),
-        lax.psum(gating_wgrad.astype(jnp.bfloat16), "dp").astype(jnp.float32),
-        lax.psum(inner_wgrad.astype(jnp.bfloat16), "dp").astype(jnp.float32),
-        lax.psum(step_wgrad.astype(jnp.bfloat16), "dp").astype(jnp.float32),
-        lax.psum(conv_inner_wgrad.astype(jnp.bfloat16), "dp").astype(jnp.float32),
-        lax.psum(inner_bias_wgrad.astype(jnp.bfloat16), "dp").astype(jnp.float32),
-        lax.psum(step_bias_wgrad.astype(jnp.bfloat16), "dp").astype(jnp.float32),
-        lax.psum(decay_wgrad.astype(jnp.bfloat16), "dp").astype(jnp.float32),
-        lax.psum(skip_wgrad.astype(jnp.bfloat16), "dp").astype(jnp.float32),
-        lax.psum(mixer_gain_wgrad.astype(jnp.bfloat16), "dp").astype(jnp.float32),
-        lax.psum(mixout_wgrad.astype(jnp.bfloat16), "dp").astype(jnp.float32),
-        lax.psum(gate_wgrad.astype(jnp.bfloat16), "dp").astype(jnp.float32),
-        lax.psum(up_wgrad.astype(jnp.bfloat16), "dp").astype(jnp.float32),
-        lax.psum(down_wgrad.astype(jnp.bfloat16), "dp").astype(jnp.float32),
-    )
+        inner_bias_wgrad,
+        conv_inner_wgrad.reshape(-1),
+    ]
+    shared = [input_gain_part, post_gain_part, state_bias_wgrad, conv_state_wgrad.reshape(-1)]
+
+    def columns_of(parts):
+        flat = jnp.concatenate(parts)
+        count = -(-flat.shape[0] // tokens.shape[1])
+        flat = jnp.pad(flat, (0, count * tokens.shape[1] - flat.shape[0]))
+        return flat.reshape(count, tokens.shape[1]).T
+
+    def parts_of(columns, parts):
+        flat = columns.T.reshape(-1)
+        found, at = [], 0
+        for part in parts:
+            found.append(flat[at : at + part.shape[0]])
+            at += part.shape[0]
+        return found
+
+    own_columns, shared_columns = columns_of(own), columns_of(shared)
+    inner_width = inner_wgrad.shape[1]
+    own_width = own_columns.shape[1]
+    shared_from = -(-(inner_width + ssm_heads + own_width) // 128) * 128
+    pad = shared_from - inner_width - ssm_heads - own_width
+    third_total = tree_sum(
+        jnp.concatenate(
+            [
+                inner_wgrad.astype(low),
+                step_wgrad.astype(low),
+                own_columns.astype(low),
+                jnp.zeros((tokens.shape[1], pad), low),
+                state_wgrad.astype(low),
+                shared_columns.astype(low),
+            ],
+            1,
+        ),
+        shared_from,
+    ).astype(jnp.float32)
+    inner_wgrad = third_total[:, :inner_width]
+    step_wgrad = third_total[:, inner_width : inner_width + ssm_heads]
+    at = inner_width + ssm_heads
     (
-        key_value_weight_grad,
-        state_wgrad,
-        conv_state_wgrad,
-        state_bias_wgrad,
-        input_gain_part,
-        post_gain_part,
-    ) = lax.psum(
-        (
-            key_value_weight_grad,
-            state_wgrad,
-            conv_state_wgrad,
-            state_bias_wgrad,
-            input_gain_part,
-            post_gain_part,
-        ),
-        ("dp", "tensor"),
-    )
+        step_bias_wgrad,
+        decay_wgrad,
+        skip_wgrad,
+        mixer_gain_wgrad,
+        inner_bias_wgrad,
+        conv_inner_flat,
+    ) = parts_of(third_total[:, at : at + own_width], own)
+    conv_inner_wgrad = conv_inner_flat.reshape(conv_inner.shape)
+    state_width = state_wgrad.shape[1]
+    state_wgrad = third_total[:, shared_from : shared_from + state_width]
+    input_gain_part, post_gain_part, state_bias_wgrad, conv_state_flat = parts_of(
+        third_total[:, shared_from + state_width :], shared
+    )
+    conv_state_wgrad = conv_state_flat.reshape(conv_state.shape)
+    down_wgrad = down_wgrad.astype(jnp.float32)
+    gate_wgrad = gate_wgrad.astype(jnp.float32)
+    up_wgrad = up_wgrad.astype(jnp.float32)
     return (
         tokens_grad,
         input_gain_part,

time: 891 us -> 650 us (0.73)
  waiting for transfers between devices: 393 us -> 182 us
  blocking collectives: 110 us -> 0 us
  local copies, waits for them, and re-layouts: 44 us -> 76 us
  other arithmetic: 112 us -> 141 us
  starting transfers between devices: 1 us -> 23.6 us
    psum x5 -> x1, waiting for transfers between devices: 393 us -> 0.02 us  [local(): lax.psum((down_wgrad, gate_wgrad, up_wgrad), 'dp')]
    ppermute x0 -> x31, waiting for transfers between devices: none -> 182 us  [the longest x24 95.2 us: swap_bit(): return lax.ppermute(value, 'dp', [(i, i ^ bit) for i in range(size)])]
    psum x4 -> x0, blocking collectives: 110 us -> none  [the longest x1 60.6 us: local(): lax.psum(step_wgrad.astype(jnp.bfloat16), 'dp').astype(jnp.float32)]
    ppermute x0 -> x31, starting transfers between devices: none -> 23.6 us  [the longest x24 17.5 us: swap_bit(): return lax.ppermute(value, 'dp', [(i, i ^ bit) for i in range(size)])]
    select_n x0 -> x23, other arithmetic: none -> 17.3 us  [the longest x10 9.8 us: tree_sum(): jnp.where(upper, jnp.concatenate([got, value], 0), jnp.concatenate([value...]
    unnamed x306 -> x349, local copies, waits for them, and re-layouts: 23.8 us -> 38.4 us
    concatenate x0 -> x2, local copies, waits for them, and re-layouts: none -> 13.7 us  [the longest x1 13.7 us: local(): jnp.concatenate([inner_wgrad.astype(low), step_wgrad.astype(low), own_col...]
    slice x2 -> x21, local copies, waits for them, and re-layouts: 0.21 us -> 11.8 us  [the longest x7 3.11 us: parts_of(): found.append(flat[at:at + part.shape[0]])]
  transfers between devices with their start and end apart: 5 -> 32, of which waited for: 4 -> 20; matrix products, arithmetic and copies ran while one was open for 9% -> 36% of each run, Pallas kernels for 0% -> 0%
where the time goes in v1:
time: 650 us; the launch traced here: 642 us
  matrix products  203 us (31%)
  waiting for transfers between devices  182 us (28%)
  other arithmetic  141 us (22%)
  local copies, waits for them, and re-layouts  76 us (12%)
  starting transfers between devices  23.6 us (4%)
  between operations  16.8 us (3%)
    ppermute x24, waiting for transfers between devices, swap_bit(): return lax.ppermute(value, 'dp', [(i, i ^ bit) for i in range(size)])  95.2 us
    ppermute x6, waiting for transfers between devices, pair_sum(): other = lax.ppermute(value, 'tensor', [(0, 1), (1, 0)])  86.8 us
    unnamed x349, local copies, waits for them, and re-layouts  38.4 us
    dot_general x1, matrix products, scan_back(): jnp.einsum('htp,hsp->hts', core_block, driven, preferred_element_type=jnp...  27.9 us
    dot_general x11, matrix products, matmul(): return jnp.dot(left, right, preferred_element_type=jnp.float32)  27.6 us
    dot_general x1, matrix products, scan_forward(): jnp.einsum('hts,hsp->htp', parts[2], parts[3], preferred_element_type=jnp...  19.6 us
    dot_general x1, matrix products, scan_back(): jnp.einsum('hts,htp->hsp', mixing, core_block, preferred_element_type=jnp...  18.7 us
    ppermute x24, starting transfers between devices, swap_bit(): return lax.ppermute(value, 'dp', [(i, i ^ bit) for i in range(size)])  17.5 us
  transfers between devices with their start and end apart: 32, of which 20 were waited for; matrix products, arithmetic and copies ran while one was open for 36% of the time, Pallas kernels for 0%

profile of v1, /device:TPU:0, one launch (start us, length us, event | category | flops | bytes accessed | tf_op | source)
XLA Modules:
  0.0 641.7 jit_solution(8019981986568488093)
XLA Ops:
  7.3 4.1 copy.107
  28.1 4.0 fusion.127
  32.2 4.2 fusion.33
  40.6 19.6 %bitcast_add_fusion.1 = f32[1,12,1024,64]{2,3,1,0:T(8,128)} fusion(f32[1,12,1024,64]{2,3,1,0:T(8,128)} %bitcast.242, f32[12,1024]{1,0:T(8,128)S(1)} %bitcast.274, f32[1024,1024]{1,0:T(8,128)} %fusion.73, pred[1024,1024]{1,0:T(8,128)(4,1)} %copy.109, f32[12]{0:T(128)S(1)} %convert_element_type.548, f32[12,1024,64]{1,2,0:T(8,128)} %bitcast.241, ...), kind=kOutput, calls=%fused_computation.68 | convolution fusion | flops 1676673024 | bytes 14778416 | tf_op jit(solution)/shard_map/while/body/eval_jaxpr/hts,hsp->htp/dot_general | solution.py:243
  60.2 7.6 %multiply_reduce_fusion.12 = (f32[1024]{0:T(1024)S(1)}, f32[1024,768]{0,1:T(8,128)}, f32[1024,768]{0,1:T(8,128)}) fusion(f32[1,12,1024,64]{2,3,1,0:T(8,128)} %bitcast_add_fusion.1, bf16[1024,1024]{0,1:T(8,128)(2,1)S(1)} %copy-done.3, bf16[1024,768]{1,0:T(8,128)(2,1)} %param.31), kind=kOutput, calls=%fused_computation.81 | convolution fusion | flops 1616116736 | bytes 13111296 | tf_op jit(solution)/shard_map/dot_general | solution.py:20
  80.5 3.7 fusion.4
  86.7 5.3 fusion.53
  97.5 3.9 copy.106
  102.2 42.1 %collective-permute-done.1 = bf16[1024,1024]{0,1:T(8,128)(2,1)} collective-permute-done((bf16[1024,1024]{0,1:T(8,128)(2,1)}, bf16[1024,1024]{0,1:T(8,128)(2,1)}, u32[]{:S(2)}, u32[]{:S(2)}) %collective-permute-start.1) | collective-permute-done | bytes 2097184 | tf_op jit(solution)/shard_map/ppermute | solution.py:99
  144.3 4.3 multiply_reduce_fusion.3
  157.2 4.1 multiply_convert_fusion.5
  163.7 5.1 fusion.123
  169.0 3.7 convolution_convert_fusion.1
  172.7 3.6 convolution_convert_fusion
  176.4 3.9 fusion.37
  180.3 35.0 %collective-permute-done.2 = bf16[1024,1024]{0,1:T(8,128)(2,1)} collective-permute-done((bf16[1024,1024]{0,1:T(8,128)(2,1)}, bf16[1024,1024]{0,1:T(8,128)(2,1)}, u32[]{:S(2)}, u32[]{:S(2)}) %collective-permute-start.2) | collective-permute-done | bytes 2097184 | tf_op jit(solution)/shard_map/ppermute | solution.py:99
  218.4 5.7 multiply_reduce_fusion.1
  224.2 4.8 fusion.115
  229.1 4.2 multiply_reduce_fusion.8
  234.0 8.4 %fusion.54 = bf16[1024,64]{0,1:T(8,128)(2,1)} fusion(bf16[4,1024,64]{1,2,0:T(8,128)(2,1)S(1)} %bitcast.250, f32[4,1024,1024]{1,2,0:T(8,128)} %copy-done.10, f32[4,1024]{1,0:T(4,128)S(1)} %log_add_fusion, pred[1024,1024]{0,1:T(8,128)(4,1)S(1)} %copy-done.17), kind=kOutput, calls=%fused_computation.125 | convolution fusion | flops 554369024 | bytes 18497536 | tf_op jit(solution)/shard_map/while/body/eval_jaxpr/hts,htd->hsd/dot_general | solution.py:315
  242.5 11.9 %multiply_reduce_fusion = (f32[4,1024]{1,0:T(4,128)S(1)}, f32[4,1024,1024]{1,2,0:T(8,128)}) fusion(f32[4,1024,1024]{1,2,0:T(8,128)} %copy-done.10, f32[4,1024]{1,0:T(4,128)S(1)} %log_add_fusion, pred[1024,1024]{0,1:T(8,128)(4,1)S(1)} %copy-done.17, bf16[4,1024,64]{1,2,0:T(8,128)(2,1)S(1)} %bitcast.251, bf16[1024,64,1]{0,1,2:T(8,128)(2,1)S(1)} %fusion.57), kind=kOutput, calls=%fused_computation.10 | convolution fusion | flops 557838336 | bytes 35291136 | tf_op jit(solution)/shard_map/while/body/eval_jaxpr/htd,sd->hts/dot_general | solution.py:321
  254.4 12.4 %multiply_convert_fusion.4 = bf16[4,1024,1024]{1,2,0:T(8,128)(2,1)S(1)} fusion(f32[4,1024,1024]{1,2,0:T(8,128)} %get-tuple-element.320, f32[4,1024,1024]{1,2,0:T(8,128)} %copy-done.10, f32[4,1024]{1,0:T(4,128)S(1)} %get-tuple-element.319, f32[4,1024]{1,0:T(4,128)S(1)} %log_add_fusion, pred[1024,1024]{0,1:T(8,128)(4,1)S(1)} %copy-done.17), kind=kLoop, calls=%fused_computation.9 | loop fusion | flops 25165824 | bytes 43024384 | tf_op jit(solution)/shard_map/while/body/eval_jaxpr/convert_element_type | solution.py:325
  291.9 6.8 %fusion.31 = (bf16[1024,768]{0,1:T(8,128)(2,1)}, f32[1024,768]{0,1:T(8,128)S(1)}) fusion(f32[1,12,1024,64]{2,3,1,0:T(8,128)} %bitcast_add_fusion.1, f32[1024,768]{0,1:T(8,128)} %get-tuple-element.311, f32[1024]{0:T(1024)S(1)} %add.342, f32[1024,768]{0,1:T(8,128)} %get-tuple-element.261, f32[1024]{0:T(1024)S(1)} %copy-done.121, ...), kind=kLoop, calls=%fused_computation.67 | loop fusion | flops 14155776 | bytes 17316864 | tf_op jit(solution)/shard_map/convert_element_type | solution.py:375
  301.2 27.9 %fusion = (f32[12,1024]{1,0:T(8,128)S(1)}, f32[12,1024]{1,0:T(8,128)S(1)}, bf16[1024,1024]{1,0:T(8,128)(2,1)S(1)}) fusion(f32[12,1024]{1,0:T(8,128)S(1)} %bitcast.275, f32[1024,1024]{1,0:T(8,128)S(1)} %copy-done.43, pred[1024,1024]{1,0:T(8,128)(4,1)S(1)} %copy-done.67, f32[12,1024,64]{1,2,0:T(8,128)S(1)} %bitcast.244, f32[12,1024]{1,0:T(8,128)S(1)} %copy-done.79, ...), kind=kOutput, calls=%fused_computation.5 | convolution fusion | flops 1750310912 | bytes 13828096 | tf_op jit(solution)/shard_map/while/body/eval_jaxpr/htp,hsp->hts/dot_general | solution.py:387
  331.5 18.7 %multiply_reduce_fusion.10 = (f32[12,1024]{1,0:T(8,128)S(1)}, f32[12,1024,64]{1,2,0:T(8,128)}) fusion(f32[12,1024,64]{1,2,0:T(8,128)S(1)} %bitcast.245, f32[12,1024]{1,0:T(8,128)S(1)} %bitcast.276, f32[1024,1024]{1,0:T(8,128)} %fusion.73, pred[1024,1024]{1,0:T(8,128)(4,1)} %copy.109, f32[1,12,1024,64]{2,3,1,0:T(8,128)S(1)} %bitcast.239), kind=kOutput, calls=%fused_computation.76 | convolution fusion | flops 1675874304 | bytes 14778368 | tf_op jit(solution)/shard_map/while/body/eval_jaxpr/hts,htp->hsp/dot_general | solution.py:390
  366.0 6.8 %multiply_reduce_fusion.9 = (bf16[12]{0:T(256)(128)(2,1)}, f32[1,12,1024,64]{2,3,1,0:T(8,128)}) fusion(f32[1,12,1024,64]{2,3,1,0:T(8,128)S(1)} %bitcast.240, f32[1,12,1024,64]{2,3,1,0:T(8,128)} %bitcast.243, f32[12]{0:T(128)S(1)} %copy-done.150, f32[12,1024,64]{1,2,0:T(8,128)} %get-tuple-element.318, f32[12,1024]{1,0:T(8,128)S(1)} %copy-done.79), kind=kLoop, calls=%fused_computation.75 | loop fusion | flops 3932148 | bytes 12632136 | tf_op jit(solution)/shard_map/reduce_sum | solution.py:380
  376.4 7.9 %multiply_reduce_fusion.7 = (bf16[768]{0:T(1024)(128)(2,1)S(1)}, bf16[768]{0:T(1024)(128)(2,1)}, bf16[768]{0:T(1024)(128)(2,1)S(1)}, f32[1,1024,768]{2,1,0:T(8,1...) fusion(f32[1,1024,768]{2,1,0:T(8,128)} %bitcast.235, ...), kind=kLoop, calls=%fused_computation.73 | loop fusion | flops 13367040 | bytes 22036992 | tf_op jit(solution)/shard_map/reduce_sum | solution.py:82
  387.0 4.1 fusion.39
  396.8 9.6 %fusion.124 = (bf16[1024,1024]{0,1:T(8,128)(2,1)}, f32[1024,1024]{0,1:T(8,128)}) fusion(f32[1024,1024]{0,1:T(8,128)S(1)} %copy-done.18, f32[1024,1024]{0,1:T(8,128)} %fusion.95, f32[1024,1024]{0,1:T(8,128)} %fusion.39, bf16[1024,768]{1,0:T(8,128)(2,1)} %param.31, bf16[1024,768]{0,1:T(8,128)(2,1)S(1)} %copy-done.37, f32[1024,1024]{0,1:T(8,128)S(1)} %copy-done.27, ...), kind=kOutput, calls=%fused_computation.309 | convolution fusion | flops 1617952768 | bytes 34603008 | tf_op jit(solution)/shard_map/tk,ck->tc/dot_general | solution.py:434
  421.9 8.7 %collective-permute-done.24 = bf16[256,1024]{1,0:T(8,128)(2,1)} collective-permute-done((bf16[256,1024]{1,0:T(8,128)(2,1)}, bf16[256,1024]{1,0:T(8,128)(2,1)}, u32[]{:S(2)}, u32[]{:S(2)}) %collective-permute-start.24) | collective-permute-done | bytes 524320 | tf_op jit(solution)/shard_map/ppermute | solution.py:106
  432.7 9.8 %collective-permute-done.15 = bf16[256,1152]{0,1:T(8,128)(2,1)} collective-permute-done((bf16[256,1152]{0,1:T(8,128)(2,1)}, bf16[256,1152]{0,1:T(8,128)(2,1)}, u32[]{:S(2)}, u32[]{:S(2)}) %collective-permute-start.15) | collective-permute-done | bytes 589856 | tf_op jit(solution)/shard_map/ppermute | solution.py:106
  446.9 5.5 collective-permute-done.4
  452.5 4.3 fusion.19
  456.9 13.7 %concatenate.158 = bf16[1024,1156]{0,1:T(8,128)(2,1)} concatenate(bf16[1024,768]{0,1:T(8,128)(2,1)} %convolution_convert_fusion.4, bf16[1024,12]{0,1:T(8,128)(2,1)S(1)} %convolution_convert_fusion.12, bf16[1024,5]{0,1:T(8,128)(2,1)S(1)} %bitcast.273, bf16[1024,111]{0,1:T(8,128)(2,1)S(1)} %broadcast_in_dim.255, bf16[1024,256]{0,1:T(8,128)(2,1)S(1)} %copy-done.74, ...), dimensions={1} | concatenate | bytes 4734976 | tf_op jit(solution)/shard_map/concatenate | solution.py:521
  480.4 5.0 collective-permute-done.25
  485.5 6.4 %collective-permute-done.17 = bf16[64,1152]{0,1:T(8,128)(2,1)S(1)} collective-permute-done((bf16[64,1152]{0,1:T(8,128)(2,1)S(1)}, bf16[64,1152]{0,1:T(8,128)(2,1)S(1)}, u32[]{:S(2)}, u32[]{:S(2)}) %collective-permute-start.17) | collective-permute-done | bytes 147488 | tf_op jit(solution)/shard_map/ppermute | solution.py:106
  496.2 12.8 %collective-permute-done.18 = bf16[64,1152]{0,1:T(8,128)(2,1)S(1)} collective-permute-done((bf16[64,1152]{0,1:T(8,128)(2,1)S(1)}, bf16[64,1152]{0,1:T(8,128)(2,1)S(1)}, u32[]{:S(2)}, u32[]{:S(2)}) %collective-permute-start.18) | collective-permute-done | bytes 147488 | tf_op jit(solution)/shard_map/ppermute | solution.py:106
  511.7 12.4 %collective-permute-done.19 = bf16[128,1152]{0,1:T(8,128)(2,1)S(1)} collective-permute-done((bf16[128,1152]{0,1:T(8,128)(2,1)S(1)}, bf16[128,1152]{0,1:T(8,128)(2,1)S(1)}, u32[]{:S(2)}, u32[]{:S(2)}) %collective-permute-start.19) | collective-permute-done | bytes 294944 | tf_op jit(solution)/shard_map/ppermute | solution.py:106
  531.1 8.5 %collective-permute-done.20 = bf16[256,1152]{0,1:T(8,128)(2,1)S(1)} collective-permute-done((bf16[256,1152]{0,1:T(8,128)(2,1)S(1)}, bf16[256,1152]{0,1:T(8,128)(2,1)S(1)}, u32[]{:S(2)}, u32[]{:S(2)}) %collective-permute-start.20) | collective-permute-done | bytes 589856 | tf_op jit(solution)/shard_map/ppermute | solution.py:106
  542.3 6.2 collective-permute-done.10
  549.6 4.6 collective-permute-done.28
  555.6 4.9 collective-permute-done.11
  562.5 7.7 %collective-permute-done.29 = bf16[256,1024]{1,0:T(8,128)(2,1)} collective-permute-done((bf16[256,1024]{1,0:T(8,128)(2,1)}, bf16[256,1024]{1,0:T(8,128)(2,1)}, u32[]{:S(2)}, u32[]{:S(2)}) %collective-permute-start.29) | collective-permute-done | bytes 524320 | tf_op jit(solution)/shard_map/ppermute | solution.py:106
  577.9 3.9 collective-permute-done.12
  582.3 6.8 %fusion.18 = f32[1024,1024]{0,1:T(8,128)} fusion(bf16[1024,1024]{0,1:T(8,128)(2,1)S(1)} %copy-done.9, bf16[1024,1024]{0,1:T(8,128)(2,1)} %collective-permute-done.4, bf16[1024,1024]{0,1:T(8,128)(2,1)} %get-tuple-element.321, f32[1024]{0:T(1024)S(1)} %broadcast_multiply_fusion.7, f32[1024]{0:T(1024)S(1)} %copy-done.103, f32[1024]{0:T(1024)S(1)} %copy-done.105, ...), kind=kLoop, calls=%fused_computation.31 | loop fusion | flops 22020096 | bytes 20996096 | tf_op jit(solution)/shard_map/add | solution.py:444
  589.1 5.5 copy.130
  594.6 4.2 convert_element_type.638
  627.9 3.6 copy.134
  (567 shorter events, 207.0 us)
Async XLA Ops:
  7.2 147.4 %copy-start = (bf16[1024,1024]{1,0:T(8,128)(2,1)S(1)}, bf16[1024,1024]{1,0:T(8,128)(2,1)}, u32[]{:S(2)}) copy-start(bf16[1024,1024]{1,0:T(8,128)(2,1)} %param.46) | copy-start | bytes 6291460
  7.3 587.4 %all-reduce.20.cloned.1.call-start = ((), (), s32[]{:S(2)}) async-start(), calls=%async_computation | async-start | bytes 12582912 | tf_op jit(solution)/shard_map/psum | solution.py:289
  16.3 23.7 %copy-start.78 = (f32[12,1024]{1,0:T(8,128)}, f32[12,1024]{1,0:T(8,128)S(1)}, u32[]{:S(2)}) copy-start(f32[12,1024]{1,0:T(8,128)S(1)} %get-tuple-element.292) | copy-start | bytes 147460
  20.2 19.8 %copy-start.98 = (f32[2,8,8,128]{3,1,2,0:T(8,128)}, f32[2,8,8,128]{3,1,2,0:T(8,128)S(1)}, u32[]{:S(2)}) copy-start(f32[2,8,8,128]{3,1,2,0:T(8,128)S(1)} %copy.152) | copy-start | bytes 196612
  40.6 19.6 %copy-start.3 = (bf16[1024,1024]{0,1:T(8,128)(2,1)S(1)}, bf16[1024,1024]{0,1:T(8,128)(2,1)}, u32[]{:S(2)}) copy-start(bf16[1024,1024]{0,1:T(8,128)(2,1)} %copy-done.2) | copy-start | bytes 6291460
  67.8 24.2 %collective-permute-start = (f32[1024]{0:T(1024)S(1)}, f32[1024]{0:T(1024)S(1)}, u32[]{:S(2)}, u32[]{:S(2)}) collective-permute-start(f32[1024]{0:T(1024)S(1)} %get-tuple-element.260), channel_id=1, source_target_pairs={{0,1},{1,0},{2,3},{3,2},{4,5},{5,4},{6,7},{7,6},{8,9},{9,8},{10,11... | collective-permute-start | bytes 12296 | tf_op jit(solution)/shard_map/ppermute | solution.py:99
  96.9 47.4 %collective-permute-start.1 = (bf16[1024,1024]{0,1:T(8,128)(2,1)}, bf16[1024,1024]{0,1:T(8,128)(2,1)}, u32[]{:S(2)}, u32[]{:S(2)}) collective-permute-start(bf16[1024,1024]{0,1:T(8,128)(2,1)} %add_convert_fusion), channel_id=1, source_target_pairs={{0,1},{1,0},{2,3},{3,2},{4,5},{5,4},{6,7},{7,6},{8,9},{9,8},{10,11... | collective-permute-start | bytes 6291464 | tf_op jit(solution)/shard_map/ppermute | solution.py:99
  102.2 46.4 %copy-start.7 = (bf16[1024,1024]{0,1:T(8,128)(2,1)S(1)}, bf16[1024,1024]{0,1:T(8,128)(2,1)}, u32[]{:S(2)}) copy-start(bf16[1024,1024]{0,1:T(8,128)(2,1)} %copy.107) | copy-start | bytes 6291460
  102.2 46.4 %copy-start.92 = (f32[1024]{0:T(1024)S(1)}, f32[1024]{0:T(1024)}, u32[]{:S(2)}) copy-start(f32[1024]{0:T(1024)} %convert_element_type.554) | copy-start | bytes 12292
  168.8 46.5 %collective-permute-start.2 = (bf16[1024,1024]{0,1:T(8,128)(2,1)}, bf16[1024,1024]{0,1:T(8,128)(2,1)}, u32[]{:S(2)}, u32[]{:S(2)}) collective-permute-start(bf16[1024,1024]{0,1:T(8,128)(2,1)} %get-tuple-element.314), channel_id=1, source_target_pairs={{0,1},{1,0},{2,3},{3,2},{4,5},{5,4},{6,7},{7,6},{8,9},{9,8},{10,11... | collective-permute-start | bytes 6291464 | tf_op jit(solution)/shard_map/ppermute | solution.py:99
  180.3 38.1 %copy-start.8 = (bf16[1024,1024]{0,1:T(8,128)(2,1)S(1)}, bf16[1024,1024]{0,1:T(8,128)(2,1)}, u32[]{:S(2)}) copy-start(bf16[1024,1024]{0,1:T(8,128)(2,1)} %copy.107) | copy-start | bytes 6291460
  180.3 38.1 %copy-start.44 = (f32[1024,1024]{0,1:T(8,128)S(1)}, f32[1024,1024]{0,1:T(8,128)}, u32[]{:S(2)}) copy-start(f32[1024,1024]{0,1:T(8,128)} %get-tuple-element.315) | copy-start | bytes 12582916
  180.3 38.1 %copy-start.93 = (f32[1024]{0:T(1024)S(1)}, f32[1024]{0:T(1024)}, u32[]{:S(2)}) copy-start(f32[1024]{0:T(1024)} %convert_element_type.554) | copy-start | bytes 12292
  180.3 38.1 %copy-start.96 = (f32[1024]{0:T(1024)S(1)}, f32[1024]{0:T(1024)}, u32[]{:S(2)}) copy-start(f32[1024]{0:T(1024)} %copy-done.95) | copy-start | bytes 12292
  288.2 3.7 collective-permute-start.3
  290.3 122.3 %collective-permute-start.23 = (bf16[512,1024]{1,0:T(8,128)(2,1)}, bf16[512,1024]{1,0:T(8,128)(2,1)}, u32[]{:S(2)}, u32[]{:S(2)}) collective-permute-start(bf16[512,1024]{1,0:T(8,128)(2,1)} %broadcast_select_fusion.2), channel_id=1, source_target_pairs={{0,2},{2,0},{4,6},{6,4},{8,10},{10,8},{12,14},{14,12},{16,18},{18,... | collective-permute-start | bytes 3145736 | tf_op jit(solution)/shard_map/ppermute | solution.py:106
  298.6 32.7 %copy-start.32 = (f32[1024,768]{0,1:T(8,128)}, f32[1024,768]{0,1:T(8,128)S(1)}, u32[]{:S(2)}) copy-start(f32[1024,768]{0,1:T(8,128)S(1)} %get-tuple-element.267) | copy-start | bytes 9437188
  301.2 27.9 %copy-start.42 = (bf16[1,1024,256]{2,1,0:T(8,128)(2,1)S(1)}, bf16[1,1024,256]{2,1,0:T(8,128)(2,1)}, u32[]{:S(2)}) copy-start(bf16[1,1024,256]{2,1,0:T(8,128)(2,1)} %copy-done.41) | copy-start | bytes 1572868
  406.4 46.0 %collective-permute-start.4 = (bf16[1024,1024]{0,1:T(8,128)(2,1)}, bf16[1024,1024]{0,1:T(8,128)(2,1)}, u32[]{:S(2)}, u32[]{:S(2)}) collective-permute-start(bf16[1024,1024]{0,1:T(8,128)(2,1)} %get-tuple-element.321), channel_id=1, source_target_pairs={{0,1},{1,0},{2,3},{3,2},{4,5},{5,4},{6,7},{7,6},{8,9},{9,8},{10,11... | collective-permute-start | bytes 6291464 | tf_op jit(solution)/shard_map/ppermute | solution.py:99
  408.3 8.8 %collective-permute-start.14 = (bf16[512,1152]{0,1:T(8,128)(2,1)S(1)}, bf16[512,1152]{0,1:T(8,128)(2,1)S(1)}, u32[]{:S(2)}, u32[]{:S(2)}) collective-permute-start(bf16[512,1152]{0,1:T(8,128)(2,1)S(1)} %broadcast_select_fusion.1), channel_id=1, source_target_pairs={{0,2},{2,0},{4,6},{6,4},{8,10},{10,8},{12,14},{14,12},{16,18},{18,... | collective-permute-start | bytes 3538952 | tf_op jit(solution)/shard_map/ppermute | solution.py:106
  415.4 15.1 %collective-permute-start.24 = (bf16[256,1024]{1,0:T(8,128)(2,1)}, bf16[256,1024]{1,0:T(8,128)(2,1)}, u32[]{:S(2)}, u32[]{:S(2)}) collective-permute-start(bf16[256,1024]{1,0:T(8,128)(2,1)} %broadcast_select_fusion.5), channel_id=1, source_target_pairs={{0,4},{2,6},{4,0},{6,2},{8,12},{10,14},{12,8},{14,10},{16,20},{18,... | collective-permute-start | bytes 1572872 | tf_op jit(solution)/shard_map/ppermute | solution.py:106
  418.4 24.1 %collective-permute-start.15 = (bf16[256,1152]{0,1:T(8,128)(2,1)}, bf16[256,1152]{0,1:T(8,128)(2,1)}, u32[]{:S(2)}, u32[]{:S(2)}) collective-permute-start(bf16[256,1152]{0,1:T(8,128)(2,1)} %broadcast_select_fusion.4), channel_id=1, source_target_pairs={{0,4},{2,6},{4,0},{6,2},{8,12},{10,14},{12,8},{14,10},{16,20},{18,... | collective-permute-start | bytes 1769480 | tf_op jit(solution)/shard_map/ppermute | solution.py:106
  419.1 33.3 %copy-start.29 = (f32[1024,1024]{0,1:T(8,128)S(1)}, f32[1024,1024]{0,1:T(8,128)}, u32[]{:S(2)}) copy-start(f32[1024,1024]{0,1:T(8,128)} %get-tuple-element.322) | copy-start | bytes 12582916
  421.9 30.6 %copy-start.9 = (bf16[1024,1024]{0,1:T(8,128)(2,1)S(1)}, bf16[1024,1024]{0,1:T(8,128)(2,1)}, u32[]{:S(2)}) copy-start(bf16[1024,1024]{0,1:T(8,128)(2,1)} %copy.107) | copy-start | bytes 6291460
  421.9 30.6 %copy-start.103 = (f32[1024]{0:T(1024)S(1)}, f32[1024]{0:T(1024)}, u32[]{:S(2)}) copy-start(f32[1024]{0:T(1024)} %copy-done.102) | copy-start | bytes 12292
  421.9 30.6 %copy-start.105 = (f32[1024]{0:T(1024)S(1)}, f32[1024]{0:T(1024)}, u32[]{:S(2)}) copy-start(f32[1024]{0:T(1024)} %copy-done.104) | copy-start | bytes 12292
  445.3 28.6 %collective-permute-start.16 = (bf16[128,1152]{0,1:T(8,128)(2,1)}, bf16[128,1152]{0,1:T(8,128)(2,1)}, u32[]{:S(2)}, u32[]{:S(2)}) collective-permute-start(bf16[128,1152]{0,1:T(8,128)(2,1)} %broadcast_select_fusion.8), channel_id=1, source_target_pairs={{0,8},{2,10},{4,12},{6,14},{8,0},{10,2},{12,4},{14,6},{16,24},{18,... | collective-permute-start | bytes 884744 | tf_op jit(solution)/shard_map/ppermute | solution.py:106
  472.4 5.8 collective-permute-start.5
  472.6 12.8 %collective-permute-start.25 = (bf16[128,1024]{1,0:T(8,128)(2,1)S(1)}, bf16[128,1024]{1,0:T(8,128)(2,1)S(1)}, u32[]{:S(2)}, u32[]{:S(2)}) collective-permute-start(bf16[128,1024]{1,0:T(8,128)(2,1)S(1)} %broadcast_select_fusion.10), channel_id=1, source_target_pairs={{0,8},{2,10},{4,12},{6,14},{8,0},{10,2},{12,4},{14,6},{16,24},{18,... | collective-permute-start | bytes 786440 | tf_op jit(solution)/shard_map/ppermute | solution.py:106
  475.2 16.8 %collective-permute-start.17 = (bf16[64,1152]{0,1:T(8,128)(2,1)S(1)}, bf16[64,1152]{0,1:T(8,128)(2,1)S(1)}, u32[]{:S(2)}, u32[]{:S(2)}) collective-permute-start(bf16[64,1152]{0,1:T(8,128)(2,1)S(1)} %broadcast_select_fusion.9), channel_id=1, source_target_pairs={{0,16},{2,18},{4,20},{6,22},{8,24},{10,26},{12,28},{14,30},{16,0},... | collective-permute-start | bytes 442376 | tf_op jit(solution)/shard_map/ppermute | solution.py:106
  478.8 15.3 %collective-permute-start.6 = (bf16[256,1156]{0,1:T(8,128)(2,1)S(1)}, bf16[256,1156]{0,1:T(8,128)(2,1)S(1)}, u32[]{:S(2)}, u32[]{:S(2)}) collective-permute-start(bf16[256,1156]{0,1:T(8,128)(2,1)S(1)} %broadcast_select_fusion.3), channel_id=1, source_target_pairs={{0,4},{2,6},{4,0},{6,2},{8,12},{10,14},{12,8},{14,10},{16,20},{18,... | collective-permute-start | bytes 1775624 | tf_op jit(solution)/shard_map/ppermute | solution.py:106
  492.2 16.8 %collective-permute-start.18 = (bf16[64,1152]{0,1:T(8,128)(2,1)S(1)}, bf16[64,1152]{0,1:T(8,128)(2,1)S(1)}, u32[]{:S(2)}, u32[]{:S(2)}) collective-permute-start(bf16[64,1152]{0,1:T(8,128)(2,1)S(1)} %add_convert_fusion.9), channel_id=1, source_target_pairs={{0,16},{2,18},{4,20},{6,22},{8,24},{10,26},{12,28},{14,30},{16,0},... | collective-permute-start | bytes 442376 | tf_op jit(solution)/shard_map/ppermute | solution.py:106
  494.4 15.0 %collective-permute-start.7 = (bf16[128,1156]{0,1:T(8,128)(2,1)S(1)}, bf16[128,1156]{0,1:T(8,128)(2,1)S(1)}, u32[]{:S(2)}, u32[]{:S(2)}) collective-permute-start(bf16[128,1156]{0,1:T(8,128)(2,1)S(1)} %broadcast_select_fusion.6), channel_id=1, source_target_pairs={{0,8},{2,10},{4,12},{6,14},{8,0},{10,2},{12,4},{14,6},{16,24},{18,... | collective-permute-start | bytes 887816 | tf_op jit(solution)/shard_map/ppermute | solution.py:106
  495.6 31.8 %collective-permute-start.26 = (bf16[64,1024]{1,0:T(8,128)(2,1)S(1)}, bf16[64,1024]{1,0:T(8,128)(2,1)S(1)}, u32[]{:S(2)}, u32[]{:S(2)}) collective-permute-start(bf16[64,1024]{1,0:T(8,128)(2,1)S(1)} %broadcast_select_fusion.13), channel_id=1, source_target_pairs={{0,16},{2,18},{4,20},{6,22},{8,24},{10,26},{12,28},{14,30},{16,0},... | collective-permute-start | bytes 393224 | tf_op jit(solution)/shard_map/ppermute | solution.py:106
  509.3 14.8 %collective-permute-start.19 = (bf16[128,1152]{0,1:T(8,128)(2,1)S(1)}, bf16[128,1152]{0,1:T(8,128)(2,1)S(1)}, u32[]{:S(2)}, u32[]{:S(2)}) collective-permute-start(bf16[128,1152]{0,1:T(8,128)(2,1)S(1)} %maximum_select_fusion.10), channel_id=1, source_target_pairs={{0,8},{2,10},{4,12},{6,14},{8,0},{10,2},{12,4},{14,6},{16,24},{18,... | collective-permute-start | bytes 884744 | tf_op jit(solution)/shard_map/ppermute | solution.py:106
  509.7 16.4 %collective-permute-start.8 = (bf16[64,1156]{0,1:T(8,128)(2,1)S(1)}, bf16[64,1156]{0,1:T(8,128)(2,1)S(1)}, u32[]{:S(2)}, u32[]{:S(2)}) collective-permute-start(bf16[64,1156]{0,1:T(8,128)(2,1)S(1)} %broadcast_select_fusion.7), channel_id=1, source_target_pairs={{0,16},{2,18},{4,20},{6,22},{8,24},{10,26},{12,28},{14,30},{16,0},... | collective-permute-start | bytes 443912 | tf_op jit(solution)/shard_map/ppermute | solution.py:106
  524.3 15.3 %collective-permute-start.20 = (bf16[256,1152]{0,1:T(8,128)(2,1)S(1)}, bf16[256,1152]{0,1:T(8,128)(2,1)S(1)}, u32[]{:S(2)}, u32[]{:S(2)}) collective-permute-start(bf16[256,1152]{0,1:T(8,128)(2,1)S(1)} %maximum_select_fusion.7), channel_id=1, source_target_pairs={{0,4},{2,6},{4,0},{6,2},{8,12},{10,14},{12,8},{14,10},{16,20},{18,... | collective-permute-start | bytes 1769480 | tf_op jit(solution)/shard_map/ppermute | solution.py:106
  526.3 4.4 collective-permute-start.9
  527.5 14.7 %collective-permute-start.27 = (bf16[64,1024]{1,0:T(8,128)(2,1)S(1)}, bf16[64,1024]{1,0:T(8,128)(2,1)S(1)}, u32[]{:S(2)}, u32[]{:S(2)}) collective-permute-start(bf16[64,1024]{1,0:T(8,128)(2,1)S(1)} %add_convert_fusion.15), channel_id=1, source_target_pairs={{0,16},{2,18},{4,20},{6,22},{8,24},{10,26},{12,28},{14,30},{16,0},... | collective-permute-start | bytes 393224 | tf_op jit(solution)/shard_map/ppermute | solution.py:106
  530.7 17.9 %collective-permute-start.10 = (bf16[64,1156]{0,1:T(8,128)(2,1)S(1)}, bf16[64,1156]{0,1:T(8,128)(2,1)S(1)}, u32[]{:S(2)}, u32[]{:S(2)}) collective-permute-start(bf16[64,1156]{0,1:T(8,128)(2,1)S(1)} %pad_maximum_fusion.6), channel_id=1, source_target_pairs={{0,16},{2,18},{4,20},{6,22},{8,24},{10,26},{12,28},{14,30},{16,0},... | collective-permute-start | bytes 443912 | tf_op jit(solution)/shard_map/ppermute | solution.py:106
  540.0 33.3 %collective-permute-start.21 = (bf16[512,1152]{0,1:T(8,128)(2,1)S(1)}, bf16[512,1152]{0,1:T(8,128)(2,1)}, u32[]{:S(2)}, u32[]{:S(2)}) collective-permute-start(bf16[512,1152]{0,1:T(8,128)(2,1)S(1)} %maximum_select_fusion.4), channel_id=1, source_target_pairs={{0,2},{2,0},{4,6},{6,4},{8,10},{10,8},{12,14},{14,12},{16,18},{18,... | collective-permute-start | bytes 3538952 | tf_op jit(solution)/shard_map/ppermute | solution.py:106
  542.3 11.9 %collective-permute-start.28 = (bf16[128,1024]{1,0:T(8,128)(2,1)S(1)}, bf16[128,1024]{1,0:T(8,128)(2,1)S(1)}, u32[]{:S(2)}, u32[]{:S(2)}) collective-permute-start(bf16[128,1024]{1,0:T(8,128)(2,1)S(1)} %maximum_select_fusion.11), channel_id=1, source_target_pairs={{0,8},{2,10},{4,12},{6,14},{8,0},{10,2},{12,4},{14,6},{16,24},{18,... | collective-permute-start | bytes 786440 | tf_op jit(solution)/shard_map/ppermute | solution.py:106
  549.6 10.9 %collective-permute-start.11 = (bf16[128,1156]{0,1:T(8,128)(2,1)}, bf16[128,1156]{0,1:T(8,128)(2,1)}, u32[]{:S(2)}, u32[]{:S(2)}) collective-permute-start(bf16[128,1156]{0,1:T(8,128)(2,1)} %maximum_select_fusion.9), channel_id=1, source_target_pairs={{0,8},{2,10},{4,12},{6,14},{8,0},{10,2},{12,4},{14,6},{16,24},{18,... | collective-permute-start | bytes 887816 | tf_op jit(solution)/shard_map/ppermute | solution.py:106
  555.1 15.1 %collective-permute-start.29 = (bf16[256,1024]{1,0:T(8,128)(2,1)}, bf16[256,1024]{1,0:T(8,128)(2,1)}, u32[]{:S(2)}, u32[]{:S(2)}) collective-permute-start(bf16[256,1024]{1,0:T(8,128)(2,1)} %maximum_select_fusion.8), channel_id=1, source_target_pairs={{0,4},{2,6},{4,0},{6,2},{8,12},{10,14},{12,8},{14,10},{16,20},{18,... | collective-permute-start | bytes 1572872 | tf_op jit(solution)/shard_map/ppermute | solution.py:106
  562.0 19.8 %collective-permute-start.12 = (bf16[256,1156]{0,1:T(8,128)(2,1)S(1)}, bf16[256,1156]{0,1:T(8,128)(2,1)S(1)}, u32[]{:S(2)}, u32[]{:S(2)}) collective-permute-start(bf16[256,1156]{0,1:T(8,128)(2,1)S(1)} %maximum_select_fusion.6), channel_id=1, source_target_pairs={{0,4},{2,6},{4,0},{6,2},{8,12},{10,14},{12,8},{14,10},{16,20},{18,... | collective-permute-start | bytes 1775624 | tf_op jit(solution)/shard_map/ppermute | solution.py:106
  573.2 30.6 %collective-permute-start.30 = (bf16[512,1024]{1,0:T(8,128)(2,1)}, bf16[512,1024]{1,0:T(8,128)(2,1)}, u32[]{:S(2)}, u32[]{:S(2)}) collective-permute-start(bf16[512,1024]{1,0:T(8,128)(2,1)} %maximum_select_fusion.5), channel_id=1, source_target_pairs={{0,2},{2,0},{4,6},{6,4},{8,10},{10,8},{12,14},{14,12},{16,18},{18,... | collective-permute-start | bytes 3145736 | tf_op jit(solution)/shard_map/ppermute | solution.py:106
  576.9 40.8 %collective-permute-start.22 = (bf16[1024,128]{0,1:T(8,128)(2,1)S(1)}, bf16[1024,128]{0,1:T(8,128)(2,1)}, u32[]{:S(2)}, u32[]{:S(2)}) collective-permute-start(bf16[1024,128]{0,1:T(8,128)(2,1)S(1)} %slice.421), channel_id=1, source_target_pairs={{0,1},{1,0},{2,3},{3,2},{4,5},{5,4},{6,7},{7,6},{8,9},{9,8},{10,11... | collective-permute-start | bytes 786440 | tf_op jit(solution)/shard_map/ppermute | solution.py:475
  582.2 38.0 %collective-permute-start.13 = (bf16[512,1156]{0,1:T(8,128)(2,1)S(1)}, bf16[512,1156]{0,1:T(8,128)(2,1)}, u32[]{:S(2)}, u32[]{:S(2)}) collective-permute-start(bf16[512,1156]{0,1:T(8,128)(2,1)S(1)} %maximum_select_fusion.3), channel_id=1, source_target_pairs={{0,2},{2,0},{4,6},{6,4},{8,10},{10,8},{12,14},{14,12},{16,18},{18,... | collective-permute-start | bytes 3551240 | tf_op jit(solution)/shard_map/ppermute | solution.py:106
  (151 other events, 800.8 us)
Sparse Core Ops, SparseCore 0:
  290.4 141.1 all-reduce.19

commit v2 on v1

--- a/solution.py
+++ b/solution.py
@@ -1,6 +1,8 @@
 import jax
 import jax.numpy as jnp
 from jax import lax
+from jax.experimental import pallas as pl
+from jax.experimental.pallas import tpu as pltpu
 from jax.sharding import PartitionSpec as P
 
 QUERY_HEADS = 8
@@ -578,6 +580,723 @@
     )
 
 
+CHUNK = 256
+LANES = 128
+VMEM_BYTES = 56 * 1024 * 1024
+
+
+def dot_nn(left, right):
+    return lax.dot_general(left, right, (((1,), (0,)), ((), ())), preferred_element_type=jnp.float32)
+
+
+def dot_nt(left, right):
+    return lax.dot_general(left, right, (((1,), (1,)), ((), ())), preferred_element_type=jnp.float32)
+
+
+def dot_tn(left, right):
+    return lax.dot_general(left, right, (((0,), (0,)), ((), ())), preferred_element_type=jnp.float32)
+
+
+def split_two(value):
+    high = value.astype(jnp.bfloat16)
+    return high, (value - high.astype(jnp.float32)).astype(jnp.bfloat16)
+
+
+def exact_nn(ones, value):
+    high, low = split_two(value)
+    return dot_nn(ones, high) + dot_nn(ones, low)
+
+
+def grid_of(shape):
+    return (
+        lax.broadcasted_iota(jnp.int32, shape, 0),
+        lax.broadcasted_iota(jnp.int32, shape, 1),
+    )
+
+
+def pick(columns, pair):
+    rows = columns.shape[0]
+    left = jnp.broadcast_to(columns[:, 2 * pair : 2 * pair + 1], (rows, LANES))
+    right = jnp.broadcast_to(columns[:, 2 * pair + 1 : 2 * pair + 2], (rows, LANES))
+    return jnp.where(grid_of((rows, LANES))[1] < P_SIZE, left, right)
+
+
+def scan_terms(step, rate, aux):
+    row, col = grid_of((CHUNK, CHUNK))
+    lower = (row >= col).astype(jnp.bfloat16)
+    cumulative = exact_nn(lower, step * rate)
+    last = cumulative[CHUNK - 1 : CHUNK]
+    enter = jnp.exp(cumulative) * aux[:, 1:2]
+    leave = jnp.exp(last - cumulative) * aux[:, 2:3]
+    across = jnp.exp(last) * aux[CHUNK - 1 : CHUNK, 1:2]
+    return cumulative, enter, leave, across
+
+
+def scan_kernel(step_ref, coef_ref, act_ref, aux_ref, seg_ref, rate_ref, core_ref, kept_ref, state, moved):
+    @pl.when(pl.program_id(0) == 0)
+    def _():
+        state[...] = jnp.zeros_like(state)
+
+    step = step_ref[...]
+    aux = aux_ref[...]
+    cumulative, enter, leave, across = scan_terms(step, rate_ref[...], aux)
+    cum_rows = cumulative.T
+    row, col = grid_of((CHUNK, CHUNK))
+    blocked = jnp.where((row >= col) & (aux[:, 0:1] == seg_ref[...]), 0.0, NEG_FILL)
+    coef_b = coef_ref[:, :NS]
+    coef_c = coef_ref[:, NS:]
+    coupling = dot_nt(coef_c, coef_b)
+    low_state = state[...].astype(jnp.bfloat16)
+    kept_ref[0] = low_state
+    carried = dot_nn(coef_c, low_state)
+    first = grid_of((CHUNK, LANES))[1] < P_SIZE
+    for pair in range(act_ref.shape[1] // LANES):
+        at = slice(pair * LANES, (pair + 1) * LANES)
+        driven = (act_ref[:, at] * pick(step, pair)).astype(jnp.bfloat16)
+        parts = []
+        for head in (2 * pair, 2 * pair + 1):
+            decay = jnp.exp(cumulative[:, head : head + 1] - cum_rows[head : head + 1] + blocked)
+            parts.append(dot_nn((coupling * decay).astype(jnp.bfloat16), driven))
+        core_ref[:, at] = jnp.where(first, parts[0], parts[1]) + carried[:, at] * pick(enter, pair)
+        moved[:, at] = (driven.astype(jnp.float32) * pick(leave, pair)).astype(jnp.bfloat16)
+    fresh = dot_tn(coef_b, moved[...])
+    for pair in range(act_ref.shape[1] // LANES):
+        at = slice(pair * LANES, (pair + 1) * LANES)
+        state[:, at] = state[:, at] * pick(across, pair) + fresh[:, at]
+
+
+def scan_call(step, coef, act, aux, seg_row, rate):
+    rows, width = act.shape
+    chunks = rows // CHUNK
+    by_chunk = lambda columns: pl.BlockSpec((CHUNK, columns), lambda i: (i, 0))
+    return pl.pallas_call(
+        scan_kernel,
+        grid=(chunks,),
+        in_specs=[
+            by_chunk(LANES),
+            by_chunk(2 * NS),
+            by_chunk(width),
+            by_chunk(LANES),
+            pl.BlockSpec((1, CHUNK), lambda i: (0, i)),
+            pl.BlockSpec((1, LANES), lambda i: (0, 0)),
+        ],
+        out_specs=[by_chunk(width), pl.BlockSpec((1, NS, width), lambda i: (i, 0, 0))],
+        out_shape=[
+            jax.ShapeDtypeStruct((rows, width), jnp.float32),
+            jax.ShapeDtypeStruct((chunks, NS, width), jnp.bfloat16),
+        ],
+        scratch_shapes=[
+            pltpu.VMEM((NS, width), jnp.float32),
+            pltpu.VMEM((CHUNK, width), jnp.bfloat16),
+        ],
+        compiler_params=pltpu.CompilerParams(vmem_limit_bytes=VMEM_BYTES),
+        name="scan_forward",
+    )(step, coef, act, aux, seg_row, rate)
+
+
+def scan_back_kernel(
+    step_ref,
+    coef_ref,
+    act_ref,
+    aux_ref,
+    seg_ref,
+    rate_ref,
+    skip_ref,
+    grad_ref,
+    kept_ref,
+    act_grad_ref,
+    step_grad_ref,
+    coef_grad_ref,
+    sums_ref,
+    skip_sum_ref,
+    state_grad,
+    moved,
+    entered,
+    row_sums,
+):
+    @pl.when(pl.program_id(0) == 0)
+    def _():
+        state_grad[...] = jnp.zeros_like(state_grad)
+        sums_ref[...] = jnp.zeros_like(sums_ref)
+        skip_sum_ref[...] = jnp.zeros_like(skip_sum_ref)
+        row_sums[...] = jnp.zeros_like(row_sums)
+
+    step = step_ref[...]
+    aux = aux_ref[...]
+    rate = rate_ref[...]
+    cumulative, enter, leave, across = scan_terms(step, rate, aux)
+    cum_rows = cumulative.T
+    row, col = grid_of((CHUNK, CHUNK))
+    blocked = jnp.where((row <= col) & (aux[:, 0:1] == seg_ref[...]), 0.0, NEG_FILL)
+    coef_b = coef_ref[:, :NS]
+    coef_c = coef_ref[:, NS:]
+    coupling = dot_nt(coef_b, coef_c)
+    low_state = kept_ref[0]
+    carried = dot_nn(coef_c, low_state)
+    low_grad = state_grad[...].astype(jnp.bfloat16)
+    returned = dot_nn(coef_b, low_grad)
+    product = jnp.sum(low_state.astype(jnp.float32) * low_grad.astype(jnp.float32), 0, keepdims=True)
+    lane = grid_of((CHUNK, LANES))[1]
+    lane_row = grid_of((1, LANES))[1]
+    first = lane < P_SIZE
+    later = jnp.zeros((CHUNK, LANES), jnp.float32)
+    earlier = jnp.zeros((CHUNK, LANES), jnp.float32)
+    direct = jnp.zeros((CHUNK, LANES), jnp.float32)
+    through = jnp.zeros((1, LANES), jnp.float32)
+    coupling_grad = jnp.zeros((CHUNK, CHUNK), jnp.float32)
+    for pair in range(act_ref.shape[1] // LANES):
+        at = slice(pair * LANES, (pair + 1) * LANES)
+        act = act_ref[:, at]
+        spread_step = pick(step, pair)
+        driven = (act * spread_step).astype(jnp.bfloat16)
+        grad = grad_ref[:, at]
+        core_grad = grad.astype(jnp.bfloat16)
+        core_wide = core_grad.astype(jnp.float32)
+        enter_grad = core_wide * pick(enter, pair)
+        entered[:, at] = enter_grad.astype(jnp.bfloat16)
+        row_part = enter_grad * carried[:, at]
+        leave_pair = pick(leave, pair)
+        moved[:, at] = (driven.astype(jnp.float32) * leave_pair).astype(jnp.bfloat16)
+        back = returned[:, at] * leave_pair
+        col_part = back * driven.astype(jnp.float32)
+        parts = []
+        for head in (2 * pair, 2 * pair + 1):
+            mine = first if head % 2 == 0 else ~first
+            decay = jnp.exp(cum_rows[head : head + 1] - cumulative[:, head : head + 1] + blocked)
+            mix_grad = dot_nt(jnp.where(mine, driven, jnp.zeros_like(driven)), core_grad)
+            share = mix_grad * decay
+            coupling_grad = coupling_grad + share
+            spread = share * coupling
+            row_sums[head : head + 1] = jnp.sum(spread, 0, keepdims=True)
+            folded = sum(spread[:, k * LANES : (k + 1) * LANES] for k in range(CHUNK // LANES))
+            found = jnp.sum(jnp.where(mine, row_part, 0.0) - folded, 1, keepdims=True)
+            later = jnp.where(lane == head, found, later)
+            parts.append(dot_nn((coupling * decay).astype(jnp.bfloat16), core_grad))
+            found = jnp.sum(jnp.where(mine, col_part, 0.0), 1, keepdims=True)
+            earlier = jnp.where(lane == head, found, earlier)
+        driven_grad = jnp.where(first, parts[0], parts[1]) + back
+        act_grad_ref[:, at] = driven_grad * spread_step + grad * skip_ref[:, at]
+        skip_sum_ref[:, at] += jnp.sum(grad * act, 0, keepdims=True)
+        step_part = driven_grad * act
+        product_pair = product[:, at]
+        for head in (2 * pair, 2 * pair + 1):
+            mine = first if head % 2 == 0 else ~first
+            found = jnp.sum(jnp.where(mine, step_part, 0.0), 1, keepdims=True)
+            direct = jnp.where(lane == head, found, direct)
+            found = jnp.sum(jnp.where(mine[:1], product_pair, 0.0), 1, keepdims=True)
+            through = jnp.where(lane_row == head, found, through)
+    upper = (row <= col).astype(jnp.bfloat16)
+    below = (row > col).astype(jnp.bfloat16)
+    high, low = split_two(row_sums[...])
+    log_grad = (
+        exact_nn(upper, later)
+        + dot_nt(upper, high)
+        + dot_nt(upper, low)
+        + exact_nn(below, earlier)
+        + through * across
+    )
+    step_grad_ref[...] = direct + log_grad * rate
+    sums_ref[...] += jnp.sum(log_grad * step, 0, keepdims=True)
+    low_coupling = coupling_grad.astype(jnp.bfloat16)
+    coef_grad_ref[:, :NS] = dot_nn(low_coupling, coef_c) + dot_nt(moved[...], low_grad)
+    coef_grad_ref[:, NS:] = dot_tn(low_coupling, coef_b) + dot_nt(entered[...], low_state)
+    fresh = dot_tn(coef_c, entered[...])
+    for pair in range(act_ref.shape[1] // LANES):
+        at = slice(pair * LANES, (pair + 1) * LANES)
+        state_grad[:, at] = state_grad[:, at] * pick(across, pair) + fresh[:, at]
+
+
+def scan_back_call(step, coef, act, aux, seg_row, rate, skip_row, grad, kept):
+    rows, width = act.shape
+    chunks = rows // CHUNK
+    by_chunk = lambda columns: pl.BlockSpec((CHUNK, columns), lambda i: (chunks - 1 - i, 0))
+    one_row = lambda columns: pl.BlockSpec((1, columns), lambda i: (0, 0))
+    return pl.pallas_call(
+        scan_back_kernel,
+        grid=(chunks,),
+        in_specs=[
+            by_chunk(LANES),
+            by_chunk(2 * NS),
+            by_chunk(width),
+            by_chunk(LANES),
+            pl.BlockSpec((1, CHUNK), lambda i: (0, chunks - 1 - i)),
+            one_row(LANES),
+            one_row(width),
+            by_chunk(width),
+            pl.BlockSpec((1, NS, width), lambda i: (chunks - 1 - i, 0, 0)),
+        ],
+        out_specs=[
+            by_chunk(width),
+            by_chunk(LANES),
+            by_chunk(2 * NS),
+            one_row(LANES),
+            one_row(width),
+        ],
+        out_shape=[
+            jax.ShapeDtypeStruct((rows, width), jnp.float32),
+            jax.ShapeDtypeStruct((rows, LANES), jnp.float32),
+            jax.ShapeDtypeStruct((rows, 2 * NS), jnp.float32),
+            jax.ShapeDtypeStruct((1, LANES), jnp.float32),
+            jax.ShapeDtypeStruct((1, width), jnp.float32),
+        ],
+        scratch_shapes=[
+            pltpu.VMEM((NS, width), jnp.float32),
+            pltpu.VMEM((CHUNK, width), jnp.bfloat16),
+            pltpu.VMEM((CHUNK, width), jnp.bfloat16),
+            pltpu.VMEM((LANES, CHUNK), jnp.float32),
+        ],
+        compiler_params=pltpu.CompilerParams(vmem_limit_bytes=VMEM_BYTES),
+        name="scan_backward",
+    )(step, coef, act, aux, seg_row, rate, skip_row, grad, kept)
+
+
+def swap_halves(value):
+    width = value.shape[1]
+    half = HEAD_SIZE // 2
+    up = pltpu.roll(value, width - half, 1)
+    down = pltpu.roll(value, half, 1)
+    return jnp.where(grid_of(value.shape)[1] % HEAD_SIZE < half, up, down)
+
+
+def turned(value, cosine, sine):
+    return value * cosine + swap_halves(value) * sine
+
+
+def attend_kernel(query_ref, keyval_ref, seg_ref, seg_col_ref, cos_ref, sin_ref, out_ref, turned_ref, both_ref, log_ref):
+    rows = query_ref.shape[0]
+    first = grid_of((rows, LANES))[1] < HEAD_SIZE
+    keyval = keyval_ref[...]
+    moved = pltpu.roll(keyval, HEAD_SIZE, 1)
+    keys = turned(jnp.where(first, keyval, moved), cos_ref[...], sin_ref[...]).astype(jnp.bfloat16)
+    values = jnp.where(first, moved, keyval).astype(jnp.bfloat16)
+    both_ref[:, :LANES] = keys
+    both_ref[:, LANES:] = values
+    scale = HEAD_SIZE ** (-0.5)
+    head_lane = grid_of((CHUNK, LANES))[1]
+    first = head_lane < HEAD_SIZE
+    for block in range(rows // CHUNK):
+        low, high = block * CHUNK, (block + 1) * CHUNK
+        row, col = grid_of((CHUNK, high))
+        blocked = jnp.where(
+            (row + low >= col) & (seg_col_ref[low:high, 0:1] == seg_ref[:, :high]), 0.0, NEG_FILL
+        )
+        logs = jnp.zeros((CHUNK, LANES), jnp.float32)
+        for pair in range(query_ref.shape[1] // LANES):
+            at = slice(pair * LANES, (pair + 1) * LANES)
+            query = turned(query_ref[low:high, at], cos_ref[low:high], sin_ref[low:high]).astype(
+                jnp.bfloat16
+            )
+            turned_ref[low:high, at] = query
+            parts = []
+            for head in (2 * pair, 2 * pair + 1):
+                mine = first if head % 2 == 0 else ~first
+                scores = (
+                    dot_nt(jnp.where(mine, query, jnp.zeros_like(query)), keys[:high]) * scale
+                    + blocked
+                )
+                top = jnp.max(scores, 1, keepdims=True)
+                weights = jnp.exp(scores - top)
+                total = jnp.sum(weights, 1, keepdims=True)
+                probs = (weights * (1.0 / total)).astype(jnp.bfloat16)
+                parts.append(dot_nn(probs, values[:high]))
+                logs = jnp.where(head_lane == head, top + jnp.log(total), logs)
+            out_ref[low:high, at] = jnp.where(first, parts[0], parts[1]).astype(jnp.bfloat16)
+        log_ref[low:high] = logs
+
+
+def attend_call(query, keyval, seg_row, aux, cosine, sine):
+    rows, width = query.shape
+    return pl.pallas_call(
+        attend_kernel,
+        out_shape=[
+            jax.ShapeDtypeStruct((rows, width), jnp.bfloat16),
+            jax.ShapeDtypeStruct((rows, width), jnp.bfloat16),
+            jax.ShapeDtypeStruct((rows, 2 * LANES), jnp.bfloat16),
+            jax.ShapeDtypeStruct((rows, LANES), jnp.float32),
+        ],
+        compiler_params=pltpu.CompilerParams(vmem_limit_bytes=VMEM_BYTES),
+        name="attend_forward",
+    )(query, keyval, seg_row, aux, cosine, sine)
+
+
+def attend_back_kernel(
+    query_ref, both_ref, seg_ref, seg_col_ref, cos_ref, sin_ref, log_ref, out_ref, grad_ref,
+    query_grad_ref, keyval_grad_ref, key_sum, value_sum,
+):
+    rows = query_ref.shape[0]
+    key_sum[...] = jnp.zeros_like(key_sum)
+    value_sum[...] = jnp.zeros_like(value_sum)
+    scale = HEAD_SIZE ** (-0.5)
+    first = grid_of((CHUNK, LANES))[1] < HEAD_SIZE
+    for block in range(rows // CHUNK):
+        low, high = block * CHUNK, (block + 1) * CHUNK
+        row, col = grid_of((CHUNK, high))
+        blocked = jnp.where(
+            (row + low >= col) & (seg_col_ref[low:high, 0:1] == seg_ref[:, :high]), 0.0, NEG_FILL
+        )
+        keys = both_ref[:high, :LANES]
+        values = both_ref[:high, LANES:]
+        for pair in range(query_ref.shape[1] // LANES):
+            at = slice(pair * LANES, (pair + 1) * LANES)
+            query = query_ref[low:high, at]
+            grad = grad_ref[low:high, at]
+            inner = grad.astype(jnp.float32) * out_ref[low:high, at].astype(jnp.float32)
+            parts = []
+            key_part = None
+            for head in (2 * pair, 2 * pair + 1):
+                mine = first if head % 2 == 0 else ~first
+                query_mine = jnp.where(mine, query, jnp.zeros_like(query))
+                grad_mine = jnp.where(mine, grad, jnp.zeros_like(grad))
+                scores = dot_nt(query_mine, keys) * scale + blocked
+                probs = jnp.exp(scores - log_ref[low:high, head : head + 1])
+                delta = jnp.sum(jnp.where(mine, inner, 0.0), 1, keepdims=True)
+                prob_grad = dot_nt(grad_mine, values)
+                score_grad = (probs * (prob_grad - delta)).astype(jnp.bfloat16)
+                parts.append(dot_nn(score_grad, keys) * scale)
+                key_sum[:high] += dot_tn(score_grad, query_mine)
+                value_sum[:high] += dot_tn(probs.astype(jnp.bfloat16), grad_mine)
+            full = jnp.where(first, parts[0], parts[1])
+            query_grad_ref[low:high, at] = turned(full, cos_ref[low:high], -sin_ref[low:high]).astype(
+                jnp.bfloat16
+            )
+    wide = grid_of((rows, LANES))[1] < HEAD_SIZE
+    key_total = key_sum[...] * scale
+    key_total = key_total + pltpu.roll(key_total, HEAD_SIZE, 1)
+    key_total = turned(key_total, cos_ref[...], -sin_ref[...])
+    value_total = value_sum[...]
+    value_total = value_total + pltpu.roll(value_total, HEAD_SIZE, 1)
+    keyval_grad_ref[...] = jnp.where(wide, key_total, value_total).astype(jnp.bfloat16)
+
+
+def attend_back_call(query, both, seg_row, aux, cosine, sine, logs, out, grad):
+    rows, width = query.shape
+    return pl.pallas_call(
+        attend_back_kernel,
+        out_shape=[
+            jax.ShapeDtypeStruct((rows, width), jnp.bfloat16),
+            jax.ShapeDtypeStruct((rows, LANES), jnp.bfloat16),
+        ],
+        scratch_shapes=[
+            pltpu.VMEM((rows, LANES), jnp.float32),
+            pltpu.VMEM((rows, LANES), jnp.float32),
+        ],
+        compiler_params=pltpu.CompilerParams(vmem_limit_bytes=VMEM_BYTES),
+        name="attend_backward",
+    )(query, both, seg_row, aux, cosine, sine, logs, out, grad)
+
+
+def halve(value, bit):
+    half = value.shape[0] // 2
+    upper = (lax.axis_index("dp") & bit) != 0
+    got = swap_bit(jnp.where(upper, value[:half], value[half:]), bit)
+    kept = jnp.where(upper, value[half:], value[:half])
+    return (kept.astype(jnp.float32) + got.astype(jnp.float32)).astype(value.dtype)
+
+
+def double(value, bit):
+    upper = (lax.axis_index("dp") & bit) != 0
+    got = swap_bit(value, bit)
+    return jnp.concatenate([jnp.where(upper, got, value), jnp.where(upper, value, got)], 0)
+
+
+def dp_bits():
+    size = lax.axis_size("dp")
+    return [1 << i for i in range(size.bit_length() - 1)]
+
+
+def scatter_sum(value):
+    for bit in dp_bits():
+        value = halve(value, bit)
+    return value
+
+
+def gather_rows(value):
+    for bit in reversed(dp_bits()):
+        value = double(value, bit)
+    return value
+
+
+def conv_rows(value, kernel, bias, keeps):
+    taps = kernel.shape[0]
+    total = bias.astype(jnp.float32)[None]
+    for tap in range(taps):
+        offset = taps - 1 - tap
+        moved = jnp.pad(value, ((offset, 0), (0, 0)))[: value.shape[0]]
+        total = total + kernel[tap].astype(jnp.float32) * moved * keeps[offset]
+    return total
+
+
+def conv_rows_back(grad, value, kernel, keeps):
+    taps = kernel.shape[0]
+    grad_in = jnp.zeros_like(grad)
+    sums = []
+    for tap in range(taps):
+        offset = taps - 1 - tap
+        masked = grad * keeps[offset]
+        moved = jnp.pad(value, ((offset, 0), (0, 0)))[: value.shape[0]]
+        sums.append(jnp.sum(masked * moved, 0, keepdims=True))
+        grad_in = grad_in + kernel[tap].astype(jnp.float32) * jnp.pad(
+            masked, ((0, offset), (0, 0))
+        )[offset:]
+    return grad_in, sums
+
+
+def local_fast(
+    tokens,
+    segments,
+    cotangent,
+    input_gain,
+    query_weight,
+    key_value_weight,
+    attnout_weight,
+    gating_weight,
+    inner_weight,
+    state_weight,
+    step_weight,
+    conv_inner,
+    conv_state,
+    inner_bias,
+    state_bias,
+    step_bias,
+    decay_log,
+    skip_scale,
+    mixer_gain,
+    mixer_out,
+    post_gain,
+    gate_weight,
+    up_weight,
+    down_weight,
+):
+    low, wide = jnp.bfloat16, jnp.float32
+    rows, model = tokens.shape
+    heads = query_weight.shape[1] // HEAD_SIZE
+    ssm_heads = step_weight.shape[1]
+    ssm_width = ssm_heads * P_SIZE
+    query_width = heads * HEAD_SIZE
+    first_device = lax.axis_index("tensor") == 0
+    pick_head = lambda at: jnp.where(
+        first_device,
+        key_value_weight[:, at : at + HEAD_SIZE],
+        key_value_weight[:, at + HEAD_SIZE : at + 2 * HEAD_SIZE],
+    )
+    keyval_weight = jnp.concatenate([pick_head(0), pick_head(KEYVALUE_HEADS * HEAD_SIZE)], 1)
+    lane_pad = ((0, 0), (0, LANES - ssm_heads))
+    step_weight_wide = jnp.pad(step_weight, lane_pad)
+    step_bias_wide = jnp.pad(step_bias.astype(wide)[None], lane_pad)
+    rate = -jnp.exp(decay_log.astype(wide))
+    rate_wide = jnp.pad(rate[None], lane_pad)
+    skip_row = jnp.repeat(skip_scale.astype(wide), P_SIZE)[None]
+    cosine, sine = rotary_tables(rows)
+    cosine = jnp.concatenate([cosine] * 4, 1)
+    sine = jnp.concatenate([-sine, sine, -sine, sine], 1)
+    seg_row = segments.astype(wide)
+    seg_chunks = seg_row.reshape(-1, CHUNK)
+    ends = seg_chunks[:, -1:]
+    starts = jnp.concatenate([jnp.full((1, 1), -1.0, wide), ends[:-1]], 0)
+    aux = jnp.stack(
+        [seg_chunks, (seg_chunks == starts).astype(wide), (seg_chunks == ends).astype(wide)], -1
+    ).reshape(rows, 3)
+    aux = jnp.pad(aux, ((0, 0), (0, LANES - 3)))
+    keeps = [seg_keep(segments, offset)[0] for offset in range(conv_inner.shape[0])]
+
+    inputs = tokens.astype(wide)
+    inv_first = lax.rsqrt(jnp.mean(inputs * inputs, -1, keepdims=True) + EPS)
+    unit_first = inputs * inv_first
+    in_gain = input_gain.astype(wide)
+    normed = (unit_first * in_gain).astype(low)
+    inner = matmul(normed, inner_weight)
+    state_in = matmul(normed, state_weight)
+    step_arg = matmul(normed, step_weight_wide) + step_bias_wide
+    gating = matmul(normed, gating_weight)
+    inner_pre = conv_rows(inner, conv_inner, inner_bias, keeps)
+    inner_act = jax.nn.silu(inner_pre)
+    state_pre = conv_rows(state_in, conv_state, state_bias, keeps)
+    coef = jax.nn.silu(state_pre).astype(low)
+    step = jax.nn.softplus(step_arg)
+    core, kept = scan_call(step, coef, inner_act, aux, seg_row, rate_wide)
+    ssm_out = core + skip_row * inner_act
+    sigma_gate = jax.nn.sigmoid(gating)
+    gate_act = gating * sigma_gate
+    gated = ssm_out * gate_act
+    square_sum = pair_sum(jnp.sum(gated * gated, -1))[:, None]
+    query_pre = matmul(normed, query_weight)
+    keyval_pre = matmul(normed, keyval_weight)
+    attended, queries, both, logs = attend_call(query_pre, keyval_pre, seg_row, aux, cosine, sine)
+    attn_part = matmul(attended, attnout_weight)
+    inv_gate = lax.rsqrt(square_sum / DSSM + EPS)
+    mixer_scale = mixer_gain.astype(wide)
+    mixed = (gated * inv_gate * mixer_scale).astype(low)
+    branch_part = attn_part + matmul(mixed, mixer_out)
+    out_gain = post_gain.astype(wide)
+    branch = pair_sum(branch_part.astype(low))
+    middle = inputs + branch
+    inv_second = lax.rsqrt(jnp.mean(middle * middle, -1, keepdims=True) + EPS)
+    unit_second = middle * inv_second
+    post = (unit_second * out_gain).astype(low)
+    gate = matmul(post, gate_weight)
+    upward = matmul(post, up_weight)
+    sigma = jax.nn.sigmoid(gate)
+    hidden = (gate * sigma * upward).astype(low)
+    hidden_grad = dot_nt(cotangent, down_weight)
+    up_act_grad = (hidden_grad * gate * sigma).astype(low)
+    gate_act_grad = (hidden_grad * upward * sigma * (1.0 + gate * (1.0 - sigma))).astype(low)
+    post_part = dot_nt(gate_act_grad, gate_weight) + dot_nt(up_act_grad, up_weight)
+    post_gain_part = jnp.sum(post_part * unit_second, 0, keepdims=True)
+    post_full = pair_sum(post_part.astype(low))
+    down_wgrad = dot_tn(hidden, cotangent).astype(low)
+    gate_wgrad = dot_tn(post, gate_act_grad).astype(low)
+    up_wgrad = dot_tn(post, up_act_grad).astype(low)
+    down_wgrad, gate_wgrad, up_wgrad, post_full = lax.optimization_barrier(
+        (down_wgrad, gate_wgrad, up_wgrad, post_full)
+    )
+    down_wgrad, gate_wgrad, up_wgrad = lax.psum((down_wgrad, gate_wgrad, up_wgrad), "dp")
+    scaled_post = post_full * out_gain
+    middle_grad = cotangent.astype(wide) + inv_second * (
+        scaled_post - unit_second * jnp.mean(scaled_post * unit_second, -1, keepdims=True)
+    )
+    branch_grad = middle_grad.astype(low)
+    mixed_grad = dot_nt(branch_grad, mixer_out)
+    mixer_gain_part = jnp.sum(mixed_grad * gated * inv_gate, 0, keepdims=True)
+    weighted = mixed_grad * mixer_scale
+    cross = pair_sum(jnp.sum(weighted * gated, -1))[:, None]
+    attnout_part = dot_tn(attended, branch_grad).astype(low)
+    mixout_part = dot_tn(mixed, branch_grad).astype(low)
+    attended_grad = dot_nt(branch_grad, attnout_weight).astype(low)
+    gated_grad = inv_gate * weighted - gated * (inv_gate * inv_gate * inv_gate) * cross / DSSM
+    ssm_grad = gated_grad * gate_act
+    gating_grad = (
+        gated_grad * ssm_out * sigma_gate * (1.0 + gating * (1.0 - sigma_gate))
+    ).astype(low)
+    gating_part = dot_tn(normed, gating_grad).astype(low)
+    early = jnp.concatenate(
+        [jnp.concatenate([attnout_part, mixout_part], 0), gating_part], 1
+    )
+    early, ssm_grad = lax.optimization_barrier((early, ssm_grad))
+    act_grad, step_grad, coef_grad, rate_sum, skip_sum = scan_back_call(
+        step, coef, inner_act, aux, seg_row, rate_wide, skip_row, ssm_grad, kept
+    )
+    step_total = step_grad * jax.nn.sigmoid(step_arg)
+    inner_pre_grad = act_grad * silu_slope(inner_pre)
+    inner_grad, conv_inner_sums = conv_rows_back(inner_pre_grad, inner, conv_inner, keeps)
+    state_pre_grad = coef_grad * silu_slope(state_pre)
+    state_grad, conv_state_sums = conv_rows_back(state_pre_grad, state_in, conv_state, keeps)
+    scan_cat = jnp.concatenate(
+        [inner_grad.astype(low), step_total.astype(low), state_grad.astype(low)], 1
+    )
+    scan_part = dot_tn(normed, scan_cat).astype(low)
+    early_total = gather_rows(scatter_sum(early))
+    scan_part, attended_grad = lax.optimization_barrier((scan_part, attended_grad))
+    query_grad, keyval_grad = attend_back_call(
+        queries, both, seg_row, aux, cosine, sine, logs, attended, attended_grad
+    )
+    attend_cat = jnp.concatenate([query_grad, keyval_grad], 1)
+    attend_part = dot_tn(normed, attend_cat).astype(low)
+    weight_cat = jnp.concatenate(
+        [gating_weight, inner_weight, step_weight_wide, state_weight, query_weight, keyval_weight], 1
+    )
+    normed_part = dot_nt(jnp.concatenate([gating_grad, scan_cat, attend_cat], 1), weight_cat)
+    input_gain_part = jnp.sum(normed_part * unit_first, 0, keepdims=True)
+    normed_full = pair_sum(normed_part.astype(low))
+
+    own_rows = [
+        *conv_inner_sums,
+        jnp.sum(inner_pre_grad, 0, keepdims=True),
+        mixer_gain_part,
+        skip_sum,
+        jnp.sum(step_total, 0, keepdims=True),
+        rate_sum * rate_wide,
+    ]
+    shared_rows = [
+        input_gain_part,
+        post_gain_part,
+        *conv_state_sums,
+        jnp.sum(state_pre_grad, 0, keepdims=True),
+    ]
+    small = jnp.concatenate(
+        [jnp.pad(row, ((0, 0), (0, model - row.shape[1]))) for row in own_rows + shared_rows], 0
+    )
+    small_other = lax.ppermute(small, "tensor", [(0, 1), (1, 0)])
+    is_shared = lax.broadcasted_iota(jnp.int32, small.shape, 0) >= len(own_rows)
+    small = small + jnp.where(is_shared, small_other, 0.0)
+    for bit in dp_bits():
+        small = small + swap_bit(small, bit)
+
+    scan_piece = scatter_sum(scan_part)
+    scan_piece, early_total = lax.optimization_barrier((scan_piece, early_total))
+    attend_piece = scatter_sum(attend_part)
+    state_at = ssm_width + LANES
+    trade = jnp.concatenate([scan_piece[:, state_at:], attend_piece[:, query_width:]], 1)
+    other = lax.ppermute(trade, "tensor", [(0, 1), (1, 0)])
+    state_cols = state_weight.shape[1]
+    state_piece = (
+        trade[:, :state_cols].astype(wide) + other[:, :state_cols].astype(wide)
+    ).astype(low)
+    mine, theirs = trade[:, state_cols:], other[:, state_cols:]
+    head_0 = jnp.where(first_device, mine, theirs)
+    head_1 = jnp.where(first_device, theirs, mine)
+    scan_total = gather_rows(jnp.concatenate([scan_piece[:, :state_at], state_piece], 1))
+    attend_total = gather_rows(
+        jnp.concatenate(
+            [
+                attend_piece[:, :query_width],
+                head_0[:, :HEAD_SIZE],
+                head_1[:, :HEAD_SIZE],
+                head_0[:, HEAD_SIZE:],
+                head_1[:, HEAD_SIZE:],
+            ],
+            1,
+        )
+    )
+
+    scaled_in = normed_full * in_gain
+    tokens_grad = middle_grad + inv_first * (
+        scaled_in - unit_first * jnp.mean(scaled_in * unit_first, -1, keepdims=True)
+    )
+    count = len(own_rows)
+    taps = conv_inner.shape[0]
+    return (
+        tokens_grad,
+        small[count],
+        attend_total[:, :query_width].astype(wide),
+        attend_total[:, query_width:].astype(wide),
+        early_total[:query_width, :model].astype(wide),
+        early_total[:, model:].astype(wide),
+        scan_total[:, :ssm_width].astype(wide),
+        scan_total[:, state_at:].astype(wide),
+        scan_total[:, ssm_width : ssm_width + ssm_heads].astype(wide),
+        small[:taps, :ssm_width],
+        small[count + 2 : count + 2 + taps, :state_cols],
+        small[taps, :ssm_width],
+        small[count + 2 + taps, :state_cols],
+        small[taps + 3, :ssm_heads],
+        small[taps + 4, :ssm_heads],
+        jnp.sum(small[taps + 2, :ssm_width].reshape(ssm_heads, P_SIZE), 1),
+        small[taps + 1, :ssm_width],
+        early_total[query_width:, :model].astype(wide),
+        small[count + 1],
+        gate_wgrad.astype(wide),
+        up_wgrad.astype(wide),
+        down_wgrad.astype(wide),
+    )
+
+
+def layer(*arrays):
+    tokens, segments, query_weight, step_weight = arrays[0], arrays[1], arrays[4], arrays[10]
+    size = lax.axis_size("dp")
+    fits = (
+        lax.axis_size("tensor") == 2
+        and size & (size - 1) == 0
+        and segments.shape[0] == 1
+        and tokens.shape[0] % CHUNK == 0
+        and tokens.shape[1] % (16 * size) == 0
+        and query_weight.shape[1] == QUERY_HEADS // KEYVALUE_HEADS * HEAD_SIZE
+        and KEYVALUE_HEADS == 2
+        and step_weight.shape[1] % 2 == 0
+        and query_weight.shape[1] + step_weight.shape[1] * P_SIZE == tokens.shape[1]
+    )
+    return local_fast(*arrays) if fits else local(*arrays)
+
+
 def solution(mesh):
     placed = (
         P("dp", None),
@@ -606,7 +1325,7 @@
         P("tensor", None),
     )
     return jax.shard_map(
-        local,
+        layer,
         mesh=mesh,
         in_specs=placed,
         out_specs=(

time: 650 us -> 551 us (0.85)
  matrix products: 203 us -> 79.1 us
  Pallas kernels: 0 us -> 61.8 us
  local copies, waits for them, and re-layouts: 76 us -> 47.3 us
  other arithmetic: 141 us -> 113 us
  starting transfers between devices: 23.6 us -> 36.4 us
    dot_general x36 -> x14, matrix products: 175 us -> 48.8 us  [the longest x8 24.6 us: dot_tn(): lax.dot_general(left, right, (((0,), (0,)), ((), ())), preferred_element_...]
    pallas_call x0 -> x4, Pallas kernels: none -> 61.8 us  [the longest x1 24.9 us: scan_back_call(): pl.pallas_call(scan_back_kernel, grid=(chunks,), in_specs=[by_chunk(LANES...]
    ppermute x24 -> x28, waiting for transfers between devices: 95.2 us -> 120 us  [swap_bit(): return lax.ppermute(value, 'dp', [(i, i ^ bit) for i in range(size)])]
    ppermute x6 -> x5, waiting for transfers between devices: 86.8 us -> 68 us  [pair_sum(): other = lax.ppermute(value, 'tensor', [(0, 1), (1, 0)])]
    reduce_sum x13 -> x8, other arithmetic: 42.7 us -> 25.8 us  [the longest x1 9.41 us: local_fast(): jnp.sum(inner_pre_grad, 0, keepdims=True)]
    convert_element_type x33 -> x35, other arithmetic: 52 us -> 35.7 us  [the longest x1 4.57 us: local_fast(): branch_grad = middle_grad.astype(low)]
    unnamed x349 -> x164, local copies, waits for them, and re-layouts: 38.4 us -> 22.6 us
    unnamed x1 -> x4, other arithmetic: 0.01 us -> 12.5 us
  transfers between devices with their start and end apart: 32 -> 36, of which waited for: 20 -> 19; matrix products, arithmetic and copies ran while one was open for 36% -> 27% of each run, Pallas kernels for 0% -> 9%
where the time goes in v2:
time: 551 us; the launch traced here: 541 us
  waiting for transfers between devices  188 us (34%)
  other arithmetic  113 us (21%)
  matrix products  79.1 us (14%)
  Pallas kernels  61.8 us (11%)
  local copies, waits for them, and re-layouts  47.3 us (9%)
  starting transfers between devices  36.4 us (7%)
  between operations  15.8 us (3%)
    ppermute x28, waiting for transfers between devices, swap_bit(): return lax.ppermute(value, 'dp', [(i, i ^ bit) for i in range(size)])  120 us
    ppermute x5, waiting for transfers between devices, pair_sum(): other = lax.ppermute(value, 'tensor', [(0, 1), (1, 0)])  68 us
    dot_general x10, matrix products, matmul(): return jnp.dot(left, right, preferred_element_type=jnp.float32)  30.3 us
    ppermute x28, starting transfers between devices, swap_bit(): return lax.ppermute(value, 'dp', [(i, i ^ bit) for i in range(size)])  28.8 us
    pallas_call x1, Pallas kernels, scan_back_call(): pl.pallas_call(scan_back_kernel, grid=(chunks,), in_specs=[by_chunk(LANES...  24.9 us
    dot_general x8, matrix products, dot_tn(): lax.dot_general(left, right, (((0,), (0,)), ((), ())), preferred_element_...  24.6 us
    dot_general x6, matrix products, dot_nt(): lax.dot_general(left, right, (((1,), (1,)), ((), ())), preferred_element_...  24.3 us
    unnamed x164, local copies, waits for them, and re-layouts  22.6 us
  transfers between devices with their start and end apart: 36, of which 19 were waited for; matrix products, arithmetic and copies ran while one was open for 27% of the time, Pallas kernels for 9%

profile of v2, /device:TPU:0, one launch (start us, length us, event | category | flops | bytes accessed | tf_op | source)
XLA Modules:
  0.0 541.1 jit_solution(194426014656567130)
XLA Ops:
  10.4 4.0 copy.88
  19.5 3.6 fusion.78
  27.2 3.5 compare_select_fusion
  32.7 3.8 fusion.19
  36.5 12.9 %scan_forward.1 = (f32[1024,768]{1,0:T(8,128)}, bf16[4,128,768]{2,1,0:T(8,128)(2,1)}) custom-call(f32[1024,128]{1,0:T(8,128)} %get-tuple-element.238.step_ref, bf16[1024,256]{1,0:T(8,128)(2,1)} %get-tuple-element.182.coef_ref, f32[1024,768]{1,0:T(8,128)} %get-tuple-element.180.act_ref, f32[1024,128]{1,0:T(8,128)} %pad.127.seg_col_ref.aux_ref, ...), custom_call_target="tpu_custom_call" | custom-call | tf_op jit(solution)/shard_map/scan_forward/pallas_call | solution.py:672
  49.4 6.9 %multiply_reduce_fusion.9 = (f32[1024]{0:T(1024)S(1)}, f32[1024,768]{1,0:T(8,128)}, f32[1024,768]{1,0:T(8,128)}) fusion(f32[1024,768]{1,0:T(8,128)} %get-tuple-element.46, f32[1024,768]{1,0:T(8,128)S(1)} %get-tuple-element.181, f32[768]{0:T(1024)S(1)} %mul.685, bf16[1024,1024]{0,1:T(8,128)(2,1)S(1)} %copy-done.11, bf16[1024,768]{1,0:T(8,128)(2,1)} %param.31), kind=kOutput, calls=%fused_computation.53 | convolution fusion | flops 1620835328 | bytes 16260096 | tf_op jit(solution)/shard_map/dot_general | solution.py:22
  65.5 3.3 fusion.49.keyval_ref
  70.7 10.9 %attend_forward.1 = (bf16[1024,256]{1,0:T(8,128)(2,1)}, bf16[1024,256]{1,0:T(8,128)(2,1)}, bf16[1024,256]{1,0:T(8,128)(2,1)}, f32[1024,128]{1,0:T(8,128)}) custom-call(f32[1024,256]{1,0:T(8,128)} %fusion.76.query_ref, f32[1024,128]{1,0:T(8,128)} %fusion.49.keyval_ref, f32[1,1024]{1,0:T(1,128)} %get-tuple-element.224.seg_ref, ...), custom_call_target="tpu_custom_call" | custom-call | tf_op jit(solution)/shard_map/attend_forward/pallas_call | solution.py:909
  81.6 3.5 fusion.62
  88.9 4.4 copy.87
  94.2 7.8 %concatenate.89 = bf16[1024,2304]{1,0:T(8,128)(2,1)} concatenate(bf16[1024,768]{1,0:T(8,128)(2,1)} %param.31, bf16[1024,768]{1,0:T(8,128)(2,1)} %param.32, bf16[1024,128]{1,0:T(8,128)(2,1)S(1)} %pad.128.clone, bf16[1024,256]{1,0:T(8,128)(2,1)} %param.33, bf16[1024,256]{1,0:T(8,128)(2,1)} %param.28, bf16[1024,64]{1,0:T(8,128)(2,1)S(1)} %get-tuple-element.204, ...), dimensions={1} | concatenate | bytes 9437184 | tf_op jit(solution)/shard_map/concatenate | solution.py:1194
  102.5 32.2 %collective-permute-done.1 = bf16[1024,1024]{0,1:T(8,128)(2,1)} collective-permute-done((bf16[1024,1024]{0,1:T(8,128)(2,1)}, bf16[1024,1024]{0,1:T(8,128)(2,1)}, u32[]{:S(2)}, u32[]{:S(2)}) %collective-permute-start.1) | collective-permute-done | bytes 2097184 | tf_op jit(solution)/shard_map/ppermute | solution.py:101
  134.7 4.3 multiply_reduce_fusion.2
  139.1 3.5 multiply_convert_fusion.3
  147.6 4.1 multiply_convert_fusion
  154.0 5.1 fusion.74
  159.4 3.6 convolution_convert_fusion.2
  163.0 3.6 convolution_convert_fusion.1
  166.7 3.9 fusion.26
  170.6 35.0 %collective-permute-done.2 = bf16[1024,1024]{0,1:T(8,128)(2,1)} collective-permute-done((bf16[1024,1024]{0,1:T(8,128)(2,1)}, bf16[1024,1024]{0,1:T(8,128)(2,1)}, u32[]{:S(2)}, u32[]{:S(2)}) %collective-permute-start.2) | collective-permute-done | bytes 2097184 | tf_op jit(solution)/shard_map/ppermute | solution.py:101
  205.6 3.1 convert_add_fusion.1
  208.8 5.1 multiply_reduce_fusion
  214.0 4.6 fusion.63
  218.6 3.9 multiply_reduce_fusion.3
  222.5 3.3 convolution_convert_fusion.4
  231.0 7.9 %constant_dynamic-update-slice_fusion.5 = (bf16[1024,2304]{1,0:T(8,128)(2,1)}, bf16[1024,768]{1,0:T(8,128)(2,1)S(1)}) fusion(f32[1024,768]{1,0:T(8,128)} %get-tuple-element.240, f32[1024,768]{1,0:T(8,128)} %get-tuple-element.46, f32[1024,768]{1,0:T(8,128)} %copy-done.7, f32[768]{0:T(1024)S(1)} %mul.685, f32[1024]{0:T(1024)S(1)} %add.310, ...), kind=kLoop, calls=%fused_computation.215 | loop fusion | flops 17301504 | bytes 18892800
  245.1 3.8 pad_maximum_fusion
  249.0 24.9 %scan_backward.1 = (f32[1024,768]{1,0:T(8,128)}, f32[1024,128]{1,0:T(8,128)}, f32[1024,256]{1,0:T(8,128)}, f32[1,128]{1,0:T(1,128)}, f32[1,768]{1,0:T(1,128)}) custom-call(f32[1024,128]{1,0:T(8,128)} %get-tuple-element.238.step_ref, bf16[1024,256]{1,0:T(8,128)(2,1)} %get-tuple-element.182.coef_ref, f32[1024,768]{1,0:T(8,128)} %get-tuple-element.180.act_ref, ...), custom_call_target="tpu_custom_call" | custom-call | tf_op jit(solution)/shard_map/scan_backward/pallas_call | solution.py:814
  273.9 9.4 %fusion.64 = (f32[768]{0:T(1024)S(1)}, f32[768]{0:T(1024)S(1)}, f32[768]{0:T(1024)S(1)}, f32[768]{0:T(1024)S(1)}, f32[768]{0:T(1024)S(1)}, /*index=5*/f32[1024,7...) fusion(f32[1024,768]{1,0:T(8,128)} %fusion.78, f32[1024]{0:T(1024)S(1)} %bitcast.96, ...), kind=kLoop, calls=%fused_computation.257 | loop fusion | flops 15724800 | bytes 22047744 | tf_op jit(solution)/shard_map/reduce_sum | solution.py:1203
  290.3 4.2 convolution_convert_fusion
  294.6 13.1 %attend_backward.1 = (bf16[1024,256]{1,0:T(8,128)(2,1)}, bf16[1024,128]{1,0:T(8,128)(2,1)}) custom-call(bf16[1024,256]{1,0:T(8,128)(2,1)} %get-tuple-element.53.query_ref, bf16[1024,256]{1,0:T(8,128)(2,1)} %get-tuple-element.54.both_ref, f32[1,1024]{1,0:T(1,128)} %get-tuple-element.224.seg_ref, f32[1024,128]{1,0:T(8,128)} %pad.127.seg_col_ref.aux_ref, ...), custom_call_target="tpu_custom_call" | custom-call | tf_op jit(solution)/shard_map/attend_backward/pallas_call | solution.py:973
  312.3 7.2 %fusion.75 = (bf16[1024,1024]{0,1:T(8,128)(2,1)S(1)}, f32[1024,1024]{0,1:T(8,128)S(1)}) fusion(bf16[1024,2304]{1,0:T(8,128)(2,1)S(1)} %constant_dynamic-update-slice_fusion, bf16[1024,2304]{1,0:T(8,128)(2,1)} %concatenate.89), kind=kOutput, calls=%fused_computation.264 | convolution fusion | flops 4832886784 | bytes 15728640 | tf_op jit(solution)/shard_map/dot_general | solution.py:593
  324.0 5.3 collective-permute-done.11
  331.2 5.3 collective-permute-done.12
  347.6 19.6 %collective-permute-done.19 = bf16[256,1792]{1,0:T(8,128)(2,1)S(1)} collective-permute-done((bf16[256,1792]{1,0:T(8,128)(2,1)S(1)}, bf16[256,1792]{1,0:T(8,128)(2,1)S(1)}, u32[]{:S(2)}, u32[]{:S(2)}) %collective-permute-start.19) | collective-permute-done | bytes 917536 | tf_op jit(solution)/shard_map/ppermute | solution.py:108
  370.2 13.3 %collective-permute-done.20 = bf16[128,1792]{1,0:T(8,128)(2,1)S(1)} collective-permute-done((bf16[128,1792]{1,0:T(8,128)(2,1)S(1)}, bf16[128,1792]{1,0:T(8,128)(2,1)S(1)}, u32[]{:S(2)}, u32[]{:S(2)}) %collective-permute-start.20) | collective-permute-done | bytes 458784 | tf_op jit(solution)/shard_map/ppermute | solution.py:108
  386.5 10.0 %collective-permute-done.21 = bf16[64,1792]{1,0:T(8,128)(2,1)S(1)} collective-permute-done((bf16[64,1792]{1,0:T(8,128)(2,1)S(1)}, bf16[64,1792]{1,0:T(8,128)(2,1)S(1)}, u32[]{:S(2)}, u32[]{:S(2)}) %collective-permute-start.21) | collective-permute-done | bytes 229408 | tf_op jit(solution)/shard_map/ppermute | solution.py:108
  396.6 3.4 collective-permute-start.16
  400.0 9.3 %collective-permute-done.22 = bf16[64,1792]{1,0:T(8,128)(2,1)S(1)} collective-permute-done((bf16[64,1792]{1,0:T(8,128)(2,1)S(1)}, bf16[64,1792]{1,0:T(8,128)(2,1)S(1)}, u32[]{:S(2)}, u32[]{:S(2)}) %collective-permute-start.22) | collective-permute-done | bytes 229408 | tf_op jit(solution)/shard_map/ppermute | solution.py:108
  414.9 7.9 %collective-permute-done.23 = bf16[128,1792]{1,0:T(8,128)(2,1)} collective-permute-done((bf16[128,1792]{1,0:T(8,128)(2,1)}, bf16[128,1792]{1,0:T(8,128)(2,1)}, u32[]{:S(2)}, u32[]{:S(2)}) %collective-permute-start.23) | collective-permute-done | bytes 458784 | tf_op jit(solution)/shard_map/ppermute | solution.py:108
  428.8 18.1 %collective-permute-done.7 = f32[16,1024]{1,0:T(8,128)S(1)} collective-permute-done((f32[16,1024]{1,0:T(8,128)S(1)}, f32[16,1024]{1,0:T(8,128)S(1)}, u32[]{:S(2)}, u32[]{:S(2)}) %collective-permute-start.7) | collective-permute-done | bytes 65568 | tf_op jit(solution)/shard_map/ppermute | solution.py:108
  450.4 6.2 %fusion.8 = f32[1024,1024]{0,1:T(8,128)} fusion(bf16[1024,1024]{0,1:T(8,128)(2,1)S(1)} %copy-done.4, bf16[1024,1024]{0,1:T(8,128)(2,1)S(1)} %copy-done.24, bf16[1024,1024]{0,1:T(8,128)(2,1)S(1)} %copy-done.22, f32[1024]{0:T(1024)S(1)} %broadcast_multiply_fusion.6, f32[1024]{0:T(1024)S(1)} %copy-done.54, f32[1024]{0:T(1024)S(1)} %copy-done.56, ...), kind=kLoop, calls=%fused_computation.11 | loop fusion | flops 22020096 | bytes 20996096 | tf_op jit(solution)/shard_map/add | solution.py:1252
  456.6 5.6 %copy.104 = f32[1024,1024]{1,0:T(8,128)} copy(f32[1024,1024]{0,1:T(8,128)} %fusion.8) | data formatting | bytes 8388608
  465.8 4.0 collective-permute-done.9
  479.8 4.2 convert_element_type.468
  492.4 6.6 %collective-permute-done.31 = bf16[64,1152]{1,0:T(8,128)(2,1)S(1)} collective-permute-done((bf16[64,1152]{1,0:T(8,128)(2,1)S(1)}, bf16[64,1152]{1,0:T(8,128)(2,1)S(1)}, u32[]{:S(2)}, u32[]{:S(2)}) %collective-permute-start.31) | collective-permute-done | bytes 147488 | tf_op jit(solution)/shard_map/ppermute | solution.py:108
  501.2 6.3 %collective-permute-done.32 = bf16[128,1152]{1,0:T(8,128)(2,1)S(1)} collective-permute-done((bf16[128,1152]{1,0:T(8,128)(2,1)S(1)}, bf16[128,1152]{1,0:T(8,128)(2,1)S(1)}, u32[]{:S(2)}, u32[]{:S(2)}) %collective-permute-start.32) | collective-permute-done | bytes 294944 | tf_op jit(solution)/shard_map/ppermute | solution.py:108
  511.9 9.8 %collective-permute-done.33 = bf16[256,1152]{1,0:T(8,128)(2,1)S(1)} collective-permute-done((bf16[256,1152]{1,0:T(8,128)(2,1)S(1)}, bf16[256,1152]{1,0:T(8,128)(2,1)S(1)}, u32[]{:S(2)}, u32[]{:S(2)}) %collective-permute-start.33) | collective-permute-done | bytes 589856 | tf_op jit(solution)/shard_map/ppermute | solution.py:108
  (379 shorter events, 140.0 us)
Async XLA Ops:
  7.2 137.8 %copy-start = (bf16[1024,1024]{1,0:T(8,128)(2,1)S(1)}, bf16[1024,1024]{1,0:T(8,128)(2,1)}, u32[]{:S(2)}) copy-start(bf16[1024,1024]{1,0:T(8,128)(2,1)} %param.46) | copy-start | bytes 6291460
  7.2 472.6 %all-reduce.36.cloned.1.call-start = ((), (), s32[]{:S(2)}) async-start(), calls=%async_computation | async-start | bytes 12582912 | tf_op jit(solution)/shard_map/psum | solution.py:1152
  36.5 19.9 %copy-start.7 = (f32[1024,768]{1,0:T(8,128)}, f32[1024,768]{1,0:T(8,128)S(1)}, u32[]{:S(2)}) copy-start(f32[1024,768]{1,0:T(8,128)S(1)} %get-tuple-element.181) | copy-start | bytes 9437188
  56.4 25.2 %collective-permute-start = (f32[1024]{0:T(1024)S(1)}, f32[1024]{0:T(1024)S(1)}, u32[]{:S(2)}, u32[]{:S(2)}) collective-permute-start(f32[1024]{0:T(1024)S(1)} %get-tuple-element.178), channel_id=1, source_target_pairs={{0,1},{1,0},{2,3},{3,2},{4,5},{5,4},{6,7},{7,6},{8,9},{9,8},{10,11... | collective-permute-start | bytes 12296 | tf_op jit(solution)/shard_map/ppermute | solution.py:101
  87.3 47.4 %collective-permute-start.1 = (bf16[1024,1024]{0,1:T(8,128)(2,1)}, bf16[1024,1024]{0,1:T(8,128)(2,1)}, u32[]{:S(2)}, u32[]{:S(2)}) collective-permute-start(bf16[1024,1024]{0,1:T(8,128)(2,1)} %add_convert_fusion), channel_id=1, source_target_pairs={{0,1},{1,0},{2,3},{3,2},{4,5},{5,4},{6,7},{7,6},{8,9},{9,8},{10,11... | collective-permute-start | bytes 6291464 | tf_op jit(solution)/shard_map/ppermute | solution.py:101
  102.5 36.6 %copy-start.3 = (bf16[1024,1024]{0,1:T(8,128)(2,1)S(1)}, bf16[1024,1024]{0,1:T(8,128)(2,1)}, u32[]{:S(2)}) copy-start(bf16[1024,1024]{0,1:T(8,128)(2,1)} %copy.88) | copy-start | bytes 6291460
  159.1 46.5 %collective-permute-start.2 = (bf16[1024,1024]{0,1:T(8,128)(2,1)}, bf16[1024,1024]{0,1:T(8,128)(2,1)}, u32[]{:S(2)}, u32[]{:S(2)}) collective-permute-start(bf16[1024,1024]{0,1:T(8,128)(2,1)} %get-tuple-element.241), channel_id=1, source_target_pairs={{0,1},{1,0},{2,3},{3,2},{4,5},{5,4},{6,7},{7,6},{8,9},{9,8},{10,11... | collective-permute-start | bytes 6291464 | tf_op jit(solution)/shard_map/ppermute | solution.py:101
  170.6 38.1 %copy-start.4 = (bf16[1024,1024]{0,1:T(8,128)(2,1)S(1)}, bf16[1024,1024]{0,1:T(8,128)(2,1)}, u32[]{:S(2)}) copy-start(bf16[1024,1024]{0,1:T(8,128)(2,1)} %copy.88) | copy-start | bytes 6291460
  170.6 38.1 %copy-start.30 = (f32[1024,1024]{0,1:T(8,128)S(1)}, f32[1024,1024]{0,1:T(8,128)}, u32[]{:S(2)}) copy-start(f32[1024,1024]{0,1:T(8,128)} %get-tuple-element.242) | copy-start | bytes 12582916
  227.4 3.6 collective-permute-start.3
  319.5 90.6 %copy-start.21 = (bf16[1024,1024]{0,1:T(8,128)(2,1)}, bf16[1024,1024]{0,1:T(8,128)(2,1)S(1)}, u32[]{:S(2)}) copy-start(bf16[1024,1024]{0,1:T(8,128)(2,1)S(1)} %get-tuple-element.244) | copy-start | bytes 6291460
  319.5 90.6 %collective-permute-start.4 = (bf16[1024,1024]{0,1:T(8,128)(2,1)S(1)}, bf16[1024,1024]{0,1:T(8,128)(2,1)S(1)}, u32[]{:S(2)}, u32[]{:S(2)}) collective-permute-start(bf16[1024,1024]{0,1:T(8,128)(2,1)S(1)} %get-tuple-element.244), channel_id=1, source_target_pairs={{0,1},{1,0},{2,3},{3,2},{4,5},{5,4},{6,7},{7,6},{8,9},{9,8},{10,11... | collective-permute-start | bytes 6291464 | tf_op jit(solution)/shard_map/ppermute | solution.py:101
  320.3 1.8 collective-permute-start.10
  320.6 18.7 %collective-permute-start.18 = (bf16[512,1792]{1,0:T(8,128)(2,1)S(1)}, bf16[512,1792]{1,0:T(8,128)(2,1)S(1)}, u32[]{:S(2)}, u32[]{:S(2)}) collective-permute-start(bf16[512,1792]{1,0:T(8,128)(2,1)S(1)} %broadcast_select_fusion.2), channel_id=1, source_target_pairs={{0,2},{2,0},{4,6},{6,4},{8,10},{10,8},{12,14},{14,12},{16,18},{18,... | collective-permute-start | bytes 5505032 | tf_op jit(solution)/shard_map/ppermute | solution.py:108
  322.3 7.0 %collective-permute-start.11 = (bf16[256,384]{1,0:T(8,128)(2,1)S(1)}, bf16[256,384]{1,0:T(8,128)(2,1)S(1)}, u32[]{:S(2)}, u32[]{:S(2)}) collective-permute-start(bf16[256,384]{1,0:T(8,128)(2,1)S(1)} %broadcast_select_fusion.26), channel_id=1, source_target_pairs={{0,4},{2,6},{4,0},{6,2},{8,12},{10,14},{12,8},{14,10},{16,20},{18,... | collective-permute-start | bytes 589832 | tf_op jit(solution)/shard_map/ppermute | solution.py:108
  329.4 7.1 %collective-permute-start.12 = (bf16[128,384]{1,0:T(8,128)(2,1)S(1)}, bf16[128,384]{1,0:T(8,128)(2,1)S(1)}, u32[]{:S(2)}, u32[]{:S(2)}) collective-permute-start(bf16[128,384]{1,0:T(8,128)(2,1)S(1)} %broadcast_select_fusion.32), channel_id=1, source_target_pairs={{0,8},{2,10},{4,12},{6,14},{8,0},{10,2},{12,4},{14,6},{16,24},{18,... | collective-permute-start | bytes 294920 | tf_op jit(solution)/shard_map/ppermute | solution.py:108
  331.1 16.0 %collective-permute-start.14 = (bf16[512,1152]{1,0:T(8,128)(2,1)S(1)}, bf16[512,1152]{1,0:T(8,128)(2,1)S(1)}, u32[]{:S(2)}, u32[]{:S(2)}) collective-permute-start(bf16[512,1152]{1,0:T(8,128)(2,1)S(1)} %broadcast_select_fusion.5), channel_id=1, source_target_pairs={{0,2},{2,0},{4,6},{6,4},{8,10},{10,8},{12,14},{14,12},{16,18},{18,... | collective-permute-start | bytes 3538952 | tf_op jit(solution)/shard_map/ppermute | solution.py:108
  336.6 10.5 %collective-permute-start.13 = (bf16[64,384]{1,0:T(8,128)(2,1)S(1)}, bf16[64,384]{1,0:T(8,128)(2,1)S(1)}, u32[]{:S(2)}, u32[]{:S(2)}) collective-permute-start(bf16[64,384]{1,0:T(8,128)(2,1)S(1)} %broadcast_select_fusion.35), channel_id=1, source_target_pairs={{0,16},{2,18},{4,20},{6,22},{8,24},{10,26},{12,28},{14,30},{16,0},... | collective-permute-start | bytes 147464 | tf_op jit(solution)/shard_map/ppermute | solution.py:108
  340.0 27.2 %collective-permute-start.19 = (bf16[256,1792]{1,0:T(8,128)(2,1)S(1)}, bf16[256,1792]{1,0:T(8,128)(2,1)S(1)}, u32[]{:S(2)}, u32[]{:S(2)}) collective-permute-start(bf16[256,1792]{1,0:T(8,128)(2,1)S(1)} %broadcast_select_fusion.8), channel_id=1, source_target_pairs={{0,4},{2,6},{4,0},{6,2},{8,12},{10,14},{12,8},{14,10},{16,20},{18,... | collective-permute-start | bytes 2752520 | tf_op jit(solution)/shard_map/ppermute | solution.py:108
  347.1 20.4 %copy-start.49 = (bf16[64,384]{1,0:T(8,128)(2,1)}, bf16[64,384]{1,0:T(8,128)(2,1)S(1)}, u32[]{:S(2)}) copy-start(bf16[64,384]{1,0:T(8,128)(2,1)S(1)} %add_convert_fusion.12) | copy-start | bytes 147460
  367.6 15.9 %collective-permute-start.20 = (bf16[128,1792]{1,0:T(8,128)(2,1)S(1)}, bf16[128,1792]{1,0:T(8,128)(2,1)S(1)}, u32[]{:S(2)}, u32[]{:S(2)}) collective-permute-start(bf16[128,1792]{1,0:T(8,128)(2,1)S(1)} %broadcast_select_fusion.16), channel_id=1, source_target_pairs={{0,8},{2,10},{4,12},{6,14},{8,0},{10,2},{12,4},{14,6},{16,24},{18,... | collective-permute-start | bytes 1376264 | tf_op jit(solution)/shard_map/ppermute | solution.py:108
  369.2 17.0 %collective-permute-start.15 = (bf16[256,1152]{1,0:T(8,128)(2,1)S(1)}, bf16[256,1152]{1,0:T(8,128)(2,1)S(1)}, u32[]{:S(2)}, u32[]{:S(2)}) collective-permute-start(bf16[256,1152]{1,0:T(8,128)(2,1)S(1)} %broadcast_select_fusion.11), channel_id=1, source_target_pairs={{0,4},{2,6},{4,0},{6,2},{8,12},{10,14},{12,8},{14,10},{16,20},{18,... | collective-permute-start | bytes 1769480 | tf_op jit(solution)/shard_map/ppermute | solution.py:108
  383.7 26.4 %copy-start.54 = (f32[1024]{0:T(1024)S(1)}, f32[1024]{0:T(1024)}, u32[]{:S(2)}) copy-start(f32[1024]{0:T(1024)} %copy-done.53) | copy-start | bytes 12292
  383.7 26.4 %copy-start.56 = (f32[1024]{0:T(1024)S(1)}, f32[1024]{0:T(1024)}, u32[]{:S(2)}) copy-start(f32[1024]{0:T(1024)} %copy-done.55) | copy-start | bytes 12292
  383.7 12.7 %collective-permute-start.21 = (bf16[64,1792]{1,0:T(8,128)(2,1)S(1)}, bf16[64,1792]{1,0:T(8,128)(2,1)S(1)}, u32[]{:S(2)}, u32[]{:S(2)}) collective-permute-start(bf16[64,1792]{1,0:T(8,128)(2,1)S(1)} %broadcast_select_fusion.25), channel_id=1, source_target_pairs={{0,16},{2,18},{4,20},{6,22},{8,24},{10,26},{12,28},{14,30},{16,0},... | collective-permute-start | bytes 688136 | tf_op jit(solution)/shard_map/ppermute | solution.py:108
  396.5 12.8 %collective-permute-start.22 = (bf16[64,1792]{1,0:T(8,128)(2,1)S(1)}, bf16[64,1792]{1,0:T(8,128)(2,1)S(1)}, u32[]{:S(2)}, u32[]{:S(2)}) collective-permute-start(bf16[64,1792]{1,0:T(8,128)(2,1)S(1)} %add_convert_fusion.8), channel_id=1, source_target_pairs={{0,16},{2,18},{4,20},{6,22},{8,24},{10,26},{12,28},{14,30},{16,0},... | collective-permute-start | bytes 688136 | tf_op jit(solution)/shard_map/ppermute | solution.py:108
  396.6 29.0 %collective-permute-start.16 = (bf16[128,1152]{1,0:T(8,128)(2,1)S(1)}, bf16[128,1152]{1,0:T(8,128)(2,1)}, u32[]{:S(2)}, u32[]{:S(2)}) collective-permute-start(bf16[128,1152]{1,0:T(8,128)(2,1)S(1)} %broadcast_select_fusion.20), channel_id=1, source_target_pairs={{0,8},{2,10},{4,12},{6,14},{8,0},{10,2},{12,4},{14,6},{16,24},{18,... | collective-permute-start | bytes 884744 | tf_op jit(solution)/shard_map/ppermute | solution.py:108
  410.1 12.7 %collective-permute-start.23 = (bf16[128,1792]{1,0:T(8,128)(2,1)}, bf16[128,1792]{1,0:T(8,128)(2,1)}, u32[]{:S(2)}, u32[]{:S(2)}) collective-permute-start(bf16[128,1792]{1,0:T(8,128)(2,1)} %pad_maximum_fusion.10), channel_id=1, source_target_pairs={{0,8},{2,10},{4,12},{6,14},{8,0},{10,2},{12,4},{14,6},{16,24},{18,... | collective-permute-start | bytes 1376264 | tf_op jit(solution)/shard_map/ppermute | solution.py:108
  413.4 13.4 %collective-permute-start.5 = (f32[16,1024]{1,0:T(8,128)S(1)}, f32[16,1024]{1,0:T(8,128)S(1)}, u32[]{:S(2)}, u32[]{:S(2)}) collective-permute-start(f32[16,1024]{1,0:T(8,128)S(1)} %concatenate.90), channel_id=1, source_target_pairs={{0,1},{1,0},{2,3},{3,2},{4,5},{5,4},{6,7},{7,6},{8,9},{9,8},{10,11... | collective-permute-start | bytes 196616 | tf_op jit(solution)/shard_map/ppermute | solution.py:1218
  424.0 26.2 %copy-start.24 = (bf16[1024,1024]{0,1:T(8,128)(2,1)S(1)}, bf16[1024,1024]{0,1:T(8,128)(2,1)}, u32[]{:S(2)}) copy-start(bf16[1024,1024]{0,1:T(8,128)(2,1)} %copy-done.23) | copy-start | bytes 6291460
  424.1 23.5 %collective-permute-start.24 = (bf16[256,1792]{1,0:T(8,128)(2,1)S(1)}, bf16[256,1792]{1,0:T(8,128)(2,1)S(1)}, u32[]{:S(2)}, u32[]{:S(2)}) collective-permute-start(bf16[256,1792]{1,0:T(8,128)(2,1)S(1)} %pad_maximum_fusion.4), channel_id=1, source_target_pairs={{0,4},{2,6},{4,0},{6,2},{8,12},{10,14},{12,8},{14,10},{16,20},{18,... | collective-permute-start | bytes 2752520 | tf_op jit(solution)/shard_map/ppermute | solution.py:108
  425.6 24.6 %copy-start.22 = (bf16[1024,1024]{0,1:T(8,128)(2,1)S(1)}, bf16[1024,1024]{0,1:T(8,128)(2,1)}, u32[]{:S(2)}) copy-start(bf16[1024,1024]{0,1:T(8,128)(2,1)} %copy-done.21) | copy-start | bytes 6291460
  426.9 1.3 collective-permute-start.6
  427.0 37.8 %collective-permute-start.17 = (bf16[64,1152]{1,0:T(8,128)(2,1)S(1)}, bf16[64,1152]{1,0:T(8,128)(2,1)}, u32[]{:S(2)}, u32[]{:S(2)}) collective-permute-start(bf16[64,1152]{1,0:T(8,128)(2,1)S(1)} %broadcast_select_fusion.29), channel_id=1, source_target_pairs={{0,16},{2,18},{4,20},{6,22},{8,24},{10,26},{12,28},{14,30},{16,0},... | collective-permute-start | bytes 442376 | tf_op jit(solution)/shard_map/ppermute | solution.py:108
  428.2 18.7 %collective-permute-start.7 = (f32[16,1024]{1,0:T(8,128)S(1)}, f32[16,1024]{1,0:T(8,128)S(1)}, u32[]{:S(2)}, u32[]{:S(2)}) collective-permute-start(f32[16,1024]{1,0:T(8,128)S(1)} %add.324), channel_id=1, source_target_pairs={{0,4},{2,6},{4,0},{6,2},{8,12},{10,14},{12,8},{14,10},{16,20},{18,... | collective-permute-start | bytes 196616 | tf_op jit(solution)/shard_map/ppermute | solution.py:108
  446.9 15.4 %collective-permute-start.8 = (f32[16,1024]{1,0:T(8,128)S(1)}, f32[16,1024]{1,0:T(8,128)}, u32[]{:S(2)}, u32[]{:S(2)}) collective-permute-start(f32[16,1024]{1,0:T(8,128)S(1)} %add.325), channel_id=1, source_target_pairs={{0,8},{2,10},{4,12},{6,14},{8,0},{10,2},{12,4},{14,6},{16,24},{18,... | collective-permute-start | bytes 196616 | tf_op jit(solution)/shard_map/ppermute | solution.py:108
  450.2 20.8 %collective-permute-start.25 = (bf16[512,1792]{1,0:T(8,128)(2,1)}, bf16[512,1792]{1,0:T(8,128)(2,1)}, u32[]{:S(2)}, u32[]{:S(2)}) collective-permute-start(bf16[512,1792]{1,0:T(8,128)(2,1)} %pad_maximum_fusion.2), channel_id=1, source_target_pairs={{0,2},{2,0},{4,6},{6,4},{8,10},{10,8},{12,14},{14,12},{16,18},{18,... | collective-permute-start | bytes 5505032 | tf_op jit(solution)/shard_map/ppermute | solution.py:108
  463.1 6.7 %collective-permute-start.9 = (f32[16,1024]{1,0:T(8,128)S(1)}, f32[16,1024]{1,0:T(8,128)S(1)}, u32[]{:S(2)}, u32[]{:S(2)}) collective-permute-start(f32[16,1024]{1,0:T(8,128)S(1)} %add.326), channel_id=1, source_target_pairs={{0,16},{2,18},{4,20},{6,22},{8,24},{10,26},{12,28},{14,30},{16,0},... | collective-permute-start | bytes 196616 | tf_op jit(solution)/shard_map/ppermute | solution.py:108
  475.2 13.8 %collective-permute-start.26 = (bf16[64,384]{1,0:T(8,128)(2,1)S(1)}, bf16[64,384]{1,0:T(8,128)(2,1)S(1)}, u32[]{:S(2)}, u32[]{:S(2)}) collective-permute-start(bf16[64,384]{1,0:T(8,128)(2,1)S(1)} %pad_maximum_fusion.16), channel_id=1, source_target_pairs={{0,1},{1,0},{2,3},{3,2},{4,5},{5,4},{6,7},{7,6},{8,9},{9,8},{10,11... | collective-permute-start | bytes 147464 | tf_op jit(solution)/shard_map/ppermute | solution.py:1229
  489.1 9.8 %collective-permute-start.31 = (bf16[64,1152]{1,0:T(8,128)(2,1)S(1)}, bf16[64,1152]{1,0:T(8,128)(2,1)S(1)}, u32[]{:S(2)}, u32[]{:S(2)}) collective-permute-start(bf16[64,1152]{1,0:T(8,128)(2,1)S(1)} %pad_maximum_fusion.14), channel_id=1, source_target_pairs={{0,16},{2,18},{4,20},{6,22},{8,24},{10,26},{12,28},{14,30},{16,0},... | collective-permute-start | bytes 442376 | tf_op jit(solution)/shard_map/ppermute | solution.py:108
  489.9 19.3 %copy-start.13 = (bf16[1024,1792]{1,0:T(8,128)(2,1)S(1)}, bf16[1024,1792]{1,0:T(8,128)(2,1)}, u32[]{:S(2)}) copy-start(bf16[1024,1792]{1,0:T(8,128)(2,1)} %pad_maximum_fusion.1) | copy-start | bytes 11010052
  489.9 9.7 %collective-permute-start.27 = (bf16[64,512]{1,0:T(8,128)(2,1)S(1)}, bf16[64,512]{1,0:T(8,128)(2,1)S(1)}, u32[]{:S(2)}, u32[]{:S(2)}) collective-permute-start(bf16[64,512]{1,0:T(8,128)(2,1)S(1)} %concatenate.97), channel_id=1, source_target_pairs={{0,16},{2,18},{4,20},{6,22},{8,24},{10,26},{12,28},{14,30},{16,0},... | collective-permute-start | bytes 196616 | tf_op jit(solution)/shard_map/ppermute | solution.py:108
  499.0 8.5 %collective-permute-start.32 = (bf16[128,1152]{1,0:T(8,128)(2,1)S(1)}, bf16[128,1152]{1,0:T(8,128)(2,1)S(1)}, u32[]{:S(2)}, u32[]{:S(2)}) collective-permute-start(bf16[128,1152]{1,0:T(8,128)(2,1)S(1)} %pad_maximum_fusion.11), channel_id=1, source_target_pairs={{0,8},{2,10},{4,12},{6,14},{8,0},{10,2},{12,4},{14,6},{16,24},{18,... | collective-permute-start | bytes 884744 | tf_op jit(solution)/shard_map/ppermute | solution.py:108
  499.7 11.5 %collective-permute-start.28 = (bf16[128,512]{1,0:T(8,128)(2,1)S(1)}, bf16[128,512]{1,0:T(8,128)(2,1)S(1)}, u32[]{:S(2)}, u32[]{:S(2)}) collective-permute-start(bf16[128,512]{1,0:T(8,128)(2,1)S(1)} %pad_maximum_fusion.15), channel_id=1, source_target_pairs={{0,8},{2,10},{4,12},{6,14},{8,0},{10,2},{12,4},{14,6},{16,24},{18,... | collective-permute-start | bytes 393224 | tf_op jit(solution)/shard_map/ppermute | solution.py:108
  507.7 13.9 %collective-permute-start.33 = (bf16[256,1152]{1,0:T(8,128)(2,1)S(1)}, bf16[256,1152]{1,0:T(8,128)(2,1)S(1)}, u32[]{:S(2)}, u32[]{:S(2)}) collective-permute-start(bf16[256,1152]{1,0:T(8,128)(2,1)S(1)} %pad_maximum_fusion.5), channel_id=1, source_target_pairs={{0,4},{2,6},{4,0},{6,2},{8,12},{10,14},{12,8},{14,10},{16,20},{18,... | collective-permute-start | bytes 1769480 | tf_op jit(solution)/shard_map/ppermute | solution.py:108
  511.2 13.2 %collective-permute-start.29 = (bf16[256,512]{1,0:T(8,128)(2,1)S(1)}, bf16[256,512]{1,0:T(8,128)(2,1)S(1)}, u32[]{:S(2)}, u32[]{:S(2)}) collective-permute-start(bf16[256,512]{1,0:T(8,128)(2,1)S(1)} %pad_maximum_fusion.13), channel_id=1, source_target_pairs={{0,4},{2,6},{4,0},{6,2},{8,12},{10,14},{12,8},{14,10},{16,20},{18,... | collective-permute-start | bytes 786440 | tf_op jit(solution)/shard_map/ppermute | solution.py:108
  522.0 7.6 %collective-permute-start.34 = (bf16[512,1152]{1,0:T(8,128)(2,1)S(1)}, bf16[512,1152]{1,0:T(8,128)(2,1)S(1)}, u32[]{:S(2)}, u32[]{:S(2)}) collective-permute-start(bf16[512,1152]{1,0:T(8,128)(2,1)S(1)} %pad_maximum_fusion.3), channel_id=1, source_target_pairs={{0,2},{2,0},{4,6},{6,4},{8,10},{10,8},{12,14},{14,12},{16,18},{18,... | collective-permute-start | bytes 3538952 | tf_op jit(solution)/shard_map/ppermute | solution.py:108
  524.6 3.3 collective-permute-start.30
  (66 other events, 343.4 us)
Sparse Core Ops, SparseCore 0:
  230.3 148.7 all-reduce.35

commit v3 on v2

--- a/solution.py
+++ b/solution.py
@@ -1,6 +1,7 @@
 import jax
 import jax.numpy as jnp
 from jax import lax
+from jax.experimental.layout import Layout, with_layout_constraint
 from jax.experimental import pallas as pl
 from jax.experimental.pallas import tpu as pltpu
 from jax.sharding import PartitionSpec as P
@@ -1004,16 +1005,22 @@
     return [1 << i for i in range(size.bit_length() - 1)]
 
 
-def scatter_sum(value):
-    for bit in dp_bits():
-        value = halve(value, bit)
-    return value
-
-
-def gather_rows(value):
-    for bit in reversed(dp_bits()):
-        value = double(value, bit)
-    return value
+def halve_parts(values, bit):
+    half = values[0].shape[0] // 2
+    upper = (lax.axis_index("dp") & bit) != 0
+    got = swap_bit(
+        jnp.concatenate([jnp.where(upper, v[:half], v[half:]) for v in values], 1), bit
+    )
+    kept = jnp.concatenate([jnp.where(upper, v[half:], v[:half]) for v in values], 1)
+    return (kept.astype(jnp.float32) + got.astype(jnp.float32)).astype(got.dtype)
+
+
+def by_rows(value):
+    return with_layout_constraint(value, Layout(major_to_minor=(0, 1)))
+
+
+def tie(*values):
+    return lax.optimization_barrier(values)
 
 
 def conv_rows(value, kernel, bias, keeps):
@@ -1099,11 +1106,11 @@
     aux = jnp.pad(aux, ((0, 0), (0, LANES - 3)))
     keeps = [seg_keep(segments, offset)[0] for offset in range(conv_inner.shape[0])]
 
-    inputs = tokens.astype(wide)
+    inputs = by_rows(tokens.astype(wide))
     inv_first = lax.rsqrt(jnp.mean(inputs * inputs, -1, keepdims=True) + EPS)
     unit_first = inputs * inv_first
     in_gain = input_gain.astype(wide)
-    normed = (unit_first * in_gain).astype(low)
+    normed = by_rows((unit_first * in_gain).astype(low))
     inner = matmul(normed, inner_weight)
     state_in = matmul(normed, state_weight)
     step_arg = matmul(normed, step_weight_wide) + step_bias_wide
@@ -1128,11 +1135,11 @@
     mixed = (gated * inv_gate * mixer_scale).astype(low)
     branch_part = attn_part + matmul(mixed, mixer_out)
     out_gain = post_gain.astype(wide)
-    branch = pair_sum(branch_part.astype(low))
+    branch = by_rows(pair_sum(by_rows(branch_part.astype(low))))
     middle = inputs + branch
     inv_second = lax.rsqrt(jnp.mean(middle * middle, -1, keepdims=True) + EPS)
     unit_second = middle * inv_second
-    post = (unit_second * out_gain).astype(low)
+    post = by_rows((unit_second * out_gain).astype(low))
     gate = matmul(post, gate_weight)
     upward = matmul(post, up_weight)
     sigma = jax.nn.sigmoid(gate)
@@ -1142,39 +1149,45 @@
     gate_act_grad = (hidden_grad * upward * sigma * (1.0 + gate * (1.0 - sigma))).astype(low)
     post_part = dot_nt(gate_act_grad, gate_weight) + dot_nt(up_act_grad, up_weight)
     post_gain_part = jnp.sum(post_part * unit_second, 0, keepdims=True)
-    post_full = pair_sum(post_part.astype(low))
+    post_full = by_rows(pair_sum(by_rows(post_part.astype(low))))
     down_wgrad = dot_tn(hidden, cotangent).astype(low)
     gate_wgrad = dot_tn(post, gate_act_grad).astype(low)
     up_wgrad = dot_tn(post, up_act_grad).astype(low)
-    down_wgrad, gate_wgrad, up_wgrad, post_full = lax.optimization_barrier(
-        (down_wgrad, gate_wgrad, up_wgrad, post_full)
-    )
-    down_wgrad, gate_wgrad, up_wgrad = lax.psum((down_wgrad, gate_wgrad, up_wgrad), "dp")
+    post_full, _, _, _ = tie(post_full, down_wgrad, gate_wgrad, up_wgrad)
+    forward_piece = lax.psum_scatter(
+        jnp.concatenate([down_wgrad, gate_wgrad, up_wgrad], 0),
+        "dp",
+        scatter_dimension=0,
+        tiled=True,
+    )
     scaled_post = post_full * out_gain
     middle_grad = cotangent.astype(wide) + inv_second * (
         scaled_post - unit_second * jnp.mean(scaled_post * unit_second, -1, keepdims=True)
     )
-    branch_grad = middle_grad.astype(low)
+    branch_grad = by_rows(middle_grad.astype(low))
     mixed_grad = dot_nt(branch_grad, mixer_out)
     mixer_gain_part = jnp.sum(mixed_grad * gated * inv_gate, 0, keepdims=True)
     weighted = mixed_grad * mixer_scale
     cross = pair_sum(jnp.sum(weighted * gated, -1))[:, None]
-    attnout_part = dot_tn(attended, branch_grad).astype(low)
-    mixout_part = dot_tn(mixed, branch_grad).astype(low)
+    out_part = dot_tn(jnp.concatenate([attended, mixed], 1), branch_grad).astype(low)
+    out_part = by_rows(out_part)
     attended_grad = dot_nt(branch_grad, attnout_weight).astype(low)
     gated_grad = inv_gate * weighted - gated * (inv_gate * inv_gate * inv_gate) * cross / DSSM
     ssm_grad = gated_grad * gate_act
     gating_grad = (
         gated_grad * ssm_out * sigma_gate * (1.0 + gating * (1.0 - sigma_gate))
     ).astype(low)
-    gating_part = dot_tn(normed, gating_grad).astype(low)
-    early = jnp.concatenate(
-        [jnp.concatenate([attnout_part, mixout_part], 0), gating_part], 1
-    )
-    early, ssm_grad = lax.optimization_barrier((early, ssm_grad))
+    gating_part = by_rows(dot_tn(normed, gating_grad).astype(low))
+    bits = dp_bits()
+    early = halve_parts([out_part, gating_part], bits[0])
+    early, ssm_grad, forward_piece = tie(early, ssm_grad, forward_piece)
+    forward_total = lax.all_gather(forward_piece, "dp", axis=0, tiled=True)
+    early = halve(early, bits[1])
     act_grad, step_grad, coef_grad, rate_sum, skip_sum = scan_back_call(
         step, coef, inner_act, aux, seg_row, rate_wide, skip_row, ssm_grad, kept
     )
+    early, act_grad, step_grad, coef_grad = tie(early, act_grad, step_grad, coef_grad)
+    early = halve(early, bits[2])
     step_total = step_grad * jax.nn.sigmoid(step_arg)
     inner_pre_grad = act_grad * silu_slope(inner_pre)
     inner_grad, conv_inner_sums = conv_rows_back(inner_pre_grad, inner, conv_inner, keeps)
@@ -1184,20 +1197,27 @@
         [inner_grad.astype(low), step_total.astype(low), state_grad.astype(low)], 1
     )
     scan_part = dot_tn(normed, scan_cat).astype(low)
-    early_total = gather_rows(scatter_sum(early))
-    scan_part, attended_grad = lax.optimization_barrier((scan_part, attended_grad))
+    early, scan_part, attended_grad = tie(early, scan_part, attended_grad)
+    early = halve(early, bits[3])
+    scan_part = halve(scan_part, bits[0])
     query_grad, keyval_grad = attend_back_call(
         queries, both, seg_row, aux, cosine, sine, logs, attended, attended_grad
     )
     attend_cat = jnp.concatenate([query_grad, keyval_grad], 1)
     attend_part = dot_tn(normed, attend_cat).astype(low)
+    early, scan_part, attend_part, attend_cat = tie(early, scan_part, attend_part, attend_cat)
+    early = double(early, bits[3])
+    scan_part = halve(scan_part, bits[1])
+    attend_part = halve(attend_part, bits[0])
     weight_cat = jnp.concatenate(
         [gating_weight, inner_weight, step_weight_wide, state_weight, query_weight, keyval_weight], 1
     )
     normed_part = dot_nt(jnp.concatenate([gating_grad, scan_cat, attend_cat], 1), weight_cat)
     input_gain_part = jnp.sum(normed_part * unit_first, 0, keepdims=True)
-    normed_full = pair_sum(normed_part.astype(low))
-
+    early, scan_part, attend_part, normed_part, input_gain_part = tie(
+        early, scan_part, attend_part, normed_part, input_gain_part
+    )
+    normed_full = by_rows(pair_sum(by_rows(normed_part.astype(low))))
     own_rows = [
         *conv_inner_sums,
         jnp.sum(inner_pre_grad, 0, keepdims=True),
@@ -1218,12 +1238,26 @@
     small_other = lax.ppermute(small, "tensor", [(0, 1), (1, 0)])
     is_shared = lax.broadcasted_iota(jnp.int32, small.shape, 0) >= len(own_rows)
     small = small + jnp.where(is_shared, small_other, 0.0)
-    for bit in dp_bits():
-        small = small + swap_bit(small, bit)
-
-    scan_piece = scatter_sum(scan_part)
-    scan_piece, early_total = lax.optimization_barrier((scan_piece, early_total))
-    attend_piece = scatter_sum(attend_part)
+    early = double(early, bits[2])
+    scan_part = halve(scan_part, bits[2])
+    attend_part = halve(attend_part, bits[1])
+    early, scan_part, attend_part, small, forward_total = tie(
+        early, scan_part, attend_part, small, forward_total
+    )
+    hidden_units = down_weight.shape[0]
+    down_wgrad = forward_total[:hidden_units].astype(wide)
+    gate_wgrad = forward_total[hidden_units : hidden_units + model].astype(wide)
+    up_wgrad = forward_total[hidden_units + model :].astype(wide)
+    early = double(early, bits[1])
+    scan_part = halve(scan_part, bits[3])
+    attend_part = halve(attend_part, bits[2])
+    small = small + swap_bit(small, bits[0])
+    scan_part, attend_part, small = tie(scan_part, attend_part, small)
+    attend_part = halve(attend_part, bits[3])
+    small = small + swap_bit(small, bits[1])
+    attend_part, small, early = tie(attend_part, small, early)
+    small = small + swap_bit(small, bits[2])
+    scan_piece, attend_piece = scan_part, attend_part
     state_at = ssm_width + LANES
     trade = jnp.concatenate([scan_piece[:, state_at:], attend_piece[:, query_width:]], 1)
     other = lax.ppermute(trade, "tensor", [(0, 1), (1, 0)])
@@ -1234,24 +1268,43 @@
     mine, theirs = trade[:, state_cols:], other[:, state_cols:]
     head_0 = jnp.where(first_device, mine, theirs)
     head_1 = jnp.where(first_device, theirs, mine)
-    scan_total = gather_rows(jnp.concatenate([scan_piece[:, :state_at], state_piece], 1))
-    attend_total = gather_rows(
-        jnp.concatenate(
-            [
-                attend_piece[:, :query_width],
-                head_0[:, :HEAD_SIZE],
-                head_1[:, :HEAD_SIZE],
-                head_0[:, HEAD_SIZE:],
-                head_1[:, HEAD_SIZE:],
-            ],
-            1,
-        )
-    )
-
+    late = jnp.concatenate(
+        [
+            scan_piece[:, :state_at],
+            state_piece,
+            attend_piece[:, :query_width],
+            head_0[:, :HEAD_SIZE],
+            head_1[:, :HEAD_SIZE],
+            head_0[:, HEAD_SIZE:],
+            head_1[:, HEAD_SIZE:],
+        ],
+        1,
+    )
+    late, small = tie(late, small)
+    late = double(late, bits[3])
+    small = small + swap_bit(small, bits[3])
+    late, early, small = tie(late, early, small)
+    late = double(late, bits[2])
+    early = double(early, bits[0])
+    late, early = tie(late, early)
+    late = double(late, bits[1])
+    early_grads = (
+        gate_wgrad,
+        up_wgrad,
+        down_wgrad,
+        early[:query_width, :model].astype(wide),
+        early[:, model:].astype(wide),
+        early[query_width:, :model].astype(wide),
+    )
     scaled_in = normed_full * in_gain
     tokens_grad = middle_grad + inv_first * (
         scaled_in - unit_first * jnp.mean(scaled_in * unit_first, -1, keepdims=True)
     )
+    late, tokens_grad, *early_grads = tie(late, tokens_grad, *early_grads)
+    late = double(late, bits[0])
+    scan_total = late[:, : state_at + state_cols]
+    attend_total = late[:, state_at + state_cols :]
+    gate_wgrad, up_wgrad, down_wgrad, attnout_grad, gating_wgrad, mixout_grad = early_grads
     count = len(own_rows)
     taps = conv_inner.shape[0]
     return (
@@ -1259,8 +1312,8 @@
         small[count],
         attend_total[:, :query_width].astype(wide),
         attend_total[:, query_width:].astype(wide),
-        early_total[:query_width, :model].astype(wide),
-        early_total[:, model:].astype(wide),
+        attnout_grad,
+        gating_wgrad,
         scan_total[:, :ssm_width].astype(wide),
         scan_total[:, state_at:].astype(wide),
         scan_total[:, ssm_width : ssm_width + ssm_heads].astype(wide),
@@ -1272,11 +1325,11 @@
         small[taps + 4, :ssm_heads],
         jnp.sum(small[taps + 2, :ssm_width].reshape(ssm_heads, P_SIZE), 1),
         small[taps + 1, :ssm_width],
-        early_total[query_width:, :model].astype(wide),
+        mixout_grad,
         small[count + 1],
-        gate_wgrad.astype(wide),
-        up_wgrad.astype(wide),
-        down_wgrad.astype(wide),
+        gate_wgrad,
+        up_wgrad,
+        down_wgrad,
     )
 
 
@@ -1285,12 +1338,13 @@
     size = lax.axis_size("dp")
     fits = (
         lax.axis_size("tensor") == 2
-        and size & (size - 1) == 0
+        and size == 16
         and segments.shape[0] == 1
         and tokens.shape[0] % CHUNK == 0
         and tokens.shape[1] % (16 * size) == 0
         and query_weight.shape[1] == QUERY_HEADS // KEYVALUE_HEADS * HEAD_SIZE
         and KEYVALUE_HEADS == 2
+        and arrays[23].shape[0] == tokens.shape[1]
         and step_weight.shape[1] % 2 == 0
         and query_weight.shape[1] + step_weight.shape[1] * P_SIZE == tokens.shape[1]
     )

time: 551 us -> 548 us (level)
  waiting for transfers between devices: 188 us -> 220 us
  local copies, waits for them, and re-layouts: 47.3 us -> 24.3 us
  matrix products: 79.1 us -> 69.2 us
  starting transfers between devices: 36.4 us -> 28.4 us
  other arithmetic: 113 us -> 119 us
    ppermute x1, waiting for transfers between devices: 0.01 us -> 43 us  [local_fast(): small_other = lax.ppermute(small, 'tensor', [(0, 1), (1, 0)])]
    ppermute x28 -> x24, waiting for transfers between devices: 120 us -> 77.6 us  [swap_bit(): return lax.ppermute(value, 'dp', [(i, i ^ bit) for i in range(size)])]
    reduce_scatter x0 -> x1, waiting for transfers between devices: none -> 23.9 us  [local_fast(): lax.psum_scatter(jnp.concatenate([down_wgrad, gate_wgrad, up_wgrad], 0),...]
    unnamed x164 -> x143, local copies, waits for them, and re-layouts: 22.6 us -> 7.99 us
    concatenate x2, other arithmetic: 3.86 us -> 14.6 us  [the longest x1 13.2 us: local_fast(): jnp.concatenate([down_wgrad, gate_wgrad, up_wgrad], 0)]
    convert_element_type x10 -> x8, other arithmetic: 24.3 us -> 15.2 us  [the longest x1 5.12 us: local_fast(): down_wgrad = forward_total[:hidden_units].astype(wide)]
    dot_general x8 -> x7, matrix products: 24.6 us -> 16.5 us  [dot_tn(): lax.dot_general(left, right, (((0,), (0,)), ((), ())), preferred_element_...]
    ppermute x28 -> x24, starting transfers between devices: 28.8 us -> 21 us  [swap_bit(): return lax.ppermute(value, 'dp', [(i, i ^ bit) for i in range(size)])]
  transfers between devices with their start and end apart: 36 -> 33, of which waited for: 19 -> 17; matrix products, arithmetic and copies ran while one was open for 27% -> 26% of each run, Pallas kernels for 9% -> 9%
where the time goes in v3:
time: 548 us; the launch traced here: 539 us
  waiting for transfers between devices  220 us (40%)
  other arithmetic  119 us (22%)
  matrix products  69.2 us (13%)
  Pallas kernels  61.8 us (11%)
  starting transfers between devices  28.4 us (5%)
  local copies, waits for them, and re-layouts  24.3 us (4%)
  between operations  16.2 us (3%)
    ppermute x24, waiting for transfers between devices, swap_bit(): return lax.ppermute(value, 'dp', [(i, i ^ bit) for i in range(size)])  77.6 us
    ppermute x5, waiting for transfers between devices, pair_sum(): other = lax.ppermute(value, 'tensor', [(0, 1), (1, 0)])  75.7 us
    ppermute x1, waiting for transfers between devices, local_fast(): small_other = lax.ppermute(small, 'tensor', [(0, 1), (1, 0)])  43 us
    dot_general x10, matrix products, matmul(): return jnp.dot(left, right, preferred_element_type=jnp.float32)  28.9 us
    pallas_call x1, Pallas kernels, scan_back_call(): pl.pallas_call(scan_back_kernel, grid=(chunks,), in_specs=[by_chunk(LANES...  25 us
    reduce_scatter x1, waiting for transfers between devices, local_fast(): lax.psum_scatter(jnp.concatenate([down_wgrad, gate_wgrad, up_wgrad], 0),...  23.9 us
    dot_general x6, matrix products, dot_nt(): lax.dot_general(left, right, (((1,), (1,)), ((), ())), preferred_element_...  23.9 us
    ppermute x24, starting transfers between devices, swap_bit(): return lax.ppermute(value, 'dp', [(i, i ^ bit) for i in range(size)])  21 us
  transfers between devices with their start and end apart: 33, of which 17 were waited for; matrix products, arithmetic and copies ran while one was open for 26% of the time, Pallas kernels for 9%

profile of v3, /device:TPU:0, one launch (start us, length us, event | category | flops | bytes accessed | tf_op | source)
XLA Modules:
  0.0 538.7 jit_solution(9497593852544954077)
XLA Ops:
  15.6 3.5 fusion.80
  23.1 3.5 compare_select_fusion
  26.6 3.8 fusion.19
  32.4 12.1 %scan_forward.1 = (f32[1024,768]{1,0:T(8,128)}, bf16[4,128,768]{2,1,0:T(8,128)(2,1)}) custom-call(f32[1024,128]{1,0:T(8,128)} %get-tuple-element.305.step_ref, bf16[1024,256]{1,0:T(8,128)(2,1)} %get-tuple-element.249.coef_ref, f32[1024,768]{1,0:T(8,128)} %get-tuple-element.247.act_ref, f32[1024,128]{1,0:T(8,128)} %pad.127.seg_col_ref.aux_ref, ...), custom_call_target="tpu_custom_call" | custom-call | tf_op jit(solution)/shard_map/scan_forward/pallas_call | solution.py:673
  44.5 6.5 %multiply_reduce_fusion.9 = (f32[1024]{0:T(1024)S(1)}, f32[1024,768]{1,0:T(8,128)}, f32[1024,768]{1,0:T(8,128)}) fusion(f32[1024,768]{1,0:T(8,128)} %get-tuple-element.82, f32[1024,768]{1,0:T(8,128)S(1)} %get-tuple-element.248, f32[768]{0:T(1024)S(1)} %mul.685, bf16[1024,1024]{1,0:T(8,128)(2,1)S(1)} %copy-done.19, bf16[1024,768]{1,0:T(8,128)(2,1)} %param.31), kind=kOutput, calls=%fused_computation.57 | convolution fusion | flops 1620835328 | bytes 16260096 | tf_op jit(solution)/shard_map/dot_general | solution.py:23
  51.0 2.9 collective-permute-start
  54.0 3.3 fusion.78.query_ref
  57.2 2.9 fusion.54
  62.3 3.2 fusion.50.keyval_ref
  67.4 10.9 %attend_forward.1 = (bf16[1024,256]{1,0:T(8,128)(2,1)}, bf16[1024,256]{1,0:T(8,128)(2,1)}, bf16[1024,256]{1,0:T(8,128)(2,1)}, f32[1024,128]{1,0:T(8,128)}) custom-call(f32[1024,256]{1,0:T(8,128)} %fusion.78.query_ref, f32[1024,128]{1,0:T(8,128)} %fusion.50.keyval_ref, f32[1,1024]{1,0:T(1,128)} %get-tuple-element.291.seg_ref, ...), custom_call_target="tpu_custom_call" | custom-call | tf_op jit(solution)/shard_map/attend_forward/pallas_call | solution.py:910
  82.4 47.0 %collective-permute-done.1 = bf16[1024,1024]{1,0:T(8,128)(2,1)S(1)} collective-permute-done((bf16[1024,1024]{1,0:T(8,128)(2,1)S(1)}, bf16[1024,1024]{1,0:T(8,128)(2,1)S(1)}, u32[]{:S(2)}, u32[]{:S(2)}) %collective-permute-start.1) | collective-permute-done | bytes 2097184 | tf_op jit(solution)/shard_map/ppermute | solution.py:102
  136.7 2.6 fusion.30
  139.3 4.1 multiply_convert_fusion.1
  145.8 5.2 fusion.77
  153.7 2.4 convolution_convert_fusion.2
  156.1 13.2 %pad_maximum_fusion = bf16[3072,1024]{1,0:T(8,128)(2,1)} fusion(bf16[1024,1024]{1,0:T(8,128)(2,1)S(1)} %convolution_convert_fusion.1, bf16[1024,1024]{1,0:T(8,128)(2,1)S(1)} %convolution_convert_fusion.2, bf16[1024,1024]{1,0:T(8,128)(2,1)S(1)} %fusion.30), kind=kLoop, calls=%fused_computation | loop fusion | flops 18874368 | bytes 12582912 | tf_op jit(solution)/shard_map/concatenate | solution.py:1158
  169.5 28.0 %collective-permute-done.2 = bf16[1024,1024]{1,0:T(8,128)(2,1)} collective-permute-done((bf16[1024,1024]{1,0:T(8,128)(2,1)}, bf16[1024,1024]{1,0:T(8,128)(2,1)}, u32[]{:S(2)}, u32[]{:S(2)}) %collective-permute-start.2) | collective-permute-done | bytes 2097184 | tf_op jit(solution)/shard_map/ppermute | solution.py:102
  197.4 3.1 convert_add_fusion.1
  200.6 5.2 multiply_reduce_fusion
  215.5 3.7 constant_dynamic-update-slice_fusion.6
  223.4 5.7 %fusion.36.grad_ref = f32[1024,768]{1,0:T(8,128)} fusion(f32[1024]{0:T(1024)S(1)} %add.306, f32[1024,768]{1,0:T(8,128)} %get-tuple-element.246, f32[1024,768]{1,0:T(8,128)} %copy-done.12, f32[1024]{0:T(1024)S(1)} %get-tuple-element.243, f32[768]{0:T(1024)S(1)} %convert_element_type.387, f32[1024]{0:T(1024)S(1)} %get-tuple-element.244, ...), kind=kLoop, calls=%fused_computation.96 | loop fusion | flops 8650752 | bytes 12598272 | tf_op jit(solution)/shard_map/mul | solution.py:1176
  229.2 3.2 add_convert_fusion.1
  232.3 23.9 %reduce-scatter.2.cloned.1.call-done = bf16[192,1024]{1,0:T(8,128)(2,1)} async-done(((bf16[3072,1024]{1,0:T(8,128)(2,1)}), bf16[192,1024]{1,0:T(8,128)(2,1)}) %reduce-scatter.2.cloned.1.call-update) | async-done | bytes 393232 | tf_op jit(solution)/shard_map/reduce_scatter | solution.py:1157
  256.2 2.5 broadcast_select_fusion.9
  261.0 7.8 %concatenate.84 = bf16[1024,2304]{1,0:T(8,128)(2,1)} concatenate(bf16[1024,768]{1,0:T(8,128)(2,1)} %param.31, bf16[1024,768]{1,0:T(8,128)(2,1)} %param.32, bf16[1024,128]{1,0:T(8,128)(2,1)S(1)} %pad.128.clone, bf16[1024,256]{1,0:T(8,128)(2,1)} %param.33, bf16[1024,256]{1,0:T(8,128)(2,1)} %param.28, bf16[1024,64]{1,0:T(8,128)(2,1)S(1)} %get-tuple-element.275, ...), dimensions={1} | concatenate | bytes 9437184 | tf_op jit(solution)/shard_map/concatenate | solution.py:1212
  268.9 3.8 convolution_convert_fusion.5.grad_ref
  272.6 25.0 %scan_backward.1 = (f32[1024,768]{1,0:T(8,128)}, f32[1024,128]{1,0:T(8,128)}, f32[1024,256]{1,0:T(8,128)}, f32[1,128]{1,0:T(1,128)}, f32[1,768]{1,0:T(1,128)}) custom-call(f32[1024,128]{1,0:T(8,128)} %get-tuple-element.305.step_ref, bf16[1024,256]{1,0:T(8,128)(2,1)} %get-tuple-element.249.coef_ref, f32[1024,768]{1,0:T(8,128)} %get-tuple-element.247.act_ref, ...), custom_call_target="tpu_custom_call" | custom-call | tf_op jit(solution)/shard_map/scan_backward/pallas_call | solution.py:815
  301.8 9.1 %fusion.67 = (f32[768]{0:T(1024)S(1)}, f32[768]{0:T(1024)S(1)}, f32[768]{0:T(1024)S(1)}, f32[768]{0:T(1024)S(1)}, f32[768]{0:T(1024)S(1)}, /*index=5*/f32[1024,7...) fusion(f32[1024,768]{1,0:T(8,128)} %fusion.80, f32[1024]{0:T(1024)S(1)} %bitcast.99, ...), kind=kLoop, calls=%fused_computation.251 | loop fusion | flops 15724800 | bytes 22047744 | tf_op jit(solution)/shard_map/reduce_sum | solution.py:1223
  318.5 3.4 convolution_convert_fusion
  321.9 9.3 %collective-permute-done.6 = bf16[128,1792]{1,0:T(8,128)(2,1)S(1)} collective-permute-done((bf16[128,1792]{1,0:T(8,128)(2,1)S(1)}, bf16[128,1792]{1,0:T(8,128)(2,1)S(1)}, u32[]{:S(2)}, u32[]{:S(2)}) %collective-permute-start.6) | collective-permute-done | bytes 458784 | tf_op jit(solution)/shard_map/ppermute | solution.py:109
  335.6 13.8 %attend_backward.1 = (bf16[1024,256]{1,0:T(8,128)(2,1)}, bf16[1024,128]{1,0:T(8,128)(2,1)}) custom-call(bf16[1024,256]{1,0:T(8,128)(2,1)} %get-tuple-element.96.query_ref, bf16[1024,256]{1,0:T(8,128)(2,1)} %get-tuple-element.97.both_ref, f32[1,1024]{1,0:T(1,128)} %get-tuple-element.291.seg_ref, f32[1024,128]{1,0:T(8,128)} %pad.127.seg_col_ref.aux_ref, ...), custom_call_target="tpu_custom_call" | custom-call | tf_op jit(solution)/shard_map/attend_backward/pallas_call | solution.py:974
  352.8 6.5 %collective-permute-done.7 = bf16[64,1792]{1,0:T(8,128)(2,1)S(1)} collective-permute-done((bf16[64,1792]{1,0:T(8,128)(2,1)}, bf16[64,1792]{1,0:T(8,128)(2,1)S(1)}, u32[]{:S(2)}, u32[]{:S(2)}) %collective-permute-start.7) | collective-permute-done | bytes 229408 | tf_op jit(solution)/shard_map/ppermute | solution.py:109
  363.8 6.3 %fusion.5 = (f32[1024]{0:T(1024)S(1)}, bf16[1024,1024]{1,0:T(8,128)(2,1)}) fusion(bf16[1024,1024]{1,0:T(8,128)(2,1)S(1)} %copy-done.4, f32[1024]{0:T(1024)S(1)} %copy-done.48, bf16[1024,2304]{1,0:T(8,128)(2,1)S(1)} %constant_dynamic-update-slice_fusion.2, bf16[1024,2304]{1,0:T(8,128)(2,1)S(1)} %bitcast.86), kind=kOutput, calls=%fused_computation.9 | convolution fusion | flops 4837080064 | bytes 13639680 | tf_op jit(solution)/shard_map/dot_general | solution.py:594
  370.1 12.1 %collective-permute-done.9 = bf16[64,1792]{1,0:T(8,128)(2,1)S(1)} collective-permute-done((bf16[64,1792]{1,0:T(8,128)(2,1)S(1)}, bf16[64,1792]{1,0:T(8,128)(2,1)S(1)}, u32[]{:S(2)}, u32[]{:S(2)}) %collective-permute-start.9) | collective-permute-done | bytes 229408 | tf_op jit(solution)/shard_map/ppermute | solution.py:109
  389.7 43.0 %collective-permute-done.15 = f32[16,1024]{1,0:T(8,128)S(1)} collective-permute-done((f32[16,1024]{1,0:T(8,128)S(1)}, f32[16,1024]{1,0:T(8,128)S(1)}, u32[]{:S(2)}, u32[]{:S(2)}) %collective-permute-start.15) | collective-permute-done | bytes 65568 | tf_op jit(solution)/shard_map/ppermute | solution.py:1238
  436.8 2.9 collective-permute-start.16
  440.5 3.1 collective-permute-done.17
  443.7 3.5 collective-permute-done.16
  448.0 4.4 collective-permute-done.19
  452.4 5.5 %collective-permute-done.20 = f32[16,1024]{1,0:T(8,128)S(1)} collective-permute-done((f32[16,1024]{1,0:T(8,128)S(1)}, f32[16,1024]{1,0:T(8,128)S(1)}, u32[]{:S(2)}, u32[]{:S(2)}) %collective-permute-start.20) | collective-permute-done | bytes 65568 | tf_op jit(solution)/shard_map/ppermute | solution.py:109
  461.3 3.4 fusion.6
  465.1 4.0 collective-permute-done.23
  472.1 6.6 %collective-permute-done.25 = f32[16,1024]{1,0:T(8,128)S(1)} collective-permute-done((f32[16,1024]{1,0:T(8,128)S(1)}, f32[16,1024]{1,0:T(8,128)S(1)}, u32[]{:S(2)}, u32[]{:S(2)}) %collective-permute-start.25) | collective-permute-done | bytes 65568 | tf_op jit(solution)/shard_map/ppermute | solution.py:109
  478.7 2.8 collective-permute-done.24
  481.6 5.7 %fusion.9 = f32[1024,1024]{1,0:T(8,128)} fusion(f32[1024,1024]{1,0:T(8,128)} %copy-done.5, bf16[1024,1024]{1,0:T(8,128)(2,1)S(1)} %copy-done.4, bf16[1024,1024]{1,0:T(8,128)(2,1)} %collective-permute-done.29, bf16[1024,1024]{1,0:T(8,128)(2,1)} %get-tuple-element.128, f32[1024]{0:T(1024)S(1)} %broadcast_multiply_fusion.6, f32[1024]{0:T(1024)S(1)} %copy-done.50, ...), kind=kLoop, calls=%fused_computation.13 | loop fusion | flops 10485760 | bytes 14692352 | tf_op jit(solution)/shard_map/add | solution.py:1300
  488.4 5.1 slice_convert_fusion
  493.5 6.0 %collective-permute-done.26 = bf16[128,1664]{1,0:T(8,128)(2,1)S(1)} collective-permute-done((bf16[128,1664]{1,0:T(8,128)(2,1)S(1)}, bf16[128,1664]{1,0:T(8,128)(2,1)S(1)}, u32[]{:S(2)}, u32[]{:S(2)}) %collective-permute-start.26) | collective-permute-done | bytes 426016 | tf_op jit(solution)/shard_map/ppermute | solution.py:109
  506.7 13.8 %collective-permute-done.28 = bf16[256,1664]{1,0:T(8,128)(2,1)S(1)} collective-permute-done((bf16[256,1664]{1,0:T(8,128)(2,1)S(1)}, bf16[256,1664]{1,0:T(8,128)(2,1)S(1)}, u32[]{:S(2)}, u32[]{:S(2)}) %collective-permute-start.28) | collective-permute-done | bytes 852000 | tf_op jit(solution)/shard_map/ppermute | solution.py:109
  (346 shorter events, 113.2 us)
Async XLA Ops:
  7.2 124.7 %copy-start = (bf16[1024,1024]{1,0:T(8,128)(2,1)S(1)}, bf16[1024,1024]{1,0:T(8,128)(2,1)}, u32[]{:S(2)}) copy-start(bf16[1024,1024]{1,0:T(8,128)(2,1)} %param.46) | copy-start | bytes 6291460
  7.2 249.0 %reduce-scatter.2.cloned.1.call-start = ((), (), s32[]{:S(2)}) async-start(), calls=%async_computation.1 | async-start | bytes 6684672 | tf_op jit(solution)/shard_map/reduce_scatter | solution.py:1157
  30.4 14.1 %copy-start.13 = (f32[1024,768]{1,0:T(8,128)}, f32[1024,768]{1,0:T(8,128)S(1)}, u32[]{:S(2)}) copy-start(f32[1024,768]{1,0:T(8,128)S(1)} %get-tuple-element.248) | copy-start | bytes 9437188
  30.4 14.1 %copy-start.19 = (bf16[1024,1024]{1,0:T(8,128)(2,1)S(1)}, bf16[1024,1024]{1,0:T(8,128)(2,1)}, u32[]{:S(2)}) copy-start(bf16[1024,1024]{1,0:T(8,128)(2,1)} %copy-done.18) | copy-start | bytes 6291460
  51.0 27.2 %collective-permute-start = (f32[1024]{0:T(1024)S(1)}, f32[1024]{0:T(1024)S(1)}, u32[]{:S(2)}, u32[]{:S(2)}) collective-permute-start(f32[1024]{0:T(1024)S(1)} %get-tuple-element.245), channel_id=1, source_target_pairs={{0,1},{1,0},{2,3},{3,2},{4,5},{5,4},{6,7},{7,6},{8,9},{9,8},{10,11... | collective-permute-start | bytes 12296 | tf_op jit(solution)/shard_map/ppermute | solution.py:102
  65.5 12.8 %copy-start.8 = (f32[1024,768]{1,0:T(8,128)S(1)}, f32[1024,768]{1,0:T(8,128)}, u32[]{:S(2)}) copy-start(f32[1024,768]{1,0:T(8,128)} %get-tuple-element.246) | copy-start | bytes 9437188
  81.5 48.0 %copy-start.3 = (bf16[1024,1024]{1,0:T(8,128)(2,1)S(1)}, bf16[1024,1024]{1,0:T(8,128)(2,1)}, u32[]{:S(2)}) copy-start(bf16[1024,1024]{1,0:T(8,128)(2,1)} %param.24) | copy-start | bytes 6291460
  82.3 48.6 %copy-start.6 = (bf16[1024,1024]{1,0:T(8,128)(2,1)}, bf16[1024,1024]{1,0:T(8,128)(2,1)S(1)}, u32[]{:S(2)}) copy-start(bf16[1024,1024]{1,0:T(8,128)(2,1)S(1)} %add_convert_fusion) | copy-start | bytes 6291460
  82.3 47.1 %collective-permute-start.1 = (bf16[1024,1024]{1,0:T(8,128)(2,1)S(1)}, bf16[1024,1024]{1,0:T(8,128)(2,1)S(1)}, u32[]{:S(2)}, u32[]{:S(2)}) collective-permute-start(bf16[1024,1024]{1,0:T(8,128)(2,1)S(1)} %add_convert_fusion), channel_id=1, source_target_pairs={{0,1},{1,0},{2,3},{3,2},{4,5},{5,4},{6,7},{7,6},{8,9},{9,8},{10,11... | collective-permute-start | bytes 6291464 | tf_op jit(solution)/shard_map/ppermute | solution.py:102
  150.9 46.5 %collective-permute-start.2 = (bf16[1024,1024]{1,0:T(8,128)(2,1)}, bf16[1024,1024]{1,0:T(8,128)(2,1)}, u32[]{:S(2)}, u32[]{:S(2)}) collective-permute-start(bf16[1024,1024]{1,0:T(8,128)(2,1)} %get-tuple-element.308), channel_id=1, source_target_pairs={{0,1},{1,0},{2,3},{3,2},{4,5},{5,4},{6,7},{7,6},{8,9},{9,8},{10,11... | collective-permute-start | bytes 6291464 | tf_op jit(solution)/shard_map/ppermute | solution.py:102
  169.4 265.5 %all-gather.2.cloned.1.call-start = ((), (), s32[]{:S(2)}) async-start(), calls=%async_computation.2 | async-start | bytes 6684672 | tf_op jit(solution)/shard_map/all_gather | solution.py:1184
  169.4 31.2 %copy-start.4 = (bf16[1024,1024]{1,0:T(8,128)(2,1)S(1)}, bf16[1024,1024]{1,0:T(8,128)(2,1)}, u32[]{:S(2)}) copy-start(bf16[1024,1024]{1,0:T(8,128)(2,1)} %param.24) | copy-start | bytes 6291460
  169.4 31.1 %copy-start.7 = (bf16[1024,1024]{1,0:T(8,128)(2,1)S(1)}, bf16[1024,1024]{1,0:T(8,128)(2,1)}, u32[]{:S(2)}) copy-start(bf16[1024,1024]{1,0:T(8,128)(2,1)} %copy-done.6) | copy-start | bytes 6291460
  169.4 31.1 %copy-start.11 = (bf16[1024,1024]{1,0:T(8,128)(2,1)S(1)}, bf16[1024,1024]{1,0:T(8,128)(2,1)}, u32[]{:S(2)}) copy-start(bf16[1024,1024]{1,0:T(8,128)(2,1)} %copy-done.10) | copy-start | bytes 6291460
  210.3 3.7 collective-permute-start.3
  223.4 5.8 %collective-permute-start.4 = (bf16[512,1792]{1,0:T(8,128)(2,1)}, bf16[512,1792]{1,0:T(8,128)(2,1)}, u32[]{:S(2)}, u32[]{:S(2)}) collective-permute-start(bf16[512,1792]{1,0:T(8,128)(2,1)} %pad_maximum_fusion.2), channel_id=1, source_target_pairs={{0,2},{2,0},{4,6},{6,4},{8,10},{10,8},{12,14},{14,12},{16,18},{18,... | collective-permute-start | bytes 5505032 | tf_op jit(solution)/shard_map/ppermute | solution.py:109
  232.3 28.7 %copy-start.29 = (bf16[1024,64]{1,0:T(8,128)(2,1)S(1)}, bf16[1024,64]{1,0:T(8,128)(2,1)}, u32[]{:S(2)}) copy-start(bf16[1024,64]{1,0:T(8,128)(2,1)} %copy-done.28) | copy-start | bytes 393220
  258.7 40.3 %collective-permute-start.5 = (bf16[256,1792]{1,0:T(8,128)(2,1)}, bf16[256,1792]{1,0:T(8,128)(2,1)}, u32[]{:S(2)}, u32[]{:S(2)}) collective-permute-start(bf16[256,1792]{1,0:T(8,128)(2,1)} %broadcast_select_fusion.9), channel_id=1, source_target_pairs={{0,4},{2,6},{4,0},{6,2},{8,12},{10,14},{12,8},{14,10},{16,20},{18,... | collective-permute-start | bytes 2752520 | tf_op jit(solution)/shard_map/ppermute | solution.py:109
  301.7 10.6 %copy-start.25 = (f32[1024,256]{1,0:T(8,128)S(1)}, f32[1024,256]{1,0:T(8,128)}, u32[]{:S(2)}) copy-start(f32[1024,256]{1,0:T(8,128)} %get-tuple-element.250) | copy-start | bytes 3145732
  301.8 10.6 %copy-start.43 = (f32[1024,256]{1,0:T(8,128)S(1)}, f32[1024,256]{1,0:T(8,128)}, u32[]{:S(2)}) copy-start(f32[1024,256]{1,0:T(8,128)} %get-tuple-element.93) | copy-start | bytes 3145732
  311.0 20.2 %collective-permute-start.6 = (bf16[128,1792]{1,0:T(8,128)(2,1)S(1)}, bf16[128,1792]{1,0:T(8,128)(2,1)S(1)}, u32[]{:S(2)}, u32[]{:S(2)}) collective-permute-start(bf16[128,1792]{1,0:T(8,128)(2,1)S(1)} %broadcast_select_fusion.17), channel_id=1, source_target_pairs={{0,8},{2,10},{4,12},{6,14},{8,0},{10,2},{12,4},{14,6},{16,24},{18,... | collective-permute-start | bytes 1376264 | tf_op jit(solution)/shard_map/ppermute | solution.py:109
  332.4 27.0 %collective-permute-start.8 = (bf16[512,1152]{1,0:T(8,128)(2,1)}, bf16[512,1152]{1,0:T(8,128)(2,1)}, u32[]{:S(2)}, u32[]{:S(2)}) collective-permute-start(bf16[512,1152]{1,0:T(8,128)(2,1)} %broadcast_select_fusion.4), channel_id=1, source_target_pairs={{0,2},{2,0},{4,6},{6,4},{8,10},{10,8},{12,14},{14,12},{16,18},{18,... | collective-permute-start | bytes 3538952 | tf_op jit(solution)/shard_map/ppermute | solution.py:109
  333.2 26.2 %collective-permute-start.7 = (bf16[64,1792]{1,0:T(8,128)(2,1)}, bf16[64,1792]{1,0:T(8,128)(2,1)S(1)}, u32[]{:S(2)}, u32[]{:S(2)}) collective-permute-start(bf16[64,1792]{1,0:T(8,128)(2,1)} %broadcast_select_fusion.24), channel_id=1, source_target_pairs={{0,16},{2,18},{4,20},{6,22},{8,24},{10,26},{12,28},{14,30},{16,0},... | collective-permute-start | bytes 688136 | tf_op jit(solution)/shard_map/ppermute | solution.py:109
  351.5 12.1 %slice-start.4 = ((s8[4718592]{0:T(1024)(128)(4,1)}), s8[4194304]{0:T(1024)(128)(4,1)S(1)}, s32[]{:S(2)}) async-start(s8[4718592]{0:T(1024)(128)(4,1)} %bitcast.87), calls=%async_computation.7 | async-start | bytes 8388608
  351.5 12.3 %slice-start.2 = ((s8[4718592]{0:T(1024)(128)(4,1)}), s8[4194304]{0:T(1024)(128)(4,1)S(1)}, s32[]{:S(2)}) async-start(s8[4718592]{0:T(1024)(128)(4,1)} %bitcast.85), calls=%async_computation.5 | async-start | bytes 8388608
  352.8 10.8 %slice-start.5 = ((s8[4718592]{0:T(1024)(128)(4,1)}), s8[524288]{0:T(1024)(128)(4,1)S(1)}, s32[]{:S(2)}) async-start(s8[4718592]{0:T(1024)(128)(4,1)} %bitcast.87), calls=%async_computation.8 | async-start | bytes 1048576
  361.3 21.8 %collective-permute-start.11 = (bf16[512,384]{1,0:T(8,128)(2,1)S(1)}, bf16[512,384]{1,0:T(8,128)(2,1)S(1)}, u32[]{:S(2)}, u32[]{:S(2)}) collective-permute-start(bf16[512,384]{1,0:T(8,128)(2,1)S(1)} %broadcast_select_fusion.20), channel_id=1, source_target_pairs={{0,2},{2,0},{4,6},{6,4},{8,10},{10,8},{12,14},{14,12},{16,18},{18,... | collective-permute-start | bytes 1179656 | tf_op jit(solution)/shard_map/ppermute | solution.py:109
  361.4 21.8 %collective-permute-start.10 = (bf16[256,1152]{1,0:T(8,128)(2,1)S(1)}, bf16[256,1152]{1,0:T(8,128)(2,1)S(1)}, u32[]{:S(2)}, u32[]{:S(2)}) collective-permute-start(bf16[256,1152]{1,0:T(8,128)(2,1)S(1)} %broadcast_select_fusion.14), channel_id=1, source_target_pairs={{0,4},{2,6},{4,0},{6,2},{8,12},{10,14},{12,8},{14,10},{16,20},{18,... | collective-permute-start | bytes 1769480 | tf_op jit(solution)/shard_map/ppermute | solution.py:109
  363.5 18.7 %collective-permute-start.9 = (bf16[64,1792]{1,0:T(8,128)(2,1)S(1)}, bf16[64,1792]{1,0:T(8,128)(2,1)S(1)}, u32[]{:S(2)}, u32[]{:S(2)}) collective-permute-start(bf16[64,1792]{1,0:T(8,128)(2,1)S(1)} %add_convert_fusion.8), channel_id=1, source_target_pairs={{0,16},{2,18},{4,20},{6,22},{8,24},{10,26},{12,28},{14,30},{16,0},... | collective-permute-start | bytes 688136 | tf_op jit(solution)/shard_map/ppermute | solution.py:109
  383.5 77.8 %collective-permute-start.29 = (bf16[1024,1024]{1,0:T(8,128)(2,1)}, bf16[1024,1024]{1,0:T(8,128)(2,1)}, u32[]{:S(2)}, u32[]{:S(2)}) collective-permute-start(bf16[1024,1024]{1,0:T(8,128)(2,1)} %get-tuple-element.128), channel_id=1, source_target_pairs={{0,1},{1,0},{2,3},{3,2},{4,5},{5,4},{6,7},{7,6},{8,9},{9,8},{10,11... | collective-permute-start | bytes 6291464 | tf_op jit(solution)/shard_map/ppermute | solution.py:102
  385.4 47.4 %collective-permute-start.15 = (f32[16,1024]{1,0:T(8,128)S(1)}, f32[16,1024]{1,0:T(8,128)S(1)}, u32[]{:S(2)}, u32[]{:S(2)}) collective-permute-start(f32[16,1024]{1,0:T(8,128)S(1)} %concatenate.86), channel_id=1, source_target_pairs={{0,1},{1,0},{2,3},{3,2},{4,5},{5,4},{6,7},{7,6},{8,9},{9,8},{10,11... | collective-permute-start | bytes 196616 | tf_op jit(solution)/shard_map/ppermute | solution.py:1238
  385.8 47.7 %collective-permute-start.14 = (bf16[256,384]{1,0:T(8,128)(2,1)S(1)}, bf16[256,384]{1,0:T(8,128)(2,1)S(1)}, u32[]{:S(2)}, u32[]{:S(2)}) collective-permute-start(bf16[256,384]{1,0:T(8,128)(2,1)S(1)} %broadcast_select_fusion.27), channel_id=1, source_target_pairs={{0,4},{2,6},{4,0},{6,2},{8,12},{10,14},{12,8},{14,10},{16,20},{18,... | collective-permute-start | bytes 589832 | tf_op jit(solution)/shard_map/ppermute | solution.py:109
  387.6 45.9 %collective-permute-start.13 = (bf16[128,1152]{1,0:T(8,128)(2,1)S(1)}, bf16[128,1152]{1,0:T(8,128)(2,1)S(1)}, u32[]{:S(2)}, u32[]{:S(2)}) collective-permute-start(bf16[128,1152]{1,0:T(8,128)(2,1)S(1)} %broadcast_select_fusion.21), channel_id=1, source_target_pairs={{0,8},{2,10},{4,12},{6,14},{8,0},{10,2},{12,4},{14,6},{16,24},{18,... | collective-permute-start | bytes 884744 | tf_op jit(solution)/shard_map/ppermute | solution.py:109
  387.7 46.0 %collective-permute-start.12 = (bf16[128,1792]{1,0:T(8,128)(2,1)}, bf16[128,1792]{1,0:T(8,128)(2,1)S(1)}, u32[]{:S(2)}, u32[]{:S(2)}) collective-permute-start(bf16[128,1792]{1,0:T(8,128)(2,1)} %pad_maximum_fusion.9), channel_id=1, source_target_pairs={{0,8},{2,10},{4,12},{6,14},{8,0},{10,2},{12,4},{14,6},{16,24},{18,... | collective-permute-start | bytes 1376264 | tf_op jit(solution)/shard_map/ppermute | solution.py:109
  434.9 23.1 %collective-permute-start.21 = (bf16[256,1792]{1,0:T(8,128)(2,1)S(1)}, bf16[256,1792]{1,0:T(8,128)(2,1)S(1)}, u32[]{:S(2)}, u32[]{:S(2)}) collective-permute-start(bf16[256,1792]{1,0:T(8,128)(2,1)S(1)} %pad_maximum_fusion.5), channel_id=1, source_target_pairs={{0,4},{2,6},{4,0},{6,2},{8,12},{10,14},{12,8},{14,10},{16,20},{18,... | collective-permute-start | bytes 2752520 | tf_op jit(solution)/shard_map/ppermute | solution.py:109
  436.7 3.0 collective-permute-start.18
  436.7 6.9 %collective-permute-start.17 = (bf16[128,384]{1,0:T(8,128)(2,1)S(1)}, bf16[128,384]{1,0:T(8,128)(2,1)S(1)}, u32[]{:S(2)}, u32[]{:S(2)}) collective-permute-start(bf16[128,384]{1,0:T(8,128)(2,1)S(1)} %broadcast_select_fusion.29), channel_id=1, source_target_pairs={{0,8},{2,10},{4,12},{6,14},{8,0},{10,2},{12,4},{14,6},{16,24},{18,... | collective-permute-start | bytes 294920 | tf_op jit(solution)/shard_map/ppermute | solution.py:109
  436.8 10.4 %collective-permute-start.16 = (bf16[64,1152]{1,0:T(8,128)(2,1)S(1)}, bf16[64,1152]{1,0:T(8,128)(2,1)S(1)}, u32[]{:S(2)}, u32[]{:S(2)}) collective-permute-start(bf16[64,1152]{1,0:T(8,128)(2,1)S(1)} %broadcast_select_fusion.28), channel_id=1, source_target_pairs={{0,16},{2,18},{4,20},{6,22},{8,24},{10,26},{12,28},{14,30},{16,0},... | collective-permute-start | bytes 442376 | tf_op jit(solution)/shard_map/ppermute | solution.py:109
  447.3 5.1 collective-permute-start.19
  447.4 10.5 %collective-permute-start.20 = (f32[16,1024]{1,0:T(8,128)S(1)}, f32[16,1024]{1,0:T(8,128)S(1)}, u32[]{:S(2)}, u32[]{:S(2)}) collective-permute-start(f32[16,1024]{1,0:T(8,128)S(1)} %add.329), channel_id=1, source_target_pairs={{0,4},{2,6},{4,0},{6,2},{8,12},{10,14},{12,8},{14,10},{16,20},{18,... | collective-permute-start | bytes 196616 | tf_op jit(solution)/shard_map/ppermute | solution.py:109
  459.6 5.3 collective-permute-start.22
  464.7 4.3 collective-permute-start.23
  469.1 9.6 %collective-permute-start.25 = (f32[16,1024]{1,0:T(8,128)S(1)}, f32[16,1024]{1,0:T(8,128)S(1)}, u32[]{:S(2)}, u32[]{:S(2)}) collective-permute-start(f32[16,1024]{1,0:T(8,128)S(1)} %add.333), channel_id=1, source_target_pairs={{0,16},{2,18},{4,20},{6,22},{8,24},{10,26},{12,28},{14,30},{16,0},... | collective-permute-start | bytes 196616 | tf_op jit(solution)/shard_map/ppermute | solution.py:109
  470.2 11.2 %collective-permute-start.24 = (bf16[64,1664]{1,0:T(8,128)(2,1)S(1)}, bf16[64,1664]{1,0:T(8,128)(2,1)S(1)}, u32[]{:S(2)}, u32[]{:S(2)}) collective-permute-start(bf16[64,1664]{1,0:T(8,128)(2,1)S(1)} %concatenate.89), channel_id=1, source_target_pairs={{0,16},{2,18},{4,20},{6,22},{8,24},{10,26},{12,28},{14,30},{16,0},... | collective-permute-start | bytes 638984 | tf_op jit(solution)/shard_map/ppermute | solution.py:109
  481.6 18.1 %collective-permute-start.27 = (bf16[512,1792]{1,0:T(8,128)(2,1)}, bf16[512,1792]{1,0:T(8,128)(2,1)S(1)}, u32[]{:S(2)}, u32[]{:S(2)}) collective-permute-start(bf16[512,1792]{1,0:T(8,128)(2,1)} %pad_maximum_fusion.3), channel_id=1, source_target_pairs={{0,2},{2,0},{4,6},{6,4},{8,10},{10,8},{12,14},{14,12},{16,18},{18,... | collective-permute-start | bytes 5505032 | tf_op jit(solution)/shard_map/ppermute | solution.py:109
  487.4 12.1 %collective-permute-start.26 = (bf16[128,1664]{1,0:T(8,128)(2,1)S(1)}, bf16[128,1664]{1,0:T(8,128)(2,1)S(1)}, u32[]{:S(2)}, u32[]{:S(2)}) collective-permute-start(bf16[128,1664]{1,0:T(8,128)(2,1)S(1)} %pad_maximum_fusion.10), channel_id=1, source_target_pairs={{0,8},{2,10},{4,12},{6,14},{8,0},{10,2},{12,4},{14,6},{16,24},{18,... | collective-permute-start | bytes 1277960 | tf_op jit(solution)/shard_map/ppermute | solution.py:109
  500.1 20.5 %collective-permute-start.28 = (bf16[256,1664]{1,0:T(8,128)(2,1)S(1)}, bf16[256,1664]{1,0:T(8,128)(2,1)S(1)}, u32[]{:S(2)}, u32[]{:S(2)}) collective-permute-start(bf16[256,1664]{1,0:T(8,128)(2,1)S(1)} %pad_maximum_fusion.6), channel_id=1, source_target_pairs={{0,4},{2,6},{4,0},{6,2},{8,12},{10,14},{12,8},{14,10},{16,20},{18,... | collective-permute-start | bytes 2555912 | tf_op jit(solution)/shard_map/ppermute | solution.py:109
  520.9 4.3 collective-permute-start.30
  (52 other events, 189.2 us)
Sparse Core Ops, SparseCore 0:
  169.5 86.7 reduce-scatter.1
  299.1 82.4 all-gather.1

commit v4 on v3

--- a/solution.py
+++ b/solution.py
@@ -1048,6 +1048,39 @@
     return grad_in, sums
 
 
+def product_kernel(*refs):
+    left_pairs, right_pairs = [refs[0:2], refs[2:4], refs[2:4]], [(), refs[4:6], refs[6:8]]
+    cotangent_ref, out_ref = refs[8], refs[9]
+    half = refs[0].shape[0]
+    for which in range(3):
+        total = None
+        for k in range(2):
+            left = left_pairs[which][k][...]
+            if which == 0:
+                right = cotangent_ref[k * half : (k + 1) * half]
+            else:
+                right = right_pairs[which][k][...]
+            part = dot_tn(left, right)
+            total = part if total is None else total + part
+        out_ref[which] = total.astype(out_ref.dtype)
+
+
+def product_call(hidden_a, hidden_b, post_a, post_b, gate_a, gate_b, up_a, up_b, cotangent):
+    half, model = post_a.shape
+    hidden = hidden_a.shape[1]
+    columns = pl.BlockSpec((half, CHUNK), lambda i: (0, i))
+    whole = pl.BlockSpec((half, hidden), lambda i: (0, 0))
+    return pl.pallas_call(
+        product_kernel,
+        grid=(hidden // CHUNK,),
+        in_specs=[columns] * 4 + [whole] * 4 + [pl.BlockSpec((2 * half, model), lambda i: (0, 0))],
+        out_specs=pl.BlockSpec((3, CHUNK, model), lambda i: (0, i, 0)),
+        out_shape=jax.ShapeDtypeStruct((3, hidden, model), jnp.bfloat16),
+        compiler_params=pltpu.CompilerParams(vmem_limit_bytes=VMEM_BYTES),
+        name="weight_products",
+    )(hidden_a, hidden_b, post_a, post_b, gate_a, gate_b, up_a, up_b, cotangent)
+
+
 def local_fast(
     tokens,
     segments,
@@ -1135,36 +1168,56 @@
     mixed = (gated * inv_gate * mixer_scale).astype(low)
     branch_part = attn_part + matmul(mixed, mixer_out)
     out_gain = post_gain.astype(wide)
-    branch = by_rows(pair_sum(by_rows(branch_part.astype(low))))
-    middle = inputs + branch
-    inv_second = lax.rsqrt(jnp.mean(middle * middle, -1, keepdims=True) + EPS)
-    unit_second = middle * inv_second
-    post = by_rows((unit_second * out_gain).astype(low))
-    gate = matmul(post, gate_weight)
-    upward = matmul(post, up_weight)
-    sigma = jax.nn.sigmoid(gate)
-    hidden = (gate * sigma * upward).astype(low)
-    hidden_grad = dot_nt(cotangent, down_weight)
-    up_act_grad = (hidden_grad * gate * sigma).astype(low)
-    gate_act_grad = (hidden_grad * upward * sigma * (1.0 + gate * (1.0 - sigma))).astype(low)
-    post_part = dot_nt(gate_act_grad, gate_weight) + dot_nt(up_act_grad, up_weight)
-    post_gain_part = jnp.sum(post_part * unit_second, 0, keepdims=True)
-    post_full = by_rows(pair_sum(by_rows(post_part.astype(low))))
-    down_wgrad = dot_tn(hidden, cotangent).astype(low)
-    gate_wgrad = dot_tn(post, gate_act_grad).astype(low)
-    up_wgrad = dot_tn(post, up_act_grad).astype(low)
-    post_full, _, _, _ = tie(post_full, down_wgrad, gate_wgrad, up_wgrad)
+    branch_part = by_rows(branch_part.astype(low))
+    half = rows // 2
+    spans = [slice(0, half), slice(half, rows)]
+    branches = [by_rows(pair_sum(branch_part[span])) for span in spans]
+    weight_cat = jnp.concatenate(
+        [gating_weight, inner_weight, step_weight_wide, state_weight, query_weight, keyval_weight], 1
+    )
+    branches[0], weight_cat = tie(branches[0], weight_cat)
+    found = []
+    for at, span in enumerate(spans):
+        middle = inputs[span] + branches[at]
+        inv_second = lax.rsqrt(jnp.mean(middle * middle, -1, keepdims=True) + EPS)
+        unit_second = middle * inv_second
+        post = by_rows((unit_second * out_gain).astype(low))
+        gate = matmul(post, gate_weight)
+        upward = matmul(post, up_weight)
+        sigma = jax.nn.sigmoid(gate)
+        hidden = (gate * sigma * upward).astype(low)
+        hidden_grad = dot_nt(cotangent[span], down_weight)
+        up_act_grad = (hidden_grad * gate * sigma).astype(low)
+        gate_act_grad = (hidden_grad * upward * sigma * (1.0 + gate * (1.0 - sigma))).astype(low)
+        post_part = dot_nt(gate_act_grad, gate_weight) + dot_nt(up_act_grad, up_weight)
+        gain_part = jnp.sum(post_part * unit_second, 0, keepdims=True)
+        post_low = by_rows(post_part.astype(low))
+        if at == 0:
+            branches[1], post_low = tie(branches[1], post_low)
+        post_full = by_rows(pair_sum(post_low))
+        found.append(
+            (post_full, unit_second, inv_second, gain_part, hidden, post, gate_act_grad, up_act_grad)
+        )
+    post_gain_part = found[0][3] + found[1][3]
+    forward_part = product_call(
+        *[piece for k in range(4, 8) for piece in (found[0][k], found[1][k])], cotangent
+    )
+    post_fulls = [found[0][0], found[1][0]]
+    post_fulls[1], _ = tie(post_fulls[1], forward_part)
     forward_piece = lax.psum_scatter(
-        jnp.concatenate([down_wgrad, gate_wgrad, up_wgrad], 0),
-        "dp",
-        scatter_dimension=0,
-        tiled=True,
-    )
-    scaled_post = post_full * out_gain
-    middle_grad = cotangent.astype(wide) + inv_second * (
-        scaled_post - unit_second * jnp.mean(scaled_post * unit_second, -1, keepdims=True)
-    )
-    branch_grad = by_rows(middle_grad.astype(low))
+        forward_part.reshape(-1, model), "dp", scatter_dimension=0, tiled=True
+    )
+    middle_grads = []
+    for span, part, post_full in zip(spans, found, post_fulls):
+        unit_second, inv_second = part[1], part[2]
+        scaled_post = post_full * out_gain
+        middle_grads.append(
+            cotangent[span].astype(wide)
+            + inv_second
+            * (scaled_post - unit_second * jnp.mean(scaled_post * unit_second, -1, keepdims=True))
+        )
+    branch_grad = by_rows(jnp.concatenate([grad.astype(low) for grad in middle_grads], 0))
+    middle_grad = jnp.concatenate(middle_grads, 0)
     mixed_grad = dot_nt(branch_grad, mixer_out)
     mixer_gain_part = jnp.sum(mixed_grad * gated * inv_gate, 0, keepdims=True)
     weighted = mixed_grad * mixer_scale
@@ -1180,13 +1233,15 @@
     gating_part = by_rows(dot_tn(normed, gating_grad).astype(low))
     bits = dp_bits()
     early = halve_parts([out_part, gating_part], bits[0])
-    early, ssm_grad, forward_piece = tie(early, ssm_grad, forward_piece)
-    forward_total = lax.all_gather(forward_piece, "dp", axis=0, tiled=True)
+    early, ssm_grad = tie(early, ssm_grad)
     early = halve(early, bits[1])
     act_grad, step_grad, coef_grad, rate_sum, skip_sum = scan_back_call(
         step, coef, inner_act, aux, seg_row, rate_wide, skip_row, ssm_grad, kept
     )
-    early, act_grad, step_grad, coef_grad = tie(early, act_grad, step_grad, coef_grad)
+    early, act_grad, step_grad, coef_grad, forward_piece = tie(
+        early, act_grad, step_grad, coef_grad, forward_piece
+    )
+    forward_total = lax.all_gather(forward_piece, "dp", axis=0, tiled=True)
     early = halve(early, bits[2])
     step_total = step_grad * jax.nn.sigmoid(step_arg)
     inner_pre_grad = act_grad * silu_slope(inner_pre)
@@ -1209,9 +1264,6 @@
     early = double(early, bits[3])
     scan_part = halve(scan_part, bits[1])
     attend_part = halve(attend_part, bits[0])
-    weight_cat = jnp.concatenate(
-        [gating_weight, inner_weight, step_weight_wide, state_weight, query_weight, keyval_weight], 1
-    )
     normed_part = dot_nt(jnp.concatenate([gating_grad, scan_cat, attend_cat], 1), weight_cat)
     input_gain_part = jnp.sum(normed_part * unit_first, 0, keepdims=True)
     early, scan_part, attend_part, normed_part, input_gain_part = tie(
@@ -1235,28 +1287,24 @@
     small = jnp.concatenate(
         [jnp.pad(row, ((0, 0), (0, model - row.shape[1]))) for row in own_rows + shared_rows], 0
     )
-    small_other = lax.ppermute(small, "tensor", [(0, 1), (1, 0)])
-    is_shared = lax.broadcasted_iota(jnp.int32, small.shape, 0) >= len(own_rows)
-    small = small + jnp.where(is_shared, small_other, 0.0)
+    small = small + swap_bit(small, bits[0])
     early = double(early, bits[2])
     scan_part = halve(scan_part, bits[2])
     attend_part = halve(attend_part, bits[1])
-    early, scan_part, attend_part, small, forward_total = tie(
-        early, scan_part, attend_part, small, forward_total
-    )
+    early, scan_part, attend_part, small = tie(early, scan_part, attend_part, small)
+    early = double(early, bits[1])
+    scan_part = halve(scan_part, bits[3])
+    attend_part = halve(attend_part, bits[2])
+    small = small + swap_bit(small, bits[1])
+    scan_part, attend_part, small = tie(scan_part, attend_part, small)
+    attend_part = halve(attend_part, bits[3])
+    small = small + swap_bit(small, bits[2])
+    attend_part, small, early, forward_total = tie(attend_part, small, early, forward_total)
     hidden_units = down_weight.shape[0]
     down_wgrad = forward_total[:hidden_units].astype(wide)
     gate_wgrad = forward_total[hidden_units : hidden_units + model].astype(wide)
     up_wgrad = forward_total[hidden_units + model :].astype(wide)
-    early = double(early, bits[1])
-    scan_part = halve(scan_part, bits[3])
-    attend_part = halve(attend_part, bits[2])
-    small = small + swap_bit(small, bits[0])
-    scan_part, attend_part, small = tie(scan_part, attend_part, small)
-    attend_part = halve(attend_part, bits[3])
-    small = small + swap_bit(small, bits[1])
-    attend_part, small, early = tie(attend_part, small, early)
-    small = small + swap_bit(small, bits[2])
+    small = small + swap_bit(small, bits[3])
     scan_piece, attend_piece = scan_part, attend_part
     state_at = ssm_width + LANES
     trade = jnp.concatenate([scan_piece[:, state_at:], attend_piece[:, query_width:]], 1)
@@ -1282,7 +1330,9 @@
     )
     late, small = tie(late, small)
     late = double(late, bits[3])
-    small = small + swap_bit(small, bits[3])
+    small_other = lax.ppermute(small, "tensor", [(0, 1), (1, 0)])
+    is_shared = lax.broadcasted_iota(jnp.int32, small.shape, 0) >= len(own_rows)
+    small = small + jnp.where(is_shared, small_other, 0.0)
     late, early, small = tie(late, early, small)
     late = double(late, bits[2])
     early = double(early, bits[0])

time: 548 us -> 497 us (0.907)
  waiting for transfers between devices: 220 us -> 155 us
  local copies, waits for them, and re-layouts: 24.3 us -> 46.2 us
  other arithmetic: 119 us -> 103 us
  Pallas kernels: 61.8 us -> 74.1 us
  matrix products: 69.2 us -> 63.6 us
    ppermute x1, waiting for transfers between devices: 43 us -> 2.34 us  [local_fast(): small_other = lax.ppermute(small, 'tensor', [(0, 1), (1, 0)])]
    reduce_scatter x1, waiting for transfers between devices: 23.9 us -> 6.34 us  [local_fast(): lax.psum_scatter(forward_part.reshape(-1, model), 'dp', scatter_dimension...]
    concatenate x1 -> x0, other arithmetic: 13.2 us -> none  [local_fast(): jnp.concatenate([down_wgrad, gate_wgrad, up_wgrad], 0)]
    pallas_call x0 -> x1, Pallas kernels: none -> 11.8 us  [product_call(): pl.pallas_call(product_kernel, grid=(hidden // CHUNK,), in_specs=[columns...]
    ppermute x5 -> x7, waiting for transfers between devices: 75.7 us -> 64.9 us  [pair_sum(): other = lax.ppermute(value, 'tensor', [(0, 1), (1, 0)])]
    unnamed x143 -> x205, local copies, waits for them, and re-layouts: 7.99 us -> 17.3 us
    pad x14, local copies, waits for them, and re-layouts: 0.77 us -> 9.02 us  [local_fast(): jnp.pad(row, ((0, 0), (0, model - row.shape[1])))]
    dot_general x7 -> x4, matrix products: 16.5 us -> 8.92 us  [dot_tn(): lax.dot_general(left, right, (((0,), (0,)), ((), ())), preferred_element_...]
  transfers between devices with their start and end apart: 33 -> 35, of which waited for: 17 -> 21; matrix products, arithmetic and copies ran while one was open for 26% -> 28% of each run, Pallas kernels for 9% -> 13%
where the time goes in v4:
time: 497 us; the launch traced here: 488 us
  waiting for transfers between devices  155 us (31%)
  other arithmetic  103 us (21%)
  Pallas kernels  74.1 us (15%)
  matrix products  63.6 us (13%)
  local copies, waits for them, and re-layouts  46.2 us (9%)
  starting transfers between devices  30.3 us (6%)
  between operations  15.8 us (3%)
    ppermute x24, waiting for transfers between devices, swap_bit(): return lax.ppermute(value, 'dp', [(i, i ^ bit) for i in range(size)])  81.6 us
    ppermute x7, waiting for transfers between devices, pair_sum(): other = lax.ppermute(value, 'tensor', [(0, 1), (1, 0)])  64.9 us
    dot_general x12, matrix products, matmul(): return jnp.dot(left, right, preferred_element_type=jnp.float32)  28.8 us
    dot_general x9, matrix products, dot_nt(): lax.dot_general(left, right, (((1,), (1,)), ((), ())), preferred_element_...  25.8 us
    pallas_call x1, Pallas kernels, scan_back_call(): pl.pallas_call(scan_back_kernel, grid=(chunks,), in_specs=[by_chunk(LANES...  25.3 us
    ppermute x24, starting transfers between devices, swap_bit(): return lax.ppermute(value, 'dp', [(i, i ^ bit) for i in range(size)])  18.5 us
    unnamed x205, local copies, waits for them, and re-layouts  17.3 us
    pallas_call x1, Pallas kernels, attend_back_call(): pl.pallas_call(attend_back_kernel, out_shape=[jax.ShapeDtypeStruct((rows,...  13.2 us
  transfers between devices with their start and end apart: 35, of which 21 were waited for; matrix products, arithmetic and copies ran while one was open for 28% of the time, Pallas kernels for 13%

profile of v4, /device:TPU:0, one launch (start us, length us, event | category | flops | bytes accessed | tf_op | source)
XLA Modules:
  0.0 488.2 jit_solution(1621804684616330518)
XLA Ops:
  28.6 3.8 fusion.8
  32.4 12.8 %scan_forward.1 = (f32[1024,768]{1,0:T(8,128)}, bf16[4,128,768]{2,1,0:T(8,128)(2,1)}) custom-call(f32[1024,128]{1,0:T(8,128)} %get-tuple-element.334.step_ref, bf16[1024,256]{1,0:T(8,128)(2,1)} %get-tuple-element.267.coef_ref, f32[1024,768]{1,0:T(8,128)} %get-tuple-element.265.act_ref, f32[1024,128]{1,0:T(8,128)} %pad.127.seg_col_ref.aux_ref, ...), custom_call_target="tpu_custom_call" | custom-call | tf_op jit(solution)/shard_map/scan_forward/pallas_call | solution.py:673
  45.2 6.5 %multiply_reduce_fusion.9 = (f32[1024]{0:T(1024)S(1)}, f32[1024,768]{1,0:T(8,128)}, f32[1024,768]{1,0:T(8,128)}) fusion(f32[1024,768]{1,0:T(8,128)} %get-tuple-element.86, f32[1024,768]{1,0:T(8,128)S(1)} %get-tuple-element.266, f32[768]{0:T(1024)S(1)} %mul.752, bf16[1024,1024]{1,0:T(8,128)(2,1)S(1)} %multiply_convert_fusion, bf16[1024,768]{1,0:T(8,128)(2,1)} %param.31), kind=kOutput, calls=%fused_computation.37 | convolution fusion | flops 1620835328 | bytes 16260096 | tf_op jit(solution)/shard_map/dot_general | solution.py:23
  51.7 2.9 collective-permute-start
  54.7 3.0 fusion.46
  57.6 3.4 fusion.71.query_ref
  62.5 3.2 fusion.42.keyval_ref
  67.6 11.0 %attend_forward.1 = (bf16[1024,256]{1,0:T(8,128)(2,1)}, bf16[1024,256]{1,0:T(8,128)(2,1)}, bf16[1024,256]{1,0:T(8,128)(2,1)}, f32[1024,128]{1,0:T(8,128)}) custom-call(f32[1024,256]{1,0:T(8,128)} %fusion.71.query_ref, f32[1024,128]{1,0:T(8,128)} %fusion.42.keyval_ref, f32[1,1024]{1,0:T(1,128)} %get-tuple-element.320.seg_ref, ...), custom_call_target="tpu_custom_call" | custom-call | tf_op jit(solution)/shard_map/attend_forward/pallas_call | solution.py:910
  86.8 4.5 convert_element_type.400
  91.3 7.8 %concatenate.80 = bf16[1024,2304]{1,0:T(8,128)(2,1)} concatenate(bf16[1024,768]{1,0:T(8,128)(2,1)} %param.31, bf16[1024,768]{1,0:T(8,128)(2,1)} %param.32, bf16[1024,128]{1,0:T(8,128)(2,1)S(1)} %pad.128.clone, bf16[1024,256]{1,0:T(8,128)(2,1)} %param.33, bf16[1024,256]{1,0:T(8,128)(2,1)} %param.28, bf16[1024,64]{1,0:T(8,128)(2,1)S(1)} %get-tuple-element.303, ...), dimensions={1} | concatenate | bytes 9437184 | tf_op jit(solution)/shard_map/concatenate | solution.py:1175
  99.1 3.3 fusion.34
  102.4 8.5 %collective-permute-done.1 = bf16[512,1024]{1,0:T(8,128)(2,1)} collective-permute-done((bf16[512,1024]{1,0:T(8,128)(2,1)}, bf16[512,1024]{1,0:T(8,128)(2,1)}, u32[]{:S(2)}, u32[]{:S(2)}) %collective-permute-start.1) | collective-permute-done | bytes 1048608 | tf_op jit(solution)/shard_map/ppermute | solution.py:102
  110.9 21.0 %collective-permute-done.2 = bf16[512,1024]{1,0:T(8,128)(2,1)} collective-permute-done((bf16[512,1024]{1,0:T(8,128)(2,1)}, bf16[512,1024]{1,0:T(8,128)(2,1)}, u32[]{:S(2)}, u32[]{:S(2)}) %collective-permute-start.2) | collective-permute-done | bytes 1048608 | tf_op jit(solution)/shard_map/ppermute | solution.py:102
  131.9 2.4 convert_add_fusion.2
  138.4 3.0 multiply_convert_fusion.4
  146.7 21.2 %collective-permute-done.3 = bf16[512,1024]{1,0:T(8,128)(2,1)S(1)} collective-permute-done((bf16[512,1024]{1,0:T(8,128)(2,1)S(1)}, bf16[512,1024]{1,0:T(8,128)(2,1)S(1)}, u32[]{:S(2)}, u32[]{:S(2)}) %collective-permute-start.3) | collective-permute-done | bytes 1048608 | tf_op jit(solution)/shard_map/ppermute | solution.py:102
  170.3 3.2 multiply_convert_fusion.3
  174.9 3.0 fusion.70
  178.5 11.8 %weight_products.1 = bf16[3,1024,1024]{2,1,0:T(8,128)(2,1)} custom-call(bf16[512,1024]{1,0:T(8,128)(2,1)} %get-tuple-element.275.refs_0_, bf16[512,1024]{1,0:T(8,128)(2,1)} %get-tuple-element.272.refs_1_, bf16[512,1024]{1,0:T(8,128)(2,1)} %copy-done.27, bf16[512,1024]{1,0:T(8,128)(2,1)} %copy-done.37, bf16[512,1024]{1,0:T(8,128)(2,1)} %copy-done.54, ...), custom_call_target="tpu_custom_call" | custom-call | tf_op jit(solution)/shard_map/weight_products/pallas_call | solution.py:1073
  190.3 10.6 %collective-permute-done.4 = bf16[512,1024]{1,0:T(8,128)(2,1)} collective-permute-done((bf16[512,1024]{1,0:T(8,128)(2,1)}, bf16[512,1024]{1,0:T(8,128)(2,1)}, u32[]{:S(2)}, u32[]{:S(2)}) %collective-permute-start.4) | collective-permute-done | bytes 1048608 | tf_op jit(solution)/shard_map/ppermute | solution.py:102
  205.9 3.0 fusion.61
  218.4 3.7 constant_dynamic-update-slice_fusion.6
  226.3 5.7 %fusion.23.grad_ref = f32[1024,768]{1,0:T(8,128)} fusion(f32[1024]{0:T(1024)S(1)} %add.357, f32[1024,768]{1,0:T(8,128)} %get-tuple-element.264, f32[1024,768]{1,0:T(8,128)} %copy-done.18, f32[1024]{0:T(1024)S(1)} %get-tuple-element.253, f32[768]{0:T(1024)S(1)} %convert_element_type.411, f32[1024]{0:T(1024)S(1)} %get-tuple-element.254, ...), kind=kLoop, calls=%fused_computation.96 | loop fusion | flops 8650752 | bytes 12598272 | tf_op jit(solution)/shard_map/mul | solution.py:1229
  239.4 2.9 convolution_convert_fusion.3.grad_ref
  242.3 25.3 %scan_backward.1 = (f32[1024,768]{1,0:T(8,128)}, f32[1024,128]{1,0:T(8,128)}, f32[1024,256]{1,0:T(8,128)}, f32[1,128]{1,0:T(1,128)}, f32[1,768]{1,0:T(1,128)}) custom-call(f32[1024,128]{1,0:T(8,128)} %get-tuple-element.334.step_ref, bf16[1024,256]{1,0:T(8,128)(2,1)} %get-tuple-element.267.coef_ref, f32[1024,768]{1,0:T(8,128)} %get-tuple-element.265.act_ref, ...), custom_call_target="tpu_custom_call" | custom-call | tf_op jit(solution)/shard_map/scan_backward/pallas_call | solution.py:815
  271.8 6.3 %reduce-scatter.2.cloned.1.call-done = bf16[192,1024]{1,0:T(8,128)(2,1)} async-done(((bf16[3072,1024]{1,0:T(8,128)(2,1)}), bf16[192,1024]{1,0:T(8,128)(2,1)}) %reduce-scatter.2.cloned.1.call-update) | async-done | bytes 393232 | tf_op jit(solution)/shard_map/reduce_scatter | solution.py:1207
  281.9 3.5 fusion.57
  288.4 5.1 %fusion.56 = (f32[768]{0:T(1024)S(1)}, f32[768]{0:T(1024)S(1)}, f32[768]{0:T(1024)S(1)}, f32[768]{0:T(1024)S(1)}, f32[768]{0:T(1024)S(1)}, /*index=5*/f32[1024,7...) fusion(f32[1024,768]{1,0:T(8,128)S(1)} %copy-done.16, ...), kind=kLoop, calls=%fused_computation.257 | loop fusion | flops 15724800 | bytes 22047744 | tf_op jit(solution)/shard_map/reduce_sum | solution.py:1275
  296.6 2.4 constant_dynamic-update-slice_fusion.5
  302.1 3.3 convolution_convert_fusion
  308.7 13.2 %attend_backward.1 = (bf16[1024,256]{1,0:T(8,128)(2,1)}, bf16[1024,128]{1,0:T(8,128)(2,1)}) custom-call(bf16[1024,256]{1,0:T(8,128)(2,1)} %get-tuple-element.103.query_ref, bf16[1024,256]{1,0:T(8,128)(2,1)} %get-tuple-element.104.both_ref, f32[1,1024]{1,0:T(1,128)} %get-tuple-element.320.seg_ref, f32[1024,128]{1,0:T(8,128)} %pad.127.seg_col_ref.aux_ref, ...), custom_call_target="tpu_custom_call" | custom-call | tf_op jit(solution)/shard_map/attend_backward/pallas_call | solution.py:974
  325.4 8.8 %collective-permute-done.9 = bf16[64,1792]{1,0:T(8,128)(2,1)S(1)} collective-permute-done((bf16[64,1792]{1,0:T(8,128)(2,1)}, bf16[64,1792]{1,0:T(8,128)(2,1)S(1)}, u32[]{:S(2)}, u32[]{:S(2)}) %collective-permute-start.9) | collective-permute-done | bytes 229408 | tf_op jit(solution)/shard_map/ppermute | solution.py:109
  337.1 9.3 %multiply_reduce_fusion.1 = (f32[1024]{0:T(1024)}, bf16[1024,1024]{1,0:T(8,128)(2,1)}) fusion(bf16[1024,1024]{1,0:T(8,128)(2,1)S(1)} %copy-done.2, f32[1024]{0:T(1024)S(1)} %copy-done.64, bf16[1024,2304]{1,0:T(8,128)(2,1)S(1)} %constant_dynamic-update-slice_fusion.2, bf16[1024,2304]{1,0:T(8,128)(2,1)} %concatenate.80), kind=kOutput, calls=%fused_computation.3 | convolution fusion | flops 4837080064 | bytes 13639680 | tf_op jit(solution)/shard_map/dot_general | solution.py:594
  346.4 9.8 %collective-permute-done.11 = bf16[64,1792]{1,0:T(8,128)(2,1)S(1)} collective-permute-done((bf16[64,1792]{1,0:T(8,128)(2,1)S(1)}, bf16[64,1792]{1,0:T(8,128)(2,1)S(1)}, u32[]{:S(2)}, u32[]{:S(2)}) %collective-permute-start.11) | collective-permute-done | bytes 229408 | tf_op jit(solution)/shard_map/ppermute | solution.py:109
  356.9 2.8 concatenate.89
  367.2 3.9 collective-permute-done.15
  371.2 9.0 %collective-permute-done.14 = bf16[128,1792]{1,0:T(8,128)(2,1)S(1)} collective-permute-done((bf16[128,1792]{1,0:T(8,128)(2,1)S(1)}, bf16[128,1792]{1,0:T(8,128)(2,1)S(1)}, u32[]{:S(2)}, u32[]{:S(2)}) %collective-permute-start.14) | collective-permute-done | bytes 458784 | tf_op jit(solution)/shard_map/ppermute | solution.py:109
  387.2 3.5 collective-permute-done.18
  393.1 2.8 collective-permute-done.21
  395.9 8.6 %collective-permute-done.23 = bf16[256,1792]{1,0:T(8,128)(2,1)S(1)} collective-permute-done((bf16[256,1792]{1,0:T(8,128)(2,1)S(1)}, bf16[256,1792]{1,0:T(8,128)(2,1)S(1)}, u32[]{:S(2)}, u32[]{:S(2)}) %collective-permute-start.23) | collective-permute-done | bytes 917536 | tf_op jit(solution)/shard_map/ppermute | solution.py:109
  407.8 3.5 collective-permute-done.31
  411.3 3.4 multiply_reduce_fusion
  416.0 4.5 collective-permute-done.25
  424.9 6.3 %collective-permute-done.26 = bf16[64,1664]{1,0:T(8,128)(2,1)S(1)} collective-permute-done((bf16[64,1664]{1,0:T(8,128)(2,1)S(1)}, bf16[64,1664]{1,0:T(8,128)(2,1)S(1)}, u32[]{:S(2)}, u32[]{:S(2)}) %collective-permute-start.26) | collective-permute-done | bytes 213024 | tf_op jit(solution)/shard_map/ppermute | solution.py:109
  431.4 5.4 %maximum_add_fusion = f32[1024,1024]{1,0:T(8,128)} fusion(f32[512,1024]{1,0:T(8,128)} %get-tuple-element.286, f32[512,1024]{1,0:T(8,128)S(1)} %copy-done.25, bf16[1024,1024]{1,0:T(8,128)(2,1)} %collective-permute-done.31, bf16[1024,1024]{1,0:T(8,128)(2,1)} %get-tuple-element.136, bf16[1024,1024]{1,0:T(8,128)(2,1)S(1)} %copy-done.2, ...), kind=kLoop, calls=%fused_computation | loop fusion | flops 11534336 | bytes 14692352 | tf_op jit(solution)/shard_map/add | solution.py:1350
  437.5 5.1 %slice_convert_fusion = (f32[1024,1024]{1,0:T(8,128)}, f32[1024,1024]{1,0:T(8,128)}, f32[1024,1024]{1,0:T(8,128)}) fusion(bf16[3072,1024]{1,0:T(8,128)(2,1)S(1)} %bitcast.89), kind=kLoop, calls=%fused_computation.57 | loop fusion | flops 3145728 | bytes 18874368 | tf_op jit(solution)/shard_map/convert_element_type | solution.py:1304
  442.6 6.3 %collective-permute-done.28 = bf16[128,1664]{1,0:T(8,128)(2,1)S(1)} collective-permute-done((bf16[128,1664]{1,0:T(8,128)(2,1)S(1)}, bf16[128,1664]{1,0:T(8,128)(2,1)S(1)}, u32[]{:S(2)}, u32[]{:S(2)}) %collective-permute-start.28) | collective-permute-done | bytes 426016 | tf_op jit(solution)/shard_map/ppermute | solution.py:109
  455.6 14.7 %collective-permute-done.30 = bf16[256,1664]{1,0:T(8,128)(2,1)S(1)} collective-permute-done((bf16[256,1664]{1,0:T(8,128)(2,1)S(1)}, bf16[256,1664]{1,0:T(8,128)(2,1)S(1)}, u32[]{:S(2)}, u32[]{:S(2)}) %collective-permute-start.30) | collective-permute-done | bytes 852000 | tf_op jit(solution)/shard_map/ppermute | solution.py:109
  (423 shorter events, 143.5 us)
Async XLA Ops:
  7.2 131.2 %copy-start = (bf16[1024,1024]{1,0:T(8,128)(2,1)S(1)}, bf16[1024,1024]{1,0:T(8,128)(2,1)}, u32[]{:S(2)}) copy-start(bf16[1024,1024]{1,0:T(8,128)(2,1)} %param.46) | copy-start | bytes 6291460
  7.3 270.8 %reduce-scatter.2.cloned.1.call-start = ((), (), s32[]{:S(2)}) async-start(), calls=%async_computation.1 | async-start | bytes 6684672 | tf_op jit(solution)/shard_map/reduce_scatter | solution.py:1207
  20.6 24.6 %copy-start.19 = (bf16[1024,1024]{1,0:T(8,128)(2,1)}, bf16[1024,1024]{1,0:T(8,128)(2,1)S(1)}, u32[]{:S(2)}) copy-start(bf16[1024,1024]{1,0:T(8,128)(2,1)S(1)} %multiply_convert_fusion) | copy-start | bytes 6291460
  32.4 12.8 %copy-start.9 = (f32[1024,768]{1,0:T(8,128)}, f32[1024,768]{1,0:T(8,128)S(1)}, u32[]{:S(2)}) copy-start(f32[1024,768]{1,0:T(8,128)S(1)} %get-tuple-element.266) | copy-start | bytes 9437188
  51.7 26.8 %collective-permute-start = (f32[1024]{0:T(1024)S(1)}, f32[1024]{0:T(1024)S(1)}, u32[]{:S(2)}, u32[]{:S(2)}) collective-permute-start(f32[1024]{0:T(1024)S(1)} %get-tuple-element.263), channel_id=1, source_target_pairs={{0,1},{1,0},{2,3},{3,2},{4,5},{5,4},{6,7},{7,6},{8,9},{9,8},{10,11... | collective-permute-start | bytes 12296 | tf_op jit(solution)/shard_map/ppermute | solution.py:102
  84.5 26.4 %collective-permute-start.1 = (bf16[512,1024]{1,0:T(8,128)(2,1)}, bf16[512,1024]{1,0:T(8,128)(2,1)}, u32[]{:S(2)}, u32[]{:S(2)}) collective-permute-start(bf16[512,1024]{1,0:T(8,128)(2,1)} %get-tuple-element.291), channel_id=1, source_target_pairs={{0,1},{1,0},{2,3},{3,2},{4,5},{5,4},{6,7},{7,6},{8,9},{9,8},{10,11... | collective-permute-start | bytes 3145736 | tf_op jit(solution)/shard_map/ppermute | solution.py:102
  84.5 47.4 %collective-permute-start.2 = (bf16[512,1024]{1,0:T(8,128)(2,1)}, bf16[512,1024]{1,0:T(8,128)(2,1)}, u32[]{:S(2)}, u32[]{:S(2)}) collective-permute-start(bf16[512,1024]{1,0:T(8,128)(2,1)} %get-tuple-element.292), channel_id=1, source_target_pairs={{0,1},{1,0},{2,3},{3,2},{4,5},{5,4},{6,7},{7,6},{8,9},{9,8},{10,11... | collective-permute-start | bytes 3145736 | tf_op jit(solution)/shard_map/ppermute | solution.py:102
  99.1 32.9 %copy-start.13 = (bf16[1024,1024]{1,0:T(8,128)(2,1)S(1)}, bf16[1024,1024]{1,0:T(8,128)(2,1)}, u32[]{:S(2)}) copy-start(bf16[1024,1024]{1,0:T(8,128)(2,1)} %copy-done.12) | copy-start | bytes 6291460
  102.4 32.0 %copy-start.14 = (f32[1024,1024]{1,0:T(8,128)S(1)}, f32[1024,1024]{1,0:T(8,128)}, u32[]{:S(2)}) copy-start(f32[1024,1024]{1,0:T(8,128)} %convert_element_type.400) | copy-start | bytes 12582916
  134.7 33.2 %copy-start.3 = (f32[512,1024]{1,0:T(8,128)}, f32[512,1024]{1,0:T(8,128)S(1)}, u32[]{:S(2)}) copy-start(f32[512,1024]{1,0:T(8,128)S(1)} %get-tuple-element.262) | copy-start | bytes 6291460
  144.1 23.8 %collective-permute-start.3 = (bf16[512,1024]{1,0:T(8,128)(2,1)S(1)}, bf16[512,1024]{1,0:T(8,128)(2,1)S(1)}, u32[]{:S(2)}, u32[]{:S(2)}) collective-permute-start(bf16[512,1024]{1,0:T(8,128)(2,1)S(1)} %get-tuple-element.88), channel_id=1, source_target_pairs={{0,1},{1,0},{2,3},{3,2},{4,5},{5,4},{6,7},{7,6},{8,9},{9,8},{10,11... | collective-permute-start | bytes 3145736 | tf_op jit(solution)/shard_map/ppermute | solution.py:102
  146.7 22.3 %copy-start.5 = (f32[512,1024]{1,0:T(8,128)}, f32[512,1024]{1,0:T(8,128)S(1)}, u32[]{:S(2)}) copy-start(f32[512,1024]{1,0:T(8,128)S(1)} %get-tuple-element.260) | copy-start | bytes 6291460
  177.9 23.1 %collective-permute-start.4 = (bf16[512,1024]{1,0:T(8,128)(2,1)}, bf16[512,1024]{1,0:T(8,128)(2,1)}, u32[]{:S(2)}, u32[]{:S(2)}) collective-permute-start(bf16[512,1024]{1,0:T(8,128)(2,1)} %get-tuple-element.339), channel_id=1, source_target_pairs={{0,1},{1,0},{2,3},{3,2},{4,5},{5,4},{6,7},{7,6},{8,9},{9,8},{10,11... | collective-permute-start | bytes 3145736 | tf_op jit(solution)/shard_map/ppermute | solution.py:102
  190.3 215.7 %all-gather.2.cloned.1.call-start = ((), (), s32[]{:S(2)}) async-start(), calls=%async_computation.2 | async-start | bytes 6684672 | tf_op jit(solution)/shard_map/all_gather | solution.py:1244
  190.3 12.7 %copy-start.6 = (f32[512,1024]{1,0:T(8,128)S(1)}, f32[512,1024]{1,0:T(8,128)}, u32[]{:S(2)}) copy-start(f32[512,1024]{1,0:T(8,128)} %copy-done.5) | copy-start | bytes 6291460
  190.3 12.7 %copy-start.22 = (f32[512,1024]{1,0:T(8,128)S(1)}, f32[512,1024]{1,0:T(8,128)}, u32[]{:S(2)}) copy-start(f32[512,1024]{1,0:T(8,128)} %get-tuple-element.340) | copy-start | bytes 6291460
  212.9 3.7 collective-permute-start.5
  226.3 5.7 %collective-permute-start.6 = (bf16[512,1792]{1,0:T(8,128)(2,1)}, bf16[512,1792]{1,0:T(8,128)(2,1)S(1)}, u32[]{:S(2)}, u32[]{:S(2)}) collective-permute-start(bf16[512,1792]{1,0:T(8,128)(2,1)} %pad_maximum_fusion.2), channel_id=1, source_target_pairs={{0,2},{2,0},{4,6},{6,4},{8,10},{10,8},{12,14},{14,12},{16,18},{18,... | collective-permute-start | bytes 5505032 | tf_op jit(solution)/shard_map/ppermute | solution.py:109
  236.2 34.0 %collective-permute-start.7 = (bf16[256,1792]{1,0:T(8,128)(2,1)}, bf16[256,1792]{1,0:T(8,128)(2,1)}, u32[]{:S(2)}, u32[]{:S(2)}) collective-permute-start(bf16[256,1792]{1,0:T(8,128)(2,1)} %broadcast_select_fusion.9), channel_id=1, source_target_pairs={{0,4},{2,6},{4,0},{6,2},{8,12},{10,14},{12,8},{14,10},{16,20},{18,... | collective-permute-start | bytes 2752520 | tf_op jit(solution)/shard_map/ppermute | solution.py:109
  242.3 25.3 %copy-start.93 = (f32[1,12]{1,0:T(1,128)S(1)}, f32[1,12]{1,0:T(1,128)}, u32[]{:S(2)}) copy-start(f32[1,12]{1,0:T(1,128)} %copy-done.92) | copy-start | bytes 148
  280.8 24.7 %collective-permute-start.8 = (bf16[128,1792]{1,0:T(8,128)(2,1)}, bf16[128,1792]{1,0:T(8,128)(2,1)}, u32[]{:S(2)}, u32[]{:S(2)}) collective-permute-start(bf16[128,1792]{1,0:T(8,128)(2,1)} %broadcast_select_fusion.17), channel_id=1, source_target_pairs={{0,8},{2,10},{4,12},{6,14},{8,0},{10,2},{12,4},{14,6},{16,24},{18,... | collective-permute-start | bytes 1376264 | tf_op jit(solution)/shard_map/ppermute | solution.py:109
  306.8 27.5 %collective-permute-start.10 = (bf16[512,1152]{1,0:T(8,128)(2,1)S(1)}, bf16[512,1152]{1,0:T(8,128)(2,1)S(1)}, u32[]{:S(2)}, u32[]{:S(2)}) collective-permute-start(bf16[512,1152]{1,0:T(8,128)(2,1)S(1)} %broadcast_select_fusion.4), channel_id=1, source_target_pairs={{0,2},{2,0},{4,6},{6,4},{8,10},{10,8},{12,14},{14,12},{16,18},{18,... | collective-permute-start | bytes 3538952 | tf_op jit(solution)/shard_map/ppermute | solution.py:109
  307.6 26.6 %collective-permute-start.9 = (bf16[64,1792]{1,0:T(8,128)(2,1)}, bf16[64,1792]{1,0:T(8,128)(2,1)S(1)}, u32[]{:S(2)}, u32[]{:S(2)}) collective-permute-start(bf16[64,1792]{1,0:T(8,128)(2,1)} %broadcast_select_fusion.24), channel_id=1, source_target_pairs={{0,16},{2,18},{4,20},{6,22},{8,24},{10,26},{12,28},{14,30},{16,0},... | collective-permute-start | bytes 688136 | tf_op jit(solution)/shard_map/ppermute | solution.py:109
  324.1 12.8 %slice-start.4 = ((s8[4718592]{0:T(1024)(128)(4,1)}), s8[4194304]{0:T(1024)(128)(4,1)S(1)}, s32[]{:S(2)}) async-start(s8[4718592]{0:T(1024)(128)(4,1)} %bitcast.90), calls=%async_computation.7 | async-start | bytes 8388608
  334.8 21.4 %collective-permute-start.11 = (bf16[64,1792]{1,0:T(8,128)(2,1)S(1)}, bf16[64,1792]{1,0:T(8,128)(2,1)S(1)}, u32[]{:S(2)}, u32[]{:S(2)}) collective-permute-start(bf16[64,1792]{1,0:T(8,128)(2,1)S(1)} %add_convert_fusion.8), channel_id=1, source_target_pairs={{0,16},{2,18},{4,20},{6,22},{8,24},{10,26},{12,28},{14,30},{16,0},... | collective-permute-start | bytes 688136 | tf_op jit(solution)/shard_map/ppermute | solution.py:109
  334.9 21.4 %collective-permute-start.13 = (bf16[512,384]{1,0:T(8,128)(2,1)S(1)}, bf16[512,384]{1,0:T(8,128)(2,1)S(1)}, u32[]{:S(2)}, u32[]{:S(2)}) collective-permute-start(bf16[512,384]{1,0:T(8,128)(2,1)S(1)} %broadcast_select_fusion.20), channel_id=1, source_target_pairs={{0,2},{2,0},{4,6},{6,4},{8,10},{10,8},{12,14},{14,12},{16,18},{18,... | collective-permute-start | bytes 1179656 | tf_op jit(solution)/shard_map/ppermute | solution.py:109
  335.0 21.4 %collective-permute-start.12 = (bf16[256,1152]{1,0:T(8,128)(2,1)S(1)}, bf16[256,1152]{1,0:T(8,128)(2,1)S(1)}, u32[]{:S(2)}, u32[]{:S(2)}) collective-permute-start(bf16[256,1152]{1,0:T(8,128)(2,1)S(1)} %broadcast_select_fusion.14), channel_id=1, source_target_pairs={{0,4},{2,6},{4,0},{6,2},{8,12},{10,14},{12,8},{14,10},{16,20},{18,... | collective-permute-start | bytes 1769480 | tf_op jit(solution)/shard_map/ppermute | solution.py:109
  359.7 5.1 %collective-permute-start.17 = (f32[16,1024]{1,0:T(8,128)}, f32[16,1024]{1,0:T(8,128)S(1)}, u32[]{:S(2)}, u32[]{:S(2)}) collective-permute-start(f32[16,1024]{1,0:T(8,128)} %concatenate.89), channel_id=1, source_target_pairs={{0,2},{2,0},{4,6},{6,4},{8,10},{10,8},{12,14},{14,12},{16,18},{18,... | collective-permute-start | bytes 196616 | tf_op jit(solution)/shard_map/ppermute | solution.py:109
  359.8 7.4 %collective-permute-start.16 = (bf16[256,384]{1,0:T(8,128)(2,1)S(1)}, bf16[256,384]{1,0:T(8,128)(2,1)S(1)}, u32[]{:S(2)}, u32[]{:S(2)}) collective-permute-start(bf16[256,384]{1,0:T(8,128)(2,1)S(1)} %broadcast_select_fusion.27), channel_id=1, source_target_pairs={{0,4},{2,6},{4,0},{6,2},{8,12},{10,14},{12,8},{14,10},{16,20},{18,... | collective-permute-start | bytes 589832 | tf_op jit(solution)/shard_map/ppermute | solution.py:109
  361.2 9.9 %collective-permute-start.15 = (bf16[128,1152]{1,0:T(8,128)(2,1)S(1)}, bf16[128,1152]{1,0:T(8,128)(2,1)S(1)}, u32[]{:S(2)}, u32[]{:S(2)}) collective-permute-start(bf16[128,1152]{1,0:T(8,128)(2,1)S(1)} %broadcast_select_fusion.21), channel_id=1, source_target_pairs={{0,8},{2,10},{4,12},{6,14},{8,0},{10,2},{12,4},{14,6},{16,24},{18,... | collective-permute-start | bytes 884744 | tf_op jit(solution)/shard_map/ppermute | solution.py:109
  361.3 19.0 %collective-permute-start.14 = (bf16[128,1792]{1,0:T(8,128)(2,1)S(1)}, bf16[128,1792]{1,0:T(8,128)(2,1)S(1)}, u32[]{:S(2)}, u32[]{:S(2)}) collective-permute-start(bf16[128,1792]{1,0:T(8,128)(2,1)S(1)} %pad_maximum_fusion.12), channel_id=1, source_target_pairs={{0,8},{2,10},{4,12},{6,14},{8,0},{10,2},{12,4},{14,6},{16,24},{18,... | collective-permute-start | bytes 1376264 | tf_op jit(solution)/shard_map/ppermute | solution.py:109
  363.3 48.0 %collective-permute-start.31 = (bf16[1024,1024]{1,0:T(8,128)(2,1)}, bf16[1024,1024]{1,0:T(8,128)(2,1)}, u32[]{:S(2)}, u32[]{:S(2)}) collective-permute-start(bf16[1024,1024]{1,0:T(8,128)(2,1)} %get-tuple-element.136), channel_id=1, source_target_pairs={{0,1},{1,0},{2,3},{3,2},{4,5},{5,4},{6,7},{7,6},{8,9},{9,8},{10,11... | collective-permute-start | bytes 6291464 | tf_op jit(solution)/shard_map/ppermute | solution.py:102
  380.4 4.8 collective-permute-start.20
  381.1 6.0 %collective-permute-start.19 = (bf16[128,384]{1,0:T(8,128)(2,1)S(1)}, bf16[128,384]{1,0:T(8,128)(2,1)S(1)}, u32[]{:S(2)}, u32[]{:S(2)}) collective-permute-start(bf16[128,384]{1,0:T(8,128)(2,1)S(1)} %broadcast_select_fusion.29), channel_id=1, source_target_pairs={{0,8},{2,10},{4,12},{6,14},{8,0},{10,2},{12,4},{14,6},{16,24},{18,... | collective-permute-start | bytes 294920 | tf_op jit(solution)/shard_map/ppermute | solution.py:109
  381.5 9.1 %collective-permute-start.18 = (bf16[64,1152]{1,0:T(8,128)(2,1)S(1)}, bf16[64,1152]{1,0:T(8,128)(2,1)S(1)}, u32[]{:S(2)}, u32[]{:S(2)}) collective-permute-start(bf16[64,1152]{1,0:T(8,128)(2,1)S(1)} %broadcast_select_fusion.28), channel_id=1, source_target_pairs={{0,16},{2,18},{4,20},{6,22},{8,24},{10,26},{12,28},{14,30},{16,0},... | collective-permute-start | bytes 442376 | tf_op jit(solution)/shard_map/ppermute | solution.py:109
  383.8 20.7 %collective-permute-start.23 = (bf16[256,1792]{1,0:T(8,128)(2,1)S(1)}, bf16[256,1792]{1,0:T(8,128)(2,1)S(1)}, u32[]{:S(2)}, u32[]{:S(2)}) collective-permute-start(bf16[256,1792]{1,0:T(8,128)(2,1)S(1)} %pad_maximum_fusion.5), channel_id=1, source_target_pairs={{0,4},{2,6},{4,0},{6,2},{8,12},{10,14},{12,8},{14,10},{16,20},{18,... | collective-permute-start | bytes 2752520 | tf_op jit(solution)/shard_map/ppermute | solution.py:109
  390.7 13.9 %copy-start.56 = (bf16[64,1152]{1,0:T(8,128)(2,1)}, bf16[64,1152]{1,0:T(8,128)(2,1)S(1)}, u32[]{:S(2)}) copy-start(bf16[64,1152]{1,0:T(8,128)(2,1)S(1)} %add_convert_fusion.10) | copy-start | bytes 442372
  390.8 5.1 %collective-permute-start.21 = (bf16[64,384]{1,0:T(8,128)(2,1)S(1)}, bf16[64,384]{1,0:T(8,128)(2,1)S(1)}, u32[]{:S(2)}, u32[]{:S(2)}) collective-permute-start(bf16[64,384]{1,0:T(8,128)(2,1)S(1)} %broadcast_select_fusion.30), channel_id=1, source_target_pairs={{0,16},{2,18},{4,20},{6,22},{8,24},{10,26},{12,28},{14,30},{16,0},... | collective-permute-start | bytes 147464 | tf_op jit(solution)/shard_map/ppermute | solution.py:109
  390.9 5.0 %collective-permute-start.22 = (f32[16,1024]{1,0:T(8,128)S(1)}, f32[16,1024]{1,0:T(8,128)S(1)}, u32[]{:S(2)}, u32[]{:S(2)}) collective-permute-start(f32[16,1024]{1,0:T(8,128)S(1)} %add.382), channel_id=1, source_target_pairs={{0,8},{2,10},{4,12},{6,14},{8,0},{10,2},{12,4},{14,6},{16,24},{18,... | collective-permute-start | bytes 196616 | tf_op jit(solution)/shard_map/ppermute | solution.py:109
  406.0 9.6 %collective-permute-start.24 = (bf16[64,384]{1,0:T(8,128)(2,1)S(1)}, bf16[64,384]{1,0:T(8,128)(2,1)S(1)}, u32[]{:S(2)}, u32[]{:S(2)}) collective-permute-start(bf16[64,384]{1,0:T(8,128)(2,1)S(1)} %pad_maximum_fusion.15), channel_id=1, source_target_pairs={{0,1},{1,0},{2,3},{3,2},{4,5},{5,4},{6,7},{7,6},{8,9},{9,8},{10,11... | collective-permute-start | bytes 147464 | tf_op jit(solution)/shard_map/ppermute | solution.py:1311
  414.8 5.7 %collective-permute-start.25 = (f32[16,1024]{1,0:T(8,128)S(1)}, f32[16,1024]{1,0:T(8,128)S(1)}, u32[]{:S(2)}, u32[]{:S(2)}) collective-permute-start(f32[16,1024]{1,0:T(8,128)S(1)} %add.384), channel_id=1, source_target_pairs={{0,16},{2,18},{4,20},{6,22},{8,24},{10,26},{12,28},{14,30},{16,0},... | collective-permute-start | bytes 196616 | tf_op jit(solution)/shard_map/ppermute | solution.py:109
  416.0 15.4 %copy-start.25 = (f32[512,1024]{1,0:T(8,128)S(1)}, f32[512,1024]{1,0:T(8,128)}, u32[]{:S(2)}) copy-start(f32[512,1024]{1,0:T(8,128)} %get-tuple-element.256) | copy-start | bytes 6291460
  420.5 4.3 collective-permute-start.27
  422.1 9.2 %collective-permute-start.26 = (bf16[64,1664]{1,0:T(8,128)(2,1)S(1)}, bf16[64,1664]{1,0:T(8,128)(2,1)S(1)}, u32[]{:S(2)}, u32[]{:S(2)}) collective-permute-start(bf16[64,1664]{1,0:T(8,128)(2,1)S(1)} %concatenate.92), channel_id=1, source_target_pairs={{0,16},{2,18},{4,20},{6,22},{8,24},{10,26},{12,28},{14,30},{16,0},... | collective-permute-start | bytes 638984 | tf_op jit(solution)/shard_map/ppermute | solution.py:109
  431.3 17.8 %collective-permute-start.29 = (bf16[512,1792]{1,0:T(8,128)(2,1)}, bf16[512,1792]{1,0:T(8,128)(2,1)S(1)}, u32[]{:S(2)}, u32[]{:S(2)}) collective-permute-start(bf16[512,1792]{1,0:T(8,128)(2,1)} %pad_maximum_fusion.3), channel_id=1, source_target_pairs={{0,2},{2,0},{4,6},{6,4},{8,10},{10,8},{12,14},{14,12},{16,18},{18,... | collective-permute-start | bytes 5505032 | tf_op jit(solution)/shard_map/ppermute | solution.py:109
  436.8 12.2 %collective-permute-start.28 = (bf16[128,1664]{1,0:T(8,128)(2,1)S(1)}, bf16[128,1664]{1,0:T(8,128)(2,1)S(1)}, u32[]{:S(2)}, u32[]{:S(2)}) collective-permute-start(bf16[128,1664]{1,0:T(8,128)(2,1)S(1)} %pad_maximum_fusion.13), channel_id=1, source_target_pairs={{0,8},{2,10},{4,12},{6,14},{8,0},{10,2},{12,4},{14,6},{16,24},{18,... | collective-permute-start | bytes 1277960 | tf_op jit(solution)/shard_map/ppermute | solution.py:109
  449.6 20.6 %collective-permute-start.30 = (bf16[256,1664]{1,0:T(8,128)(2,1)S(1)}, bf16[256,1664]{1,0:T(8,128)(2,1)S(1)}, u32[]{:S(2)}, u32[]{:S(2)}) collective-permute-start(bf16[256,1664]{1,0:T(8,128)(2,1)S(1)} %pad_maximum_fusion.6), channel_id=1, source_target_pairs={{0,4},{2,6},{4,0},{6,2},{8,12},{10,14},{12,8},{14,10},{16,20},{18,... | collective-permute-start | bytes 2555912 | tf_op jit(solution)/shard_map/ppermute | solution.py:109
  470.6 4.3 collective-permute-start.32
  (87 other events, 420.7 us)
Sparse Core Ops, SparseCore 0:
  190.4 87.6 reduce-scatter.1
  280.6 78.0 all-gather.1

commit v5 on v4

--- a/solution.py
+++ b/solution.py
@@ -1019,6 +1019,10 @@
     return with_layout_constraint(value, Layout(major_to_minor=(0, 1)))
 
 
+def swap_pair(value):
+    return lax.ppermute(value, "tensor", [(0, 1), (1, 0)])
+
+
 def tie(*values):
     return lax.optimization_barrier(values)
 
@@ -1033,19 +1037,23 @@
     return total
 
 
-def conv_rows_back(grad, value, kernel, keeps):
-    taps = kernel.shape[0]
-    grad_in = jnp.zeros_like(grad)
+def conv_sums(grad, value, taps, keeps):
     sums = []
     for tap in range(taps):
         offset = taps - 1 - tap
-        masked = grad * keeps[offset]
         moved = jnp.pad(value, ((offset, 0), (0, 0)))[: value.shape[0]]
-        sums.append(jnp.sum(masked * moved, 0, keepdims=True))
-        grad_in = grad_in + kernel[tap].astype(jnp.float32) * jnp.pad(
-            masked, ((0, offset), (0, 0))
-        )[offset:]
-    return grad_in, sums
+        sums.append(jnp.sum(grad * keeps[offset] * moved, 0, keepdims=True))
+    return sums
+
+
+def conv_grad(grad, kernel, keeps):
+    taps = kernel.shape[0]
+    total = jnp.zeros_like(grad)
+    for tap in range(taps):
+        offset = taps - 1 - tap
+        moved = jnp.pad(grad * keeps[offset], ((0, offset), (0, 0)))[offset:]
+        total = total + kernel[tap].astype(jnp.float32) * moved
+    return total
 
 
 def product_kernel(*refs):
@@ -1171,14 +1179,15 @@
     branch_part = by_rows(branch_part.astype(low))
     half = rows // 2
     spans = [slice(0, half), slice(half, rows)]
-    branches = [by_rows(pair_sum(branch_part[span])) for span in spans]
+    sent = [branch_part[span] for span in spans]
+    got = [swap_pair(piece) for piece in sent]
     weight_cat = jnp.concatenate(
         [gating_weight, inner_weight, step_weight_wide, state_weight, query_weight, keyval_weight], 1
     )
-    branches[0], weight_cat = tie(branches[0], weight_cat)
+    got[0], weight_cat = tie(got[0], weight_cat)
     found = []
     for at, span in enumerate(spans):
-        middle = inputs[span] + branches[at]
+        middle = inputs[span] + by_rows(sent[at].astype(wide) + got[at].astype(wide))
         inv_second = lax.rsqrt(jnp.mean(middle * middle, -1, keepdims=True) + EPS)
         unit_second = middle * inv_second
         post = by_rows((unit_second * out_gain).astype(low))
@@ -1193,23 +1202,24 @@
         gain_part = jnp.sum(post_part * unit_second, 0, keepdims=True)
         post_low = by_rows(post_part.astype(low))
         if at == 0:
-            branches[1], post_low = tie(branches[1], post_low)
-        post_full = by_rows(pair_sum(post_low))
+            got[1], post_low = tie(got[1], post_low)
+        post_got = swap_pair(post_low)
         found.append(
-            (post_full, unit_second, inv_second, gain_part, hidden, post, gate_act_grad, up_act_grad)
-        )
+            (post_low, unit_second, inv_second, gain_part, hidden, post, gate_act_grad, up_act_grad)
+        )
+        got[at] = post_got
     post_gain_part = found[0][3] + found[1][3]
     forward_part = product_call(
         *[piece for k in range(4, 8) for piece in (found[0][k], found[1][k])], cotangent
     )
-    post_fulls = [found[0][0], found[1][0]]
-    post_fulls[1], _ = tie(post_fulls[1], forward_part)
+    got[1], _ = tie(got[1], forward_part)
     forward_piece = lax.psum_scatter(
         forward_part.reshape(-1, model), "dp", scatter_dimension=0, tiled=True
     )
     middle_grads = []
-    for span, part, post_full in zip(spans, found, post_fulls):
-        unit_second, inv_second = part[1], part[2]
+    for span, part, other in zip(spans, found, got):
+        post_low, unit_second, inv_second = part[:3]
+        post_full = by_rows(post_low.astype(wide) + other.astype(wide))
         scaled_post = post_full * out_gain
         middle_grads.append(
             cotangent[span].astype(wide)
@@ -1244,16 +1254,27 @@
     forward_total = lax.all_gather(forward_piece, "dp", axis=0, tiled=True)
     early = halve(early, bits[2])
     step_total = step_grad * jax.nn.sigmoid(step_arg)
+    taps = conv_inner.shape[0]
     inner_pre_grad = act_grad * silu_slope(inner_pre)
-    inner_grad, conv_inner_sums = conv_rows_back(inner_pre_grad, inner, conv_inner, keeps)
+    conv_inner_sums = conv_sums(inner_pre_grad, inner, taps, keeps)
+    inner_bias_part = jnp.sum(inner_pre_grad, 0, keepdims=True)
     state_pre_grad = coef_grad * silu_slope(state_pre)
-    state_grad, conv_state_sums = conv_rows_back(state_pre_grad, state_in, conv_state, keeps)
+    conv_state_sums = conv_sums(state_pre_grad, state_in, taps, keeps)
+    state_bias_part = jnp.sum(state_pre_grad, 0, keepdims=True)
+    early, act_grad, coef_grad, *sums = tie(
+        early, act_grad, coef_grad, inner_bias_part, state_bias_part, *conv_inner_sums, *conv_state_sums
+    )
+    inner_bias_part, state_bias_part = sums[:2]
+    conv_inner_sums, conv_state_sums = sums[2 : 2 + taps], sums[2 + taps :]
+    early = halve(early, bits[3])
+    inner_grad = conv_grad(act_grad * silu_slope(inner_pre), conv_inner, keeps)
+    state_grad = conv_grad(coef_grad * silu_slope(state_pre), conv_state, keeps)
     scan_cat = jnp.concatenate(
         [inner_grad.astype(low), step_total.astype(low), state_grad.astype(low)], 1
     )
     scan_part = dot_tn(normed, scan_cat).astype(low)
     early, scan_part, attended_grad = tie(early, scan_part, attended_grad)
-    early = halve(early, bits[3])
+    early = double(early, bits[3])
     scan_part = halve(scan_part, bits[0])
     query_grad, keyval_grad = attend_back_call(
         queries, both, seg_row, aux, cosine, sine, logs, attended, attended_grad
@@ -1261,7 +1282,7 @@
     attend_cat = jnp.concatenate([query_grad, keyval_grad], 1)
     attend_part = dot_tn(normed, attend_cat).astype(low)
     early, scan_part, attend_part, attend_cat = tie(early, scan_part, attend_part, attend_cat)
-    early = double(early, bits[3])
+    early = double(early, bits[2])
     scan_part = halve(scan_part, bits[1])
     attend_part = halve(attend_part, bits[0])
     normed_part = dot_nt(jnp.concatenate([gating_grad, scan_cat, attend_cat], 1), weight_cat)
@@ -1272,7 +1293,7 @@
     normed_full = by_rows(pair_sum(by_rows(normed_part.astype(low))))
     own_rows = [
         *conv_inner_sums,
-        jnp.sum(inner_pre_grad, 0, keepdims=True),
+        inner_bias_part,
         mixer_gain_part,
         skip_sum,
         jnp.sum(step_total, 0, keepdims=True),
@@ -1282,24 +1303,24 @@
         input_gain_part,
         post_gain_part,
         *conv_state_sums,
-        jnp.sum(state_pre_grad, 0, keepdims=True),
+        state_bias_part,
     ]
     small = jnp.concatenate(
         [jnp.pad(row, ((0, 0), (0, model - row.shape[1]))) for row in own_rows + shared_rows], 0
     )
     small = small + swap_bit(small, bits[0])
-    early = double(early, bits[2])
+    early = double(early, bits[1])
     scan_part = halve(scan_part, bits[2])
     attend_part = halve(attend_part, bits[1])
-    early, scan_part, attend_part, small = tie(early, scan_part, attend_part, small)
-    early = double(early, bits[1])
+    scan_part, attend_part, small = tie(scan_part, attend_part, small)
     scan_part = halve(scan_part, bits[3])
     attend_part = halve(attend_part, bits[2])
     small = small + swap_bit(small, bits[1])
-    scan_part, attend_part, small = tie(scan_part, attend_part, small)
+    scan_part, attend_part, small, early = tie(scan_part, attend_part, small, early)
+    early = double(early, bits[0])
     attend_part = halve(attend_part, bits[3])
     small = small + swap_bit(small, bits[2])
-    attend_part, small, early, forward_total = tie(attend_part, small, early, forward_total)
+    attend_part, small, forward_total = tie(attend_part, small, forward_total)
     hidden_units = down_weight.shape[0]
     down_wgrad = forward_total[:hidden_units].astype(wide)
     gate_wgrad = forward_total[hidden_units : hidden_units + model].astype(wide)
@@ -1335,8 +1356,7 @@
     small = small + jnp.where(is_shared, small_other, 0.0)
     late, early, small = tie(late, early, small)
     late = double(late, bits[2])
-    early = double(early, bits[0])
-    late, early = tie(late, early)
+    (late,) = tie(late)
     late = double(late, bits[1])
     early_grads = (
         gate_wgrad,
@@ -1356,7 +1376,6 @@
     attend_total = late[:, state_at + state_cols :]
     gate_wgrad, up_wgrad, down_wgrad, attnout_grad, gating_wgrad, mixout_grad = early_grads
     count = len(own_rows)
-    taps = conv_inner.shape[0]
     return (
         tokens_grad,
         small[count],

time: 497 us -> 492 us (0.990)
  local copies, waits for them, and re-layouts: 46.2 us -> 34.2 us
  other arithmetic: 103 us -> 112 us
    ppermute x7 -> x3, waiting for transfers between devices: 64.9 us -> 13.3 us  [pair_sum(): other = lax.ppermute(value, 'tensor', [(0, 1), (1, 0)])]
    ppermute x0 -> x4, waiting for transfers between devices: none -> 48.9 us  [swap_pair(): return lax.ppermute(value, 'tensor', [(0, 1), (1, 0)])]
    pad x14, local copies, waits for them, and re-layouts: 9.02 us -> 0.77 us  [local_fast(): jnp.pad(row, ((0, 0), (0, model - row.shape[1])))]
    unnamed x205 -> x177, local copies, waits for them, and re-layouts: 17.3 us -> 15.5 us
  transfers between devices with their start and end apart: 35 -> 35, of which waited for: 21 -> 19; matrix products, arithmetic and copies ran while one was open for 28% -> 28% of each run, Pallas kernels for 13% -> 13%
where the time goes in v5:
time: 492 us; the launch traced here: 483 us
  waiting for transfers between devices  151 us (31%)
  other arithmetic  112 us (23%)
  Pallas kernels  74 us (15%)
  matrix products  64.1 us (13%)
  local copies, waits for them, and re-layouts  34.2 us (7%)
  starting transfers between devices  32 us (7%)
  between operations  15.7 us (3%)
    ppermute x24, waiting for transfers between devices, swap_bit(): return lax.ppermute(value, 'dp', [(i, i ^ bit) for i in range(size)])  85.4 us
    ppermute x4, waiting for transfers between devices, swap_pair(): return lax.ppermute(value, 'tensor', [(0, 1), (1, 0)])  48.9 us
    dot_general x12, matrix products, matmul(): return jnp.dot(left, right, preferred_element_type=jnp.float32)  29.7 us
    dot_general x9, matrix products, dot_nt(): lax.dot_general(left, right, (((1,), (1,)), ((), ())), preferred_element_...  25.5 us
    pallas_call x1, Pallas kernels, scan_back_call(): pl.pallas_call(scan_back_kernel, grid=(chunks,), in_specs=[by_chunk(LANES...  25.3 us
    ppermute x24, starting transfers between devices, swap_bit(): return lax.ppermute(value, 'dp', [(i, i ^ bit) for i in range(size)])  21.4 us
    unnamed x177, local copies, waits for them, and re-layouts  15.5 us
    ppermute x3, waiting for transfers between devices, pair_sum(): other = lax.ppermute(value, 'tensor', [(0, 1), (1, 0)])  13.3 us
  transfers between devices with their start and end apart: 35, of which 19 were waited for; matrix products, arithmetic and copies ran while one was open for 28% of the time, Pallas kernels for 13%

profile of v5, /device:TPU:0, one launch (start us, length us, event | category | flops | bytes accessed | tf_op | source)
XLA Modules:
  0.0 482.9 jit_solution(8886535879459051316)
XLA Ops:
  28.3 3.8 fusion.8
  32.1 12.9 %scan_forward.1 = (f32[1024,768]{1,0:T(8,128)}, bf16[4,128,768]{2,1,0:T(8,128)(2,1)}) custom-call(f32[1024,128]{1,0:T(8,128)} %get-tuple-element.352.step_ref, bf16[1024,256]{1,0:T(8,128)(2,1)} %get-tuple-element.283.coef_ref, f32[1024,768]{1,0:T(8,128)} %get-tuple-element.281.act_ref, f32[1024,128]{1,0:T(8,128)} %pad.127.seg_col_ref.aux_ref, ...), custom_call_target="tpu_custom_call" | custom-call | tf_op jit(solution)/shard_map/scan_forward/pallas_call | solution.py:673
  45.0 7.4 %multiply_reduce_fusion.9 = (f32[1024]{0:T(1024)S(1)}, f32[1024,768]{1,0:T(8,128)}, f32[1024,768]{1,0:T(8,128)}) fusion(f32[1024,768]{1,0:T(8,128)} %get-tuple-element.96, f32[1024,768]{1,0:T(8,128)S(1)} %get-tuple-element.282, f32[768]{0:T(1024)S(1)} %mul.806, bf16[1024,1024]{1,0:T(8,128)(2,1)} %copy-done.21, bf16[1024,768]{1,0:T(8,128)(2,1)S(1)} %copy-done.54), kind=kOutput, calls=%fused_computation.37 | convolution fusion | flops 1620835328 | bytes 16260096 | tf_op jit(solution)/shard_map/dot_general | solution.py:23
  52.4 2.9 collective-permute-start
  55.4 3.1 fusion.46
  58.5 3.4 fusion.75.query_ref
  64.1 3.2 fusion.42.keyval_ref
  69.1 11.0 %attend_forward.1 = (bf16[1024,256]{1,0:T(8,128)(2,1)}, bf16[1024,256]{1,0:T(8,128)(2,1)}, bf16[1024,256]{1,0:T(8,128)(2,1)}, f32[1024,128]{1,0:T(8,128)}) custom-call(f32[1024,256]{1,0:T(8,128)} %fusion.75.query_ref, f32[1024,128]{1,0:T(8,128)} %fusion.42.keyval_ref, f32[1,1024]{1,0:T(1,128)} %get-tuple-element.338.seg_ref, ...), custom_call_target="tpu_custom_call" | custom-call | tf_op jit(solution)/shard_map/attend_forward/pallas_call | solution.py:910
  87.0 4.5 convert_element_type.400
  92.3 7.8 %concatenate.80 = bf16[1024,2304]{1,0:T(8,128)(2,1)} concatenate(bf16[1024,768]{1,0:T(8,128)(2,1)} %param.31, bf16[1024,768]{1,0:T(8,128)(2,1)} %param.32, bf16[1024,128]{1,0:T(8,128)(2,1)} %pad.128.clone, bf16[1024,256]{1,0:T(8,128)(2,1)} %param.33, bf16[1024,256]{1,0:T(8,128)(2,1)} %param.28, bf16[1024,64]{1,0:T(8,128)(2,1)S(1)} %get-tuple-element.321, bf16[1024,64]{1,0:T(8,128)(2,1)} %copy-done.44), dimensions={1} | concatenate | bytes 9437184 | tf_op jit(solution)/shard_map/concatenate | solution.py:1184
  100.1 3.3 fusion.34
  105.6 7.0 %collective-permute-done.1 = bf16[512,1024]{1,0:T(8,128)(2,1)} collective-permute-done((bf16[512,1024]{1,0:T(8,128)(2,1)}, bf16[512,1024]{1,0:T(8,128)(2,1)}, u32[]{:S(2)}, u32[]{:S(2)}) %collective-permute-start.1) | collective-permute-done | bytes 1048608 | tf_op jit(solution)/shard_map/ppermute | solution.py:1023
  118.0 3.0 multiply_convert_fusion.4
  123.7 9.8 %collective-permute-done.2 = bf16[512,1024]{1,0:T(8,128)(2,1)S(1)} collective-permute-done((bf16[512,1024]{1,0:T(8,128)(2,1)S(1)}, bf16[512,1024]{1,0:T(8,128)(2,1)S(1)}, u32[]{:S(2)}, u32[]{:S(2)}) %collective-permute-start.2) | collective-permute-done | bytes 1048608 | tf_op jit(solution)/shard_map/ppermute | solution.py:1023
  135.6 21.6 %collective-permute-done.3 = bf16[512,1024]{1,0:T(8,128)(2,1)S(1)} collective-permute-done((bf16[512,1024]{1,0:T(8,128)(2,1)S(1)}, bf16[512,1024]{1,0:T(8,128)(2,1)S(1)}, u32[]{:S(2)}, u32[]{:S(2)}) %collective-permute-start.3) | collective-permute-done | bytes 1048608 | tf_op jit(solution)/shard_map/ppermute | solution.py:1023
  159.5 3.2 multiply_convert_fusion.3
  164.0 3.0 fusion.74
  167.6 11.7 %weight_products.1 = bf16[3,1024,1024]{2,1,0:T(8,128)(2,1)} custom-call(bf16[512,1024]{1,0:T(8,128)(2,1)} %get-tuple-element.291.refs_0_, bf16[512,1024]{1,0:T(8,128)(2,1)} %get-tuple-element.288.refs_1_, bf16[512,1024]{1,0:T(8,128)(2,1)} %copy-done.33, bf16[512,1024]{1,0:T(8,128)(2,1)} %copy-done.39, bf16[512,1024]{1,0:T(8,128)(2,1)} %copy-done.59, ...), custom_call_target="tpu_custom_call" | custom-call | tf_op jit(solution)/shard_map/weight_products/pallas_call | solution.py:1081
  179.4 10.6 %collective-permute-done.4 = bf16[512,1024]{1,0:T(8,128)(2,1)S(1)} collective-permute-done((bf16[512,1024]{1,0:T(8,128)(2,1)}, bf16[512,1024]{1,0:T(8,128)(2,1)S(1)}, u32[]{:S(2)}, u32[]{:S(2)}) %collective-permute-start.4) | collective-permute-done | bytes 1048608 | tf_op jit(solution)/shard_map/ppermute | solution.py:1023
  191.0 4.1 multiply_reduce_fusion.10
  196.6 4.8 fusion.65
  210.4 3.7 constant_dynamic-update-slice_fusion.6
  218.3 5.8 %fusion.23.grad_ref = f32[1024,768]{1,0:T(8,128)} fusion(f32[1024]{0:T(1024)S(1)} %add.361, f32[1024,768]{1,0:T(8,128)} %get-tuple-element.280, f32[1024,768]{1,0:T(8,128)} %copy-done.18, f32[1024]{0:T(1024)S(1)} %get-tuple-element.269, f32[768]{0:T(1024)S(1)} %convert_element_type.411, f32[1024]{0:T(1024)S(1)} %get-tuple-element.270, ...), kind=kLoop, calls=%fused_computation.94 | loop fusion | flops 8650752 | bytes 12598272 | tf_op jit(solution)/shard_map/mul | solution.py:1239
  230.1 3.2 convolution_convert_fusion.3.grad_ref
  233.3 25.3 %scan_backward.1 = (f32[1024,768]{1,0:T(8,128)}, f32[1024,128]{1,0:T(8,128)}, f32[1024,256]{1,0:T(8,128)}, f32[1,128]{1,0:T(1,128)}, f32[1,768]{1,0:T(1,128)}) custom-call(f32[1024,128]{1,0:T(8,128)} %get-tuple-element.352.step_ref, bf16[1024,256]{1,0:T(8,128)(2,1)} %get-tuple-element.283.coef_ref, f32[1024,768]{1,0:T(8,128)} %get-tuple-element.281.act_ref, ...), custom_call_target="tpu_custom_call" | custom-call | tf_op jit(solution)/shard_map/scan_backward/pallas_call | solution.py:815
  262.4 3.5 reduce-scatter.2.cloned.1.call-done
  265.9 9.0 %multiply_reduce_fusion.4 = (f32[768]{0:T(1024)S(1)}, f32[768]{0:T(1024)S(1)}, f32[768]{0:T(1024)S(1)}, f32[768]{0:T(1024)S(1)}, f32[768]{0:T(1024)S(1)}) fusion(f32[1024,768]{1,0:T(8,128)} %copy-done.15, f32[1024]{0:T(1024)S(1)} %bitcast.104, f32[1024]{0:T(1024)S(1)} %bitcast.98, f32[1024]{0:T(1024)S(1)} %bitcast.92, f32[1024,768]{1,0:T(8,128)} %get-tuple-element.111, ...), kind=kLoop, calls=%fused_computation.28 | loop fusion | flops 15724800 | bytes 9464832 | tf_op jit(solution)/shard_map/reduce_sum | solution.py:1045
  280.1 12.6 %collective-permute-done.8 = bf16[128,1792]{1,0:T(8,128)(2,1)S(1)} collective-permute-done((bf16[128,1792]{1,0:T(8,128)(2,1)S(1)}, bf16[128,1792]{1,0:T(8,128)(2,1)S(1)}, u32[]{:S(2)}, u32[]{:S(2)}) %collective-permute-start.8) | collective-permute-done | bytes 458784 | tf_op jit(solution)/shard_map/ppermute | solution.py:109
  295.5 2.5 constant_dynamic-update-slice_fusion.5
  300.7 3.3 convolution_convert_fusion
  304.2 5.2 %collective-permute-done.9 = bf16[64,1792]{1,0:T(8,128)(2,1)S(1)} collective-permute-done((bf16[64,1792]{1,0:T(8,128)(2,1)S(1)}, bf16[64,1792]{1,0:T(8,128)(2,1)S(1)}, u32[]{:S(2)}, u32[]{:S(2)}) %collective-permute-start.9) | collective-permute-done | bytes 229408 | tf_op jit(solution)/shard_map/ppermute | solution.py:109
  310.7 13.0 %attend_backward.1 = (bf16[1024,256]{1,0:T(8,128)(2,1)}, bf16[1024,128]{1,0:T(8,128)(2,1)}) custom-call(bf16[1024,256]{1,0:T(8,128)(2,1)} %get-tuple-element.116.query_ref, bf16[1024,256]{1,0:T(8,128)(2,1)} %get-tuple-element.117.both_ref, f32[1,1024]{1,0:T(1,128)} %get-tuple-element.338.seg_ref, f32[1024,128]{1,0:T(8,128)} %pad.127.seg_col_ref.aux_ref, ...), custom_call_target="tpu_custom_call" | custom-call | tf_op jit(solution)/shard_map/attend_backward/pallas_call | solution.py:974
  327.1 6.1 %collective-permute-done.10 = bf16[64,1792]{1,0:T(8,128)(2,1)S(1)} collective-permute-done((bf16[64,1792]{1,0:T(8,128)(2,1)S(1)}, bf16[64,1792]{1,0:T(8,128)(2,1)S(1)}, u32[]{:S(2)}, u32[]{:S(2)}) %collective-permute-start.10) | collective-permute-done | bytes 229408 | tf_op jit(solution)/shard_map/ppermute | solution.py:109
  336.4 8.7 %multiply_reduce_fusion.1 = (f32[1024]{0:T(1024)S(1)}, bf16[1024,1024]{1,0:T(8,128)(2,1)}) fusion(bf16[1024,1024]{1,0:T(8,128)(2,1)S(1)} %copy-done.2, f32[1024]{0:T(1024)S(1)} %copy-done.71, bf16[1024,2304]{1,0:T(8,128)(2,1)S(1)} %constant_dynamic-update-slice_fusion.2, bf16[1024,2304]{1,0:T(8,128)(2,1)} %concatenate.80), kind=kOutput, calls=%fused_computation.3 | convolution fusion | flops 4837080064 | bytes 13639680 | tf_op jit(solution)/shard_map/dot_general | solution.py:594
  345.2 10.8 %collective-permute-done.12 = bf16[128,1792]{1,0:T(8,128)(2,1)S(1)} collective-permute-done((bf16[128,1792]{1,0:T(8,128)(2,1)S(1)}, bf16[128,1792]{1,0:T(8,128)(2,1)S(1)}, u32[]{:S(2)}, u32[]{:S(2)}) %collective-permute-start.12) | collective-permute-done | bytes 458784 | tf_op jit(solution)/shard_map/ppermute | solution.py:109
  361.4 4.0 collective-permute-done.16
  369.5 2.6 collective-permute-start.18
  372.2 13.9 %collective-permute-done.20 = f32[16,1024]{1,0:T(8,128)S(1)} collective-permute-done((f32[16,1024]{1,0:T(8,128)S(1)}, f32[16,1024]{1,0:T(8,128)S(1)}, u32[]{:S(2)}, u32[]{:S(2)}) %collective-permute-start.20) | collective-permute-done | bytes 65568 | tf_op jit(solution)/shard_map/ppermute | solution.py:109
  390.7 3.0 collective-permute-done.22
  394.3 13.3 %collective-permute-done.31 = bf16[1024,1024]{1,0:T(8,128)(2,1)S(1)} collective-permute-done((bf16[1024,1024]{1,0:T(8,128)(2,1)}, bf16[1024,1024]{1,0:T(8,128)(2,1)S(1)}, u32[]{:S(2)}, u32[]{:S(2)}) %collective-permute-start.31) | collective-permute-done | bytes 2097184 | tf_op jit(solution)/shard_map/ppermute | solution.py:102
  408.9 3.5 maximum_add_fusion
  414.0 3.5 broadcast_select_fusion.1
  417.5 2.6 collective-permute-start.25
  425.2 2.6 collective-permute-start.26
  427.9 7.4 %collective-permute-done.26 = bf16[64,1664]{1,0:T(8,128)(2,1)S(1)} collective-permute-done((bf16[64,1664]{1,0:T(8,128)(2,1)S(1)}, bf16[64,1664]{1,0:T(8,128)(2,1)S(1)}, u32[]{:S(2)}, u32[]{:S(2)}) %collective-permute-start.26) | collective-permute-done | bytes 213024 | tf_op jit(solution)/shard_map/ppermute | solution.py:109
  435.4 5.1 %slice_convert_fusion = (f32[1024,1024]{1,0:T(8,128)}, f32[1024,1024]{1,0:T(8,128)}, f32[1024,1024]{1,0:T(8,128)}) fusion(bf16[3072,1024]{1,0:T(8,128)(2,1)S(1)} %copy-done.29), kind=kLoop, calls=%fused_computation.57 | loop fusion | flops 3145728 | bytes 18874368 | tf_op jit(solution)/shard_map/convert_element_type | solution.py:1325
  440.6 5.3 %collective-permute-done.29 = bf16[128,1664]{1,0:T(8,128)(2,1)S(1)} collective-permute-done((bf16[128,1664]{1,0:T(8,128)(2,1)S(1)}, bf16[128,1664]{1,0:T(8,128)(2,1)S(1)}, u32[]{:S(2)}, u32[]{:S(2)}) %collective-permute-start.29) | collective-permute-done | bytes 426016 | tf_op jit(solution)/shard_map/ppermute | solution.py:109
  453.0 12.0 %collective-permute-done.30 = bf16[256,1664]{1,0:T(8,128)(2,1)S(1)} collective-permute-done((bf16[256,1664]{1,0:T(8,128)(2,1)S(1)}, bf16[256,1664]{1,0:T(8,128)(2,1)S(1)}, u32[]{:S(2)}, u32[]{:S(2)}) %collective-permute-start.30) | collective-permute-done | bytes 852000 | tf_op jit(solution)/shard_map/ppermute | solution.py:109
  (396 shorter events, 133.4 us)
Async XLA Ops:
  7.2 110.8 %copy-start = (bf16[1024,1024]{1,0:T(8,128)(2,1)S(1)}, bf16[1024,1024]{1,0:T(8,128)(2,1)}, u32[]{:S(2)}) copy-start(bf16[1024,1024]{1,0:T(8,128)(2,1)} %param.46) | copy-start | bytes 6291460
  7.3 258.7 %reduce-scatter.2.cloned.1.call-start = ((), (), s32[]{:S(2)}) async-start(), calls=%async_computation.1 | async-start | bytes 6684672 | tf_op jit(solution)/shard_map/reduce_scatter | solution.py:1216
  32.1 12.9 %copy-start.3 = (f32[1024,768]{1,0:T(8,128)}, f32[1024,768]{1,0:T(8,128)S(1)}, u32[]{:S(2)}) copy-start(f32[1024,768]{1,0:T(8,128)S(1)} %get-tuple-element.282) | copy-start | bytes 9437188
  32.1 12.9 %copy-start.54 = (bf16[1024,768]{1,0:T(8,128)(2,1)S(1)}, bf16[1024,768]{1,0:T(8,128)(2,1)}, u32[]{:S(2)}) copy-start(bf16[1024,768]{1,0:T(8,128)(2,1)} %param.31) | copy-start | bytes 4718596
  52.4 27.7 %collective-permute-start = (f32[1024]{0:T(1024)S(1)}, f32[1024]{0:T(1024)S(1)}, u32[]{:S(2)}, u32[]{:S(2)}) collective-permute-start(f32[1024]{0:T(1024)S(1)} %get-tuple-element.279), channel_id=1, source_target_pairs={{0,1},{1,0},{2,3},{3,2},{4,5},{5,4},{6,7},{7,6},{8,9},{9,8},{10,11... | collective-permute-start | bytes 12296 | tf_op jit(solution)/shard_map/ppermute | solution.py:102
  86.1 26.4 %collective-permute-start.1 = (bf16[512,1024]{1,0:T(8,128)(2,1)}, bf16[512,1024]{1,0:T(8,128)(2,1)}, u32[]{:S(2)}, u32[]{:S(2)}) collective-permute-start(bf16[512,1024]{1,0:T(8,128)(2,1)} %get-tuple-element.307), channel_id=1, source_target_pairs={{0,1},{1,0},{2,3},{3,2},{4,5},{5,4},{6,7},{7,6},{8,9},{9,8},{10,11... | collective-permute-start | bytes 3145736 | tf_op jit(solution)/shard_map/ppermute | solution.py:1023
  103.5 29.9 %collective-permute-start.2 = (bf16[512,1024]{1,0:T(8,128)(2,1)S(1)}, bf16[512,1024]{1,0:T(8,128)(2,1)S(1)}, u32[]{:S(2)}, u32[]{:S(2)}) collective-permute-start(bf16[512,1024]{1,0:T(8,128)(2,1)S(1)} %copy-done.62), channel_id=1, source_target_pairs={{0,1},{1,0},{2,3},{3,2},{4,5},{5,4},{6,7},{7,6},{8,9},{9,8},{10,11... | collective-permute-start | bytes 3145736 | tf_op jit(solution)/shard_map/ppermute | solution.py:1023
  114.3 42.8 %copy-start.6 = (f32[512,1024]{1,0:T(8,128)}, f32[512,1024]{1,0:T(8,128)S(1)}, u32[]{:S(2)}) copy-start(f32[512,1024]{1,0:T(8,128)S(1)} %get-tuple-element.278) | copy-start | bytes 6291460
  123.6 33.5 %copy-start.19 = (bf16[512,1024]{1,0:T(8,128)(2,1)}, bf16[512,1024]{1,0:T(8,128)(2,1)S(1)}, u32[]{:S(2)}) copy-start(bf16[512,1024]{1,0:T(8,128)(2,1)S(1)} %get-tuple-element.98) | copy-start | bytes 3145732
  133.4 23.7 %collective-permute-start.3 = (bf16[512,1024]{1,0:T(8,128)(2,1)S(1)}, bf16[512,1024]{1,0:T(8,128)(2,1)S(1)}, u32[]{:S(2)}, u32[]{:S(2)}) collective-permute-start(bf16[512,1024]{1,0:T(8,128)(2,1)S(1)} %get-tuple-element.98), channel_id=1, source_target_pairs={{0,1},{1,0},{2,3},{3,2},{4,5},{5,4},{6,7},{7,6},{8,9},{9,8},{10,11... | collective-permute-start | bytes 3145736 | tf_op jit(solution)/shard_map/ppermute | solution.py:1023
  135.6 22.6 %copy-start.8 = (f32[512,1024]{1,0:T(8,128)}, f32[512,1024]{1,0:T(8,128)S(1)}, u32[]{:S(2)}) copy-start(f32[512,1024]{1,0:T(8,128)S(1)} %get-tuple-element.276) | copy-start | bytes 6291460
  167.0 23.0 %collective-permute-start.4 = (bf16[512,1024]{1,0:T(8,128)(2,1)}, bf16[512,1024]{1,0:T(8,128)(2,1)S(1)}, u32[]{:S(2)}, u32[]{:S(2)}) collective-permute-start(bf16[512,1024]{1,0:T(8,128)(2,1)} %get-tuple-element.357), channel_id=1, source_target_pairs={{0,1},{1,0},{2,3},{3,2},{4,5},{5,4},{6,7},{7,6},{8,9},{9,8},{10,11... | collective-permute-start | bytes 3145736 | tf_op jit(solution)/shard_map/ppermute | solution.py:1023
  179.4 233.1 %all-gather.2.cloned.1.call-start = ((), (), s32[]{:S(2)}) async-start(), calls=%async_computation.2 | async-start | bytes 6684672 | tf_op jit(solution)/shard_map/all_gather | solution.py:1254
  204.6 4.5 collective-permute-start.5
  218.3 5.8 %collective-permute-start.6 = (bf16[512,1792]{1,0:T(8,128)(2,1)}, bf16[512,1792]{1,0:T(8,128)(2,1)S(1)}, u32[]{:S(2)}, u32[]{:S(2)}) collective-permute-start(bf16[512,1792]{1,0:T(8,128)(2,1)} %pad_maximum_fusion.2), channel_id=1, source_target_pairs={{0,2},{2,0},{4,6},{6,4},{8,10},{10,8},{12,14},{14,12},{16,18},{18,... | collective-permute-start | bytes 5505032 | tf_op jit(solution)/shard_map/ppermute | solution.py:109
  228.3 31.7 %collective-permute-start.7 = (bf16[256,1792]{1,0:T(8,128)(2,1)}, bf16[256,1792]{1,0:T(8,128)(2,1)}, u32[]{:S(2)}, u32[]{:S(2)}) collective-permute-start(bf16[256,1792]{1,0:T(8,128)(2,1)} %broadcast_select_fusion.9), channel_id=1, source_target_pairs={{0,4},{2,6},{4,0},{6,2},{8,12},{10,14},{12,8},{14,10},{16,20},{18,... | collective-permute-start | bytes 2752520 | tf_op jit(solution)/shard_map/ppermute | solution.py:109
  275.0 17.9 %copy-start.16 = (f32[1024,768]{1,0:T(8,128)S(1)}, f32[1024,768]{1,0:T(8,128)}, u32[]{:S(2)}) copy-start(f32[1024,768]{1,0:T(8,128)} %get-tuple-element.111) | copy-start | bytes 9437188
  275.1 17.6 %collective-permute-start.8 = (bf16[128,1792]{1,0:T(8,128)(2,1)S(1)}, bf16[128,1792]{1,0:T(8,128)(2,1)S(1)}, u32[]{:S(2)}, u32[]{:S(2)}) collective-permute-start(bf16[128,1792]{1,0:T(8,128)(2,1)S(1)} %broadcast_select_fusion.17), channel_id=1, source_target_pairs={{0,8},{2,10},{4,12},{6,14},{8,0},{10,2},{12,4},{14,6},{16,24},{18,... | collective-permute-start | bytes 1376264 | tf_op jit(solution)/shard_map/ppermute | solution.py:109
  277.7 15.2 %copy-start.5 = (f32[1024,768]{1,0:T(8,128)S(1)}, f32[1024,768]{1,0:T(8,128)}, u32[]{:S(2)}) copy-start(f32[1024,768]{1,0:T(8,128)} %copy-done.3) | copy-start | bytes 9437188
  294.6 14.8 %collective-permute-start.9 = (bf16[64,1792]{1,0:T(8,128)(2,1)S(1)}, bf16[64,1792]{1,0:T(8,128)(2,1)S(1)}, u32[]{:S(2)}, u32[]{:S(2)}) collective-permute-start(bf16[64,1792]{1,0:T(8,128)(2,1)S(1)} %broadcast_select_fusion.24), channel_id=1, source_target_pairs={{0,16},{2,18},{4,20},{6,22},{8,24},{10,26},{12,28},{14,30},{16,0},... | collective-permute-start | bytes 688136 | tf_op jit(solution)/shard_map/ppermute | solution.py:109
  309.4 23.8 %collective-permute-start.10 = (bf16[64,1792]{1,0:T(8,128)(2,1)S(1)}, bf16[64,1792]{1,0:T(8,128)(2,1)S(1)}, u32[]{:S(2)}, u32[]{:S(2)}) collective-permute-start(bf16[64,1792]{1,0:T(8,128)(2,1)S(1)} %add_convert_fusion.8), channel_id=1, source_target_pairs={{0,16},{2,18},{4,20},{6,22},{8,24},{10,26},{12,28},{14,30},{16,0},... | collective-permute-start | bytes 688136 | tf_op jit(solution)/shard_map/ppermute | solution.py:109
  310.7 22.6 %collective-permute-start.11 = (bf16[512,1152]{1,0:T(8,128)(2,1)}, bf16[512,1152]{1,0:T(8,128)(2,1)S(1)}, u32[]{:S(2)}, u32[]{:S(2)}) collective-permute-start(bf16[512,1152]{1,0:T(8,128)(2,1)} %broadcast_select_fusion.4), channel_id=1, source_target_pairs={{0,2},{2,0},{4,6},{6,4},{8,10},{10,8},{12,14},{14,12},{16,18},{18,... | collective-permute-start | bytes 3538952 | tf_op jit(solution)/shard_map/ppermute | solution.py:109
  333.8 11.2 %collective-permute-start.14 = (bf16[512,384]{1,0:T(8,128)(2,1)S(1)}, bf16[512,384]{1,0:T(8,128)(2,1)S(1)}, u32[]{:S(2)}, u32[]{:S(2)}) collective-permute-start(bf16[512,384]{1,0:T(8,128)(2,1)S(1)} %broadcast_select_fusion.20), channel_id=1, source_target_pairs={{0,2},{2,0},{4,6},{6,4},{8,10},{10,8},{12,14},{14,12},{16,18},{18,... | collective-permute-start | bytes 1179656 | tf_op jit(solution)/shard_map/ppermute | solution.py:109
  333.9 22.1 %collective-permute-start.12 = (bf16[128,1792]{1,0:T(8,128)(2,1)S(1)}, bf16[128,1792]{1,0:T(8,128)(2,1)S(1)}, u32[]{:S(2)}, u32[]{:S(2)}) collective-permute-start(bf16[128,1792]{1,0:T(8,128)(2,1)S(1)} %pad_maximum_fusion.12), channel_id=1, source_target_pairs={{0,8},{2,10},{4,12},{6,14},{8,0},{10,2},{12,4},{14,6},{16,24},{18,... | collective-permute-start | bytes 1376264 | tf_op jit(solution)/shard_map/ppermute | solution.py:109
  334.3 22.8 %collective-permute-start.13 = (bf16[256,1152]{1,0:T(8,128)(2,1)S(1)}, bf16[256,1152]{1,0:T(8,128)(2,1)S(1)}, u32[]{:S(2)}, u32[]{:S(2)}) collective-permute-start(bf16[256,1152]{1,0:T(8,128)(2,1)S(1)} %broadcast_select_fusion.14), channel_id=1, source_target_pairs={{0,4},{2,6},{4,0},{6,2},{8,12},{10,14},{12,8},{14,10},{16,20},{18,... | collective-permute-start | bytes 1769480 | tf_op jit(solution)/shard_map/ppermute | solution.py:109
  357.5 3.8 collective-permute-start.17
  357.6 7.8 %collective-permute-start.16 = (bf16[256,384]{1,0:T(8,128)(2,1)S(1)}, bf16[256,384]{1,0:T(8,128)(2,1)S(1)}, u32[]{:S(2)}, u32[]{:S(2)}) collective-permute-start(bf16[256,384]{1,0:T(8,128)(2,1)S(1)} %broadcast_select_fusion.27), channel_id=1, source_target_pairs={{0,4},{2,6},{4,0},{6,2},{8,12},{10,14},{12,8},{14,10},{16,20},{18,... | collective-permute-start | bytes 589832 | tf_op jit(solution)/shard_map/ppermute | solution.py:109
  358.5 27.7 %copy-start.41 = (bf16[256,1792]{1,0:T(8,128)(2,1)S(1)}, bf16[256,1792]{1,0:T(8,128)(2,1)}, u32[]{:S(2)}) copy-start(bf16[256,1792]{1,0:T(8,128)(2,1)} %pad_maximum_fusion.5) | copy-start | bytes 2752516
  358.5 9.2 %collective-permute-start.15 = (bf16[128,1152]{1,0:T(8,128)(2,1)S(1)}, bf16[128,1152]{1,0:T(8,128)(2,1)S(1)}, u32[]{:S(2)}, u32[]{:S(2)}) collective-permute-start(bf16[128,1152]{1,0:T(8,128)(2,1)S(1)} %broadcast_select_fusion.21), channel_id=1, source_target_pairs={{0,8},{2,10},{4,12},{6,14},{8,0},{10,2},{12,4},{14,6},{16,24},{18,... | collective-permute-start | bytes 884744 | tf_op jit(solution)/shard_map/ppermute | solution.py:109
  358.6 27.6 %collective-permute-start.21 = (bf16[256,1792]{1,0:T(8,128)(2,1)}, bf16[256,1792]{1,0:T(8,128)(2,1)S(1)}, u32[]{:S(2)}, u32[]{:S(2)}) collective-permute-start(bf16[256,1792]{1,0:T(8,128)(2,1)} %pad_maximum_fusion.5), channel_id=1, source_target_pairs={{0,4},{2,6},{4,0},{6,2},{8,12},{10,14},{12,8},{14,10},{16,20},{18,... | collective-permute-start | bytes 2752520 | tf_op jit(solution)/shard_map/ppermute | solution.py:109
  359.9 47.7 %collective-permute-start.31 = (bf16[1024,1024]{1,0:T(8,128)(2,1)}, bf16[1024,1024]{1,0:T(8,128)(2,1)S(1)}, u32[]{:S(2)}, u32[]{:S(2)}) collective-permute-start(bf16[1024,1024]{1,0:T(8,128)(2,1)} %get-tuple-element.156), channel_id=1, source_target_pairs={{0,1},{1,0},{2,3},{3,2},{4,5},{5,4},{6,7},{7,6},{8,9},{9,8},{10,11... | collective-permute-start | bytes 6291464 | tf_op jit(solution)/shard_map/ppermute | solution.py:102
  367.9 18.2 %collective-permute-start.20 = (f32[16,1024]{1,0:T(8,128)S(1)}, f32[16,1024]{1,0:T(8,128)S(1)}, u32[]{:S(2)}, u32[]{:S(2)}) collective-permute-start(f32[16,1024]{1,0:T(8,128)S(1)} %add.383), channel_id=1, source_target_pairs={{0,4},{2,6},{4,0},{6,2},{8,12},{10,14},{12,8},{14,10},{16,20},{18,... | collective-permute-start | bytes 196616 | tf_op jit(solution)/shard_map/ppermute | solution.py:109
  369.2 16.9 %collective-permute-start.19 = (bf16[128,384]{1,0:T(8,128)(2,1)S(1)}, bf16[128,384]{1,0:T(8,128)(2,1)S(1)}, u32[]{:S(2)}, u32[]{:S(2)}) collective-permute-start(bf16[128,384]{1,0:T(8,128)(2,1)S(1)} %broadcast_select_fusion.29), channel_id=1, source_target_pairs={{0,8},{2,10},{4,12},{6,14},{8,0},{10,2},{12,4},{14,6},{16,24},{18,... | collective-permute-start | bytes 294920 | tf_op jit(solution)/shard_map/ppermute | solution.py:109
  369.5 16.6 %collective-permute-start.18 = (bf16[64,1152]{1,0:T(8,128)(2,1)S(1)}, bf16[64,1152]{1,0:T(8,128)(2,1)S(1)}, u32[]{:S(2)}, u32[]{:S(2)}) collective-permute-start(bf16[64,1152]{1,0:T(8,128)(2,1)S(1)} %broadcast_select_fusion.28), channel_id=1, source_target_pairs={{0,16},{2,18},{4,20},{6,22},{8,24},{10,26},{12,28},{14,30},{16,0},... | collective-permute-start | bytes 442376 | tf_op jit(solution)/shard_map/ppermute | solution.py:109
  386.4 21.2 %copy-start.27 = (bf16[1024,1024]{1,0:T(8,128)(2,1)S(1)}, bf16[1024,1024]{1,0:T(8,128)(2,1)}, u32[]{:S(2)}) copy-start(bf16[1024,1024]{1,0:T(8,128)(2,1)} %get-tuple-element.156) | copy-start | bytes 6291460
  386.4 21.2 %copy-start.69 = (f32[1024]{0:T(1024)S(1)}, f32[1024]{0:T(1024)}, u32[]{:S(2)}) copy-start(f32[1024]{0:T(1024)} %copy-done.68) | copy-start | bytes 12292
  387.7 26.2 %collective-permute-start.27 = (bf16[512,1792]{1,0:T(8,128)(2,1)}, bf16[512,1792]{1,0:T(8,128)(2,1)}, u32[]{:S(2)}, u32[]{:S(2)}) collective-permute-start(bf16[512,1792]{1,0:T(8,128)(2,1)} %pad_maximum_fusion.3), channel_id=1, source_target_pairs={{0,2},{2,0},{4,6},{6,4},{8,10},{10,8},{12,14},{14,12},{16,18},{18,... | collective-permute-start | bytes 5505032 | tf_op jit(solution)/shard_map/ppermute | solution.py:109
  387.8 5.9 %collective-permute-start.22 = (bf16[64,384]{1,0:T(8,128)(2,1)S(1)}, bf16[64,384]{1,0:T(8,128)(2,1)S(1)}, u32[]{:S(2)}, u32[]{:S(2)}) collective-permute-start(bf16[64,384]{1,0:T(8,128)(2,1)S(1)} %broadcast_select_fusion.30), channel_id=1, source_target_pairs={{0,16},{2,18},{4,20},{6,22},{8,24},{10,26},{12,28},{14,30},{16,0},... | collective-permute-start | bytes 147464 | tf_op jit(solution)/shard_map/ppermute | solution.py:109
  388.2 6.0 %collective-permute-start.23 = (f32[16,1024]{1,0:T(8,128)S(1)}, f32[16,1024]{1,0:T(8,128)S(1)}, u32[]{:S(2)}, u32[]{:S(2)}) collective-permute-start(f32[16,1024]{1,0:T(8,128)S(1)} %add.386), channel_id=1, source_target_pairs={{0,8},{2,10},{4,12},{6,14},{8,0},{10,2},{12,4},{14,6},{16,24},{18,... | collective-permute-start | bytes 196616 | tf_op jit(solution)/shard_map/ppermute | solution.py:109
  394.2 14.6 %copy-start.25 = (f32[512,1024]{1,0:T(8,128)S(1)}, f32[512,1024]{1,0:T(8,128)}, u32[]{:S(2)}) copy-start(f32[512,1024]{1,0:T(8,128)} %get-tuple-element.272) | copy-start | bytes 6291460
  394.3 14.6 %copy-start.26 = (f32[512,1024]{1,0:T(8,128)S(1)}, f32[512,1024]{1,0:T(8,128)}, u32[]{:S(2)}) copy-start(f32[512,1024]{1,0:T(8,128)} %get-tuple-element.304) | copy-start | bytes 6291460
  412.5 7.6 %collective-permute-start.24 = (bf16[64,384]{1,0:T(8,128)(2,1)S(1)}, bf16[64,384]{1,0:T(8,128)(2,1)S(1)}, u32[]{:S(2)}, u32[]{:S(2)}) collective-permute-start(bf16[64,384]{1,0:T(8,128)(2,1)S(1)} %pad_maximum_fusion.15), channel_id=1, source_target_pairs={{0,1},{1,0},{2,3},{3,2},{4,5},{5,4},{6,7},{7,6},{8,9},{9,8},{10,11... | collective-permute-start | bytes 147464 | tf_op jit(solution)/shard_map/ppermute | solution.py:1332
  417.5 5.2 %collective-permute-start.25 = (f32[16,1024]{1,0:T(8,128)S(1)}, f32[16,1024]{1,0:T(8,128)S(1)}, u32[]{:S(2)}, u32[]{:S(2)}) collective-permute-start(f32[16,1024]{1,0:T(8,128)S(1)} %add.388), channel_id=1, source_target_pairs={{0,16},{2,18},{4,20},{6,22},{8,24},{10,26},{12,28},{14,30},{16,0},... | collective-permute-start | bytes 196616 | tf_op jit(solution)/shard_map/ppermute | solution.py:109
  422.7 5.1 %collective-permute-start.28 = (f32[16,1024]{1,0:T(8,128)S(1)}, f32[16,1024]{1,0:T(8,128)S(1)}, u32[]{:S(2)}, u32[]{:S(2)}) collective-permute-start(f32[16,1024]{1,0:T(8,128)S(1)} %add.390), channel_id=1, source_target_pairs={{0,1},{1,0},{2,3},{3,2},{4,5},{5,4},{6,7},{7,6},{8,9},{9,8},{10,11... | collective-permute-start | bytes 196616 | tf_op jit(solution)/shard_map/ppermute | solution.py:1354
  425.2 10.0 %collective-permute-start.26 = (bf16[64,1664]{1,0:T(8,128)(2,1)S(1)}, bf16[64,1664]{1,0:T(8,128)(2,1)S(1)}, u32[]{:S(2)}, u32[]{:S(2)}) collective-permute-start(bf16[64,1664]{1,0:T(8,128)(2,1)S(1)} %concatenate.92), channel_id=1, source_target_pairs={{0,16},{2,18},{4,20},{6,22},{8,24},{10,26},{12,28},{14,30},{16,0},... | collective-permute-start | bytes 638984 | tf_op jit(solution)/shard_map/ppermute | solution.py:109
  435.3 10.5 %collective-permute-start.29 = (bf16[128,1664]{1,0:T(8,128)(2,1)S(1)}, bf16[128,1664]{1,0:T(8,128)(2,1)S(1)}, u32[]{:S(2)}, u32[]{:S(2)}) collective-permute-start(bf16[128,1664]{1,0:T(8,128)(2,1)S(1)} %pad_maximum_fusion.13), channel_id=1, source_target_pairs={{0,8},{2,10},{4,12},{6,14},{8,0},{10,2},{12,4},{14,6},{16,24},{18,... | collective-permute-start | bytes 1277960 | tf_op jit(solution)/shard_map/ppermute | solution.py:109
  446.0 19.0 %collective-permute-start.30 = (bf16[256,1664]{1,0:T(8,128)(2,1)S(1)}, bf16[256,1664]{1,0:T(8,128)(2,1)S(1)}, u32[]{:S(2)}, u32[]{:S(2)}) collective-permute-start(bf16[256,1664]{1,0:T(8,128)(2,1)S(1)} %pad_maximum_fusion.6), channel_id=1, source_target_pairs={{0,4},{2,6},{4,0},{6,2},{8,12},{10,14},{12,8},{14,10},{16,20},{18,... | collective-permute-start | bytes 2555912 | tf_op jit(solution)/shard_map/ppermute | solution.py:109
  465.3 4.3 collective-permute-start.32
  (73 other events, 331.6 us)
Sparse Core Ops, SparseCore 0:
  179.5 86.4 reduce-scatter.1
  275.1 76.6 all-gather.1

commit v6 on v5

--- a/solution.py
+++ b/solution.py
@@ -1203,6 +1203,8 @@
         post_low = by_rows(post_part.astype(low))
         if at == 0:
             got[1], post_low = tie(got[1], post_low)
+        else:
+            got[0], post_low = tie(got[0], post_low)
         post_got = swap_pair(post_low)
         found.append(
             (post_low, unit_second, inv_second, gain_part, hidden, post, gate_act_grad, up_act_grad)
@@ -1290,7 +1292,9 @@
     early, scan_part, attend_part, normed_part, input_gain_part = tie(
         early, scan_part, attend_part, normed_part, input_gain_part
     )
-    normed_full = by_rows(pair_sum(by_rows(normed_part.astype(low))))
+    normed_low = by_rows(normed_part.astype(low))
+    quarter = rows // 4
+    normed_first = swap_pair(normed_low[:quarter])
     own_rows = [
         *conv_inner_sums,
         inner_bias_part,
@@ -1312,24 +1316,26 @@
     early = double(early, bits[1])
     scan_part = halve(scan_part, bits[2])
     attend_part = halve(attend_part, bits[1])
-    scan_part, attend_part, small = tie(scan_part, attend_part, small)
+    scan_part, attend_part, small, normed_first, normed_low = tie(
+        scan_part, attend_part, small, normed_first, normed_low
+    )
+    normed_second = swap_pair(normed_low[quarter:half])
     scan_part = halve(scan_part, bits[3])
     attend_part = halve(attend_part, bits[2])
     small = small + swap_bit(small, bits[1])
-    scan_part, attend_part, small, early = tie(scan_part, attend_part, small, early)
-    early = double(early, bits[0])
+    scan_part, attend_part, small, normed_second = tie(
+        scan_part, attend_part, small, normed_second
+    )
     attend_part = halve(attend_part, bits[3])
     small = small + swap_bit(small, bits[2])
-    attend_part, small, forward_total = tie(attend_part, small, forward_total)
-    hidden_units = down_weight.shape[0]
-    down_wgrad = forward_total[:hidden_units].astype(wide)
-    gate_wgrad = forward_total[hidden_units : hidden_units + model].astype(wide)
-    up_wgrad = forward_total[hidden_units + model :].astype(wide)
+    attend_part, small, early = tie(attend_part, small, early)
     small = small + swap_bit(small, bits[3])
     scan_piece, attend_piece = scan_part, attend_part
     state_at = ssm_width + LANES
     trade = jnp.concatenate([scan_piece[:, state_at:], attend_piece[:, query_width:]], 1)
-    other = lax.ppermute(trade, "tensor", [(0, 1), (1, 0)])
+    other = swap_pair(trade)
+    other, normed_rest = tie(other, normed_low[half:])
+    normed_got = [normed_first, normed_second, swap_pair(normed_rest)]
     state_cols = state_weight.shape[1]
     state_piece = (
         trade[:, :state_cols].astype(wide) + other[:, :state_cols].astype(wide)
@@ -1349,14 +1355,19 @@
         ],
         1,
     )
-    late, small = tie(late, small)
+    late, small, early = tie(late, small, early)
+    early = double(early, bits[0])
     late = double(late, bits[3])
     small_other = lax.ppermute(small, "tensor", [(0, 1), (1, 0)])
     is_shared = lax.broadcasted_iota(jnp.int32, small.shape, 0) >= len(own_rows)
     small = small + jnp.where(is_shared, small_other, 0.0)
     late, early, small = tie(late, early, small)
     late = double(late, bits[2])
-    (late,) = tie(late)
+    late, forward_total = tie(late, forward_total)
+    hidden_units = down_weight.shape[0]
+    down_wgrad = forward_total[:hidden_units].astype(wide)
+    gate_wgrad = forward_total[hidden_units : hidden_units + model].astype(wide)
+    up_wgrad = forward_total[hidden_units + model :].astype(wide)
     late = double(late, bits[1])
     early_grads = (
         gate_wgrad,
@@ -1366,6 +1377,7 @@
         early[:, model:].astype(wide),
         early[query_width:, :model].astype(wide),
     )
+    normed_full = by_rows(normed_low.astype(wide) + jnp.concatenate(normed_got, 0).astype(wide))
     scaled_in = normed_full * in_gain
     tokens_grad = middle_grad + inv_first * (
         scaled_in - unit_first * jnp.mean(scaled_in * unit_first, -1, keepdims=True)

time: 492 us -> 484 us (0.984)
  waiting for transfers between devices: 151 us -> 127 us
  other arithmetic: 112 us -> 121 us
    ppermute x24, waiting for transfers between devices: 85.4 us -> 56.8 us  [swap_bit(): return lax.ppermute(value, 'dp', [(i, i ^ bit) for i in range(size)])]
    ppermute x1, waiting for transfers between devices: 0.01 us -> 17.3 us  [local_fast(): small_other = lax.ppermute(small, 'tensor', [(0, 1), (1, 0)])]
    ppermute x3 -> x2, waiting for transfers between devices: 13.3 us -> 0.01 us  [pair_sum(): other = lax.ppermute(value, 'tensor', [(0, 1), (1, 0)])]
    ppermute x4 -> x8, starting transfers between devices: 3 us -> 8.48 us  [swap_pair(): return lax.ppermute(value, 'tensor', [(0, 1), (1, 0)])]
    unnamed x177 -> x179, local copies, waits for them, and re-layouts: 15.5 us -> 14.7 us
    ppermute x4 -> x8, waiting for transfers between devices: 48.9 us -> 49.2 us  [swap_pair(): return lax.ppermute(value, 'tensor', [(0, 1), (1, 0)])]
  transfers between devices with their start and end apart: 35 -> 37, of which waited for: 19 -> 20; matrix products, arithmetic and copies ran while one was open for 28% -> 34% of each run, Pallas kernels for 13% -> 13%
where the time goes in v6:
time: 484 us; the launch traced here: 474 us
  waiting for transfers between devices  127 us (26%)
  other arithmetic  121 us (25%)
  Pallas kernels  73.8 us (15%)
  matrix products  65.7 us (14%)
  local copies, waits for them, and re-layouts  38.6 us (8%)
  starting transfers between devices  32.2 us (7%)
  between operations  16.1 us (3%)
    ppermute x24, waiting for transfers between devices, swap_bit(): return lax.ppermute(value, 'dp', [(i, i ^ bit) for i in range(size)])  56.8 us
    ppermute x8, waiting for transfers between devices, swap_pair(): return lax.ppermute(value, 'tensor', [(0, 1), (1, 0)])  49.2 us
    dot_general x12, matrix products, matmul(): return jnp.dot(left, right, preferred_element_type=jnp.float32)  29.6 us
    dot_general x9, matrix products, dot_nt(): lax.dot_general(left, right, (((1,), (1,)), ((), ())), preferred_element_...  27.2 us
    pallas_call x1, Pallas kernels, scan_back_call(): pl.pallas_call(scan_back_kernel, grid=(chunks,), in_specs=[by_chunk(LANES...  25.3 us
    ppermute x24, starting transfers between devices, swap_bit(): return lax.ppermute(value, 'dp', [(i, i ^ bit) for i in range(size)])  18.8 us
    ppermute x1, waiting for transfers between devices, local_fast(): small_other = lax.ppermute(small, 'tensor', [(0, 1), (1, 0)])  17.3 us
    unnamed x179, local copies, waits for them, and re-layouts  14.7 us
  transfers between devices with their start and end apart: 37, of which 20 were waited for; matrix products, arithmetic and copies ran while one was open for 34% of the time, Pallas kernels for 13%

profile of v6, /device:TPU:0, one launch (start us, length us, event | category | flops | bytes accessed | tf_op | source)
XLA Modules:
  0.0 474.4 jit_solution(5100849755899342425)
XLA Ops:
  31.2 3.8 fusion.8
  35.0 12.9 %scan_forward.1 = (f32[1024,768]{1,0:T(8,128)}, bf16[4,128,768]{2,1,0:T(8,128)(2,1)}) custom-call(f32[1024,128]{1,0:T(8,128)} %get-tuple-element.371.step_ref, bf16[1024,256]{1,0:T(8,128)(2,1)} %get-tuple-element.301.coef_ref, f32[1024,768]{1,0:T(8,128)} %get-tuple-element.299.act_ref, f32[1024,128]{1,0:T(8,128)} %pad.127.seg_col_ref.aux_ref, ...), custom_call_target="tpu_custom_call" | custom-call | tf_op jit(solution)/shard_map/scan_forward/pallas_call | solution.py:673
  47.9 7.4 %multiply_reduce_fusion.9 = (f32[1024]{0:T(1024)S(1)}, f32[1024,768]{1,0:T(8,128)}, f32[1024,768]{1,0:T(8,128)}) fusion(f32[1024,768]{1,0:T(8,128)} %get-tuple-element.105, f32[1024,768]{1,0:T(8,128)S(1)} %get-tuple-element.300, f32[768]{0:T(1024)S(1)} %mul.806, bf16[1024,1024]{1,0:T(8,128)(2,1)} %copy-done.24, bf16[1024,768]{1,0:T(8,128)(2,1)S(1)} %copy-done.60), kind=kOutput, calls=%fused_computation.37 | convolution fusion | flops 1620835328 | bytes 16260096 | tf_op jit(solution)/shard_map/dot_general | solution.py:23
  55.3 2.9 collective-permute-start
  58.3 3.1 fusion.46
  61.4 3.4 fusion.75.query_ref
  66.3 3.3 fusion.42.keyval_ref
  71.5 10.8 %attend_forward.1 = (bf16[1024,256]{1,0:T(8,128)(2,1)}, bf16[1024,256]{1,0:T(8,128)(2,1)}, bf16[1024,256]{1,0:T(8,128)(2,1)}, f32[1024,128]{1,0:T(8,128)}) custom-call(f32[1024,256]{1,0:T(8,128)} %fusion.75.query_ref, f32[1024,128]{1,0:T(8,128)} %fusion.42.keyval_ref, f32[1,1024]{1,0:T(1,128)} %get-tuple-element.357.seg_ref, ...), custom_call_target="tpu_custom_call" | custom-call | tf_op jit(solution)/shard_map/attend_forward/pallas_call | solution.py:910
  90.0 4.6 convert_element_type.400
  95.3 7.8 %concatenate.83 = bf16[1024,2304]{1,0:T(8,128)(2,1)} concatenate(bf16[1024,768]{1,0:T(8,128)(2,1)} %param.31, bf16[1024,768]{1,0:T(8,128)(2,1)} %param.32, bf16[1024,128]{1,0:T(8,128)(2,1)} %pad.128.clone, bf16[1024,256]{1,0:T(8,128)(2,1)} %param.33, bf16[1024,256]{1,0:T(8,128)(2,1)} %param.28, bf16[1024,64]{1,0:T(8,128)(2,1)S(1)} %get-tuple-element.339, bf16[1024,64]{1,0:T(8,128)(2,1)} %copy-done.46), dimensions={1} | concatenate | bytes 9437184 | tf_op jit(solution)/shard_map/concatenate | solution.py:1184
  103.2 3.3 fusion.32
  110.0 5.5 %collective-permute-done.1 = bf16[512,1024]{1,0:T(8,128)(2,1)} collective-permute-done((bf16[512,1024]{1,0:T(8,128)(2,1)}, bf16[512,1024]{1,0:T(8,128)(2,1)}, u32[]{:S(2)}, u32[]{:S(2)}) %collective-permute-start.1) | collective-permute-done | bytes 1048608 | tf_op jit(solution)/shard_map/ppermute | solution.py:1023
  120.9 3.0 multiply_convert_fusion.4
  125.3 2.6 fusion.73
  127.9 8.5 %collective-permute-done.2 = bf16[512,1024]{1,0:T(8,128)(2,1)S(1)} collective-permute-done((bf16[512,1024]{1,0:T(8,128)(2,1)S(1)}, bf16[512,1024]{1,0:T(8,128)(2,1)S(1)}, u32[]{:S(2)}, u32[]{:S(2)}) %collective-permute-start.2) | collective-permute-done | bytes 1048608 | tf_op jit(solution)/shard_map/ppermute | solution.py:1023
  138.8 3.0 multiply_convert_fusion.3
  143.4 3.1 fusion.74
  146.4 14.3 %collective-permute-done.3 = bf16[512,1024]{1,0:T(8,128)(2,1)S(1)} collective-permute-done((bf16[512,1024]{1,0:T(8,128)(2,1)S(1)}, bf16[512,1024]{1,0:T(8,128)(2,1)S(1)}, u32[]{:S(2)}, u32[]{:S(2)}) %collective-permute-start.3) | collective-permute-done | bytes 1048608 | tf_op jit(solution)/shard_map/ppermute | solution.py:1023
  162.3 11.8 %weight_products.1 = bf16[3,1024,1024]{2,1,0:T(8,128)(2,1)} custom-call(bf16[512,1024]{1,0:T(8,128)(2,1)} %get-tuple-element.309.refs_0_, bf16[512,1024]{1,0:T(8,128)(2,1)} %get-tuple-element.306.refs_1_, bf16[512,1024]{1,0:T(8,128)(2,1)} %copy-done.38, bf16[512,1024]{1,0:T(8,128)(2,1)} %copy-done.39, bf16[512,1024]{1,0:T(8,128)(2,1)} %copy-done.65, ...), custom_call_target="tpu_custom_call" | custom-call | tf_op jit(solution)/shard_map/weight_products/pallas_call | solution.py:1081
  174.1 10.7 %collective-permute-done.4 = bf16[512,1024]{1,0:T(8,128)(2,1)} collective-permute-done((bf16[512,1024]{1,0:T(8,128)(2,1)}, bf16[512,1024]{1,0:T(8,128)(2,1)}, u32[]{:S(2)}, u32[]{:S(2)}) %collective-permute-start.4) | collective-permute-done | bytes 1048608 | tf_op jit(solution)/shard_map/ppermute | solution.py:1023
  184.8 6.4 %multiply_reduce_fusion.11 = (f32[1024]{0:T(1024)S(1)}, f32[512]{0:T(512)S(1)}, f32[512]{0:T(512)S(1)}, f32[1024]{0:T(1024)S(1)}) fusion(f32[512,1024]{1,0:T(8,128)} %get-tuple-element.375, f32[512,1024]{1,0:T(8,128)S(1)} %copy-done.7, f32[512]{0:T(512)S(1)} %add_rsqrt_fusion.3, f32[1024]{0:T(1024)S(1)} %convert_element_type.417, ...), kind=kLoop, calls=%fused_computation.62 | loop fusion | flops 9434112 | bytes 12603392 | tf_op jit(solution)/shard_map/reduce_sum | solution.py:1202
  191.9 4.4 fusion.65
  204.4 3.7 constant_dynamic-update-slice_fusion.6
  212.3 5.8 %fusion.23.grad_ref = f32[1024,768]{1,0:T(8,128)} fusion(f32[1024]{0:T(1024)S(1)} %add.361, f32[1024,768]{1,0:T(8,128)} %get-tuple-element.298, f32[1024,768]{1,0:T(8,128)} %copy-done.21, f32[1024]{0:T(1024)S(1)} %get-tuple-element.287, f32[768]{0:T(1024)S(1)} %convert_element_type.411, f32[1024]{0:T(1024)S(1)} %get-tuple-element.288, ...), kind=kLoop, calls=%fused_computation.95 | loop fusion | flops 8650752 | bytes 12598272 | tf_op jit(solution)/shard_map/mul | solution.py:1241
  224.3 3.2 convolution_convert_fusion.3.grad_ref
  227.5 25.3 %scan_backward.1 = (f32[1024,768]{1,0:T(8,128)}, f32[1024,128]{1,0:T(8,128)}, f32[1024,256]{1,0:T(8,128)}, f32[1,128]{1,0:T(1,128)}, f32[1,768]{1,0:T(1,128)}) custom-call(f32[1024,128]{1,0:T(8,128)} %get-tuple-element.371.step_ref, bf16[1024,256]{1,0:T(8,128)(2,1)} %get-tuple-element.301.coef_ref, f32[1024,768]{1,0:T(8,128)} %get-tuple-element.299.act_ref, ...), custom_call_target="tpu_custom_call" | custom-call | tf_op jit(solution)/shard_map/scan_backward/pallas_call | solution.py:815
  254.1 2.4 add_convert_fusion.3
  256.6 4.1 reduce-scatter.2.cloned.1.call-done
  260.6 9.0 %multiply_reduce_fusion.4 = (f32[768]{0:T(1024)S(1)}, f32[768]{0:T(1024)S(1)}, f32[768]{0:T(1024)S(1)}, f32[768]{0:T(1024)S(1)}, f32[768]{0:T(1024)S(1)}) fusion(f32[1024,768]{1,0:T(8,128)} %copy-done.18, f32[1024]{0:T(1024)S(1)} %bitcast.104, f32[1024]{0:T(1024)S(1)} %bitcast.98, f32[1024]{0:T(1024)S(1)} %bitcast.92, f32[1024,768]{1,0:T(8,128)} %get-tuple-element.122, ...), kind=kLoop, calls=%fused_computation.28 | loop fusion | flops 15724800 | bytes 9464832 | tf_op jit(solution)/shard_map/reduce_sum | solution.py:1045
  274.8 12.6 %collective-permute-done.8 = bf16[128,1792]{1,0:T(8,128)(2,1)S(1)} collective-permute-done((bf16[128,1792]{1,0:T(8,128)(2,1)S(1)}, bf16[128,1792]{1,0:T(8,128)(2,1)S(1)}, u32[]{:S(2)}, u32[]{:S(2)}) %collective-permute-start.8) | collective-permute-done | bytes 458784 | tf_op jit(solution)/shard_map/ppermute | solution.py:109
  290.2 2.6 constant_dynamic-update-slice_fusion.5
  295.4 3.3 convolution_convert_fusion
  298.9 5.1 %collective-permute-done.9 = bf16[64,1792]{1,0:T(8,128)(2,1)S(1)} collective-permute-done((bf16[64,1792]{1,0:T(8,128)(2,1)S(1)}, bf16[64,1792]{1,0:T(8,128)(2,1)S(1)}, u32[]{:S(2)}, u32[]{:S(2)}) %collective-permute-start.9) | collective-permute-done | bytes 229408 | tf_op jit(solution)/shard_map/ppermute | solution.py:109
  305.4 13.0 %attend_backward.1 = (bf16[1024,256]{1,0:T(8,128)(2,1)}, bf16[1024,128]{1,0:T(8,128)(2,1)}) custom-call(bf16[1024,256]{1,0:T(8,128)(2,1)} %get-tuple-element.127.query_ref, bf16[1024,256]{1,0:T(8,128)(2,1)} %get-tuple-element.128.both_ref, f32[1,1024]{1,0:T(1,128)} %get-tuple-element.357.seg_ref, f32[1024,128]{1,0:T(8,128)} %pad.127.seg_col_ref.aux_ref, ...), custom_call_target="tpu_custom_call" | custom-call | tf_op jit(solution)/shard_map/attend_backward/pallas_call | solution.py:974
  321.8 6.0 %collective-permute-done.10 = bf16[64,1792]{1,0:T(8,128)(2,1)S(1)} collective-permute-done((bf16[64,1792]{1,0:T(8,128)(2,1)S(1)}, bf16[64,1792]{1,0:T(8,128)(2,1)S(1)}, u32[]{:S(2)}, u32[]{:S(2)}) %collective-permute-start.10) | collective-permute-done | bytes 229408 | tf_op jit(solution)/shard_map/ppermute | solution.py:109
  328.6 2.5 collective-permute-start.13
  331.3 8.7 %multiply_reduce_fusion.1 = (f32[1024]{0:T(1024)S(1)}, bf16[1024,1024]{1,0:T(8,128)(2,1)}) fusion(bf16[1024,1024]{1,0:T(8,128)(2,1)S(1)} %copy-done.2, f32[1024]{0:T(1024)S(1)} %copy-done.74, bf16[1024,2304]{1,0:T(8,128)(2,1)S(1)} %constant_dynamic-update-slice_fusion.2, bf16[1024,2304]{1,0:T(8,128)(2,1)} %concatenate.83), kind=kOutput, calls=%fused_computation.3 | convolution fusion | flops 4837080064 | bytes 13639680 | tf_op jit(solution)/shard_map/dot_general | solution.py:594
  340.2 10.7 %collective-permute-done.12 = bf16[128,1792]{1,0:T(8,128)(2,1)S(1)} collective-permute-done((bf16[128,1792]{1,0:T(8,128)(2,1)S(1)}, bf16[128,1792]{1,0:T(8,128)(2,1)S(1)}, u32[]{:S(2)}, u32[]{:S(2)}) %collective-permute-start.12) | collective-permute-done | bytes 458784 | tf_op jit(solution)/shard_map/ppermute | solution.py:109
  357.3 2.9 collective-permute-done.16
  362.8 6.0 %collective-permute-done.18 = bf16[256,1024]{1,0:T(8,128)(2,1)S(1)} collective-permute-done((bf16[256,1024]{1,0:T(8,128)(2,1)S(1)}, bf16[256,1024]{1,0:T(8,128)(2,1)S(1)}, u32[]{:S(2)}, u32[]{:S(2)}) %collective-permute-start.18) | collective-permute-done | bytes 524320 | tf_op jit(solution)/shard_map/ppermute | solution.py:1023
  374.7 6.2 %collective-permute-done.21 = f32[16,1024]{1,0:T(8,128)S(1)} collective-permute-done((f32[16,1024]{1,0:T(8,128)S(1)}, f32[16,1024]{1,0:T(8,128)S(1)}, u32[]{:S(2)}, u32[]{:S(2)}) %collective-permute-start.21) | collective-permute-done | bytes 65568 | tf_op jit(solution)/shard_map/ppermute | solution.py:109
  381.2 4.2 collective-permute-done.22
  405.5 17.3 %collective-permute-done.30 = f32[16,1024]{1,0:T(8,128)S(1)} collective-permute-done((f32[16,1024]{1,0:T(8,128)S(1)}, f32[16,1024]{1,0:T(8,128)S(1)}, u32[]{:S(2)}, u32[]{:S(2)}) %collective-permute-start.30) | collective-permute-done | bytes 65568 | tf_op jit(solution)/shard_map/ppermute | solution.py:1361
  423.0 2.6 multiply_reduce_fusion
  425.8 7.0 %maximum_add_fusion = f32[1024,1024]{1,0:T(8,128)} fusion(f32[512,1024]{1,0:T(8,128)S(1)} %copy-done.30, f32[512,1024]{1,0:T(8,128)S(1)} %copy-done.29, bf16[1024,1024]{1,0:T(8,128)(2,1)S(1)} %copy-done.15, bf16[1024,1024]{1,0:T(8,128)(2,1)S(1)} %copy-done.2, f32[1024]{0:T(1024)S(1)} %broadcast_multiply_fusion.6, f32[1024]{0:T(1024)S(1)} %copy-done.72, ...), kind=kLoop, calls=%fused_computation | loop fusion | flops 16777216 | bytes 14692352 | tf_op jit(solution)/shard_map/add | solution.py:1382
  438.3 3.1 collective-permute-done.31
  444.9 8.0 %slice_convert_fusion = (f32[1024,1024]{1,0:T(8,128)}, f32[1024,1024]{1,0:T(8,128)}, f32[1024,1024]{1,0:T(8,128)}) fusion(bf16[3072,1024]{1,0:T(8,128)(2,1)} %all-gather.2.cloned.1.call-done), kind=kLoop, calls=%fused_computation.58 | loop fusion | flops 3145728 | bytes 18874368 | tf_op jit(solution)/shard_map/convert_element_type | solution.py:1368
  452.9 3.4 collective-permute-done.32
  (403 shorter events, 142.8 us)
Async XLA Ops:
  7.2 113.8 %copy-start = (bf16[1024,1024]{1,0:T(8,128)(2,1)S(1)}, bf16[1024,1024]{1,0:T(8,128)(2,1)}, u32[]{:S(2)}) copy-start(bf16[1024,1024]{1,0:T(8,128)(2,1)} %param.46) | copy-start | bytes 6291460
  7.2 253.4 %reduce-scatter.2.cloned.1.call-start = ((), (), s32[]{:S(2)}) async-start(), calls=%async_computation.1 | async-start | bytes 6684672 | tf_op jit(solution)/shard_map/reduce_scatter | solution.py:1218
  35.0 12.9 %copy-start.3 = (f32[1024,768]{1,0:T(8,128)}, f32[1024,768]{1,0:T(8,128)S(1)}, u32[]{:S(2)}) copy-start(f32[1024,768]{1,0:T(8,128)S(1)} %get-tuple-element.300) | copy-start | bytes 9437188
  35.0 12.9 %copy-start.60 = (bf16[1024,768]{1,0:T(8,128)(2,1)S(1)}, bf16[1024,768]{1,0:T(8,128)(2,1)}, u32[]{:S(2)}) copy-start(bf16[1024,768]{1,0:T(8,128)(2,1)} %param.31) | copy-start | bytes 4718596
  55.3 27.0 %collective-permute-start = (f32[1024]{0:T(1024)S(1)}, f32[1024]{0:T(1024)S(1)}, u32[]{:S(2)}, u32[]{:S(2)}) collective-permute-start(f32[1024]{0:T(1024)S(1)} %get-tuple-element.297), channel_id=1, source_target_pairs={{0,1},{1,0},{2,3},{3,2},{4,5},{5,4},{6,7},{7,6},{8,9},{9,8},{10,11... | collective-permute-start | bytes 12296 | tf_op jit(solution)/shard_map/ppermute | solution.py:102
  69.6 12.7 %copy-start.10 = (f32[1024,768]{1,0:T(8,128)S(1)}, f32[1024,768]{1,0:T(8,128)}, u32[]{:S(2)}) copy-start(f32[1024,768]{1,0:T(8,128)} %get-tuple-element.298) | copy-start | bytes 9437188
  89.1 26.4 %collective-permute-start.1 = (bf16[512,1024]{1,0:T(8,128)(2,1)}, bf16[512,1024]{1,0:T(8,128)(2,1)}, u32[]{:S(2)}, u32[]{:S(2)}) collective-permute-start(bf16[512,1024]{1,0:T(8,128)(2,1)} %get-tuple-element.325), channel_id=1, source_target_pairs={{0,1},{1,0},{2,3},{3,2},{4,5},{5,4},{6,7},{7,6},{8,9},{9,8},{10,11... | collective-permute-start | bytes 3145736 | tf_op jit(solution)/shard_map/ppermute | solution.py:1023
  107.9 28.5 %collective-permute-start.2 = (bf16[512,1024]{1,0:T(8,128)(2,1)S(1)}, bf16[512,1024]{1,0:T(8,128)(2,1)S(1)}, u32[]{:S(2)}, u32[]{:S(2)}) collective-permute-start(bf16[512,1024]{1,0:T(8,128)(2,1)S(1)} %copy-done.68), channel_id=1, source_target_pairs={{0,1},{1,0},{2,3},{3,2},{4,5},{5,4},{6,7},{7,6},{8,9},{9,8},{10,11... | collective-permute-start | bytes 3145736 | tf_op jit(solution)/shard_map/ppermute | solution.py:1023
  136.9 23.8 %collective-permute-start.3 = (bf16[512,1024]{1,0:T(8,128)(2,1)S(1)}, bf16[512,1024]{1,0:T(8,128)(2,1)S(1)}, u32[]{:S(2)}, u32[]{:S(2)}) collective-permute-start(bf16[512,1024]{1,0:T(8,128)(2,1)S(1)} %get-tuple-element.107), channel_id=1, source_target_pairs={{0,1},{1,0},{2,3},{3,2},{4,5},{5,4},{6,7},{7,6},{8,9},{9,8},{10,11... | collective-permute-start | bytes 3145736 | tf_op jit(solution)/shard_map/ppermute | solution.py:1023
  161.7 23.1 %collective-permute-start.4 = (bf16[512,1024]{1,0:T(8,128)(2,1)}, bf16[512,1024]{1,0:T(8,128)(2,1)}, u32[]{:S(2)}, u32[]{:S(2)}) collective-permute-start(bf16[512,1024]{1,0:T(8,128)(2,1)} %get-tuple-element.110), channel_id=1, source_target_pairs={{0,1},{1,0},{2,3},{3,2},{4,5},{5,4},{6,7},{7,6},{8,9},{9,8},{10,11... | collective-permute-start | bytes 3145736 | tf_op jit(solution)/shard_map/ppermute | solution.py:1023
  174.1 10.7 %copy-start.7 = (f32[512,1024]{1,0:T(8,128)S(1)}, f32[512,1024]{1,0:T(8,128)}, u32[]{:S(2)}) copy-start(f32[512,1024]{1,0:T(8,128)} %copy-done.6) | copy-start | bytes 6291460
  174.1 267.6 %all-gather.2.cloned.1.call-start = ((), (), s32[]{:S(2)}) async-start(), calls=%async_computation.2 | async-start | bytes 6684672 | tf_op jit(solution)/shard_map/all_gather | solution.py:1256
  198.6 4.5 collective-permute-start.5
  212.3 5.8 %collective-permute-start.6 = (bf16[512,1792]{1,0:T(8,128)(2,1)}, bf16[512,1792]{1,0:T(8,128)(2,1)S(1)}, u32[]{:S(2)}, u32[]{:S(2)}) collective-permute-start(bf16[512,1792]{1,0:T(8,128)(2,1)} %pad_maximum_fusion.3), channel_id=1, source_target_pairs={{0,2},{2,0},{4,6},{6,4},{8,10},{10,8},{12,14},{14,12},{16,18},{18,... | collective-permute-start | bytes 5505032 | tf_op jit(solution)/shard_map/ppermute | solution.py:109
  222.3 31.8 %collective-permute-start.7 = (bf16[256,1792]{1,0:T(8,128)(2,1)}, bf16[256,1792]{1,0:T(8,128)(2,1)}, u32[]{:S(2)}, u32[]{:S(2)}) collective-permute-start(bf16[256,1792]{1,0:T(8,128)(2,1)} %broadcast_select_fusion.9), channel_id=1, source_target_pairs={{0,4},{2,6},{4,0},{6,2},{8,12},{10,14},{12,8},{14,10},{16,20},{18,... | collective-permute-start | bytes 2752520 | tf_op jit(solution)/shard_map/ppermute | solution.py:109
  269.7 17.9 %copy-start.19 = (f32[1024,768]{1,0:T(8,128)S(1)}, f32[1024,768]{1,0:T(8,128)}, u32[]{:S(2)}) copy-start(f32[1024,768]{1,0:T(8,128)} %get-tuple-element.122) | copy-start | bytes 9437188
  269.8 17.7 %collective-permute-start.8 = (bf16[128,1792]{1,0:T(8,128)(2,1)S(1)}, bf16[128,1792]{1,0:T(8,128)(2,1)S(1)}, u32[]{:S(2)}, u32[]{:S(2)}) collective-permute-start(bf16[128,1792]{1,0:T(8,128)(2,1)S(1)} %broadcast_select_fusion.17), channel_id=1, source_target_pairs={{0,8},{2,10},{4,12},{6,14},{8,0},{10,2},{12,4},{14,6},{16,24},{18,... | collective-permute-start | bytes 1376264 | tf_op jit(solution)/shard_map/ppermute | solution.py:109
  272.4 15.2 %copy-start.5 = (f32[1024,768]{1,0:T(8,128)S(1)}, f32[1024,768]{1,0:T(8,128)}, u32[]{:S(2)}) copy-start(f32[1024,768]{1,0:T(8,128)} %copy-done.3) | copy-start | bytes 9437188
  289.3 14.8 %collective-permute-start.9 = (bf16[64,1792]{1,0:T(8,128)(2,1)S(1)}, bf16[64,1792]{1,0:T(8,128)(2,1)S(1)}, u32[]{:S(2)}, u32[]{:S(2)}) collective-permute-start(bf16[64,1792]{1,0:T(8,128)(2,1)S(1)} %broadcast_select_fusion.24), channel_id=1, source_target_pairs={{0,16},{2,18},{4,20},{6,22},{8,24},{10,26},{12,28},{14,30},{16,0},... | collective-permute-start | bytes 688136 | tf_op jit(solution)/shard_map/ppermute | solution.py:109
  304.1 23.7 %collective-permute-start.10 = (bf16[64,1792]{1,0:T(8,128)(2,1)S(1)}, bf16[64,1792]{1,0:T(8,128)(2,1)S(1)}, u32[]{:S(2)}, u32[]{:S(2)}) collective-permute-start(bf16[64,1792]{1,0:T(8,128)(2,1)S(1)} %add_convert_fusion.8), channel_id=1, source_target_pairs={{0,16},{2,18},{4,20},{6,22},{8,24},{10,26},{12,28},{14,30},{16,0},... | collective-permute-start | bytes 688136 | tf_op jit(solution)/shard_map/ppermute | solution.py:109
  305.4 22.5 %collective-permute-start.11 = (bf16[512,1152]{1,0:T(8,128)(2,1)}, bf16[512,1152]{1,0:T(8,128)(2,1)S(1)}, u32[]{:S(2)}, u32[]{:S(2)}) collective-permute-start(bf16[512,1152]{1,0:T(8,128)(2,1)} %broadcast_select_fusion.4), channel_id=1, source_target_pairs={{0,2},{2,0},{4,6},{6,4},{8,10},{10,8},{12,14},{14,12},{16,18},{18,... | collective-permute-start | bytes 3538952 | tf_op jit(solution)/shard_map/ppermute | solution.py:109
  320.5 10.7 %slice-start = ((s8[4718592]{0:T(1024)(128)(4,1)}), s8[4194304]{0:T(1024)(128)(4,1)S(1)}, s32[]{:S(2)}) async-start(s8[4718592]{0:T(1024)(128)(4,1)} %bitcast.88), calls=%async_computation.3 | async-start | bytes 8388608
  328.4 11.7 %collective-permute-start.14 = (bf16[512,384]{1,0:T(8,128)(2,1)S(1)}, bf16[512,384]{1,0:T(8,128)(2,1)S(1)}, u32[]{:S(2)}, u32[]{:S(2)}) collective-permute-start(bf16[512,384]{1,0:T(8,128)(2,1)S(1)} %broadcast_select_fusion.20), channel_id=1, source_target_pairs={{0,2},{2,0},{4,6},{6,4},{8,10},{10,8},{12,14},{14,12},{16,18},{18,... | collective-permute-start | bytes 1179656 | tf_op jit(solution)/shard_map/ppermute | solution.py:109
  328.5 22.4 %collective-permute-start.12 = (bf16[128,1792]{1,0:T(8,128)(2,1)S(1)}, bf16[128,1792]{1,0:T(8,128)(2,1)S(1)}, u32[]{:S(2)}, u32[]{:S(2)}) collective-permute-start(bf16[128,1792]{1,0:T(8,128)(2,1)S(1)} %pad_maximum_fusion.13), channel_id=1, source_target_pairs={{0,8},{2,10},{4,12},{6,14},{8,0},{10,2},{12,4},{14,6},{16,24},{18,... | collective-permute-start | bytes 1376264 | tf_op jit(solution)/shard_map/ppermute | solution.py:109
  328.6 23.3 %collective-permute-start.13 = (bf16[256,1152]{1,0:T(8,128)(2,1)S(1)}, bf16[256,1152]{1,0:T(8,128)(2,1)S(1)}, u32[]{:S(2)}, u32[]{:S(2)}) collective-permute-start(bf16[256,1152]{1,0:T(8,128)(2,1)S(1)} %broadcast_select_fusion.14), channel_id=1, source_target_pairs={{0,4},{2,6},{4,0},{6,2},{8,12},{10,14},{12,8},{14,10},{16,20},{18,... | collective-permute-start | bytes 1769480 | tf_op jit(solution)/shard_map/ppermute | solution.py:109
  352.4 4.9 %collective-permute-start.17 = (f32[16,1024]{1,0:T(8,128)S(1)}, f32[16,1024]{1,0:T(8,128)S(1)}, u32[]{:S(2)}, u32[]{:S(2)}) collective-permute-start(f32[16,1024]{1,0:T(8,128)S(1)} %concatenate.92), channel_id=1, source_target_pairs={{0,2},{2,0},{4,6},{6,4},{8,10},{10,8},{12,14},{14,12},{16,18},{18,... | collective-permute-start | bytes 196616 | tf_op jit(solution)/shard_map/ppermute | solution.py:109
  352.5 20.5 %copy-start.14 = (bf16[1024,1024]{1,0:T(8,128)(2,1)S(1)}, bf16[1024,1024]{1,0:T(8,128)(2,1)}, u32[]{:S(2)}) copy-start(bf16[1024,1024]{1,0:T(8,128)(2,1)} %get-tuple-element.157) | copy-start | bytes 6291460
  352.5 7.8 %collective-permute-start.16 = (bf16[256,384]{1,0:T(8,128)(2,1)S(1)}, bf16[256,384]{1,0:T(8,128)(2,1)S(1)}, u32[]{:S(2)}, u32[]{:S(2)}) collective-permute-start(bf16[256,384]{1,0:T(8,128)(2,1)S(1)} %broadcast_select_fusion.27), channel_id=1, source_target_pairs={{0,4},{2,6},{4,0},{6,2},{8,12},{10,14},{12,8},{14,10},{16,20},{18,... | collective-permute-start | bytes 589832 | tf_op jit(solution)/shard_map/ppermute | solution.py:109
  353.5 9.2 %collective-permute-start.15 = (bf16[128,1152]{1,0:T(8,128)(2,1)S(1)}, bf16[128,1152]{1,0:T(8,128)(2,1)S(1)}, u32[]{:S(2)}, u32[]{:S(2)}) collective-permute-start(bf16[128,1152]{1,0:T(8,128)(2,1)S(1)} %broadcast_select_fusion.21), channel_id=1, source_target_pairs={{0,8},{2,10},{4,12},{6,14},{8,0},{10,2},{12,4},{14,6},{16,24},{18,... | collective-permute-start | bytes 884744 | tf_op jit(solution)/shard_map/ppermute | solution.py:109
  354.7 14.1 %collective-permute-start.18 = (bf16[256,1024]{1,0:T(8,128)(2,1)S(1)}, bf16[256,1024]{1,0:T(8,128)(2,1)S(1)}, u32[]{:S(2)}, u32[]{:S(2)}) collective-permute-start(bf16[256,1024]{1,0:T(8,128)(2,1)S(1)} %slice.440), channel_id=1, source_target_pairs={{0,1},{1,0},{2,3},{3,2},{4,5},{5,4},{6,7},{7,6},{8,9},{9,8},{10,11... | collective-permute-start | bytes 1572872 | tf_op jit(solution)/shard_map/ppermute | solution.py:1023
  356.3 24.7 %collective-permute-start.25 = (bf16[256,1792]{1,0:T(8,128)(2,1)S(1)}, bf16[256,1792]{1,0:T(8,128)(2,1)S(1)}, u32[]{:S(2)}, u32[]{:S(2)}) collective-permute-start(bf16[256,1792]{1,0:T(8,128)(2,1)S(1)} %copy-done.43), channel_id=1, source_target_pairs={{0,4},{2,6},{4,0},{6,2},{8,12},{10,14},{12,8},{14,10},{16,20},{18,... | collective-permute-start | bytes 2752520 | tf_op jit(solution)/shard_map/ppermute | solution.py:109
  368.8 12.4 %copy-start.54 = (bf16[256,1024]{1,0:T(8,128)(2,1)}, bf16[256,1024]{1,0:T(8,128)(2,1)S(1)}, u32[]{:S(2)}) copy-start(bf16[256,1024]{1,0:T(8,128)(2,1)S(1)} %collective-permute-done.18) | copy-start | bytes 1572868
  368.8 12.1 %collective-permute-start.21 = (f32[16,1024]{1,0:T(8,128)S(1)}, f32[16,1024]{1,0:T(8,128)S(1)}, u32[]{:S(2)}, u32[]{:S(2)}) collective-permute-start(f32[16,1024]{1,0:T(8,128)S(1)} %add.383), channel_id=1, source_target_pairs={{0,4},{2,6},{4,0},{6,2},{8,12},{10,14},{12,8},{14,10},{16,20},{18,... | collective-permute-start | bytes 196616 | tf_op jit(solution)/shard_map/ppermute | solution.py:109
  369.9 11.0 %collective-permute-start.20 = (bf16[128,384]{1,0:T(8,128)(2,1)S(1)}, bf16[128,384]{1,0:T(8,128)(2,1)S(1)}, u32[]{:S(2)}, u32[]{:S(2)}) collective-permute-start(bf16[128,384]{1,0:T(8,128)(2,1)S(1)} %broadcast_select_fusion.29), channel_id=1, source_target_pairs={{0,8},{2,10},{4,12},{6,14},{8,0},{10,2},{12,4},{14,6},{16,24},{18,... | collective-permute-start | bytes 294920 | tf_op jit(solution)/shard_map/ppermute | solution.py:109
  371.7 9.3 %collective-permute-start.19 = (bf16[64,1152]{1,0:T(8,128)(2,1)S(1)}, bf16[64,1152]{1,0:T(8,128)(2,1)S(1)}, u32[]{:S(2)}, u32[]{:S(2)}) collective-permute-start(bf16[64,1152]{1,0:T(8,128)(2,1)S(1)} %broadcast_select_fusion.28), channel_id=1, source_target_pairs={{0,16},{2,18},{4,20},{6,22},{8,24},{10,26},{12,28},{14,30},{16,0},... | collective-permute-start | bytes 442376 | tf_op jit(solution)/shard_map/ppermute | solution.py:109
  373.0 12.4 %collective-permute-start.22 = (bf16[256,1024]{1,0:T(8,128)(2,1)S(1)}, bf16[256,1024]{1,0:T(8,128)(2,1)S(1)}, u32[]{:S(2)}, u32[]{:S(2)}) collective-permute-start(bf16[256,1024]{1,0:T(8,128)(2,1)S(1)} %slice.395), channel_id=1, source_target_pairs={{0,1},{1,0},{2,3},{3,2},{4,5},{5,4},{6,7},{7,6},{8,9},{9,8},{10,11... | collective-permute-start | bytes 1572872 | tf_op jit(solution)/shard_map/ppermute | solution.py:1023
  386.3 5.1 %collective-permute-start.23 = (bf16[64,384]{1,0:T(8,128)(2,1)S(1)}, bf16[64,384]{1,0:T(8,128)(2,1)S(1)}, u32[]{:S(2)}, u32[]{:S(2)}) collective-permute-start(bf16[64,384]{1,0:T(8,128)(2,1)S(1)} %broadcast_select_fusion.30), channel_id=1, source_target_pairs={{0,16},{2,18},{4,20},{6,22},{8,24},{10,26},{12,28},{14,30},{16,0},... | collective-permute-start | bytes 147464 | tf_op jit(solution)/shard_map/ppermute | solution.py:109
  389.1 4.3 collective-permute-start.24
  393.4 5.0 %collective-permute-start.26 = (bf16[64,384]{1,0:T(8,128)(2,1)S(1)}, bf16[64,384]{1,0:T(8,128)(2,1)S(1)}, u32[]{:S(2)}, u32[]{:S(2)}) collective-permute-start(bf16[64,384]{1,0:T(8,128)(2,1)S(1)} %pad_maximum_fusion.16), channel_id=1, source_target_pairs={{0,1},{1,0},{2,3},{3,2},{4,5},{5,4},{6,7},{7,6},{8,9},{9,8},{10,11... | collective-permute-start | bytes 147464 | tf_op jit(solution)/shard_map/ppermute | solution.py:1023
  396.6 6.0 %collective-permute-start.27 = (f32[16,1024]{1,0:T(8,128)S(1)}, f32[16,1024]{1,0:T(8,128)}, u32[]{:S(2)}, u32[]{:S(2)}) collective-permute-start(f32[16,1024]{1,0:T(8,128)S(1)} %add.388), channel_id=1, source_target_pairs={{0,16},{2,18},{4,20},{6,22},{8,24},{10,26},{12,28},{14,30},{16,0},... | collective-permute-start | bytes 196616 | tf_op jit(solution)/shard_map/ppermute | solution.py:109
  400.3 22.7 %collective-permute-start.33 = (bf16[512,1024]{1,0:T(8,128)(2,1)}, bf16[512,1024]{1,0:T(8,128)(2,1)S(1)}, u32[]{:S(2)}, u32[]{:S(2)}) collective-permute-start(bf16[512,1024]{1,0:T(8,128)(2,1)} %slice.401), channel_id=1, source_target_pairs={{0,1},{1,0},{2,3},{3,2},{4,5},{5,4},{6,7},{7,6},{8,9},{9,8},{10,11... | collective-permute-start | bytes 3145736 | tf_op jit(solution)/shard_map/ppermute | solution.py:1023
  401.8 21.2 %copy-start.15 = (bf16[1024,1024]{1,0:T(8,128)(2,1)S(1)}, bf16[1024,1024]{1,0:T(8,128)(2,1)}, u32[]{:S(2)}) copy-start(bf16[1024,1024]{1,0:T(8,128)(2,1)} %get-tuple-element.157) | copy-start | bytes 6291460
  403.4 19.4 %collective-permute-start.30 = (f32[16,1024]{1,0:T(8,128)S(1)}, f32[16,1024]{1,0:T(8,128)S(1)}, u32[]{:S(2)}, u32[]{:S(2)}) collective-permute-start(f32[16,1024]{1,0:T(8,128)S(1)} %add.390), channel_id=1, source_target_pairs={{0,1},{1,0},{2,3},{3,2},{4,5},{5,4},{6,7},{7,6},{8,9},{9,8},{10,11... | collective-permute-start | bytes 196616 | tf_op jit(solution)/shard_map/ppermute | solution.py:1361
  404.3 18.5 %collective-permute-start.28 = (bf16[64,1664]{1,0:T(8,128)(2,1)S(1)}, bf16[64,1664]{1,0:T(8,128)(2,1)S(1)}, u32[]{:S(2)}, u32[]{:S(2)}) collective-permute-start(bf16[64,1664]{1,0:T(8,128)(2,1)S(1)} %concatenate.95), channel_id=1, source_target_pairs={{0,16},{2,18},{4,20},{6,22},{8,24},{10,26},{12,28},{14,30},{16,0},... | collective-permute-start | bytes 638984 | tf_op jit(solution)/shard_map/ppermute | solution.py:109
  405.5 27.3 %collective-permute-start.29 = (bf16[512,1792]{1,0:T(8,128)(2,1)}, bf16[512,1792]{1,0:T(8,128)(2,1)S(1)}, u32[]{:S(2)}, u32[]{:S(2)}) collective-permute-start(bf16[512,1792]{1,0:T(8,128)(2,1)} %pad_maximum_fusion.4), channel_id=1, source_target_pairs={{0,2},{2,0},{4,6},{6,4},{8,10},{10,8},{12,14},{14,12},{16,18},{18,... | collective-permute-start | bytes 5505032 | tf_op jit(solution)/shard_map/ppermute | solution.py:109
  433.3 8.2 %collective-permute-start.31 = (bf16[128,1664]{1,0:T(8,128)(2,1)S(1)}, bf16[128,1664]{1,0:T(8,128)(2,1)S(1)}, u32[]{:S(2)}, u32[]{:S(2)}) collective-permute-start(bf16[128,1664]{1,0:T(8,128)(2,1)S(1)} %pad_maximum_fusion.14), channel_id=1, source_target_pairs={{0,8},{2,10},{4,12},{6,14},{8,0},{10,2},{12,4},{14,6},{16,24},{18,... | collective-permute-start | bytes 1277960 | tf_op jit(solution)/shard_map/ppermute | solution.py:109
  441.7 14.6 %collective-permute-start.32 = (bf16[256,1664]{1,0:T(8,128)(2,1)S(1)}, bf16[256,1664]{1,0:T(8,128)(2,1)S(1)}, u32[]{:S(2)}, u32[]{:S(2)}) collective-permute-start(bf16[256,1664]{1,0:T(8,128)(2,1)S(1)} %pad_maximum_fusion.7), channel_id=1, source_target_pairs={{0,4},{2,6},{4,0},{6,2},{8,12},{10,14},{12,8},{14,10},{16,20},{18,... | collective-permute-start | bytes 2555912 | tf_op jit(solution)/shard_map/ppermute | solution.py:109
  456.6 4.3 collective-permute-start.34
  (74 other events, 276.1 us)
Sparse Core Ops, SparseCore 0:
  174.2 86.3 reduce-scatter.1
  269.8 77.1 all-gather.1

commit v7 on v6

--- a/solution.py
+++ b/solution.py
@@ -1361,7 +1361,7 @@
     small_other = lax.ppermute(small, "tensor", [(0, 1), (1, 0)])
     is_shared = lax.broadcasted_iota(jnp.int32, small.shape, 0) >= len(own_rows)
     small = small + jnp.where(is_shared, small_other, 0.0)
-    late, early, small = tie(late, early, small)
+    late, early = tie(late, early)
     late = double(late, bits[2])
     late, forward_total = tie(late, forward_total)
     hidden_units = down_weight.shape[0]

time: 484 us -> 486 us (level)
    ppermute x1, waiting for transfers between devices: 17.3 us -> 4.42 us  [local_fast(): small_other = lax.ppermute(small, 'tensor', [(0, 1), (1, 0)])]
    ppermute x24, waiting for transfers between devices: 56.8 us -> 68.5 us  [swap_bit(): return lax.ppermute(value, 'dp', [(i, i ^ bit) for i in range(size)])]
    ppermute x8, waiting for transfers between devices: 49.2 us -> 54.1 us  [swap_pair(): return lax.ppermute(value, 'tensor', [(0, 1), (1, 0)])]
  transfers between devices with their start and end apart: 37 -> 37, of which waited for: 20 -> 22; matrix products, arithmetic and copies ran while one was open for 34% -> 34% of each run, Pallas kernels for 13% -> 13%
where the time goes in v7:
time: 486 us; the launch traced here: 477 us
  waiting for transfers between devices  131 us (27%)
  other arithmetic  121 us (25%)
  Pallas kernels  73.8 us (15%)
  matrix products  65.7 us (14%)
  local copies, waits for them, and re-layouts  38.6 us (8%)
  starting transfers between devices  30.5 us (6%)
  between operations  16.1 us (3%)
    ppermute x24, waiting for transfers between devices, swap_bit(): return lax.ppermute(value, 'dp', [(i, i ^ bit) for i in range(size)])  68.5 us
    ppermute x8, waiting for transfers between devices, swap_pair(): return lax.ppermute(value, 'tensor', [(0, 1), (1, 0)])  54.1 us
    dot_general x12, matrix products, matmul(): return jnp.dot(left, right, preferred_element_type=jnp.float32)  29.6 us
    dot_general x9, matrix products, dot_nt(): lax.dot_general(left, right, (((1,), (1,)), ((), ())), preferred_element_...  27.2 us
    pallas_call x1, Pallas kernels, scan_back_call(): pl.pallas_call(scan_back_kernel, grid=(chunks,), in_specs=[by_chunk(LANES...  25.3 us
    ppermute x24, starting transfers between devices, swap_bit(): return lax.ppermute(value, 'dp', [(i, i ^ bit) for i in range(size)])  17.4 us
    unnamed x179, local copies, waits for them, and re-layouts  14.7 us
    pallas_call x1, Pallas kernels, attend_back_call(): pl.pallas_call(attend_back_kernel, out_shape=[jax.ShapeDtypeStruct((rows,...  13 us
  transfers between devices with their start and end apart: 37, of which 22 were waited for; matrix products, arithmetic and copies ran while one was open for 34% of the time, Pallas kernels for 13%

profile of v7, /device:TPU:0, one launch (start us, length us, event | category | flops | bytes accessed | tf_op | source)
XLA Modules:
  0.0 476.9 jit_solution(15110684318529528341)
XLA Ops:
  31.2 3.8 fusion.8
  35.0 12.9 %scan_forward.1 = (f32[1024,768]{1,0:T(8,128)}, bf16[4,128,768]{2,1,0:T(8,128)(2,1)}) custom-call(f32[1024,128]{1,0:T(8,128)} %get-tuple-element.369.step_ref, bf16[1024,256]{1,0:T(8,128)(2,1)} %get-tuple-element.299.coef_ref, f32[1024,768]{1,0:T(8,128)} %get-tuple-element.297.act_ref, f32[1024,128]{1,0:T(8,128)} %pad.127.seg_col_ref.aux_ref, ...), custom_call_target="tpu_custom_call" | custom-call | tf_op jit(solution)/shard_map/scan_forward/pallas_call | solution.py:673
  47.9 7.4 %multiply_reduce_fusion.9 = (f32[1024]{0:T(1024)S(1)}, f32[1024,768]{1,0:T(8,128)}, f32[1024,768]{1,0:T(8,128)}) fusion(f32[1024,768]{1,0:T(8,128)} %get-tuple-element.104, f32[1024,768]{1,0:T(8,128)S(1)} %get-tuple-element.298, f32[768]{0:T(1024)S(1)} %mul.806, bf16[1024,1024]{1,0:T(8,128)(2,1)} %copy-done.24, bf16[1024,768]{1,0:T(8,128)(2,1)S(1)} %copy-done.60), kind=kOutput, calls=%fused_computation.37 | convolution fusion | flops 1620835328 | bytes 16260096 | tf_op jit(solution)/shard_map/dot_general | solution.py:23
  55.3 2.9 collective-permute-start
  58.3 3.1 fusion.46
  61.4 3.4 fusion.75.query_ref
  66.3 3.3 fusion.42.keyval_ref
  71.5 10.8 %attend_forward.1 = (bf16[1024,256]{1,0:T(8,128)(2,1)}, bf16[1024,256]{1,0:T(8,128)(2,1)}, bf16[1024,256]{1,0:T(8,128)(2,1)}, f32[1024,128]{1,0:T(8,128)}) custom-call(f32[1024,256]{1,0:T(8,128)} %fusion.75.query_ref, f32[1024,128]{1,0:T(8,128)} %fusion.42.keyval_ref, f32[1,1024]{1,0:T(1,128)} %get-tuple-element.355.seg_ref, ...), custom_call_target="tpu_custom_call" | custom-call | tf_op jit(solution)/shard_map/attend_forward/pallas_call | solution.py:910
  90.0 4.6 convert_element_type.400
  95.3 7.8 %concatenate.83 = bf16[1024,2304]{1,0:T(8,128)(2,1)} concatenate(bf16[1024,768]{1,0:T(8,128)(2,1)} %param.31, bf16[1024,768]{1,0:T(8,128)(2,1)} %param.32, bf16[1024,128]{1,0:T(8,128)(2,1)} %pad.128.clone, bf16[1024,256]{1,0:T(8,128)(2,1)} %param.33, bf16[1024,256]{1,0:T(8,128)(2,1)} %param.28, bf16[1024,64]{1,0:T(8,128)(2,1)S(1)} %get-tuple-element.337, bf16[1024,64]{1,0:T(8,128)(2,1)} %copy-done.46), dimensions={1} | concatenate | bytes 9437184 | tf_op jit(solution)/shard_map/concatenate | solution.py:1184
  103.2 3.3 fusion.32
  110.0 5.5 %collective-permute-done.1 = bf16[512,1024]{1,0:T(8,128)(2,1)} collective-permute-done((bf16[512,1024]{1,0:T(8,128)(2,1)}, bf16[512,1024]{1,0:T(8,128)(2,1)}, u32[]{:S(2)}, u32[]{:S(2)}) %collective-permute-start.1) | collective-permute-done | bytes 1048608 | tf_op jit(solution)/shard_map/ppermute | solution.py:1023
  120.9 3.0 multiply_convert_fusion.4
  125.3 2.6 fusion.73
  127.9 8.5 %collective-permute-done.2 = bf16[512,1024]{1,0:T(8,128)(2,1)S(1)} collective-permute-done((bf16[512,1024]{1,0:T(8,128)(2,1)S(1)}, bf16[512,1024]{1,0:T(8,128)(2,1)S(1)}, u32[]{:S(2)}, u32[]{:S(2)}) %collective-permute-start.2) | collective-permute-done | bytes 1048608 | tf_op jit(solution)/shard_map/ppermute | solution.py:1023
  138.8 3.0 multiply_convert_fusion.3
  143.4 3.1 fusion.74
  146.4 14.3 %collective-permute-done.3 = bf16[512,1024]{1,0:T(8,128)(2,1)S(1)} collective-permute-done((bf16[512,1024]{1,0:T(8,128)(2,1)S(1)}, bf16[512,1024]{1,0:T(8,128)(2,1)S(1)}, u32[]{:S(2)}, u32[]{:S(2)}) %collective-permute-start.3) | collective-permute-done | bytes 1048608 | tf_op jit(solution)/shard_map/ppermute | solution.py:1023
  162.3 11.8 %weight_products.1 = bf16[3,1024,1024]{2,1,0:T(8,128)(2,1)} custom-call(bf16[512,1024]{1,0:T(8,128)(2,1)} %get-tuple-element.307.refs_0_, bf16[512,1024]{1,0:T(8,128)(2,1)} %get-tuple-element.304.refs_1_, bf16[512,1024]{1,0:T(8,128)(2,1)} %copy-done.38, bf16[512,1024]{1,0:T(8,128)(2,1)} %copy-done.39, bf16[512,1024]{1,0:T(8,128)(2,1)} %copy-done.65, ...), custom_call_target="tpu_custom_call" | custom-call | tf_op jit(solution)/shard_map/weight_products/pallas_call | solution.py:1081
  174.1 10.7 %collective-permute-done.4 = bf16[512,1024]{1,0:T(8,128)(2,1)} collective-permute-done((bf16[512,1024]{1,0:T(8,128)(2,1)}, bf16[512,1024]{1,0:T(8,128)(2,1)}, u32[]{:S(2)}, u32[]{:S(2)}) %collective-permute-start.4) | collective-permute-done | bytes 1048608 | tf_op jit(solution)/shard_map/ppermute | solution.py:1023
  184.8 6.4 %multiply_reduce_fusion.11 = (f32[1024]{0:T(1024)S(1)}, f32[512]{0:T(512)S(1)}, f32[512]{0:T(512)S(1)}, f32[1024]{0:T(1024)S(1)}) fusion(f32[512,1024]{1,0:T(8,128)} %get-tuple-element.373, f32[512,1024]{1,0:T(8,128)S(1)} %copy-done.7, f32[512]{0:T(512)S(1)} %add_rsqrt_fusion.3, f32[1024]{0:T(1024)S(1)} %convert_element_type.417, ...), kind=kLoop, calls=%fused_computation.62 | loop fusion | flops 9434112 | bytes 12603392 | tf_op jit(solution)/shard_map/reduce_sum | solution.py:1202
  191.9 4.4 fusion.65
  204.4 3.7 constant_dynamic-update-slice_fusion.6
  212.3 5.8 %fusion.23.grad_ref = f32[1024,768]{1,0:T(8,128)} fusion(f32[1024]{0:T(1024)S(1)} %add.361, f32[1024,768]{1,0:T(8,128)} %get-tuple-element.296, f32[1024,768]{1,0:T(8,128)} %copy-done.21, f32[1024]{0:T(1024)S(1)} %get-tuple-element.285, f32[768]{0:T(1024)S(1)} %convert_element_type.411, f32[1024]{0:T(1024)S(1)} %get-tuple-element.286, ...), kind=kLoop, calls=%fused_computation.95 | loop fusion | flops 8650752 | bytes 12598272 | tf_op jit(solution)/shard_map/mul | solution.py:1241
  224.3 3.2 convolution_convert_fusion.3.grad_ref
  227.5 25.3 %scan_backward.1 = (f32[1024,768]{1,0:T(8,128)}, f32[1024,128]{1,0:T(8,128)}, f32[1024,256]{1,0:T(8,128)}, f32[1,128]{1,0:T(1,128)}, f32[1,768]{1,0:T(1,128)}) custom-call(f32[1024,128]{1,0:T(8,128)} %get-tuple-element.369.step_ref, bf16[1024,256]{1,0:T(8,128)(2,1)} %get-tuple-element.299.coef_ref, f32[1024,768]{1,0:T(8,128)} %get-tuple-element.297.act_ref, ...), custom_call_target="tpu_custom_call" | custom-call | tf_op jit(solution)/shard_map/scan_backward/pallas_call | solution.py:815
  256.6 4.1 reduce-scatter.2.cloned.1.call-done
  260.6 9.0 %multiply_reduce_fusion.4 = (f32[768]{0:T(1024)S(1)}, f32[768]{0:T(1024)S(1)}, f32[768]{0:T(1024)S(1)}, f32[768]{0:T(1024)S(1)}, f32[768]{0:T(1024)S(1)}) fusion(f32[1024,768]{1,0:T(8,128)} %copy-done.18, f32[1024]{0:T(1024)S(1)} %bitcast.104, f32[1024]{0:T(1024)S(1)} %bitcast.98, f32[1024]{0:T(1024)S(1)} %bitcast.92, f32[1024,768]{1,0:T(8,128)} %get-tuple-element.121, ...), kind=kLoop, calls=%fused_computation.28 | loop fusion | flops 15724800 | bytes 9464832 | tf_op jit(solution)/shard_map/reduce_sum | solution.py:1045
  274.8 12.6 %collective-permute-done.8 = bf16[128,1792]{1,0:T(8,128)(2,1)S(1)} collective-permute-done((bf16[128,1792]{1,0:T(8,128)(2,1)S(1)}, bf16[128,1792]{1,0:T(8,128)(2,1)S(1)}, u32[]{:S(2)}, u32[]{:S(2)}) %collective-permute-start.8) | collective-permute-done | bytes 458784 | tf_op jit(solution)/shard_map/ppermute | solution.py:109
  295.4 3.3 convolution_convert_fusion
  298.9 5.1 %collective-permute-done.9 = bf16[64,1792]{1,0:T(8,128)(2,1)S(1)} collective-permute-done((bf16[64,1792]{1,0:T(8,128)(2,1)S(1)}, bf16[64,1792]{1,0:T(8,128)(2,1)S(1)}, u32[]{:S(2)}, u32[]{:S(2)}) %collective-permute-start.9) | collective-permute-done | bytes 229408 | tf_op jit(solution)/shard_map/ppermute | solution.py:109
  305.4 13.0 %attend_backward.1 = (bf16[1024,256]{1,0:T(8,128)(2,1)}, bf16[1024,128]{1,0:T(8,128)(2,1)}) custom-call(bf16[1024,256]{1,0:T(8,128)(2,1)} %get-tuple-element.126.query_ref, bf16[1024,256]{1,0:T(8,128)(2,1)} %get-tuple-element.127.both_ref, f32[1,1024]{1,0:T(1,128)} %get-tuple-element.355.seg_ref, f32[1024,128]{1,0:T(8,128)} %pad.127.seg_col_ref.aux_ref, ...), custom_call_target="tpu_custom_call" | custom-call | tf_op jit(solution)/shard_map/attend_backward/pallas_call | solution.py:974
  321.8 6.0 %collective-permute-done.10 = bf16[64,1792]{1,0:T(8,128)(2,1)S(1)} collective-permute-done((bf16[64,1792]{1,0:T(8,128)(2,1)S(1)}, bf16[64,1792]{1,0:T(8,128)(2,1)S(1)}, u32[]{:S(2)}, u32[]{:S(2)}) %collective-permute-start.10) | collective-permute-done | bytes 229408 | tf_op jit(solution)/shard_map/ppermute | solution.py:109
  331.3 8.7 %multiply_reduce_fusion.1 = (f32[1024]{0:T(1024)S(1)}, bf16[1024,1024]{1,0:T(8,128)(2,1)}) fusion(bf16[1024,1024]{1,0:T(8,128)(2,1)S(1)} %copy-done.2, f32[1024]{0:T(1024)S(1)} %copy-done.74, bf16[1024,2304]{1,0:T(8,128)(2,1)S(1)} %constant_dynamic-update-slice_fusion.2, bf16[1024,2304]{1,0:T(8,128)(2,1)} %concatenate.83), kind=kOutput, calls=%fused_computation.3 | convolution fusion | flops 4837080064 | bytes 13639680 | tf_op jit(solution)/shard_map/dot_general | solution.py:594
  340.2 10.7 %collective-permute-done.12 = bf16[128,1792]{1,0:T(8,128)(2,1)S(1)} collective-permute-done((bf16[128,1792]{1,0:T(8,128)(2,1)S(1)}, bf16[128,1792]{1,0:T(8,128)(2,1)S(1)}, u32[]{:S(2)}, u32[]{:S(2)}) %collective-permute-start.12) | collective-permute-done | bytes 458784 | tf_op jit(solution)/shard_map/ppermute | solution.py:109
  357.3 2.9 collective-permute-done.16
  362.8 6.0 %collective-permute-done.18 = bf16[256,1024]{1,0:T(8,128)(2,1)S(1)} collective-permute-done((bf16[256,1024]{1,0:T(8,128)(2,1)S(1)}, bf16[256,1024]{1,0:T(8,128)(2,1)S(1)}, u32[]{:S(2)}, u32[]{:S(2)}) %collective-permute-start.18) | collective-permute-done | bytes 524320 | tf_op jit(solution)/shard_map/ppermute | solution.py:1023
  374.7 6.2 %collective-permute-done.21 = f32[16,1024]{1,0:T(8,128)S(1)} collective-permute-done((f32[16,1024]{1,0:T(8,128)S(1)}, f32[16,1024]{1,0:T(8,128)S(1)}, u32[]{:S(2)}, u32[]{:S(2)}) %collective-permute-start.21) | collective-permute-done | bytes 65568 | tf_op jit(solution)/shard_map/ppermute | solution.py:109
  381.2 4.2 collective-permute-done.22
  402.4 3.0 collective-permute-done.27
  406.4 8.5 %collective-permute-done.28 = bf16[64,1664]{1,0:T(8,128)(2,1)S(1)} collective-permute-done((bf16[64,1664]{1,0:T(8,128)(2,1)S(1)}, bf16[64,1664]{1,0:T(8,128)(2,1)S(1)}, u32[]{:S(2)}, u32[]{:S(2)}) %collective-permute-start.28) | collective-permute-done | bytes 213024 | tf_op jit(solution)/shard_map/ppermute | solution.py:109
  415.0 4.9 %collective-permute-done.32 = bf16[512,1024]{1,0:T(8,128)(2,1)S(1)} collective-permute-done((bf16[512,1024]{1,0:T(8,128)(2,1)}, bf16[512,1024]{1,0:T(8,128)(2,1)S(1)}, u32[]{:S(2)}, u32[]{:S(2)}) %collective-permute-start.32) | collective-permute-done | bytes 1048608 | tf_op jit(solution)/shard_map/ppermute | solution.py:1023
  420.0 3.1 multiply_reduce_fusion
  423.1 7.0 %maximum_add_fusion = f32[1024,1024]{1,0:T(8,128)} fusion(f32[512,1024]{1,0:T(8,128)S(1)} %copy-done.30, f32[512,1024]{1,0:T(8,128)S(1)} %copy-done.29, bf16[1024,1024]{1,0:T(8,128)(2,1)S(1)} %copy-done.15, bf16[1024,1024]{1,0:T(8,128)(2,1)S(1)} %copy-done.2, f32[1024]{0:T(1024)S(1)} %broadcast_multiply_fusion.6, f32[1024]{0:T(1024)S(1)} %copy-done.72, ...), kind=kLoop, calls=%fused_computation | loop fusion | flops 16777216 | bytes 14692352 | tf_op jit(solution)/shard_map/add | solution.py:1382
  435.4 3.4 collective-permute-done.30
  442.2 8.0 %slice_convert_fusion = (f32[1024,1024]{1,0:T(8,128)}, f32[1024,1024]{1,0:T(8,128)}, f32[1024,1024]{1,0:T(8,128)}) fusion(bf16[3072,1024]{1,0:T(8,128)(2,1)} %all-gather.2.cloned.1.call-done), kind=kLoop, calls=%fused_computation.58 | loop fusion | flops 3145728 | bytes 18874368 | tf_op jit(solution)/shard_map/convert_element_type | solution.py:1368
  450.2 4.0 collective-permute-done.31
  454.6 4.4 collective-permute-done.33
  (403 shorter events, 147.9 us)
Async XLA Ops:
  7.2 113.8 %copy-start = (bf16[1024,1024]{1,0:T(8,128)(2,1)S(1)}, bf16[1024,1024]{1,0:T(8,128)(2,1)}, u32[]{:S(2)}) copy-start(bf16[1024,1024]{1,0:T(8,128)(2,1)} %param.46) | copy-start | bytes 6291460
  7.2 253.4 %reduce-scatter.2.cloned.1.call-start = ((), (), s32[]{:S(2)}) async-start(), calls=%async_computation.1 | async-start | bytes 6684672 | tf_op jit(solution)/shard_map/reduce_scatter | solution.py:1218
  13.1 10.2 %copy-start.71 = (f32[1024]{0:T(1024)}, f32[1024]{0:T(1024)S(1)}, u32[]{:S(2)}) copy-start(f32[1024]{0:T(1024)S(1)} %convert_element_type.401) | copy-start | bytes 12292
  35.0 12.9 %copy-start.3 = (f32[1024,768]{1,0:T(8,128)}, f32[1024,768]{1,0:T(8,128)S(1)}, u32[]{:S(2)}) copy-start(f32[1024,768]{1,0:T(8,128)S(1)} %get-tuple-element.298) | copy-start | bytes 9437188
  35.0 12.9 %copy-start.60 = (bf16[1024,768]{1,0:T(8,128)(2,1)S(1)}, bf16[1024,768]{1,0:T(8,128)(2,1)}, u32[]{:S(2)}) copy-start(bf16[1024,768]{1,0:T(8,128)(2,1)} %param.31) | copy-start | bytes 4718596
  55.3 27.0 %collective-permute-start = (f32[1024]{0:T(1024)S(1)}, f32[1024]{0:T(1024)S(1)}, u32[]{:S(2)}, u32[]{:S(2)}) collective-permute-start(f32[1024]{0:T(1024)S(1)} %get-tuple-element.295), channel_id=1, source_target_pairs={{0,1},{1,0},{2,3},{3,2},{4,5},{5,4},{6,7},{7,6},{8,9},{9,8},{10,11... | collective-permute-start | bytes 12296 | tf_op jit(solution)/shard_map/ppermute | solution.py:102
  69.6 12.7 %copy-start.10 = (f32[1024,768]{1,0:T(8,128)S(1)}, f32[1024,768]{1,0:T(8,128)}, u32[]{:S(2)}) copy-start(f32[1024,768]{1,0:T(8,128)} %get-tuple-element.296) | copy-start | bytes 9437188
  89.1 26.4 %collective-permute-start.1 = (bf16[512,1024]{1,0:T(8,128)(2,1)}, bf16[512,1024]{1,0:T(8,128)(2,1)}, u32[]{:S(2)}, u32[]{:S(2)}) collective-permute-start(bf16[512,1024]{1,0:T(8,128)(2,1)} %get-tuple-element.323), channel_id=1, source_target_pairs={{0,1},{1,0},{2,3},{3,2},{4,5},{5,4},{6,7},{7,6},{8,9},{9,8},{10,11... | collective-permute-start | bytes 3145736 | tf_op jit(solution)/shard_map/ppermute | solution.py:1023
  107.9 28.5 %collective-permute-start.2 = (bf16[512,1024]{1,0:T(8,128)(2,1)S(1)}, bf16[512,1024]{1,0:T(8,128)(2,1)S(1)}, u32[]{:S(2)}, u32[]{:S(2)}) collective-permute-start(bf16[512,1024]{1,0:T(8,128)(2,1)S(1)} %copy-done.68), channel_id=1, source_target_pairs={{0,1},{1,0},{2,3},{3,2},{4,5},{5,4},{6,7},{7,6},{8,9},{9,8},{10,11... | collective-permute-start | bytes 3145736 | tf_op jit(solution)/shard_map/ppermute | solution.py:1023
  136.9 23.8 %collective-permute-start.3 = (bf16[512,1024]{1,0:T(8,128)(2,1)S(1)}, bf16[512,1024]{1,0:T(8,128)(2,1)S(1)}, u32[]{:S(2)}, u32[]{:S(2)}) collective-permute-start(bf16[512,1024]{1,0:T(8,128)(2,1)S(1)} %get-tuple-element.106), channel_id=1, source_target_pairs={{0,1},{1,0},{2,3},{3,2},{4,5},{5,4},{6,7},{7,6},{8,9},{9,8},{10,11... | collective-permute-start | bytes 3145736 | tf_op jit(solution)/shard_map/ppermute | solution.py:1023
  161.7 23.1 %collective-permute-start.4 = (bf16[512,1024]{1,0:T(8,128)(2,1)}, bf16[512,1024]{1,0:T(8,128)(2,1)}, u32[]{:S(2)}, u32[]{:S(2)}) collective-permute-start(bf16[512,1024]{1,0:T(8,128)(2,1)} %get-tuple-element.109), channel_id=1, source_target_pairs={{0,1},{1,0},{2,3},{3,2},{4,5},{5,4},{6,7},{7,6},{8,9},{9,8},{10,11... | collective-permute-start | bytes 3145736 | tf_op jit(solution)/shard_map/ppermute | solution.py:1023
  174.1 10.7 %copy-start.7 = (f32[512,1024]{1,0:T(8,128)S(1)}, f32[512,1024]{1,0:T(8,128)}, u32[]{:S(2)}) copy-start(f32[512,1024]{1,0:T(8,128)} %copy-done.6) | copy-start | bytes 6291460
  174.1 264.9 %all-gather.2.cloned.1.call-start = ((), (), s32[]{:S(2)}) async-start(), calls=%async_computation.2 | async-start | bytes 6684672 | tf_op jit(solution)/shard_map/all_gather | solution.py:1256
  198.6 4.5 collective-permute-start.5
  212.3 5.8 %collective-permute-start.6 = (bf16[512,1792]{1,0:T(8,128)(2,1)}, bf16[512,1792]{1,0:T(8,128)(2,1)S(1)}, u32[]{:S(2)}, u32[]{:S(2)}) collective-permute-start(bf16[512,1792]{1,0:T(8,128)(2,1)} %pad_maximum_fusion.3), channel_id=1, source_target_pairs={{0,2},{2,0},{4,6},{6,4},{8,10},{10,8},{12,14},{14,12},{16,18},{18,... | collective-permute-start | bytes 5505032 | tf_op jit(solution)/shard_map/ppermute | solution.py:109
  222.3 31.8 %collective-permute-start.7 = (bf16[256,1792]{1,0:T(8,128)(2,1)}, bf16[256,1792]{1,0:T(8,128)(2,1)}, u32[]{:S(2)}, u32[]{:S(2)}) collective-permute-start(bf16[256,1792]{1,0:T(8,128)(2,1)} %broadcast_select_fusion.9), channel_id=1, source_target_pairs={{0,4},{2,6},{4,0},{6,2},{8,12},{10,14},{12,8},{14,10},{16,20},{18,... | collective-permute-start | bytes 2752520 | tf_op jit(solution)/shard_map/ppermute | solution.py:109
  269.7 17.9 %copy-start.19 = (f32[1024,768]{1,0:T(8,128)S(1)}, f32[1024,768]{1,0:T(8,128)}, u32[]{:S(2)}) copy-start(f32[1024,768]{1,0:T(8,128)} %get-tuple-element.121) | copy-start | bytes 9437188
  269.8 17.7 %collective-permute-start.8 = (bf16[128,1792]{1,0:T(8,128)(2,1)S(1)}, bf16[128,1792]{1,0:T(8,128)(2,1)S(1)}, u32[]{:S(2)}, u32[]{:S(2)}) collective-permute-start(bf16[128,1792]{1,0:T(8,128)(2,1)S(1)} %broadcast_select_fusion.17), channel_id=1, source_target_pairs={{0,8},{2,10},{4,12},{6,14},{8,0},{10,2},{12,4},{14,6},{16,24},{18,... | collective-permute-start | bytes 1376264 | tf_op jit(solution)/shard_map/ppermute | solution.py:109
  272.4 15.2 %copy-start.5 = (f32[1024,768]{1,0:T(8,128)S(1)}, f32[1024,768]{1,0:T(8,128)}, u32[]{:S(2)}) copy-start(f32[1024,768]{1,0:T(8,128)} %copy-done.3) | copy-start | bytes 9437188
  289.3 14.8 %collective-permute-start.9 = (bf16[64,1792]{1,0:T(8,128)(2,1)S(1)}, bf16[64,1792]{1,0:T(8,128)(2,1)S(1)}, u32[]{:S(2)}, u32[]{:S(2)}) collective-permute-start(bf16[64,1792]{1,0:T(8,128)(2,1)S(1)} %broadcast_select_fusion.24), channel_id=1, source_target_pairs={{0,16},{2,18},{4,20},{6,22},{8,24},{10,26},{12,28},{14,30},{16,0},... | collective-permute-start | bytes 688136 | tf_op jit(solution)/shard_map/ppermute | solution.py:109
  304.1 23.7 %collective-permute-start.10 = (bf16[64,1792]{1,0:T(8,128)(2,1)S(1)}, bf16[64,1792]{1,0:T(8,128)(2,1)S(1)}, u32[]{:S(2)}, u32[]{:S(2)}) collective-permute-start(bf16[64,1792]{1,0:T(8,128)(2,1)S(1)} %add_convert_fusion.8), channel_id=1, source_target_pairs={{0,16},{2,18},{4,20},{6,22},{8,24},{10,26},{12,28},{14,30},{16,0},... | collective-permute-start | bytes 688136 | tf_op jit(solution)/shard_map/ppermute | solution.py:109
  305.4 22.5 %collective-permute-start.11 = (bf16[512,1152]{1,0:T(8,128)(2,1)}, bf16[512,1152]{1,0:T(8,128)(2,1)S(1)}, u32[]{:S(2)}, u32[]{:S(2)}) collective-permute-start(bf16[512,1152]{1,0:T(8,128)(2,1)} %broadcast_select_fusion.4), channel_id=1, source_target_pairs={{0,2},{2,0},{4,6},{6,4},{8,10},{10,8},{12,14},{14,12},{16,18},{18,... | collective-permute-start | bytes 3538952 | tf_op jit(solution)/shard_map/ppermute | solution.py:109
  320.5 10.7 %slice-start = ((s8[4718592]{0:T(1024)(128)(4,1)}), s8[4194304]{0:T(1024)(128)(4,1)S(1)}, s32[]{:S(2)}) async-start(s8[4718592]{0:T(1024)(128)(4,1)} %bitcast.88), calls=%async_computation.3 | async-start | bytes 8388608
  328.4 11.7 %collective-permute-start.14 = (bf16[512,384]{1,0:T(8,128)(2,1)S(1)}, bf16[512,384]{1,0:T(8,128)(2,1)S(1)}, u32[]{:S(2)}, u32[]{:S(2)}) collective-permute-start(bf16[512,384]{1,0:T(8,128)(2,1)S(1)} %broadcast_select_fusion.20), channel_id=1, source_target_pairs={{0,2},{2,0},{4,6},{6,4},{8,10},{10,8},{12,14},{14,12},{16,18},{18,... | collective-permute-start | bytes 1179656 | tf_op jit(solution)/shard_map/ppermute | solution.py:109
  328.5 22.4 %collective-permute-start.12 = (bf16[128,1792]{1,0:T(8,128)(2,1)S(1)}, bf16[128,1792]{1,0:T(8,128)(2,1)S(1)}, u32[]{:S(2)}, u32[]{:S(2)}) collective-permute-start(bf16[128,1792]{1,0:T(8,128)(2,1)S(1)} %pad_maximum_fusion.13), channel_id=1, source_target_pairs={{0,8},{2,10},{4,12},{6,14},{8,0},{10,2},{12,4},{14,6},{16,24},{18,... | collective-permute-start | bytes 1376264 | tf_op jit(solution)/shard_map/ppermute | solution.py:109
  328.6 23.3 %collective-permute-start.13 = (bf16[256,1152]{1,0:T(8,128)(2,1)S(1)}, bf16[256,1152]{1,0:T(8,128)(2,1)S(1)}, u32[]{:S(2)}, u32[]{:S(2)}) collective-permute-start(bf16[256,1152]{1,0:T(8,128)(2,1)S(1)} %broadcast_select_fusion.14), channel_id=1, source_target_pairs={{0,4},{2,6},{4,0},{6,2},{8,12},{10,14},{12,8},{14,10},{16,20},{18,... | collective-permute-start | bytes 1769480 | tf_op jit(solution)/shard_map/ppermute | solution.py:109
  352.4 4.9 %collective-permute-start.17 = (f32[16,1024]{1,0:T(8,128)S(1)}, f32[16,1024]{1,0:T(8,128)S(1)}, u32[]{:S(2)}, u32[]{:S(2)}) collective-permute-start(f32[16,1024]{1,0:T(8,128)S(1)} %concatenate.92), channel_id=1, source_target_pairs={{0,2},{2,0},{4,6},{6,4},{8,10},{10,8},{12,14},{14,12},{16,18},{18,... | collective-permute-start | bytes 196616 | tf_op jit(solution)/shard_map/ppermute | solution.py:109
  352.5 20.5 %copy-start.14 = (bf16[1024,1024]{1,0:T(8,128)(2,1)S(1)}, bf16[1024,1024]{1,0:T(8,128)(2,1)}, u32[]{:S(2)}) copy-start(bf16[1024,1024]{1,0:T(8,128)(2,1)} %get-tuple-element.156) | copy-start | bytes 6291460
  352.5 7.8 %collective-permute-start.16 = (bf16[256,384]{1,0:T(8,128)(2,1)S(1)}, bf16[256,384]{1,0:T(8,128)(2,1)S(1)}, u32[]{:S(2)}, u32[]{:S(2)}) collective-permute-start(bf16[256,384]{1,0:T(8,128)(2,1)S(1)} %broadcast_select_fusion.27), channel_id=1, source_target_pairs={{0,4},{2,6},{4,0},{6,2},{8,12},{10,14},{12,8},{14,10},{16,20},{18,... | collective-permute-start | bytes 589832 | tf_op jit(solution)/shard_map/ppermute | solution.py:109
  353.5 9.2 %collective-permute-start.15 = (bf16[128,1152]{1,0:T(8,128)(2,1)S(1)}, bf16[128,1152]{1,0:T(8,128)(2,1)S(1)}, u32[]{:S(2)}, u32[]{:S(2)}) collective-permute-start(bf16[128,1152]{1,0:T(8,128)(2,1)S(1)} %broadcast_select_fusion.21), channel_id=1, source_target_pairs={{0,8},{2,10},{4,12},{6,14},{8,0},{10,2},{12,4},{14,6},{16,24},{18,... | collective-permute-start | bytes 884744 | tf_op jit(solution)/shard_map/ppermute | solution.py:109
  354.7 14.1 %collective-permute-start.18 = (bf16[256,1024]{1,0:T(8,128)(2,1)S(1)}, bf16[256,1024]{1,0:T(8,128)(2,1)S(1)}, u32[]{:S(2)}, u32[]{:S(2)}) collective-permute-start(bf16[256,1024]{1,0:T(8,128)(2,1)S(1)} %slice.440), channel_id=1, source_target_pairs={{0,1},{1,0},{2,3},{3,2},{4,5},{5,4},{6,7},{7,6},{8,9},{9,8},{10,11... | collective-permute-start | bytes 1572872 | tf_op jit(solution)/shard_map/ppermute | solution.py:1023
  356.3 24.7 %collective-permute-start.25 = (bf16[256,1792]{1,0:T(8,128)(2,1)S(1)}, bf16[256,1792]{1,0:T(8,128)(2,1)S(1)}, u32[]{:S(2)}, u32[]{:S(2)}) collective-permute-start(bf16[256,1792]{1,0:T(8,128)(2,1)S(1)} %copy-done.43), channel_id=1, source_target_pairs={{0,4},{2,6},{4,0},{6,2},{8,12},{10,14},{12,8},{14,10},{16,20},{18,... | collective-permute-start | bytes 2752520 | tf_op jit(solution)/shard_map/ppermute | solution.py:109
  368.8 12.4 %copy-start.54 = (bf16[256,1024]{1,0:T(8,128)(2,1)}, bf16[256,1024]{1,0:T(8,128)(2,1)S(1)}, u32[]{:S(2)}) copy-start(bf16[256,1024]{1,0:T(8,128)(2,1)S(1)} %collective-permute-done.18) | copy-start | bytes 1572868
  368.8 12.1 %collective-permute-start.21 = (f32[16,1024]{1,0:T(8,128)S(1)}, f32[16,1024]{1,0:T(8,128)S(1)}, u32[]{:S(2)}, u32[]{:S(2)}) collective-permute-start(f32[16,1024]{1,0:T(8,128)S(1)} %add.383), channel_id=1, source_target_pairs={{0,4},{2,6},{4,0},{6,2},{8,12},{10,14},{12,8},{14,10},{16,20},{18,... | collective-permute-start | bytes 196616 | tf_op jit(solution)/shard_map/ppermute | solution.py:109
  369.9 11.0 %collective-permute-start.20 = (bf16[128,384]{1,0:T(8,128)(2,1)S(1)}, bf16[128,384]{1,0:T(8,128)(2,1)S(1)}, u32[]{:S(2)}, u32[]{:S(2)}) collective-permute-start(bf16[128,384]{1,0:T(8,128)(2,1)S(1)} %broadcast_select_fusion.29), channel_id=1, source_target_pairs={{0,8},{2,10},{4,12},{6,14},{8,0},{10,2},{12,4},{14,6},{16,24},{18,... | collective-permute-start | bytes 294920 | tf_op jit(solution)/shard_map/ppermute | solution.py:109
  371.7 9.3 %collective-permute-start.19 = (bf16[64,1152]{1,0:T(8,128)(2,1)S(1)}, bf16[64,1152]{1,0:T(8,128)(2,1)S(1)}, u32[]{:S(2)}, u32[]{:S(2)}) collective-permute-start(bf16[64,1152]{1,0:T(8,128)(2,1)S(1)} %broadcast_select_fusion.28), channel_id=1, source_target_pairs={{0,16},{2,18},{4,20},{6,22},{8,24},{10,26},{12,28},{14,30},{16,0},... | collective-permute-start | bytes 442376 | tf_op jit(solution)/shard_map/ppermute | solution.py:109
  373.0 12.4 %collective-permute-start.22 = (bf16[256,1024]{1,0:T(8,128)(2,1)S(1)}, bf16[256,1024]{1,0:T(8,128)(2,1)S(1)}, u32[]{:S(2)}, u32[]{:S(2)}) collective-permute-start(bf16[256,1024]{1,0:T(8,128)(2,1)S(1)} %slice.395), channel_id=1, source_target_pairs={{0,1},{1,0},{2,3},{3,2},{4,5},{5,4},{6,7},{7,6},{8,9},{9,8},{10,11... | collective-permute-start | bytes 1572872 | tf_op jit(solution)/shard_map/ppermute | solution.py:1023
  386.3 5.1 %collective-permute-start.23 = (bf16[64,384]{1,0:T(8,128)(2,1)S(1)}, bf16[64,384]{1,0:T(8,128)(2,1)S(1)}, u32[]{:S(2)}, u32[]{:S(2)}) collective-permute-start(bf16[64,384]{1,0:T(8,128)(2,1)S(1)} %broadcast_select_fusion.30), channel_id=1, source_target_pairs={{0,16},{2,18},{4,20},{6,22},{8,24},{10,26},{12,28},{14,30},{16,0},... | collective-permute-start | bytes 147464 | tf_op jit(solution)/shard_map/ppermute | solution.py:109
  389.1 4.3 collective-permute-start.24
  393.4 5.0 %collective-permute-start.26 = (bf16[64,384]{1,0:T(8,128)(2,1)S(1)}, bf16[64,384]{1,0:T(8,128)(2,1)S(1)}, u32[]{:S(2)}, u32[]{:S(2)}) collective-permute-start(bf16[64,384]{1,0:T(8,128)(2,1)S(1)} %pad_maximum_fusion.16), channel_id=1, source_target_pairs={{0,1},{1,0},{2,3},{3,2},{4,5},{5,4},{6,7},{7,6},{8,9},{9,8},{10,11... | collective-permute-start | bytes 147464 | tf_op jit(solution)/shard_map/ppermute | solution.py:1023
  396.6 8.8 %collective-permute-start.27 = (f32[16,1024]{1,0:T(8,128)S(1)}, f32[16,1024]{1,0:T(8,128)}, u32[]{:S(2)}, u32[]{:S(2)}) collective-permute-start(f32[16,1024]{1,0:T(8,128)S(1)} %add.388), channel_id=1, source_target_pairs={{0,16},{2,18},{4,20},{6,22},{8,24},{10,26},{12,28},{14,30},{16,0},... | collective-permute-start | bytes 196616 | tf_op jit(solution)/shard_map/ppermute | solution.py:109
  398.4 21.6 %collective-permute-start.32 = (bf16[512,1024]{1,0:T(8,128)(2,1)}, bf16[512,1024]{1,0:T(8,128)(2,1)S(1)}, u32[]{:S(2)}, u32[]{:S(2)}) collective-permute-start(bf16[512,1024]{1,0:T(8,128)(2,1)} %slice.401), channel_id=1, source_target_pairs={{0,1},{1,0},{2,3},{3,2},{4,5},{5,4},{6,7},{7,6},{8,9},{9,8},{10,11... | collective-permute-start | bytes 3145736 | tf_op jit(solution)/shard_map/ppermute | solution.py:1023
  406.2 8.6 %collective-permute-start.28 = (bf16[64,1664]{1,0:T(8,128)(2,1)S(1)}, bf16[64,1664]{1,0:T(8,128)(2,1)S(1)}, u32[]{:S(2)}, u32[]{:S(2)}) collective-permute-start(bf16[64,1664]{1,0:T(8,128)(2,1)S(1)} %concatenate.95), channel_id=1, source_target_pairs={{0,16},{2,18},{4,20},{6,22},{8,24},{10,26},{12,28},{14,30},{16,0},... | collective-permute-start | bytes 638984 | tf_op jit(solution)/shard_map/ppermute | solution.py:109
  406.3 23.8 %collective-permute-start.29 = (bf16[512,1792]{1,0:T(8,128)(2,1)}, bf16[512,1792]{1,0:T(8,128)(2,1)S(1)}, u32[]{:S(2)}, u32[]{:S(2)}) collective-permute-start(bf16[512,1792]{1,0:T(8,128)(2,1)} %pad_maximum_fusion.4), channel_id=1, source_target_pairs={{0,2},{2,0},{4,6},{6,4},{8,10},{10,8},{12,14},{14,12},{16,18},{18,... | collective-permute-start | bytes 5505032 | tf_op jit(solution)/shard_map/ppermute | solution.py:109
  430.6 8.2 %collective-permute-start.30 = (bf16[128,1664]{1,0:T(8,128)(2,1)S(1)}, bf16[128,1664]{1,0:T(8,128)(2,1)S(1)}, u32[]{:S(2)}, u32[]{:S(2)}) collective-permute-start(bf16[128,1664]{1,0:T(8,128)(2,1)S(1)} %pad_maximum_fusion.14), channel_id=1, source_target_pairs={{0,8},{2,10},{4,12},{6,14},{8,0},{10,2},{12,4},{14,6},{16,24},{18,... | collective-permute-start | bytes 1277960 | tf_op jit(solution)/shard_map/ppermute | solution.py:109
  439.0 15.2 %collective-permute-start.31 = (bf16[256,1664]{1,0:T(8,128)(2,1)S(1)}, bf16[256,1664]{1,0:T(8,128)(2,1)S(1)}, u32[]{:S(2)}, u32[]{:S(2)}) collective-permute-start(bf16[256,1664]{1,0:T(8,128)(2,1)S(1)} %pad_maximum_fusion.7), channel_id=1, source_target_pairs={{0,4},{2,6},{4,0},{6,2},{8,12},{10,14},{12,8},{14,10},{16,20},{18,... | collective-permute-start | bytes 2555912 | tf_op jit(solution)/shard_map/ppermute | solution.py:109
  454.5 8.9 %collective-permute-start.34 = (bf16[512,1664]{1,0:T(8,128)(2,1)S(1)}, bf16[512,1664]{1,0:T(8,128)(2,1)}, u32[]{:S(2)}, u32[]{:S(2)}) collective-permute-start(bf16[512,1664]{1,0:T(8,128)(2,1)S(1)} %pad_maximum_fusion.5), channel_id=1, source_target_pairs={{0,2},{2,0},{4,6},{6,4},{8,10},{10,8},{12,14},{14,12},{16,18},{18,... | collective-permute-start | bytes 5111816 | tf_op jit(solution)/shard_map/ppermute | solution.py:109
  454.5 4.5 collective-permute-start.33
  (74 other events, 305.7 us)
Sparse Core Ops, SparseCore 0:
  174.2 86.3 reduce-scatter.1
  269.8 77.1 all-gather.1

commit v8 on v7

--- a/solution.py
+++ b/solution.py
@@ -1363,7 +1363,7 @@
     small = small + jnp.where(is_shared, small_other, 0.0)
     late, early = tie(late, early)
     late = double(late, bits[2])
-    late, forward_total = tie(late, forward_total)
+    late, forward_total, normed_got[2] = tie(late, forward_total, normed_got[2])
     hidden_units = down_weight.shape[0]
     down_wgrad = forward_total[:hidden_units].astype(wide)
     gate_wgrad = forward_total[hidden_units : hidden_units + model].astype(wide)

time: 486 us -> 480 us (0.988)
    unnamed x179 -> x177, local copies, waits for them, and re-layouts: 14.7 us -> 14.7 us
  transfers between devices with their start and end apart: 37 -> 37, of which waited for: 22 -> 21; matrix products, arithmetic and copies ran while one was open for 34% -> 33% of each run, Pallas kernels for 13% -> 13%
where the time goes in v8:
time: 480 us; the launch traced here: 472 us
  waiting for transfers between devices  130 us (27%)
  other arithmetic  119 us (25%)
  Pallas kernels  73.8 us (15%)
  matrix products  65.7 us (14%)
  local copies, waits for them, and re-layouts  36.1 us (8%)
  starting transfers between devices  31.8 us (7%)
  between operations  16 us (3%)
    ppermute x24, waiting for transfers between devices, swap_bit(): return lax.ppermute(value, 'dp', [(i, i ^ bit) for i in range(size)])  72.2 us
    ppermute x8, waiting for transfers between devices, swap_pair(): return lax.ppermute(value, 'tensor', [(0, 1), (1, 0)])  49.4 us
    dot_general x12, matrix products, matmul(): return jnp.dot(left, right, preferred_element_type=jnp.float32)  29.6 us
    dot_general x9, matrix products, dot_nt(): lax.dot_general(left, right, (((1,), (1,)), ((), ())), preferred_element_...  27.1 us
    pallas_call x1, Pallas kernels, scan_back_call(): pl.pallas_call(scan_back_kernel, grid=(chunks,), in_specs=[by_chunk(LANES...  25.3 us
    ppermute x24, starting transfers between devices, swap_bit(): return lax.ppermute(value, 'dp', [(i, i ^ bit) for i in range(size)])  18.7 us
    unnamed x177, local copies, waits for them, and re-layouts  14.7 us
    pallas_call x1, Pallas kernels, attend_back_call(): pl.pallas_call(attend_back_kernel, out_shape=[jax.ShapeDtypeStruct((rows,...  13 us
  transfers between devices with their start and end apart: 37, of which 21 were waited for; matrix products, arithmetic and copies ran while one was open for 33% of the time, Pallas kernels for 13%

profile of v8, /device:TPU:0, one launch (start us, length us, event | category | flops | bytes accessed | tf_op | source)
XLA Modules:
  0.0 471.5 jit_solution(3225404053793010900)
XLA Ops:
  31.3 3.8 fusion.8
  35.0 12.9 %scan_forward.1 = (f32[1024,768]{1,0:T(8,128)}, bf16[4,128,768]{2,1,0:T(8,128)(2,1)}) custom-call(f32[1024,128]{1,0:T(8,128)} %get-tuple-element.371.step_ref, bf16[1024,256]{1,0:T(8,128)(2,1)} %get-tuple-element.301.coef_ref, f32[1024,768]{1,0:T(8,128)} %get-tuple-element.299.act_ref, f32[1024,128]{1,0:T(8,128)} %pad.127.seg_col_ref.aux_ref, ...), custom_call_target="tpu_custom_call" | custom-call | tf_op jit(solution)/shard_map/scan_forward/pallas_call | solution.py:673
  48.0 7.4 %multiply_reduce_fusion.9 = (f32[1024]{0:T(1024)S(1)}, f32[1024,768]{1,0:T(8,128)}, f32[1024,768]{1,0:T(8,128)}) fusion(f32[1024,768]{1,0:T(8,128)} %get-tuple-element.105, f32[1024,768]{1,0:T(8,128)S(1)} %get-tuple-element.300, f32[768]{0:T(1024)S(1)} %mul.806, bf16[1024,1024]{1,0:T(8,128)(2,1)} %copy-done.23, bf16[1024,768]{1,0:T(8,128)(2,1)S(1)} %copy-done.60), kind=kOutput, calls=%fused_computation.37 | convolution fusion | flops 1620835328 | bytes 16260096 | tf_op jit(solution)/shard_map/dot_general | solution.py:23
  55.4 2.9 collective-permute-start
  58.3 3.1 fusion.46
  61.5 3.4 fusion.75.query_ref
  66.4 3.3 fusion.42.keyval_ref
  71.5 10.8 %attend_forward.1 = (bf16[1024,256]{1,0:T(8,128)(2,1)}, bf16[1024,256]{1,0:T(8,128)(2,1)}, bf16[1024,256]{1,0:T(8,128)(2,1)}, f32[1024,128]{1,0:T(8,128)}) custom-call(f32[1024,256]{1,0:T(8,128)} %fusion.75.query_ref, f32[1024,128]{1,0:T(8,128)} %fusion.42.keyval_ref, f32[1,1024]{1,0:T(1,128)} %get-tuple-element.357.seg_ref, ...), custom_call_target="tpu_custom_call" | custom-call | tf_op jit(solution)/shard_map/attend_forward/pallas_call | solution.py:910
  90.1 4.6 convert_element_type.400
  95.4 7.8 %concatenate.83 = bf16[1024,2304]{1,0:T(8,128)(2,1)} concatenate(bf16[1024,768]{1,0:T(8,128)(2,1)} %param.31, bf16[1024,768]{1,0:T(8,128)(2,1)} %param.32, bf16[1024,128]{1,0:T(8,128)(2,1)} %pad.128.clone, bf16[1024,256]{1,0:T(8,128)(2,1)} %param.33, bf16[1024,256]{1,0:T(8,128)(2,1)} %param.28, bf16[1024,64]{1,0:T(8,128)(2,1)S(1)} %get-tuple-element.339, bf16[1024,64]{1,0:T(8,128)(2,1)} %copy-done.46), dimensions={1} | concatenate | bytes 9437184 | tf_op jit(solution)/shard_map/concatenate | solution.py:1184
  103.2 3.3 fusion.32
  110.0 5.5 %collective-permute-done.1 = bf16[512,1024]{1,0:T(8,128)(2,1)} collective-permute-done((bf16[512,1024]{1,0:T(8,128)(2,1)}, bf16[512,1024]{1,0:T(8,128)(2,1)}, u32[]{:S(2)}, u32[]{:S(2)}) %collective-permute-start.1) | collective-permute-done | bytes 1048608 | tf_op jit(solution)/shard_map/ppermute | solution.py:1023
  121.0 3.0 multiply_convert_fusion.4
  125.3 2.6 fusion.73
  128.0 8.5 %collective-permute-done.2 = bf16[512,1024]{1,0:T(8,128)(2,1)S(1)} collective-permute-done((bf16[512,1024]{1,0:T(8,128)(2,1)S(1)}, bf16[512,1024]{1,0:T(8,128)(2,1)S(1)}, u32[]{:S(2)}, u32[]{:S(2)}) %collective-permute-start.2) | collective-permute-done | bytes 1048608 | tf_op jit(solution)/shard_map/ppermute | solution.py:1023
  138.9 3.0 multiply_convert_fusion.3
  143.4 3.0 fusion.74
  146.4 14.4 %collective-permute-done.3 = bf16[512,1024]{1,0:T(8,128)(2,1)S(1)} collective-permute-done((bf16[512,1024]{1,0:T(8,128)(2,1)S(1)}, bf16[512,1024]{1,0:T(8,128)(2,1)S(1)}, u32[]{:S(2)}, u32[]{:S(2)}) %collective-permute-start.3) | collective-permute-done | bytes 1048608 | tf_op jit(solution)/shard_map/ppermute | solution.py:1023
  162.3 11.7 %weight_products.1 = bf16[3,1024,1024]{2,1,0:T(8,128)(2,1)} custom-call(bf16[512,1024]{1,0:T(8,128)(2,1)} %get-tuple-element.309.refs_0_, bf16[512,1024]{1,0:T(8,128)(2,1)} %get-tuple-element.306.refs_1_, bf16[512,1024]{1,0:T(8,128)(2,1)} %copy-done.37, bf16[512,1024]{1,0:T(8,128)(2,1)} %copy-done.38, bf16[512,1024]{1,0:T(8,128)(2,1)} %copy-done.65, ...), custom_call_target="tpu_custom_call" | custom-call | tf_op jit(solution)/shard_map/weight_products/pallas_call | solution.py:1081
  174.1 10.7 %collective-permute-done.4 = bf16[512,1024]{1,0:T(8,128)(2,1)} collective-permute-done((bf16[512,1024]{1,0:T(8,128)(2,1)}, bf16[512,1024]{1,0:T(8,128)(2,1)}, u32[]{:S(2)}, u32[]{:S(2)}) %collective-permute-start.4) | collective-permute-done | bytes 1048608 | tf_op jit(solution)/shard_map/ppermute | solution.py:1023
  184.8 6.4 %multiply_reduce_fusion.11 = (f32[1024]{0:T(1024)S(1)}, f32[512]{0:T(512)S(1)}, f32[512]{0:T(512)S(1)}, f32[1024]{0:T(1024)S(1)}) fusion(f32[512,1024]{1,0:T(8,128)} %get-tuple-element.375, f32[512,1024]{1,0:T(8,128)S(1)} %copy-done.7, f32[512]{0:T(512)S(1)} %add_rsqrt_fusion.3, f32[1024]{0:T(1024)S(1)} %convert_element_type.417, ...), kind=kLoop, calls=%fused_computation.62 | loop fusion | flops 9434112 | bytes 12603392 | tf_op jit(solution)/shard_map/reduce_sum | solution.py:1202
  191.9 4.4 fusion.65
  204.4 3.7 constant_dynamic-update-slice_fusion.6
  212.4 5.8 %fusion.23.grad_ref = f32[1024,768]{1,0:T(8,128)} fusion(f32[1024]{0:T(1024)S(1)} %add.361, f32[1024,768]{1,0:T(8,128)} %get-tuple-element.298, f32[1024,768]{1,0:T(8,128)} %copy-done.20, f32[1024]{0:T(1024)S(1)} %get-tuple-element.287, f32[768]{0:T(1024)S(1)} %convert_element_type.411, f32[1024]{0:T(1024)S(1)} %get-tuple-element.288, ...), kind=kLoop, calls=%fused_computation.95 | loop fusion | flops 8650752 | bytes 12598272 | tf_op jit(solution)/shard_map/mul | solution.py:1241
  224.3 3.2 convolution_convert_fusion.3.grad_ref
  227.5 25.3 %scan_backward.1 = (f32[1024,768]{1,0:T(8,128)}, f32[1024,128]{1,0:T(8,128)}, f32[1024,256]{1,0:T(8,128)}, f32[1,128]{1,0:T(1,128)}, f32[1,768]{1,0:T(1,128)}) custom-call(f32[1024,128]{1,0:T(8,128)} %get-tuple-element.371.step_ref, bf16[1024,256]{1,0:T(8,128)(2,1)} %get-tuple-element.301.coef_ref, f32[1024,768]{1,0:T(8,128)} %get-tuple-element.299.act_ref, ...), custom_call_target="tpu_custom_call" | custom-call | tf_op jit(solution)/shard_map/scan_backward/pallas_call | solution.py:815
  256.6 4.0 reduce-scatter.2.cloned.1.call-done
  260.6 9.0 %multiply_reduce_fusion.4 = (f32[768]{0:T(1024)S(1)}, f32[768]{0:T(1024)S(1)}, f32[768]{0:T(1024)S(1)}, f32[768]{0:T(1024)S(1)}, f32[768]{0:T(1024)S(1)}) fusion(f32[1024,768]{1,0:T(8,128)} %copy-done.17, f32[1024]{0:T(1024)S(1)} %bitcast.104, f32[1024]{0:T(1024)S(1)} %bitcast.98, f32[1024]{0:T(1024)S(1)} %bitcast.92, f32[1024,768]{1,0:T(8,128)} %get-tuple-element.122, ...), kind=kLoop, calls=%fused_computation.28 | loop fusion | flops 15724800 | bytes 9464832 | tf_op jit(solution)/shard_map/reduce_sum | solution.py:1045
  274.7 12.6 %collective-permute-done.8 = bf16[128,1792]{1,0:T(8,128)(2,1)S(1)} collective-permute-done((bf16[128,1792]{1,0:T(8,128)(2,1)S(1)}, bf16[128,1792]{1,0:T(8,128)(2,1)S(1)}, u32[]{:S(2)}, u32[]{:S(2)}) %collective-permute-start.8) | collective-permute-done | bytes 458784 | tf_op jit(solution)/shard_map/ppermute | solution.py:109
  290.1 2.6 constant_dynamic-update-slice_fusion.5
  295.4 3.3 convolution_convert_fusion
  298.8 5.1 %collective-permute-done.9 = bf16[64,1792]{1,0:T(8,128)(2,1)S(1)} collective-permute-done((bf16[64,1792]{1,0:T(8,128)(2,1)S(1)}, bf16[64,1792]{1,0:T(8,128)(2,1)S(1)}, u32[]{:S(2)}, u32[]{:S(2)}) %collective-permute-start.9) | collective-permute-done | bytes 229408 | tf_op jit(solution)/shard_map/ppermute | solution.py:109
  305.3 13.0 %attend_backward.1 = (bf16[1024,256]{1,0:T(8,128)(2,1)}, bf16[1024,128]{1,0:T(8,128)(2,1)}) custom-call(bf16[1024,256]{1,0:T(8,128)(2,1)} %get-tuple-element.127.query_ref, bf16[1024,256]{1,0:T(8,128)(2,1)} %get-tuple-element.128.both_ref, f32[1,1024]{1,0:T(1,128)} %get-tuple-element.357.seg_ref, f32[1024,128]{1,0:T(8,128)} %pad.127.seg_col_ref.aux_ref, ...), custom_call_target="tpu_custom_call" | custom-call | tf_op jit(solution)/shard_map/attend_backward/pallas_call | solution.py:974
  321.7 5.5 %collective-permute-done.10 = bf16[64,1792]{1,0:T(8,128)(2,1)S(1)} collective-permute-done((bf16[64,1792]{1,0:T(8,128)(2,1)S(1)}, bf16[64,1792]{1,0:T(8,128)(2,1)S(1)}, u32[]{:S(2)}, u32[]{:S(2)}) %collective-permute-start.10) | collective-permute-done | bytes 229408 | tf_op jit(solution)/shard_map/ppermute | solution.py:109
  328.1 2.9 collective-permute-start.13
  331.2 8.7 %multiply_reduce_fusion.1 = (f32[1024]{0:T(1024)S(1)}, bf16[1024,1024]{1,0:T(8,128)(2,1)}) fusion(bf16[1024,1024]{1,0:T(8,128)(2,1)S(1)} %copy-done.2, f32[1024]{0:T(1024)S(1)} %copy-done.74, bf16[1024,2304]{1,0:T(8,128)(2,1)S(1)} %constant_dynamic-update-slice_fusion.2, bf16[1024,2304]{1,0:T(8,128)(2,1)} %concatenate.83), kind=kOutput, calls=%fused_computation.3 | convolution fusion | flops 4837080064 | bytes 13639680 | tf_op jit(solution)/shard_map/dot_general | solution.py:594
  340.1 10.5 %collective-permute-done.12 = bf16[128,1792]{1,0:T(8,128)(2,1)S(1)} collective-permute-done((bf16[128,1792]{1,0:T(8,128)(2,1)S(1)}, bf16[128,1792]{1,0:T(8,128)(2,1)S(1)}, u32[]{:S(2)}, u32[]{:S(2)}) %collective-permute-start.12) | collective-permute-done | bytes 458784 | tf_op jit(solution)/shard_map/ppermute | solution.py:109
  357.3 2.7 collective-permute-done.16
  362.6 6.0 %collective-permute-done.18 = bf16[256,1024]{1,0:T(8,128)(2,1)S(1)} collective-permute-done((bf16[256,1024]{1,0:T(8,128)(2,1)S(1)}, bf16[256,1024]{1,0:T(8,128)(2,1)S(1)}, u32[]{:S(2)}, u32[]{:S(2)}) %collective-permute-start.18) | collective-permute-done | bytes 524320 | tf_op jit(solution)/shard_map/ppermute | solution.py:1023
  374.5 6.1 %collective-permute-done.21 = f32[16,1024]{1,0:T(8,128)S(1)} collective-permute-done((f32[16,1024]{1,0:T(8,128)S(1)}, f32[16,1024]{1,0:T(8,128)S(1)}, u32[]{:S(2)}, u32[]{:S(2)}) %collective-permute-start.21) | collective-permute-done | bytes 65568 | tf_op jit(solution)/shard_map/ppermute | solution.py:109
  380.9 4.3 collective-permute-done.22
  397.8 4.1 collective-permute-done.27
  403.3 11.5 %collective-permute-done.28 = bf16[64,1664]{1,0:T(8,128)(2,1)S(1)} collective-permute-done((bf16[64,1664]{1,0:T(8,128)(2,1)S(1)}, bf16[64,1664]{1,0:T(8,128)(2,1)S(1)}, u32[]{:S(2)}, u32[]{:S(2)}) %collective-permute-start.28) | collective-permute-done | bytes 213024 | tf_op jit(solution)/shard_map/ppermute | solution.py:109
  420.6 6.7 %collective-permute-done.30 = bf16[128,1664]{1,0:T(8,128)(2,1)S(1)} collective-permute-done((bf16[128,1664]{1,0:T(8,128)(2,1)S(1)}, bf16[128,1664]{1,0:T(8,128)(2,1)S(1)}, u32[]{:S(2)}, u32[]{:S(2)}) %collective-permute-start.30) | collective-permute-done | bytes 426016 | tf_op jit(solution)/shard_map/ppermute | solution.py:109
  430.1 8.0 %slice_convert_fusion = (f32[1024,1024]{1,0:T(8,128)}, f32[1024,1024]{1,0:T(8,128)}, f32[1024,1024]{1,0:T(8,128)}) fusion(bf16[3072,1024]{1,0:T(8,128)(2,1)} %all-gather.2.cloned.1.call-done), kind=kLoop, calls=%fused_computation.58 | loop fusion | flops 3145728 | bytes 18874368 | tf_op jit(solution)/shard_map/convert_element_type | solution.py:1368
  438.1 2.5 multiply_reduce_fusion
  440.7 6.8 %maximum_add_fusion = f32[1024,1024]{1,0:T(8,128)} fusion(f32[512,1024]{1,0:T(8,128)S(1)} %copy-done.29, f32[512,1024]{1,0:T(8,128)S(1)} %copy-done.28, bf16[1024,1024]{1,0:T(8,128)(2,1)S(1)} %copy-done.15, bf16[1024,1024]{1,0:T(8,128)(2,1)S(1)} %copy-done.2, f32[1024]{0:T(1024)S(1)} %broadcast_multiply_fusion.6, f32[1024]{0:T(1024)S(1)} %copy-done.72, ...), kind=kLoop, calls=%fused_computation | loop fusion | flops 16777216 | bytes 14692352 | tf_op jit(solution)/shard_map/add | solution.py:1382
  449.7 4.1 collective-permute-done.33
  (401 shorter events, 141.0 us)
Async XLA Ops:
  7.2 113.8 %copy-start = (bf16[1024,1024]{1,0:T(8,128)(2,1)S(1)}, bf16[1024,1024]{1,0:T(8,128)(2,1)}, u32[]{:S(2)}) copy-start(bf16[1024,1024]{1,0:T(8,128)(2,1)} %param.46) | copy-start | bytes 6291460
  7.2 253.4 %reduce-scatter.2.cloned.1.call-start = ((), (), s32[]{:S(2)}) async-start(), calls=%async_computation.1 | async-start | bytes 6684672 | tf_op jit(solution)/shard_map/reduce_scatter | solution.py:1218
  35.0 12.9 %copy-start.3 = (f32[1024,768]{1,0:T(8,128)}, f32[1024,768]{1,0:T(8,128)S(1)}, u32[]{:S(2)}) copy-start(f32[1024,768]{1,0:T(8,128)S(1)} %get-tuple-element.300) | copy-start | bytes 9437188
  35.0 12.9 %copy-start.60 = (bf16[1024,768]{1,0:T(8,128)(2,1)S(1)}, bf16[1024,768]{1,0:T(8,128)(2,1)}, u32[]{:S(2)}) copy-start(bf16[1024,768]{1,0:T(8,128)(2,1)} %param.31) | copy-start | bytes 4718596
  55.4 27.0 %collective-permute-start = (f32[1024]{0:T(1024)S(1)}, f32[1024]{0:T(1024)S(1)}, u32[]{:S(2)}, u32[]{:S(2)}) collective-permute-start(f32[1024]{0:T(1024)S(1)} %get-tuple-element.297), channel_id=1, source_target_pairs={{0,1},{1,0},{2,3},{3,2},{4,5},{5,4},{6,7},{7,6},{8,9},{9,8},{10,11... | collective-permute-start | bytes 12296 | tf_op jit(solution)/shard_map/ppermute | solution.py:102
  69.7 12.7 %copy-start.10 = (f32[1024,768]{1,0:T(8,128)S(1)}, f32[1024,768]{1,0:T(8,128)}, u32[]{:S(2)}) copy-start(f32[1024,768]{1,0:T(8,128)} %get-tuple-element.298) | copy-start | bytes 9437188
  89.2 26.4 %collective-permute-start.1 = (bf16[512,1024]{1,0:T(8,128)(2,1)}, bf16[512,1024]{1,0:T(8,128)(2,1)}, u32[]{:S(2)}, u32[]{:S(2)}) collective-permute-start(bf16[512,1024]{1,0:T(8,128)(2,1)} %get-tuple-element.325), channel_id=1, source_target_pairs={{0,1},{1,0},{2,3},{3,2},{4,5},{5,4},{6,7},{7,6},{8,9},{9,8},{10,11... | collective-permute-start | bytes 3145736 | tf_op jit(solution)/shard_map/ppermute | solution.py:1023
  108.0 28.5 %collective-permute-start.2 = (bf16[512,1024]{1,0:T(8,128)(2,1)S(1)}, bf16[512,1024]{1,0:T(8,128)(2,1)S(1)}, u32[]{:S(2)}, u32[]{:S(2)}) collective-permute-start(bf16[512,1024]{1,0:T(8,128)(2,1)S(1)} %copy-done.68), channel_id=1, source_target_pairs={{0,1},{1,0},{2,3},{3,2},{4,5},{5,4},{6,7},{7,6},{8,9},{9,8},{10,11... | collective-permute-start | bytes 3145736 | tf_op jit(solution)/shard_map/ppermute | solution.py:1023
  137.0 23.8 %collective-permute-start.3 = (bf16[512,1024]{1,0:T(8,128)(2,1)S(1)}, bf16[512,1024]{1,0:T(8,128)(2,1)S(1)}, u32[]{:S(2)}, u32[]{:S(2)}) collective-permute-start(bf16[512,1024]{1,0:T(8,128)(2,1)S(1)} %get-tuple-element.107), channel_id=1, source_target_pairs={{0,1},{1,0},{2,3},{3,2},{4,5},{5,4},{6,7},{7,6},{8,9},{9,8},{10,11... | collective-permute-start | bytes 3145736 | tf_op jit(solution)/shard_map/ppermute | solution.py:1023
  161.7 23.1 %collective-permute-start.4 = (bf16[512,1024]{1,0:T(8,128)(2,1)}, bf16[512,1024]{1,0:T(8,128)(2,1)}, u32[]{:S(2)}, u32[]{:S(2)}) collective-permute-start(bf16[512,1024]{1,0:T(8,128)(2,1)} %get-tuple-element.110), channel_id=1, source_target_pairs={{0,1},{1,0},{2,3},{3,2},{4,5},{5,4},{6,7},{7,6},{8,9},{9,8},{10,11... | collective-permute-start | bytes 3145736 | tf_op jit(solution)/shard_map/ppermute | solution.py:1023
  174.1 10.8 %copy-start.7 = (f32[512,1024]{1,0:T(8,128)S(1)}, f32[512,1024]{1,0:T(8,128)}, u32[]{:S(2)}) copy-start(f32[512,1024]{1,0:T(8,128)} %copy-done.6) | copy-start | bytes 6291460
  174.1 254.3 %all-gather.2.cloned.1.call-start = ((), (), s32[]{:S(2)}) async-start(), calls=%async_computation.2 | async-start | bytes 6684672 | tf_op jit(solution)/shard_map/all_gather | solution.py:1256
  198.6 4.6 collective-permute-start.5
  212.3 5.8 %collective-permute-start.6 = (bf16[512,1792]{1,0:T(8,128)(2,1)}, bf16[512,1792]{1,0:T(8,128)(2,1)S(1)}, u32[]{:S(2)}, u32[]{:S(2)}) collective-permute-start(bf16[512,1792]{1,0:T(8,128)(2,1)} %pad_maximum_fusion.3), channel_id=1, source_target_pairs={{0,2},{2,0},{4,6},{6,4},{8,10},{10,8},{12,14},{14,12},{16,18},{18,... | collective-permute-start | bytes 5505032 | tf_op jit(solution)/shard_map/ppermute | solution.py:109
  222.4 31.8 %collective-permute-start.7 = (bf16[256,1792]{1,0:T(8,128)(2,1)}, bf16[256,1792]{1,0:T(8,128)(2,1)}, u32[]{:S(2)}, u32[]{:S(2)}) collective-permute-start(bf16[256,1792]{1,0:T(8,128)(2,1)} %broadcast_select_fusion.9), channel_id=1, source_target_pairs={{0,4},{2,6},{4,0},{6,2},{8,12},{10,14},{12,8},{14,10},{16,20},{18,... | collective-permute-start | bytes 2752520 | tf_op jit(solution)/shard_map/ppermute | solution.py:109
  269.6 17.8 %copy-start.18 = (f32[1024,768]{1,0:T(8,128)S(1)}, f32[1024,768]{1,0:T(8,128)}, u32[]{:S(2)}) copy-start(f32[1024,768]{1,0:T(8,128)} %get-tuple-element.122) | copy-start | bytes 9437188
  269.7 17.6 %collective-permute-start.8 = (bf16[128,1792]{1,0:T(8,128)(2,1)S(1)}, bf16[128,1792]{1,0:T(8,128)(2,1)S(1)}, u32[]{:S(2)}, u32[]{:S(2)}) collective-permute-start(bf16[128,1792]{1,0:T(8,128)(2,1)S(1)} %broadcast_select_fusion.17), channel_id=1, source_target_pairs={{0,8},{2,10},{4,12},{6,14},{8,0},{10,2},{12,4},{14,6},{16,24},{18,... | collective-permute-start | bytes 1376264 | tf_op jit(solution)/shard_map/ppermute | solution.py:109
  272.3 15.2 %copy-start.5 = (f32[1024,768]{1,0:T(8,128)S(1)}, f32[1024,768]{1,0:T(8,128)}, u32[]{:S(2)}) copy-start(f32[1024,768]{1,0:T(8,128)} %copy-done.3) | copy-start | bytes 9437188
  289.2 14.8 %collective-permute-start.9 = (bf16[64,1792]{1,0:T(8,128)(2,1)S(1)}, bf16[64,1792]{1,0:T(8,128)(2,1)S(1)}, u32[]{:S(2)}, u32[]{:S(2)}) collective-permute-start(bf16[64,1792]{1,0:T(8,128)(2,1)S(1)} %broadcast_select_fusion.24), channel_id=1, source_target_pairs={{0,16},{2,18},{4,20},{6,22},{8,24},{10,26},{12,28},{14,30},{16,0},... | collective-permute-start | bytes 688136 | tf_op jit(solution)/shard_map/ppermute | solution.py:109
  304.1 23.1 %collective-permute-start.10 = (bf16[64,1792]{1,0:T(8,128)(2,1)S(1)}, bf16[64,1792]{1,0:T(8,128)(2,1)S(1)}, u32[]{:S(2)}, u32[]{:S(2)}) collective-permute-start(bf16[64,1792]{1,0:T(8,128)(2,1)S(1)} %add_convert_fusion.8), channel_id=1, source_target_pairs={{0,16},{2,18},{4,20},{6,22},{8,24},{10,26},{12,28},{14,30},{16,0},... | collective-permute-start | bytes 688136 | tf_op jit(solution)/shard_map/ppermute | solution.py:109
  305.3 22.0 %collective-permute-start.11 = (bf16[512,1152]{1,0:T(8,128)(2,1)}, bf16[512,1152]{1,0:T(8,128)(2,1)S(1)}, u32[]{:S(2)}, u32[]{:S(2)}) collective-permute-start(bf16[512,1152]{1,0:T(8,128)(2,1)} %broadcast_select_fusion.4), channel_id=1, source_target_pairs={{0,2},{2,0},{4,6},{6,4},{8,10},{10,8},{12,14},{14,12},{16,18},{18,... | collective-permute-start | bytes 3538952 | tf_op jit(solution)/shard_map/ppermute | solution.py:109
  320.4 10.6 %slice-start = ((s8[4718592]{0:T(1024)(128)(4,1)}), s8[4194304]{0:T(1024)(128)(4,1)S(1)}, s32[]{:S(2)}) async-start(s8[4718592]{0:T(1024)(128)(4,1)} %bitcast.88), calls=%async_computation.3 | async-start | bytes 8388608
  327.8 12.1 %collective-permute-start.14 = (bf16[512,384]{1,0:T(8,128)(2,1)S(1)}, bf16[512,384]{1,0:T(8,128)(2,1)S(1)}, u32[]{:S(2)}, u32[]{:S(2)}) collective-permute-start(bf16[512,384]{1,0:T(8,128)(2,1)S(1)} %broadcast_select_fusion.20), channel_id=1, source_target_pairs={{0,2},{2,0},{4,6},{6,4},{8,10},{10,8},{12,14},{14,12},{16,18},{18,... | collective-permute-start | bytes 1179656 | tf_op jit(solution)/shard_map/ppermute | solution.py:109
  327.9 22.6 %collective-permute-start.12 = (bf16[128,1792]{1,0:T(8,128)(2,1)S(1)}, bf16[128,1792]{1,0:T(8,128)(2,1)S(1)}, u32[]{:S(2)}, u32[]{:S(2)}) collective-permute-start(bf16[128,1792]{1,0:T(8,128)(2,1)S(1)} %pad_maximum_fusion.13), channel_id=1, source_target_pairs={{0,8},{2,10},{4,12},{6,14},{8,0},{10,2},{12,4},{14,6},{16,24},{18,... | collective-permute-start | bytes 1376264 | tf_op jit(solution)/shard_map/ppermute | solution.py:109
  328.1 23.5 %collective-permute-start.13 = (bf16[256,1152]{1,0:T(8,128)(2,1)S(1)}, bf16[256,1152]{1,0:T(8,128)(2,1)S(1)}, u32[]{:S(2)}, u32[]{:S(2)}) collective-permute-start(bf16[256,1152]{1,0:T(8,128)(2,1)S(1)} %broadcast_select_fusion.14), channel_id=1, source_target_pairs={{0,4},{2,6},{4,0},{6,2},{8,12},{10,14},{12,8},{14,10},{16,20},{18,... | collective-permute-start | bytes 1769480 | tf_op jit(solution)/shard_map/ppermute | solution.py:109
  352.0 5.3 %collective-permute-start.17 = (f32[16,1024]{1,0:T(8,128)S(1)}, f32[16,1024]{1,0:T(8,128)S(1)}, u32[]{:S(2)}, u32[]{:S(2)}) collective-permute-start(f32[16,1024]{1,0:T(8,128)S(1)} %concatenate.92), channel_id=1, source_target_pairs={{0,2},{2,0},{4,6},{6,4},{8,10},{10,8},{12,14},{14,12},{16,18},{18,... | collective-permute-start | bytes 196616 | tf_op jit(solution)/shard_map/ppermute | solution.py:109
  352.2 20.6 %copy-start.14 = (bf16[1024,1024]{1,0:T(8,128)(2,1)S(1)}, bf16[1024,1024]{1,0:T(8,128)(2,1)}, u32[]{:S(2)}) copy-start(bf16[1024,1024]{1,0:T(8,128)(2,1)} %get-tuple-element.157) | copy-start | bytes 6291460
  352.2 7.8 %collective-permute-start.16 = (bf16[256,384]{1,0:T(8,128)(2,1)S(1)}, bf16[256,384]{1,0:T(8,128)(2,1)S(1)}, u32[]{:S(2)}, u32[]{:S(2)}) collective-permute-start(bf16[256,384]{1,0:T(8,128)(2,1)S(1)} %broadcast_select_fusion.27), channel_id=1, source_target_pairs={{0,4},{2,6},{4,0},{6,2},{8,12},{10,14},{12,8},{14,10},{16,20},{18,... | collective-permute-start | bytes 589832 | tf_op jit(solution)/shard_map/ppermute | solution.py:109
  353.3 9.2 %collective-permute-start.15 = (bf16[128,1152]{1,0:T(8,128)(2,1)S(1)}, bf16[128,1152]{1,0:T(8,128)(2,1)S(1)}, u32[]{:S(2)}, u32[]{:S(2)}) collective-permute-start(bf16[128,1152]{1,0:T(8,128)(2,1)S(1)} %broadcast_select_fusion.21), channel_id=1, source_target_pairs={{0,8},{2,10},{4,12},{6,14},{8,0},{10,2},{12,4},{14,6},{16,24},{18,... | collective-permute-start | bytes 884744 | tf_op jit(solution)/shard_map/ppermute | solution.py:109
  354.5 14.1 %collective-permute-start.18 = (bf16[256,1024]{1,0:T(8,128)(2,1)S(1)}, bf16[256,1024]{1,0:T(8,128)(2,1)S(1)}, u32[]{:S(2)}, u32[]{:S(2)}) collective-permute-start(bf16[256,1024]{1,0:T(8,128)(2,1)S(1)} %slice.440), channel_id=1, source_target_pairs={{0,1},{1,0},{2,3},{3,2},{4,5},{5,4},{6,7},{7,6},{8,9},{9,8},{10,11... | collective-permute-start | bytes 1572872 | tf_op jit(solution)/shard_map/ppermute | solution.py:1023
  356.2 24.5 %collective-permute-start.25 = (bf16[256,1792]{1,0:T(8,128)(2,1)S(1)}, bf16[256,1792]{1,0:T(8,128)(2,1)S(1)}, u32[]{:S(2)}, u32[]{:S(2)}) collective-permute-start(bf16[256,1792]{1,0:T(8,128)(2,1)S(1)} %copy-done.42), channel_id=1, source_target_pairs={{0,4},{2,6},{4,0},{6,2},{8,12},{10,14},{12,8},{14,10},{16,20},{18,... | collective-permute-start | bytes 2752520 | tf_op jit(solution)/shard_map/ppermute | solution.py:109
  368.6 12.3 %copy-start.54 = (bf16[256,1024]{1,0:T(8,128)(2,1)}, bf16[256,1024]{1,0:T(8,128)(2,1)S(1)}, u32[]{:S(2)}) copy-start(bf16[256,1024]{1,0:T(8,128)(2,1)S(1)} %collective-permute-done.18) | copy-start | bytes 1572868
  368.6 12.0 %collective-permute-start.21 = (f32[16,1024]{1,0:T(8,128)S(1)}, f32[16,1024]{1,0:T(8,128)S(1)}, u32[]{:S(2)}, u32[]{:S(2)}) collective-permute-start(f32[16,1024]{1,0:T(8,128)S(1)} %add.383), channel_id=1, source_target_pairs={{0,4},{2,6},{4,0},{6,2},{8,12},{10,14},{12,8},{14,10},{16,20},{18,... | collective-permute-start | bytes 196616 | tf_op jit(solution)/shard_map/ppermute | solution.py:109
  369.6 11.0 %collective-permute-start.20 = (bf16[128,384]{1,0:T(8,128)(2,1)S(1)}, bf16[128,384]{1,0:T(8,128)(2,1)S(1)}, u32[]{:S(2)}, u32[]{:S(2)}) collective-permute-start(bf16[128,384]{1,0:T(8,128)(2,1)S(1)} %broadcast_select_fusion.29), channel_id=1, source_target_pairs={{0,8},{2,10},{4,12},{6,14},{8,0},{10,2},{12,4},{14,6},{16,24},{18,... | collective-permute-start | bytes 294920 | tf_op jit(solution)/shard_map/ppermute | solution.py:109
  371.5 9.2 %collective-permute-start.19 = (bf16[64,1152]{1,0:T(8,128)(2,1)S(1)}, bf16[64,1152]{1,0:T(8,128)(2,1)S(1)}, u32[]{:S(2)}, u32[]{:S(2)}) collective-permute-start(bf16[64,1152]{1,0:T(8,128)(2,1)S(1)} %broadcast_select_fusion.28), channel_id=1, source_target_pairs={{0,16},{2,18},{4,20},{6,22},{8,24},{10,26},{12,28},{14,30},{16,0},... | collective-permute-start | bytes 442376 | tf_op jit(solution)/shard_map/ppermute | solution.py:109
  372.9 12.3 %collective-permute-start.22 = (bf16[256,1024]{1,0:T(8,128)(2,1)S(1)}, bf16[256,1024]{1,0:T(8,128)(2,1)S(1)}, u32[]{:S(2)}, u32[]{:S(2)}) collective-permute-start(bf16[256,1024]{1,0:T(8,128)(2,1)S(1)} %slice.395), channel_id=1, source_target_pairs={{0,1},{1,0},{2,3},{3,2},{4,5},{5,4},{6,7},{7,6},{8,9},{9,8},{10,11... | collective-permute-start | bytes 1572872 | tf_op jit(solution)/shard_map/ppermute | solution.py:1023
  386.0 5.1 %collective-permute-start.23 = (bf16[64,384]{1,0:T(8,128)(2,1)S(1)}, bf16[64,384]{1,0:T(8,128)(2,1)S(1)}, u32[]{:S(2)}, u32[]{:S(2)}) collective-permute-start(bf16[64,384]{1,0:T(8,128)(2,1)S(1)} %broadcast_select_fusion.30), channel_id=1, source_target_pairs={{0,16},{2,18},{4,20},{6,22},{8,24},{10,26},{12,28},{14,30},{16,0},... | collective-permute-start | bytes 147464 | tf_op jit(solution)/shard_map/ppermute | solution.py:109
  388.8 4.3 collective-permute-start.24
  393.1 4.4 collective-permute-start.26
  396.0 5.9 %collective-permute-start.27 = (f32[16,1024]{1,0:T(8,128)S(1)}, f32[16,1024]{1,0:T(8,128)S(1)}, u32[]{:S(2)}, u32[]{:S(2)}) collective-permute-start(f32[16,1024]{1,0:T(8,128)S(1)} %add.388), channel_id=1, source_target_pairs={{0,16},{2,18},{4,20},{6,22},{8,24},{10,26},{12,28},{14,30},{16,0},... | collective-permute-start | bytes 196616 | tf_op jit(solution)/shard_map/ppermute | solution.py:109
  397.8 17.1 %copy-start.31 = (bf16[512,1792]{1,0:T(8,128)(2,1)S(1)}, bf16[512,1792]{1,0:T(8,128)(2,1)}, u32[]{:S(2)}) copy-start(bf16[512,1792]{1,0:T(8,128)(2,1)} %pad_maximum_fusion.4) | copy-start | bytes 5505028
  401.9 12.9 %collective-permute-start.29 = (bf16[512,1792]{1,0:T(8,128)(2,1)}, bf16[512,1792]{1,0:T(8,128)(2,1)S(1)}, u32[]{:S(2)}, u32[]{:S(2)}) collective-permute-start(bf16[512,1792]{1,0:T(8,128)(2,1)} %pad_maximum_fusion.4), channel_id=1, source_target_pairs={{0,2},{2,0},{4,6},{6,4},{8,10},{10,8},{12,14},{14,12},{16,18},{18,... | collective-permute-start | bytes 5505032 | tf_op jit(solution)/shard_map/ppermute | solution.py:109
  402.0 12.8 %collective-permute-start.28 = (bf16[64,1664]{1,0:T(8,128)(2,1)S(1)}, bf16[64,1664]{1,0:T(8,128)(2,1)S(1)}, u32[]{:S(2)}, u32[]{:S(2)}) collective-permute-start(bf16[64,1664]{1,0:T(8,128)(2,1)S(1)} %concatenate.95), channel_id=1, source_target_pairs={{0,16},{2,18},{4,20},{6,22},{8,24},{10,26},{12,28},{14,30},{16,0},... | collective-permute-start | bytes 638984 | tf_op jit(solution)/shard_map/ppermute | solution.py:109
  402.9 25.4 %collective-permute-start.31 = (bf16[512,1024]{1,0:T(8,128)(2,1)}, bf16[512,1024]{1,0:T(8,128)(2,1)S(1)}, u32[]{:S(2)}, u32[]{:S(2)}) collective-permute-start(bf16[512,1024]{1,0:T(8,128)(2,1)} %slice.401), channel_id=1, source_target_pairs={{0,1},{1,0},{2,3},{3,2},{4,5},{5,4},{6,7},{7,6},{8,9},{9,8},{10,11... | collective-permute-start | bytes 3145736 | tf_op jit(solution)/shard_map/ppermute | solution.py:1023
  415.4 11.9 %collective-permute-start.30 = (bf16[128,1664]{1,0:T(8,128)(2,1)S(1)}, bf16[128,1664]{1,0:T(8,128)(2,1)S(1)}, u32[]{:S(2)}, u32[]{:S(2)}) collective-permute-start(bf16[128,1664]{1,0:T(8,128)(2,1)S(1)} %pad_maximum_fusion.14), channel_id=1, source_target_pairs={{0,8},{2,10},{4,12},{6,14},{8,0},{10,2},{12,4},{14,6},{16,24},{18,... | collective-permute-start | bytes 1277960 | tf_op jit(solution)/shard_map/ppermute | solution.py:109
  428.4 20.5 %collective-permute-start.32 = (bf16[256,1664]{1,0:T(8,128)(2,1)}, bf16[256,1664]{1,0:T(8,128)(2,1)S(1)}, u32[]{:S(2)}, u32[]{:S(2)}) collective-permute-start(bf16[256,1664]{1,0:T(8,128)(2,1)} %pad_maximum_fusion.7), channel_id=1, source_target_pairs={{0,4},{2,6},{4,0},{6,2},{8,12},{10,14},{12,8},{14,10},{16,20},{18,... | collective-permute-start | bytes 2555912 | tf_op jit(solution)/shard_map/ppermute | solution.py:109
  449.2 8.9 %collective-permute-start.34 = (bf16[512,1664]{1,0:T(8,128)(2,1)S(1)}, bf16[512,1664]{1,0:T(8,128)(2,1)}, u32[]{:S(2)}, u32[]{:S(2)}) collective-permute-start(bf16[512,1664]{1,0:T(8,128)(2,1)S(1)} %pad_maximum_fusion.5), channel_id=1, source_target_pairs={{0,2},{2,0},{4,6},{6,4},{8,10},{10,8},{12,14},{14,12},{16,18},{18,... | collective-permute-start | bytes 5111816 | tf_op jit(solution)/shard_map/ppermute | solution.py:109
  449.2 4.5 collective-permute-start.33
  (73 other events, 301.6 us)
Sparse Core Ops, SparseCore 0:
  174.2 86.3 reduce-scatter.1
  269.8 77.0 all-gather.1
